TPU v7x, 32 devices: a whole 2x2x4 slice. The times are simulated.
32 devices in a mesh: dp: 4 (over y, x), seq: 2 (over core), head: 4 (over z).
Axes of the slice: x: 2, y: 2, z: 4, core: 2. Of those that a mesh axis runs over, the one named last changes fastest.
Arguments:
- tokens: bfloat16 [4, 1024, 1024], P('dp', 'seq'), may hold values from -6 to 6
- qkv_weight: bfloat16 [2, 1024, 3072], P(None, ('dp', 'seq'), 'head'), may hold values from -0.1875 to 0.1875
- dense_weight: bfloat16 [2, 1024, 1024], P(None, 'head', ('dp', 'seq')), may hold values from -0.75 to 0.75
- up_weight: bfloat16 [2, 1024, 4096], P(None, ('dp', 'seq'), 'head'), may hold values from -0.1875 to 0.1875
- down_weight: bfloat16 [2, 4096, 1024], P(None, 'head', ('dp', 'seq')), may hold values from -0.125 to 0.125
- first_gain: float32 [2, 1024], P(None, ('dp', 'seq')), may hold values from 0.25 to 1.75
- first_shift: float32 [2, 1024], P(None, ('dp', 'seq')), may hold values from -4 to 4
- query_bias: float32 [2, 16, 64], P(None, 'head', ('dp', 'seq')), may hold values from -6 to 6
- value_bias: float32 [2, 16, 64], P(None, 'head', ('dp', 'seq')), may hold values from -6 to 6
- dense_bias: float32 [2, 1024], P(None, ('dp', 'seq')), may hold values from -6 to 6
- second_gain: float32 [2, 1024], P(None, ('dp', 'seq')), may hold values from 0.25 to 1.75
- second_shift: float32 [2, 1024], P(None, ('dp', 'seq')), may hold values from -4 to 4
- up_bias: float32 [2, 16, 256], P(None, 'head', ('dp', 'seq')), may hold values from -6 to 6
- down_bias: float32 [2, 1024], P(None, ('dp', 'seq')), may hold values from -6 to 6
- cotangent: bfloat16 [4, 1024, 1024], P('dp', 'seq'), may hold values from -6 to 6
Outputs:
- output: bfloat16 [4, 1024, 1024], P('dp', 'seq')
- tokens_grad: float32 [4, 1024, 1024], P('dp', 'seq')
- qkv_weight_grad: float32 [2, 1024, 3072], P(None, ('dp', 'seq'), 'head')
- dense_weight_grad: float32 [2, 1024, 1024], P(None, 'head', ('dp', 'seq'))
- up_weight_grad: float32 [2, 1024, 4096], P(None, ('dp', 'seq'), 'head')
- down_weight_grad: float32 [2, 4096, 1024], P(None, 'head', ('dp', 'seq'))
- first_gain_grad: float32 [2, 1024], P(None, ('dp', 'seq'))
- first_shift_grad: float32 [2, 1024], P(None, ('dp', 'seq'))
- query_bias_grad: float32 [2, 16, 64], P(None, 'head', ('dp', 'seq'))
- value_bias_grad: float32 [2, 16, 64], P(None, 'head', ('dp', 'seq'))
- dense_bias_grad: float32 [2, 1024], P(None, ('dp', 'seq'))
- second_gain_grad: float32 [2, 1024], P(None, ('dp', 'seq'))
- second_shift_grad: float32 [2, 1024], P(None, ('dp', 'seq'))
- up_bias_grad: float32 [2, 16, 256], P(None, 'head', ('dp', 'seq'))
- down_bias_grad: float32 [2, 1024], P(None, ('dp', 'seq'))
All inputs are finite; a program needn't handle non-finite values.
Results may differ from a plain program's by a relative error of at most 0.035.
Values may be sent and summed in bfloat16 or wider, within the bound.
No kernel may reach another device: no remote copies, remote signals or barrier semaphores. Data moves between devices by JAX's collectives and lax.ppermute only.
A program may use at most 192 MiB of HBM per device.

v0:
```python
import math

import jax
import jax.numpy as jnp
from jax import lax
from jax.sharding import PartitionSpec as P

H = 16
HD = 64
LAYERS = 2


epsilon = 1e-05
masked_value = -1000000000.0


def layer_norm(values, gain_row, shift_row):
    row_mean = jnp.mean(values, axis=-1, keepdims=True)
    centred = values - row_mean
    spread = jnp.mean(centred * centred, axis=-1, keepdims=True)
    return centred * lax.rsqrt(spread + epsilon) * gain_row + shift_row


def gelu_tanh(values):
    argument = 0.7978845608028654 * (values + 0.044715 * values * values * values)
    return 0.5 * values * (1.0 + jnp.tanh(argument))


def sum_heads(partial_value):
    return lax.psum(partial_value.astype(jnp.bfloat16), "head").astype(jnp.float32)


def sum_head_grads(partial_value):
    return lax.psum(partial_value.astype(jnp.bfloat16), "head").astype(jnp.float32)


def fetch_layer(params, layer_index):
    return (
        lax.all_gather(params[0][layer_index], ("dp", "seq"), axis=0, tiled=True),
        lax.all_gather(params[1][layer_index], ("dp", "seq"), axis=1, tiled=True),
        lax.all_gather(params[2][layer_index], ("dp", "seq"), axis=0, tiled=True),
        lax.all_gather(params[3][layer_index], ("dp", "seq"), axis=1, tiled=True),
        lax.all_gather(
            params[4][layer_index].astype(jnp.bfloat16), ("dp", "seq"), axis=0, tiled=True
        ).astype(jnp.float32),
        lax.all_gather(
            params[5][layer_index].astype(jnp.bfloat16), ("dp", "seq"), axis=0, tiled=True
        ).astype(jnp.float32),
        lax.all_gather(
            params[6][layer_index].astype(jnp.bfloat16), ("dp", "seq"), axis=1, tiled=True
        ).astype(jnp.float32),
        lax.all_gather(
            params[7][layer_index].astype(jnp.bfloat16), ("dp", "seq"), axis=1, tiled=True
        ).astype(jnp.float32),
        lax.all_gather(
            params[8][layer_index].astype(jnp.bfloat16), ("dp", "seq"), axis=0, tiled=True
        ).astype(jnp.float32),
        lax.all_gather(
            params[9][layer_index].astype(jnp.bfloat16), ("dp", "seq"), axis=0, tiled=True
        ).astype(jnp.float32),
        lax.all_gather(
            params[10][layer_index].astype(jnp.bfloat16), ("dp", "seq"), axis=0, tiled=True
        ).astype(jnp.float32),
        lax.all_gather(
            params[11][layer_index].astype(jnp.bfloat16), ("dp", "seq"), axis=1, tiled=True
        ).astype(jnp.float32),
        lax.all_gather(
            params[12][layer_index].astype(jnp.bfloat16), ("dp", "seq"), axis=0, tiled=True
        ).astype(jnp.float32),
    )


def fetch_again(params, layer_index):
    return (
        lax.all_gather(params[0][layer_index], ("dp", "seq"), axis=0, tiled=True),
        lax.all_gather(params[1][layer_index], ("dp", "seq"), axis=1, tiled=True),
        lax.all_gather(params[2][layer_index], ("dp", "seq"), axis=0, tiled=True),
        lax.all_gather(params[3][layer_index], ("dp", "seq"), axis=1, tiled=True),
        lax.all_gather(
            params[4][layer_index].astype(jnp.bfloat16), ("dp", "seq"), axis=0, tiled=True
        ).astype(jnp.float32),
        lax.all_gather(
            params[5][layer_index].astype(jnp.bfloat16), ("dp", "seq"), axis=0, tiled=True
        ).astype(jnp.float32),
        lax.all_gather(
            params[6][layer_index].astype(jnp.bfloat16), ("dp", "seq"), axis=1, tiled=True
        ).astype(jnp.float32),
        lax.all_gather(
            params[7][layer_index].astype(jnp.bfloat16), ("dp", "seq"), axis=1, tiled=True
        ).astype(jnp.float32),
        lax.all_gather(
            params[8][layer_index].astype(jnp.bfloat16), ("dp", "seq"), axis=0, tiled=True
        ).astype(jnp.float32),
        lax.all_gather(
            params[9][layer_index].astype(jnp.bfloat16), ("dp", "seq"), axis=0, tiled=True
        ).astype(jnp.float32),
        lax.all_gather(
            params[10][layer_index].astype(jnp.bfloat16), ("dp", "seq"), axis=0, tiled=True
        ).astype(jnp.float32),
        lax.all_gather(
            params[11][layer_index].astype(jnp.bfloat16), ("dp", "seq"), axis=1, tiled=True
        ).astype(jnp.float32),
        lax.all_gather(
            params[12][layer_index].astype(jnp.bfloat16), ("dp", "seq"), axis=0, tiled=True
        ).astype(jnp.float32),
    )


def block_scores(query_block, key_block, offset, slope_vals):
    query_pos = offset + jnp.arange(query_block.shape[2], dtype=jnp.int32)
    key_pos = jnp.arange(key_block.shape[2], dtype=jnp.int32)
    causal = key_pos[None, :] <= query_pos[:, None]
    offsets = (key_pos[None, :] - query_pos[:, None]).astype(jnp.float32)
    products = jnp.einsum(
        "hdq,hdk->hqk", query_block, key_block, preferred_element_type=jnp.float32
    )
    scores = products * (1.0 / math.sqrt(HD)) + slope_vals[:, None, None] * offsets[None]
    return jnp.where(causal[None], scores, masked_value)


def attend_forward(query_block, key_block, value_block, offset, slope_vals):
    scores = block_scores(query_block, key_block, offset, slope_vals)
    row_max = jnp.max(scores, axis=-1, keepdims=True)
    shifted = jnp.exp(scores - row_max)
    row_total = jnp.sum(shifted, axis=-1, keepdims=True)
    prob_low = (shifted / row_total).astype(jnp.bfloat16)
    context = jnp.einsum("hqk,hdk->hdq", prob_low, value_block, preferred_element_type=jnp.float32)
    return (context, (row_max + jnp.log(row_total))[..., 0])


def attend_backward(query_block, key_block, value_block, grad_block, log_total, offset, slope_vals):
    scores = block_scores(query_block, key_block, offset, slope_vals)
    attn_probs = jnp.exp(scores - log_total[..., None])
    prob_low = attn_probs.astype(jnp.bfloat16)
    prob_grad = jnp.einsum(
        "hdq,hdk->hqk", grad_block, value_block, preferred_element_type=jnp.float32
    )
    row_inner = jnp.sum(attn_probs * prob_grad, axis=-1, keepdims=True)
    score_grad = (attn_probs * (prob_grad - row_inner)).astype(jnp.bfloat16)
    factor = 1.0 / math.sqrt(HD)
    query_grad = (
        jnp.einsum("hqk,hdk->hdq", score_grad, key_block, preferred_element_type=jnp.float32)
        * factor
    )
    key_grad = (
        jnp.einsum("hqk,hdq->hdk", score_grad, query_block, preferred_element_type=jnp.float32)
        * factor
    )
    value_grad = jnp.einsum(
        "hqk,hdq->hdk", prob_low, grad_block, preferred_element_type=jnp.float32
    )
    return (query_grad, key_grad, value_grad)


def forward_layer(hidden, fetched, offset, slope_vals, seq_count, slice_len):
    (
        w_qkv,
        w_dense,
        w_up,
        w_down,
        gain_one,
        shift_one,
        bias_query,
        bias_value,
        bias_dense,
        gain_two,
        shift_two,
        bias_up,
        bias_down,
    ) = fetched
    row_count = hidden.shape[0]
    heads_local = bias_query.shape[0]
    normed_one = layer_norm(hidden, gain_one, shift_one).astype(jnp.bfloat16)
    projected = jnp.dot(normed_one, w_qkv, preferred_element_type=jnp.float32)
    projected = projected.reshape(seq_count, slice_len, heads_local, 3, HD).transpose(0, 2, 3, 4, 1)
    queries = (projected[:, :, 0] + bias_query[None, :, :, None]).astype(jnp.bfloat16)
    key_local = (
        projected[:, :, 1].astype(jnp.bfloat16).reshape(seq_count, heads_local * HD, slice_len)
    )
    value_local = (projected[:, :, 2] + bias_value[None, :, :, None]).astype(jnp.bfloat16)
    value_local = value_local.reshape(seq_count, heads_local * HD, slice_len)
    key_full, value_full = (
        lax.all_gather(key_local, "seq", axis=2, tiled=True),
        lax.all_gather(value_local, "seq", axis=2, tiled=True),
    )
    full_len = key_full.shape[2]
    key_full = key_full.reshape(seq_count, heads_local, HD, full_len)
    value_full = value_full.reshape(seq_count, heads_local, HD, full_len)
    context, log_total = lax.map(
        lambda triple: attend_forward(triple[0], triple[1], triple[2], offset, slope_vals),
        (queries, key_full, value_full),
    )
    context_low = (
        context.transpose(0, 3, 1, 2).reshape(row_count, heads_local * HD).astype(jnp.bfloat16)
    )
    hidden_mid = (
        hidden
        + sum_heads(jnp.dot(context_low, w_dense, preferred_element_type=jnp.float32))
        + bias_dense
    )
    normed_two = layer_norm(hidden_mid, gain_two, shift_two).astype(jnp.bfloat16)
    pre_up = jnp.dot(normed_two, w_up, preferred_element_type=jnp.float32) + bias_up.reshape(-1)
    activation = gelu_tanh(pre_up).astype(jnp.bfloat16)
    hidden_out = (
        hidden_mid
        + sum_heads(jnp.dot(activation, w_down, preferred_element_type=jnp.float32))
        + bias_down
    )
    record = (
        hidden,
        normed_one,
        queries,
        key_full,
        value_full,
        log_total,
        context_low,
        hidden_mid,
        normed_two,
        pre_up,
        activation,
    )
    return (hidden_out, record)


def backward_layer(gradient, fetched, record, offset, slope_vals):
    (
        w_qkv,
        w_dense,
        w_up,
        w_down,
        gain_one,
        shift_one,
        bias_query,
        bias_value,
        bias_dense,
        gain_two,
        shift_two,
        bias_up,
        bias_down,
    ) = fetched
    (
        hidden,
        normed_one,
        queries,
        key_full,
        value_full,
        log_total,
        context_low,
        hidden_mid,
        normed_two,
        pre_up,
        activation,
    ) = record
    seq_count, heads_local, slice_len = (queries.shape[0], queries.shape[1], queries.shape[3])
    full_len = key_full.shape[3]
    row_count = hidden.shape[0]
    down_bias_grad = jnp.sum(gradient, axis=0)
    grad_low = gradient.astype(jnp.bfloat16)
    down_grad = jnp.einsum("rf,rd->fd", activation, grad_low, preferred_element_type=jnp.float32)
    act_grad = jnp.einsum("rd,fd->rf", grad_low, w_down, preferred_element_type=jnp.float32)
    pre_grad = jax.vjp(gelu_tanh, pre_up)[1](act_grad)[0].astype(jnp.bfloat16)
    up_bias_grad = jnp.sum(pre_grad, axis=0, dtype=jnp.float32).reshape(bias_up.shape)
    up_grad = jnp.einsum("rd,rf->df", normed_two, pre_grad, preferred_element_type=jnp.float32)
    normed_grad = sum_head_grads(
        jnp.einsum("rf,df->rd", pre_grad, w_up, preferred_element_type=jnp.float32)
    )
    part_mid, gain_two_grad, shift_two_grad = jax.vjp(layer_norm, hidden_mid, gain_two, shift_two)[
        1
    ](normed_grad)
    mid_grad = gradient + part_mid
    dense_bias_grad = jnp.sum(mid_grad, axis=0)
    mid_low = mid_grad.astype(jnp.bfloat16)
    dense_grad = jnp.einsum("rc,rd->cd", context_low, mid_low, preferred_element_type=jnp.float32)
    context_grad = jnp.einsum("rd,cd->rc", mid_low, w_dense, preferred_element_type=jnp.float32)
    context_grad = context_grad.astype(jnp.bfloat16).reshape(seq_count, slice_len, heads_local, HD)
    context_grad = context_grad.transpose(0, 2, 3, 1)
    query_grad, key_grad, value_grad = lax.map(
        lambda bundle: attend_backward(
            bundle[0], bundle[1], bundle[2], bundle[3], bundle[4], offset, slope_vals
        ),
        (queries, key_full, value_full, context_grad, log_total),
    )
    key_own, value_own = (
        lax.psum_scatter(
            key_grad.reshape(seq_count, heads_local * HD, full_len).astype(jnp.bfloat16),
            "seq",
            scatter_dimension=2,
            tiled=True,
        ).astype(jnp.float32),
        lax.psum_scatter(
            value_grad.reshape(seq_count, heads_local * HD, full_len).astype(jnp.bfloat16),
            "seq",
            scatter_dimension=2,
            tiled=True,
        ).astype(jnp.float32),
    )
    query_low = (
        query_grad.transpose(0, 3, 1, 2).reshape(row_count, heads_local, HD).astype(jnp.bfloat16)
    )
    key_low = key_own.reshape(seq_count, heads_local, HD, slice_len).transpose(0, 3, 1, 2)
    key_low = key_low.reshape(row_count, heads_local, HD).astype(jnp.bfloat16)
    value_low = value_own.reshape(seq_count, heads_local, HD, slice_len).transpose(0, 3, 1, 2)
    value_low = value_low.reshape(row_count, heads_local, HD).astype(jnp.bfloat16)
    query_bias_grad = jnp.sum(query_low, axis=0, dtype=jnp.float32)
    value_bias_grad = jnp.sum(value_low, axis=0, dtype=jnp.float32)
    joined_grad = jnp.stack((query_low, key_low, value_low), axis=2).reshape(
        row_count, heads_local * 3 * HD
    )
    qkv_grad = jnp.einsum("rd,rc->dc", normed_one, joined_grad, preferred_element_type=jnp.float32)
    first_grad = sum_head_grads(
        jnp.einsum("rc,dc->rd", joined_grad, w_qkv, preferred_element_type=jnp.float32)
    )
    part_in, gain_one_grad, shift_one_grad = jax.vjp(layer_norm, hidden, gain_one, shift_one)[1](
        first_grad
    )
    grad_in = mid_grad + part_in
    shares = (
        lax.psum_scatter(
            qkv_grad.astype(jnp.bfloat16), ("dp", "seq"), scatter_dimension=0, tiled=True
        ).astype(jnp.float32),
        lax.psum_scatter(
            dense_grad.astype(jnp.bfloat16), ("dp", "seq"), scatter_dimension=1, tiled=True
        ).astype(jnp.float32),
        lax.psum_scatter(
            up_grad.astype(jnp.bfloat16), ("dp", "seq"), scatter_dimension=0, tiled=True
        ).astype(jnp.float32),
        lax.psum_scatter(
            down_grad.astype(jnp.bfloat16), ("dp", "seq"), scatter_dimension=1, tiled=True
        ).astype(jnp.float32),
        lax.psum_scatter(
            gain_one_grad.astype(jnp.bfloat16), ("dp", "seq"), scatter_dimension=0, tiled=True
        ).astype(jnp.float32),
        lax.psum_scatter(
            shift_one_grad.astype(jnp.bfloat16), ("dp", "seq"), scatter_dimension=0, tiled=True
        ).astype(jnp.float32),
        lax.psum_scatter(
            query_bias_grad.astype(jnp.bfloat16), ("dp", "seq"), scatter_dimension=1, tiled=True
        ).astype(jnp.float32),
        lax.psum_scatter(
            value_bias_grad.astype(jnp.bfloat16), ("dp", "seq"), scatter_dimension=1, tiled=True
        ).astype(jnp.float32),
        lax.psum_scatter(
            dense_bias_grad.astype(jnp.bfloat16), ("dp", "seq"), scatter_dimension=0, tiled=True
        ).astype(jnp.float32),
        lax.psum_scatter(
            gain_two_grad.astype(jnp.bfloat16), ("dp", "seq"), scatter_dimension=0, tiled=True
        ).astype(jnp.float32),
        lax.psum_scatter(
            shift_two_grad.astype(jnp.bfloat16), ("dp", "seq"), scatter_dimension=0, tiled=True
        ).astype(jnp.float32),
        lax.psum_scatter(
            up_bias_grad.astype(jnp.bfloat16), ("dp", "seq"), scatter_dimension=1, tiled=True
        ).astype(jnp.float32),
        lax.psum_scatter(
            down_bias_grad.astype(jnp.bfloat16), ("dp", "seq"), scatter_dimension=0, tiled=True
        ).astype(jnp.float32),
    )
    return (grad_in, shares)


def per_device(
    tokens,
    qkv_weight,
    dense_weight,
    up_weight,
    down_weight,
    first_gain,
    first_shift,
    query_bias,
    value_bias,
    dense_bias,
    second_gain,
    second_shift,
    up_bias,
    down_bias,
    cotangent,
):
    params = (
        qkv_weight,
        dense_weight,
        up_weight,
        down_weight,
        first_gain,
        first_shift,
        query_bias,
        value_bias,
        dense_bias,
        second_gain,
        second_shift,
        up_bias,
        down_bias,
    )
    seq_count, slice_len, model_width = tokens.shape
    row_count = seq_count * slice_len
    heads_local = query_bias.shape[1]
    offset = lax.axis_index("seq") * slice_len
    head_ids = lax.axis_index("head") * heads_local + jnp.arange(heads_local, dtype=jnp.int32)
    slope_vals = 2.0 ** (-8.0 * (head_ids + 1).astype(jnp.float32) / H)
    hidden = tokens.reshape(row_count, model_width).astype(jnp.float32)
    records = []
    for layer_index in range(LAYERS):
        fetched = fetch_layer(params, layer_index)
        hidden, record = forward_layer(hidden, fetched, offset, slope_vals, seq_count, slice_len)
        records.append(record)
    output = hidden.reshape(seq_count, slice_len, model_width).astype(jnp.bfloat16)
    gradient = cotangent.reshape(row_count, model_width).astype(jnp.float32)
    collected = [None] * LAYERS
    for layer_index in reversed(range(LAYERS)):
        fetched = fetch_again(params, layer_index)
        gradient, shares = backward_layer(
            gradient, fetched, records[layer_index], offset, slope_vals
        )
        collected[layer_index] = shares
    stacked = tuple(
        (
            jnp.stack([collected[layer_index][member] for layer_index in range(LAYERS)])
            for member in range(13)
        )
    )
    tokens_grad = gradient.reshape(seq_count, slice_len, model_width)
    return (
        output,
        tokens_grad,
        stacked[0],
        stacked[1],
        stacked[2],
        stacked[3],
        stacked[4],
        stacked[5],
        stacked[6],
        stacked[7],
        stacked[8],
        stacked[9],
        stacked[10],
        stacked[11],
        stacked[12],
    )


def solution(mesh):
    placed = (
        P("dp", "seq", None),
        P(None, ("dp", "seq"), "head"),
        P(None, "head", ("dp", "seq")),
        P(None, ("dp", "seq"), "head"),
        P(None, "head", ("dp", "seq")),
        P(None, ("dp", "seq")),
        P(None, ("dp", "seq")),
        P(None, "head", ("dp", "seq")),
        P(None, "head", ("dp", "seq")),
        P(None, ("dp", "seq")),
        P(None, ("dp", "seq")),
        P(None, ("dp", "seq")),
        P(None, "head", ("dp", "seq")),
        P(None, ("dp", "seq")),
        P("dp", "seq", None),
    )
    return jax.shard_map(
        per_device,
        mesh=mesh,
        in_specs=placed,
        out_specs=(
            P("dp", "seq", None),
            P("dp", "seq", None),
            P(None, ("dp", "seq"), "head"),
            P(None, "head", ("dp", "seq")),
            P(None, ("dp", "seq"), "head"),
            P(None, "head", ("dp", "seq")),
            P(None, ("dp", "seq")),
            P(None, ("dp", "seq")),
            P(None, "head", ("dp", "seq")),
            P(None, "head", ("dp", "seq")),
            P(None, ("dp", "seq")),
            P(None, ("dp", "seq")),
            P(None, ("dp", "seq")),
            P(None, "head", ("dp", "seq")),
            P(None, ("dp", "seq")),
        ),
        check_vma=False,
    )
```

profile of v0, /device:TPU:0, one launch (start us, length us, event | category | flops | bytes accessed | tf_op | source)
XLA Modules:
  0.0 1168.7 jit_solution(13824203062160155742)
XLA Ops:
  10.6 10.2 all-gather
  39.8 9.0 all-gather.3
  117.1 14.9 %all-reduce.26.cloned.1.call-done = bf16[512,1024]{1,0:T(8,128)(2,1)} async-done(((bf16[512,1024]{1,0:T(8,128)(2,1)}), bf16[512,1024]{1,0:T(8,128)(2,1)}) %all-reduce.26.cloned.1.call-update) | async-done | bytes 1048592 | tf_op jit(solution)/shard_map/psum | solution.py:30
  134.3 27.6 %all-gather.35.cloned.1.call-done = bf16[1,1024,1024]{2,1,0:T(8,128)(2,1)} async-done(((bf16[1,128,1024]{2,1,0:T(8,128)(2,1)}), bf16[1,1024,1024]{2,1,0:T(8,128)(2,1)}) %all-gather.35.cloned.1.call-update) | async-done | bytes 2097168 | tf_op jit(solution)/shard_map/all_gather | solution.py:41
  166.3 26.4 %all-gather.37.cloned.1.call-done = bf16[1,1024,1024]{2,1,0:T(8,128)(2,1)} async-done(((bf16[1,1024,128]{2,1,0:T(8,128)(2,1)}), bf16[1,1024,1024]{2,1,0:T(8,128)(2,1)}) %all-gather.37.cloned.1.call-update) | async-done | bytes 2097168 | tf_op jit(solution)/shard_map/all_gather | solution.py:42
  232.6 9.0 all-gather.16
  241.7 10.1 all-gather.18
  254.4 21.8 %all-gather.39.cloned.1.call-done = bf16[1,1024,768]{2,1,0:T(8,128)(2,1)} async-done(((bf16[1,128,768]{2,1,0:T(8,128)(2,1)}), bf16[1,1024,768]{2,1,0:T(8,128)(2,1)}) %all-gather.39.cloned.1.call-update) | async-done | bytes 1572880 | tf_op jit(solution)/shard_map/all_gather | solution.py:39
  328.8 16.9 %all-reduce.30.cloned.1.call-done = bf16[512,1024]{1,0:T(8,128)(2,1)} async-done(((bf16[512,1024]{1,0:T(8,128)(2,1)}), bf16[512,1024]{1,0:T(8,128)(2,1)}) %all-reduce.30.cloned.1.call-update) | async-done | bytes 1048592 | tf_op jit(solution)/shard_map/psum | solution.py:30
  348.2 26.8 %all-gather.41.cloned.1.call-done = bf16[1,1024,1024]{2,1,0:T(8,128)(2,1)} async-done(((bf16[1,128,1024]{2,1,0:T(8,128)(2,1)}), bf16[1,1024,1024]{2,1,0:T(8,128)(2,1)}) %all-gather.41.cloned.1.call-update) | async-done | bytes 2097168 | tf_op jit(solution)/shard_map/all_gather | solution.py:41
  379.2 26.6 %all-gather.43.cloned.1.call-done = bf16[1,1024,1024]{2,1,0:T(8,128)(2,1)} async-done(((bf16[1,1024,128]{2,1,0:T(8,128)(2,1)}), bf16[1,1024,1024]{2,1,0:T(8,128)(2,1)}) %all-gather.43.cloned.1.call-update) | async-done | bytes 2097168 | tf_op jit(solution)/shard_map/all_gather | solution.py:42
  414.9 51.7 %all-reduce.32.cloned.1.call-done = bf16[512,1024]{1,0:T(8,128)(2,1)} async-done(((bf16[512,1024]{1,0:T(8,128)(2,1)}), bf16[512,1024]{1,0:T(8,128)(2,1)}) %all-reduce.32.cloned.1.call-update) | async-done | bytes 1048592 | tf_op jit(solution)/shard_map/psum | solution.py:34
  505.2 53.1 %all-reduce.34.cloned.1.call-done = bf16[512,1024]{1,0:T(8,128)(2,1)} async-done(((bf16[512,1024]{1,0:T(8,128)(2,1)}), bf16[512,1024]{1,0:T(8,128)(2,1)}) %all-reduce.34.cloned.1.call-update) | async-done | bytes 1048592 | tf_op jit(solution)/shard_map/psum | solution.py:34
  571.4 51.1 %all-reduce.36.cloned.1.call-done = bf16[512,1024]{1,0:T(8,128)(2,1)} async-done(((bf16[512,1024]{1,0:T(8,128)(2,1)}), bf16[512,1024]{1,0:T(8,128)(2,1)}) %all-reduce.36.cloned.1.call-update) | async-done | bytes 1048592 | tf_op jit(solution)/shard_map/psum | solution.py:34
  720.6 13.9 %reduce-scatter.49.cloned.1.call-done = bf16[128,256]{1,0:T(8,128)(2,1)} async-done(((bf16[1024,256]{1,0:T(8,128)(2,1)}), bf16[128,256]{1,0:T(8,128)(2,1)}) %reduce-scatter.49.cloned.1.call-update) | async-done | bytes 65552
  738.1 40.8 %reduce-scatter.53.cloned.1.call-done = bf16[128,1024]{1,0:T(8,128)(2,1)} async-done(((bf16[1024,1024]{1,0:T(8,128)(2,1)}), bf16[128,1024]{1,0:T(8,128)(2,1)}) %reduce-scatter.53.cloned.1.call-update) | async-done | bytes 262160
  780.7 34.6 %reduce-scatter.55.cloned.1.call-done = bf16[32,4]{1,0:T(8,128)(2,1)} async-done(((bf16[256,4]{1,0:T(8,128)(2,1)}), bf16[32,4]{1,0:T(8,128)(2,1)}) %reduce-scatter.55.cloned.1.call-update) | async-done | bytes 272
  818.7 33.8 %reduce-scatter.47.cloned.1.call-done = bf16[128,256]{1,0:T(8,128)(2,1)} async-done(((bf16[1024,256]{1,0:T(8,128)(2,1)}), bf16[128,256]{1,0:T(8,128)(2,1)}) %reduce-scatter.47.cloned.1.call-update) | async-done | bytes 65552
  858.0 39.4 %reduce-scatter.51.cloned.1.call-done = bf16[128,1024]{1,0:T(8,128)(2,1)} async-done(((bf16[1024,1024]{1,0:T(8,128)(2,1)}), bf16[128,1024]{1,0:T(8,128)(2,1)}) %reduce-scatter.51.cloned.1.call-update) | async-done | bytes 262160
  899.2 42.7 %reduce-scatter.45.cloned.1.call-done = bf16[128,1024]{1,0:T(8,128)(2,1)} async-done(((bf16[1024,1024]{1,0:T(8,128)(2,1)}), bf16[128,1024]{1,0:T(8,128)(2,1)}) %reduce-scatter.45.cloned.1.call-update) | async-done | bytes 262160 | tf_op jit(solution)/shard_map/reduce_scatter | solution.py:324
  942.0 44.7 %reduce-scatter.43.cloned.1.call-done = bf16[128,1024]{1,0:T(8,128)(2,1)} async-done(((bf16[1024,1024]{1,0:T(8,128)(2,1)}), bf16[128,1024]{1,0:T(8,128)(2,1)}) %reduce-scatter.43.cloned.1.call-update) | async-done | bytes 262160 | tf_op jit(solution)/shard_map/reduce_scatter | solution.py:324
  990.8 86.0 %all-reduce.38.cloned.1.call-done = (bf16[512,1024]{1,0:T(8,128)(2,1)}, bf16[512,1024]{1,0:T(8,128)(2,1)}) async-done(((bf16[512,1024]{1,0:T(8,128)(2,1)}, bf16[512,1024]{1,0:T(8,128)(2,1)}), (bf16[512,1024]{1,0:T(8,128)(2,1)}, bf16[512,1024]{1,0:T(8,128)(2,1)})) %all-reduce.38.cloned.1.call-update) | async-done | bytes 2097168 | tf_op jit(solution)/shard_map/psum | solution.py:30
  1082.6 24.3 %all-reduce.16 = (bf16[1024]{0:T(1024)(128)(2,1)S(1)}, bf16[1024]{0:T(1024)(128)(2,1)S(1)}, bf16[1024]{0:T(1024)(128)(2,1)S(1)}, bf16[1024]{0:T(1024)(128)(2,1)S...) all-reduce(bf16[1024]{0:T(1024)(128)(2,1)S(1)} %copy-done.61, ...), channel_id=41, replica_groups=mesh['dp'=4,'seq'=2,'head'=4] {'dp','seq'}, use_global_device_ids=true, to_apply=%region_45.46.clone | all-reduce | flops 13312 | bytes 53248
  1117.8 41.9 %reduce-scatter.39.cloned.1.call-done = bf16[128,768]{1,0:T(8,128)(2,1)} async-done(((bf16[1024,768]{1,0:T(8,128)(2,1)}), bf16[128,768]{1,0:T(8,128)(2,1)}) %reduce-scatter.39.cloned.1.call-update) | async-done | bytes 196624 | tf_op jit(solution)/shard_map/reduce_scatter | solution.py:318
  (461 shorter events, 394.2 us)
Async XLA Ops:
  9.1 122.9 %all-reduce.26.cloned.1.call-start = ((), (), s32[]{:S(2)}) async-start(), calls=%async_computation.14 | async-start | bytes 2097152 | tf_op jit(solution)/shard_map/psum | solution.py:30
  79.7 82.2 %all-gather.35.cloned.1.call-start = ((), (), s32[]{:S(2)}) async-start(), calls=%async_computation.29 | async-start | bytes 2359296 | tf_op jit(solution)/shard_map/all_gather | solution.py:41
  80.6 112.0 %all-gather.37.cloned.1.call-start = ((), (), s32[]{:S(2)}) async-start(), calls=%async_computation.30 | async-start | bytes 2359296 | tf_op jit(solution)/shard_map/all_gather | solution.py:42
  81.5 170.3 %all-reduce.28.cloned.1.call-start = ((), (), s32[]{:S(2)}) async-start(), calls=%async_computation.15 | async-start | bytes 2097152 | tf_op jit(solution)/shard_map/psum | solution.py:30
  197.4 78.8 %all-gather.39.cloned.1.call-start = ((), (), s32[]{:S(2)}) async-start(), calls=%async_computation.31 | async-start | bytes 1769472 | tf_op jit(solution)/shard_map/all_gather | solution.py:39
  198.0 147.7 %all-reduce.30.cloned.1.call-start = ((), (), s32[]{:S(2)}) async-start(), calls=%async_computation.16 | async-start | bytes 2097152 | tf_op jit(solution)/shard_map/psum | solution.py:30
  293.7 81.3 %all-gather.41.cloned.1.call-start = ((), (), s32[]{:S(2)}) async-start(), calls=%async_computation.32 | async-start | bytes 2359296 | tf_op jit(solution)/shard_map/all_gather | solution.py:41
  294.4 111.4 %all-gather.43.cloned.1.call-start = ((), (), s32[]{:S(2)}) async-start(), calls=%async_computation.33 | async-start | bytes 2359296 | tf_op jit(solution)/shard_map/all_gather | solution.py:42
  295.2 171.5 %all-reduce.32.cloned.1.call-start = ((), (), s32[]{:S(2)}) async-start(), calls=%async_computation.17 | async-start | bytes 2097152 | tf_op jit(solution)/shard_map/psum | solution.py:34
  414.7 82.0 %reduce-scatter.33.cloned.1.call-start = ((), (), s32[]{:S(2)}) async-start(), calls=%async_computation.19 | async-start | bytes 786432 | tf_op jit(solution)/shard_map/reduce_scatter | solution.py:290
  491.6 66.7 %all-reduce.34.cloned.1.call-start = ((), (), s32[]{:S(2)}) async-start(), calls=%async_computation.20 | async-start | bytes 2097152 | tf_op jit(solution)/shard_map/psum | solution.py:34
  505.2 117.3 %all-reduce.36.cloned.1.call-start = ((), (), s32[]{:S(2)}) async-start(), calls=%async_computation.21 | async-start | bytes 2097152 | tf_op jit(solution)/shard_map/psum | solution.py:34
  571.1 125.4 %reduce-scatter.37.cloned.1.call-start = ((), (), s32[]{:S(2)}) async-start(), calls=%async_computation.23 | async-start | bytes 786432 | tf_op jit(solution)/shard_map/reduce_scatter | solution.py:290
  650.6 67.2 %reduce-scatter.57.cloned.1.call-start = ((), (), s32[]{:S(2)}) async-start(), calls=%async_computation.39 | async-start | bytes 73728
  651.4 83.0 %reduce-scatter.49.cloned.1.call-start = ((), (), s32[]{:S(2)}) async-start(), calls=%async_computation.35 | async-start | bytes 589824
  656.5 122.4 %reduce-scatter.53.cloned.1.call-start = ((), (), s32[]{:S(2)}) async-start(), calls=%async_computation.37 | async-start | bytes 2359296
  665.5 149.8 %reduce-scatter.55.cloned.1.call-start = ((), (), s32[]{:S(2)}) async-start(), calls=%async_computation.38 | async-start | bytes 73728
  666.3 186.2 %reduce-scatter.47.cloned.1.call-start = ((), (), s32[]{:S(2)}) async-start(), calls=%async_computation.34 | async-start | bytes 589824
  671.3 226.2 %reduce-scatter.51.cloned.1.call-start = ((), (), s32[]{:S(2)}) async-start(), calls=%async_computation.36 | async-start | bytes 2359296
  680.9 261.0 %reduce-scatter.45.cloned.1.call-start = ((), (), s32[]{:S(2)}) async-start(), calls=%async_computation.27 | async-start | bytes 2359296 | tf_op jit(solution)/shard_map/reduce_scatter | solution.py:324
  685.0 301.7 %reduce-scatter.43.cloned.1.call-start = ((), (), s32[]{:S(2)}) async-start(), calls=%async_computation.26 | async-start | bytes 2359296 | tf_op jit(solution)/shard_map/reduce_scatter | solution.py:324
  689.5 387.3 %all-reduce.38.cloned.1.call-start = ((), (), s32[]{:S(2)}) async-start(), calls=%async_computation.40 | async-start | bytes 4194304 | tf_op jit(solution)/shard_map/psum | solution.py:30
  700.7 417.1 %reduce-scatter.41.cloned.1.call-start = ((), (), s32[]{:S(2)}) async-start(), calls=%async_computation.25 | async-start | bytes 1769472 | tf_op jit(solution)/shard_map/reduce_scatter | solution.py:318
  705.0 454.8 %reduce-scatter.39.cloned.1.call-start = ((), (), s32[]{:S(2)}) async-start(), calls=%async_computation.24 | async-start | bytes 1769472 | tf_op jit(solution)/shard_map/reduce_scatter | solution.py:318
  (98 other events, 1598.3 us)
Sparse Core Ops, SparseCore 0:
  10.5 28.4 all-gather.32
  79.8 52.1 all-reduce.25
  134.6 27.2 all-gather.34
  164.4 28.1 all-gather.36
  197.5 51.7 all-reduce.27
  251.1 25.0 all-gather.38
  293.8 51.8 all-reduce.29
  347.7 27.2 all-gather.40
  377.6 28.1 all-gather.42
  414.8 51.7 all-reduce.31
  491.7 9.0 reduce-scatter.30
  505.3 52.9 all-reduce.33
  571.2 51.2 all-reduce.35
  662.6 34.3 reduce-scatter.56
  700.3 34.1 reduce-scatter.48
  737.7 41.1 reduce-scatter.52
  782.1 33.2 reduce-scatter.54
  818.4 34.1 reduce-scatter.46
  856.2 41.2 reduce-scatter.50
  900.7 41.1 reduce-scatter.44
  945.4 41.2 reduce-scatter.42
  989.7 87.0 all-reduce.37
  1080.3 37.4 reduce-scatter.40
  1121.3 38.4 reduce-scatter.38
  (3 shorter events, 23.0 us)
where the time goes:
time: 1180 us; the launch traced here: 1170 us
  waiting for transfers between devices  702 us (59%)
  blocking collectives  207 us (18%)
  matrix products  111 us (9%)
  other arithmetic  84.9 us (7%)
  local copies, waits for them, and re-layouts  44.5 us (4%)
  between operations  17.1 us (1%)
    unnamed x33, waiting for transfers between devices  165 us
    psum x3, waiting for transfers between devices, sum_head_grads(): lax.psum(partial_value.astype(jnp.bfloat16), 'head').astype(jnp.float32)  156 us
    psum x4, waiting for transfers between devices, sum_heads(): lax.psum(partial_value.astype(jnp.bfloat16), 'head').astype(jnp.float32)  118 us
    reduce_scatter x2, waiting for transfers between devices, backward_layer(): lax.psum_scatter(up_grad.astype(jnp.bfloat16), ('dp', 'seq'), scatter_dim...  87.5 us
    all_gather x2, waiting for transfers between devices, fetch_layer(): lax.all_gather(params[2][layer_index], ('dp', 'seq'), axis=0, tiled=True)  54.4 us
    all_gather x2, waiting for transfers between devices, fetch_layer(): lax.all_gather(params[3][layer_index], ('dp', 'seq'), axis=1, tiled=True)  53 us
    reduce_scatter x2, waiting for transfers between devices, backward_layer(): lax.psum_scatter(qkv_grad.astype(jnp.bfloat16), ('dp', 'seq'), scatter_di...  42.8 us
    unnamed x208, local copies, waits for them, and re-layouts  33.4 us
  transfers between devices with their start and end apart: 27, of which 21 were waited for; matrix products, arithmetic and copies ran while one was open for 13% of the time, Pallas kernels for 0%

commit v1 on v0

v1 whole, which is shorter than its diff:
```python
import functools
import math

import jax
import jax.numpy as jnp
from jax import lax
from jax.sharding import PartitionSpec as P

H = 16
HD = 64
LAYERS = 2
DP, SEQ, HEAD = "dp", "seq", "head"

epsilon = 1e-05
masked_value = -1000000000.0
bf16 = jnp.bfloat16
f32 = jnp.float32


def flip(array, index, axis=0):
    size = array.shape[axis]
    bit = 1
    while bit < size:
        shape = array.shape[:axis] + (size // (2 * bit), 2, bit) + array.shape[axis + 1 :]
        cut = array.reshape(shape)
        turned = lax.rev(cut, (axis + 1,))
        array = jnp.where((index & bit) != 0, turned, cut).reshape(array.shape)
        bit *= 2
    return array


def swap(array, name, size, step):
    return lax.ppermute(array, name, [(i, i ^ step) for i in range(size)])


def gather(array, name, size):
    return [array] + [swap(array, name, size, step) for step in range(1, size)]


def deal(blocks, name, size):
    return [blocks[0]] + [swap(blocks[step], name, size, step) for step in range(1, size)]


def sum_blocks(blocks, name, size):
    total = blocks[0]
    for step in range(1, size):
        total = total + swap(blocks[step].astype(bf16), name, size, step).astype(f32)
    return total


def after(array, *others):
    return lax.optimization_barrier((array,) + others)[0]


def norm_parts(values):
    row_mean = jnp.mean(values, axis=-1, keepdims=True)
    centred = values - row_mean
    scale = lax.rsqrt(jnp.mean(centred * centred, axis=-1, keepdims=True) + epsilon)
    return centred * scale, scale


def norm_forward(values, gain, shift):
    xhat, _ = norm_parts(values)
    return (xhat * gain + shift).astype(bf16)


def norm_backward(values, gain, e):
    xhat, scale = norm_parts(values)
    eg = e * gain
    grad = scale * (
        eg
        - jnp.mean(eg, axis=-1, keepdims=True)
        - xhat * jnp.mean(eg * xhat, axis=-1, keepdims=True)
    )
    return grad, jnp.sum(e * xhat, axis=0), jnp.sum(e, axis=0)


def gelu_tanh(values):
    argument = 0.7978845608028654 * (values + 0.044715 * values * values * values)
    return 0.5 * values * (1.0 + jnp.tanh(argument))


def product(spec, left, right):
    return jnp.einsum(spec, left, right, preferred_element_type=f32)


def block_scores(queries, keys, query_pos, key_pos, slopes):
    causal = key_pos[None, :] <= query_pos[:, None]
    offsets = (key_pos[None, :] - query_pos[:, None]).astype(f32)
    scores = product("hqd,hkd->hqk", queries, keys) * (1.0 / math.sqrt(HD))
    scores = scores + slopes[:, None, None] * offsets[None]
    return jnp.where(causal[None], scores, masked_value)


def attend_forward(queries, keys, values, query_pos, key_pos, slopes):
    scores = block_scores(queries, keys, query_pos, key_pos, slopes)
    row_max = jnp.max(scores, axis=-1, keepdims=True)
    shifted = jnp.exp(scores - row_max)
    row_total = jnp.sum(shifted, axis=-1, keepdims=True)
    prob_low = (shifted / row_total).astype(bf16)
    context = product("hqk,hkd->hqd", prob_low, values)
    return context, (row_max + jnp.log(row_total))[..., 0]


def attend_backward(queries, keys, values, grads, log_total, query_pos, key_pos, slopes):
    scores = block_scores(queries, keys, query_pos, key_pos, slopes)
    probs = jnp.exp(scores - log_total[..., None])
    prob_grad = product("hqd,hkd->hqk", grads, values)
    row_inner = jnp.sum(probs * prob_grad, axis=-1, keepdims=True)
    score_grad = (probs * (prob_grad - row_inner)).astype(bf16)
    factor = 1.0 / math.sqrt(HD)
    query_grad = product("hqk,hkd->hqd", score_grad, keys) * factor
    key_grad = product("hqk,hqd->hkd", score_grad, queries) * factor
    value_grad = product("hqk,hqd->hkd", probs.astype(bf16), grads)
    return query_grad, key_grad, value_grad


def per_device(
    sizes,
    tokens,
    qkv_weight,
    dense_weight,
    up_weight,
    down_weight,
    first_gain,
    first_shift,
    query_bias,
    value_bias,
    dense_bias,
    second_gain,
    second_shift,
    up_bias,
    down_bias,
    cotangent,
):
    n_t, n_s, n_z = sizes
    seq_count, slice_len, width = tokens.shape
    assert seq_count == 1 and n_t == n_z
    d, c, z = (lax.axis_index(name) for name in (DP, SEQ, HEAD))
    rows = slice_len // n_t
    cut = qkv_weight.shape[1]
    part = cut * n_t
    heads = query_bias.shape[1]
    assert heads == n_t
    units = up_bias.shape[2] * n_t * n_s

    def to_inner(array):
        lead = array.shape[:-1]
        array = array.reshape(lead + (n_t, n_s, cut))
        array = jnp.moveaxis(array, -2, -3)
        return flip(array, c, len(lead)).reshape(lead + (width,))

    def to_outer(array):
        lead = array.shape[:-1]
        array = flip(array.reshape(lead + (n_s, n_t, cut)), c, len(lead))
        return jnp.moveaxis(array, -2, -3).reshape(lead + (width,))

    def own_rows(array):
        blocks = flip(array.reshape(n_t, rows, width), d)
        total = jnp.where(d == z, blocks[0], jnp.zeros_like(blocks[0]))
        for step in range(1, n_t):
            pairs = [(i * n_z + i, (i ^ step) * n_z + i) for i in range(n_t)]
            total = total + lax.ppermute(blocks[step], (DP, HEAD), pairs)
        return total

    def all_rows(array):
        return jnp.concatenate(gather(array, DP, n_t), axis=0)

    def sum_rows(partial):
        blocks = partial.reshape(n_t, rows, width)
        return sum_blocks([blocks[step] for step in range(n_t)], DP, n_t)

    def to_output(array):
        blocks = flip(jnp.stack(gather(array, HEAD, n_z)), z)
        blocks = flip(blocks, d)
        got = deal([blocks[step] for step in range(n_t)], DP, n_t)
        return flip(jnp.stack(got), d).reshape(1, slice_len, width)

    wide = jnp.stack(
        (first_gain, first_shift, dense_bias, second_gain, second_shift, down_bias), axis=1
    )
    small = jnp.concatenate(
        [
            wide.reshape(-1),
            query_bias.reshape(-1),
            value_bias.reshape(-1),
            up_bias.reshape(-1),
        ]
    )
    small = lax.all_gather(small, (DP, SEQ, HEAD), axis=0, tiled=False)
    small = small.reshape(n_t, n_s, n_z, -1)
    n_wide = LAYERS * 6 * cut
    wide = small[:, :, 0, :n_wide].reshape(n_t, n_s, LAYERS, 6, cut)
    wide = flip(wide, c, 1).transpose(2, 3, 1, 0, 4).reshape(LAYERS, 6, width)
    tall = []
    begin = n_wide
    for source in (query_bias, value_bias, up_bias):
        size = source.shape[2]
        count = LAYERS * heads * size
        piece = small[:, :, :, begin : begin + count].reshape(n_t, n_s, n_z, LAYERS, heads, size)
        begin += count
        piece = lax.dynamic_index_in_dim(piece, d, axis=4, keepdims=False)
        piece = flip(piece, z, 2).transpose(3, 2, 0, 1, 4)
        tall.append(piece.reshape(LAYERS, n_z, n_t * n_s * size))

    def packed(layer):
        qkv = qkv_weight[layer].reshape(cut, n_t, -1)
        dense = dense_weight[layer].T.reshape(cut, n_t, -1)
        up = up_weight[layer].reshape(cut, n_t, -1)
        down = down_weight[layer].T.reshape(cut, n_t, -1)
        return (jnp.concatenate((qkv, dense), axis=2), up, down)

    def to_planes(array):
        blocks = flip(array.transpose(1, 0, 2), d)
        got = deal([blocks[step] for step in range(n_t)], DP, n_t)
        return flip(jnp.stack(got), d).reshape(part, -1)

    def along_z(array):
        return gather(array, HEAD, n_z)

    def join(blocks):
        full = [jnp.concatenate(gather(block, SEQ, n_s), axis=0) for block in blocks]
        return jnp.stack(full, axis=1)

    hidden = to_inner(own_rows(tokens[0])).astype(f32)

    weights = []
    previous = None
    for layer in range(LAYERS):
        kinds = []
        for shard in packed(layer):
            shard = to_planes(shard)
            if previous is not None:
                shard = after(shard, *previous)
            blocks = along_z(shard)
            previous = blocks
            kinds.append(join(blocks))
        weights.append(kinds)

    qkv_columns = 3 * HD
    head_ids = (z ^ jnp.arange(n_z, dtype=jnp.int32)) * heads + d
    slopes = 2.0 ** (-8.0 * (head_ids + 1).astype(f32) / H)
    block_ids = (d ^ jnp.arange(n_t, dtype=jnp.int32)) * rows
    own_pos = (block_ids[:, None] + jnp.arange(rows, dtype=jnp.int32)[None]).reshape(-1)
    query_pos = c * slice_len + own_pos
    others = (c ^ jnp.arange(n_s, dtype=jnp.int32)) * slice_len
    key_pos = (others[:, None] + own_pos[None]).reshape(-1)

    records = []
    for layer in range(LAYERS):
        mixed, w_up, w_down = weights[layer]
        w_qkv = mixed[:, :, :qkv_columns].reshape(width, -1)
        w_dense = mixed[:, :, qkv_columns:].reshape(width, -1)
        w_up = w_up.reshape(width, -1)
        w_down = w_down.reshape(width, -1)
        gain_one, shift_one, bias_dense, gain_two, shift_two, bias_down = (
            wide[layer, i] for i in range(6)
        )
        bias_query, bias_value, bias_up = (piece[layer] for piece in tall)
        normed_one = all_rows(norm_forward(hidden, gain_one, shift_one))
        projected = product("rd,dn->rn", normed_one, w_qkv)
        projected = projected.reshape(slice_len, n_z, 3, HD)
        queries = (projected[:, :, 0] + bias_query[None]).astype(bf16).transpose(1, 0, 2)
        keys = projected[:, :, 1].astype(bf16)
        values = (projected[:, :, 2] + bias_value[None]).astype(bf16)
        both = jnp.concatenate((keys, values), axis=2).transpose(1, 0, 2)
        both = jnp.concatenate(gather(both, SEQ, n_s), axis=1)
        keys, values = both[..., :HD], both[..., HD:]
        context, log_total = attend_forward(queries, keys, values, query_pos, key_pos, slopes)
        context = context.astype(bf16).transpose(1, 0, 2).reshape(slice_len, -1)
        hidden_mid = hidden + sum_rows(product("rc,dc->rd", context, w_dense)) + bias_dense
        normed_two = all_rows(norm_forward(hidden_mid, gain_two, shift_two))
        pre_up = product("rd,df->rf", normed_two, w_up) + bias_up.reshape(-1)
        activation = gelu_tanh(pre_up).astype(bf16)
        hidden_next = hidden_mid + sum_rows(product("rf,df->rd", activation, w_down)) + bias_down
        records.append(
            (
                (w_qkv, w_dense, w_up, w_down, gain_one, gain_two),
                (hidden, hidden_mid, normed_one, normed_two),
                (queries, keys, values, log_total, context, pre_up, activation),
            )
        )
        hidden = hidden_next

    output = to_output(to_outer(hidden.astype(bf16)))

    start = to_inner(own_rows(cotangent[0]))
    gradient = start.astype(f32)
    weight_grads = [None] * LAYERS
    wide_grads = [None] * LAYERS
    tall_grads = [None] * LAYERS
    chain = [None]

    def give_back(grad):
        blocks = grad.reshape(n_s, part, n_z, -1)
        mine = sum_blocks([blocks[step] for step in range(n_s)], SEQ, n_s)
        if chain[0] is not None:
            mine = after(mine, chain[0])
        mine = sum_blocks([mine[:, step] for step in range(n_z)], HEAD, n_z).astype(bf16)
        chain[0] = mine
        mine = flip(mine.reshape(n_t, cut, -1), d)
        got = deal([mine[step] for step in range(n_t)], DP, n_t)
        return flip(jnp.stack(got, axis=1), d, 1).astype(f32)

    for layer in reversed(range(LAYERS)):
        (
            (w_qkv, w_dense, w_up, w_down, gain_one, gain_two),
            (hidden, hidden_mid, normed_one, normed_two),
            (queries, keys, values, log_total, context, pre_up, activation),
        ) = records[layer]
        down_bias_grad = jnp.sum(gradient, axis=0)
        grad_low = all_rows(gradient.astype(bf16))
        act_grad = product("rd,df->rf", grad_low, w_down)
        pre_grad = jax.vjp(gelu_tanh, pre_up)[1](act_grad)[0].astype(bf16)
        e = sum_rows(product("rf,df->rd", pre_grad, w_up))
        down_grad = product("rd,rf->df", grad_low, activation).reshape(width, n_z, -1)
        up_grad = product("rd,rf->df", normed_two, pre_grad).reshape(width, n_z, -1)
        up_bias_grad = jnp.sum(pre_grad, axis=0, dtype=f32).reshape(n_z, -1)
        down_share = give_back(down_grad)
        up_share = give_back(up_grad)
        part_mid, gain_two_grad, shift_two_grad = norm_backward(hidden_mid, gain_two, e)
        mid_grad = gradient + part_mid
        dense_bias_grad = jnp.sum(mid_grad, axis=0)
        mid_low = all_rows(mid_grad.astype(bf16))
        context_grad = product("rd,dc->rc", mid_low, w_dense).astype(bf16)
        context_grad = context_grad.reshape(slice_len, n_z, HD).transpose(1, 0, 2)
        dense_grad = product("rd,rc->dc", mid_low, context).reshape(width, n_z, -1)
        query_grad, key_grad, value_grad = attend_backward(
            queries, keys, values, context_grad, log_total, query_pos, key_pos, slopes
        )
        both = jnp.concatenate((key_grad, value_grad), axis=2)
        both = both.reshape(n_z, n_s, slice_len, 2 * HD)
        both = sum_blocks([both[:, step] for step in range(n_s)], SEQ, n_s).astype(bf16)
        query_grad = query_grad.astype(bf16)
        query_bias_grad = jnp.sum(query_grad, axis=1, dtype=f32)
        value_bias_grad = jnp.sum(both[..., HD:], axis=1, dtype=f32)
        joined = jnp.concatenate((query_grad, both), axis=2)
        joined = joined.transpose(1, 0, 2).reshape(slice_len, -1)
        qkv_grad = product("rd,rn->dn", normed_one, joined).reshape(width, n_z, -1)
        mixed_share = give_back(jnp.concatenate((qkv_grad, dense_grad), axis=2))
        e = sum_rows(product("rn,dn->rd", joined, w_qkv))
        part_in, gain_one_grad, shift_one_grad = norm_backward(hidden, gain_one, e)
        gradient = mid_grad + part_in
        weight_grads[layer] = (
            mixed_share[:, :, :qkv_columns].reshape(cut, -1),
            mixed_share[:, :, qkv_columns:].reshape(cut, -1).T,
            up_share.reshape(cut, -1),
            down_share.reshape(cut, -1).T,
        )
        wide_grads[layer] = jnp.stack(
            (
                gain_one_grad,
                shift_one_grad,
                dense_bias_grad,
                gain_two_grad,
                shift_two_grad,
                down_bias_grad,
            )
        )
        tall_grads[layer] = jnp.concatenate(
            (query_bias_grad, value_bias_grad, up_bias_grad), axis=1
        )

    tokens_grad = to_output(to_outer(gradient.astype(bf16))).astype(f32)

    def fold(arrays, name, size):
        total = arrays[0]
        for step in range(1, size):
            total = total + swap(arrays[step], name, size, step)
        return total

    wide = jnp.stack(wide_grads).reshape(LAYERS * 6, n_s, n_t, cut)
    sizes_tall = (HD, HD, units)
    pieces, begin = [], 0
    tall = jnp.stack(tall_grads)
    for size in sizes_tall:
        piece = tall[:, :, begin : begin + size]
        begin += size
        piece = piece.reshape(LAYERS, n_z, n_t, n_s, size // (n_t * n_s))
        pieces.append(flip(piece, c, 3))
    tall = jnp.concatenate(
        [piece.transpose(3, 1, 2, 0, 4).reshape(n_s, n_z, n_t, -1) for piece in pieces], axis=3
    )
    wide = wide.transpose(1, 2, 0, 3).reshape(n_s, n_t, -1)
    n_wide = wide.shape[2]
    wide = jnp.broadcast_to(wide[:, None], (n_s, n_z) + wide.shape[1:])
    joint = jnp.concatenate((wide, tall), axis=3)
    joint = fold([joint[step] for step in range(n_s)], SEQ, n_s)
    joint = fold([joint[step] for step in range(n_z)], HEAD, n_z)
    joint = flip(joint, d)
    got = deal([joint[step] for step in range(n_t)], DP, n_t)
    wide = functools.reduce(jnp.add, [item[:n_wide] for item in got])
    wide = wide.reshape(LAYERS, 6, cut)
    tall = flip(jnp.stack([item[n_wide:] for item in got]), d)
    outs, begin = [], 0
    for size in sizes_tall:
        size = size // (n_t * n_s)
        piece = tall[:, begin : begin + LAYERS * size].reshape(n_t, LAYERS, size)
        begin += LAYERS * size
        outs.append(piece.transpose(1, 0, 2))
    query_bias_grad, value_bias_grad, up_bias_grad = outs
    qkv_grad, dense_grad, up_grad, down_grad = (
        jnp.stack([weight_grads[layer][kind] for layer in range(LAYERS)]) for kind in range(4)
    )
    return (
        output,
        tokens_grad,
        qkv_grad,
        dense_grad,
        up_grad,
        down_grad,
        wide[:, 0],
        wide[:, 1],
        query_bias_grad,
        value_bias_grad,
        wide[:, 2],
        wide[:, 3],
        wide[:, 4],
        up_bias_grad,
        wide[:, 5],
    )


def solution(mesh):
    sizes = tuple(mesh.shape[name] for name in (DP, SEQ, HEAD))
    rows = P(DP, SEQ, None)
    tall = P(None, (DP, SEQ), HEAD)
    flat = P(None, HEAD, (DP, SEQ))
    vector = P(None, (DP, SEQ))
    params = (
        tall,
        flat,
        tall,
        flat,
        vector,
        vector,
        flat,
        flat,
        vector,
        vector,
        vector,
        flat,
        vector,
    )
    return jax.shard_map(
        functools.partial(per_device, sizes),
        mesh=mesh,
        in_specs=(rows,) + params + (rows,),
        out_specs=(rows, rows) + params,
        check_vma=False,
    )
```

time: 1180 us -> 819 us (0.69)
  waiting for transfers between devices: 702 us -> 227 us
  starting transfers between devices: 1.91 us -> 210 us
  blocking collectives: 207 us -> 67.8 us
  local copies, waits for them, and re-layouts: 44.5 us -> 134 us
  matrix products: 111 us -> 65 us
  other arithmetic: 84.9 us -> 102 us
  between operations: 17.1 us -> 5.06 us
    psum x7 -> x0, waiting for transfers between devices: 274 us -> none  [the longest x3 156 us: sum_head_grads(): lax.psum(partial_value.astype(jnp.bfloat16), 'head').astype(jnp.float32)]
    ppermute x0 -> x179, waiting for transfers between devices: none -> 227 us  [the longest x173 227 us: swap(): return lax.ppermute(array, name, [(i, i ^ step) for i in range(size)])]
    ppermute x0 -> x179, starting transfers between devices: none -> 210 us  [the longest x173 196 us: swap(): return lax.ppermute(array, name, [(i, i ^ step) for i in range(size)])]
    unnamed x33 -> x0, waiting for transfers between devices: 165 us -> none
    reduce_scatter x8 -> x0, waiting for transfers between devices: 134 us -> none  [the longest x2 87.5 us: backward_layer(): lax.psum_scatter(up_grad.astype(jnp.bfloat16), ('dp', 'seq'), scatter_dim...]
    all_gather x6 -> x0, waiting for transfers between devices: 129 us -> none  [the longest x2 54.4 us: fetch_layer(): lax.all_gather(params[2][layer_index], ('dp', 'seq'), axis=0, tiled=True)]
    all_gather x24 -> x1, blocking collectives: 183 us -> 67.8 us  [per_device(): small = lax.all_gather(small, (DP, SEQ, HEAD), axis=0, tiled=False)]
    dot_general x36, matrix products: 111 us -> 65 us  [product(): return jnp.einsum(spec, left, right, preferred_element_type=f32)]
  transfers between devices with their start and end apart: 27 -> 179, of which waited for: 21 -> 55; matrix products, arithmetic and copies ran while one was open for 13% -> 32% of each run, Pallas kernels for 0% -> 0%
where the time goes in v1:
time: 819 us; the launch traced here: 811 us
  waiting for transfers between devices  227 us (28%)
  starting transfers between devices  210 us (26%)
  local copies, waits for them, and re-layouts  134 us (16%)
  other arithmetic  102 us (12%)
  blocking collectives  67.8 us (8%)
  matrix products  65 us (8%)
    ppermute x173, waiting for transfers between devices, swap(): return lax.ppermute(array, name, [(i, i ^ step) for i in range(size)])  227 us
    ppermute x173, starting transfers between devices, swap(): return lax.ppermute(array, name, [(i, i ^ step) for i in range(size)])  196 us
    all_gather x1, blocking collectives, per_device(): small = lax.all_gather(small, (DP, SEQ, HEAD), axis=0, tiled=False)  67.8 us
    dot_general x36, matrix products, product(): return jnp.einsum(spec, left, right, preferred_element_type=f32)  65 us
    rev x23, local copies, waits for them, and re-layouts, flip(): turned = lax.rev(cut, (axis + 1,))  29.9 us
    unnamed x300, local copies, waits for them, and re-layouts  20.4 us
  transfers between devices with their start and end apart: 179, of which 55 were waited for; matrix products, arithmetic and copies ran while one was open for 32% of the time, Pallas kernels for 0%

profile of v1, /device:TPU:0, one launch (start us, length us, event | category | flops | bytes accessed | tf_op | source)
XLA Modules:
  0.0 811.3 jit_solution(11250346301091123077)
XLA Ops:
  17.8 67.8 %all-gather.1 = f32[32,1,1920]{2,1,0:T(1,128)S(1)} all-gather(f32[1,1,1920]{2,1,0:T(1,128)S(1)} %reshape.912), channel_id=2, replica_groups=mesh['dp'=4,'seq'=2,'head'=4] {'dp','seq','head'}, dimensions={0}, use_global_device_ids=true | all-gather | bytes 253440 | tf_op jit(solution)/shard_map/all_gather | solution.py:190
  140.3 4.5 collective-permute-start
  171.4 4.3 collective-permute-start.10
  180.4 4.6 collective-permute-done.12
  196.2 12.1 %collective-permute-done.29 = bf16[512,256]{0,1:T(8,128)(2,1)S(1)} collective-permute-done((bf16[512,256]{0,1:T(8,128)(2,1)S(1)}, bf16[512,256]{0,1:T(8,128)(2,1)S(1)}, u32[]{:S(2)}, u32[]{:S(2)}) %collective-permute-start.29) | collective-permute-done | bytes 262176 | tf_op jit(solution)/shard_map/ppermute | solution.py:33
  225.4 13.2 %collective-permute-done.39 = bf16[512,256]{0,1:T(8,128)(2,1)S(1)} collective-permute-done((bf16[512,256]{0,1:T(8,128)(2,1)S(1)}, bf16[512,256]{0,1:T(8,128)(2,1)S(1)}, u32[]{:S(2)}, u32[]{:S(2)}) %collective-permute-start.39) | collective-permute-done | bytes 262176 | tf_op jit(solution)/shard_map/ppermute | solution.py:33
  263.2 5.2 collective-permute-done.19
  296.6 5.0 collective-permute-done.45
  320.3 12.5 %collective-permute-done.82 = bf16[512,256]{0,1:T(8,128)(2,1)S(1)} collective-permute-done((bf16[512,256]{0,1:T(8,128)(2,1)S(1)}, bf16[512,256]{0,1:T(8,128)(2,1)S(1)}, u32[]{:S(2)}, u32[]{:S(2)}) %collective-permute-start.82) | collective-permute-done | bytes 262176 | tf_op jit(solution)/shard_map/ppermute | solution.py:33
  346.8 5.4 collective-permute-done.60
  352.2 6.1 collective-permute-done.62
  364.2 6.4 collective-permute-done.65
  401.6 4.9 collective-permute-done.88
  421.2 9.9 %collective-permute-done.90 = bf16[128,1024]{0,1:T(8,128)(2,1)} collective-permute-done((bf16[128,1024]{0,1:T(8,128)(2,1)S(1)}, bf16[128,1024]{0,1:T(8,128)(2,1)}, u32[]{:S(2)}, u32[]{:S(2)}) %collective-permute-start.90) | collective-permute-done | bytes 262176 | tf_op jit(solution)/shard_map/ppermute | solution.py:33
  485.8 9.3 %collective-permute-done.137 = bf16[512,256]{0,1:T(8,128)(2,1)S(1)} collective-permute-done((bf16[512,256]{0,1:T(8,128)(2,1)S(1)}, bf16[512,256]{0,1:T(8,128)(2,1)S(1)}, u32[]{:S(2)}, u32[]{:S(2)}) %collective-permute-start.137) | collective-permute-done | bytes 262176 | tf_op jit(solution)/shard_map/ppermute | solution.py:33
  525.0 12.3 %collective-permute-done.140 = bf16[512,256]{0,1:T(8,128)(2,1)} collective-permute-done((bf16[512,256]{0,1:T(8,128)(2,1)S(1)}, bf16[512,256]{0,1:T(8,128)(2,1)}, u32[]{:S(2)}, u32[]{:S(2)}) %collective-permute-start.140) | collective-permute-done | bytes 262176 | tf_op jit(solution)/shard_map/ppermute | solution.py:33
  544.8 4.9 convert_reduce_fusion.1
  564.1 4.4 collective-permute-done.114
  601.3 5.0 collective-permute-done.143
  651.7 9.2 %collective-permute-done.146 = bf16[512,256]{0,1:T(8,128)(2,1)} collective-permute-done((bf16[512,256]{0,1:T(8,128)(2,1)}, bf16[512,256]{0,1:T(8,128)(2,1)}, u32[]{:S(2)}, u32[]{:S(2)}) %collective-permute-start.146) | collective-permute-done | bytes 262176 | tf_op jit(solution)/shard_map/ppermute | solution.py:33
  721.6 12.1 %collective-permute-start.124 = (bf16[128,1024]{0,1:T(8,128)(2,1)}, bf16[128,1024]{0,1:T(8,128)(2,1)}, u32[]{:S(2)}, u32[]{:S(2)}) collective-permute-start(bf16[128,1024]{0,1:T(8,128)(2,1)} %bitcast.236), channel_id=1, source_target_pairs={{0,1},{1,0},{2,3},{3,2},{4,5},{5,4},{6,7},{7,6},{8,9},{9,8},{10,11... | collective-permute-start | bytes 786440 | tf_op jit(solution)/shard_map/ppermute | solution.py:33
  733.7 5.1 collective-permute-done.149
  775.2 8.6 %collective-permute-done.151 = bf16[512,256]{0,1:T(8,128)(2,1)S(1)} collective-permute-done((bf16[512,256]{0,1:T(8,128)(2,1)S(1)}, bf16[512,256]{0,1:T(8,128)(2,1)S(1)}, u32[]{:S(2)}, u32[]{:S(2)}) %collective-permute-start.151) | collective-permute-done | bytes 262176 | tf_op jit(solution)/shard_map/ppermute | solution.py:33
  786.9 10.0 %collective-permute-done.152 = bf16[512,256]{0,1:T(8,128)(2,1)S(1)} collective-permute-done((bf16[512,256]{0,1:T(8,128)(2,1)S(1)}, bf16[512,256]{0,1:T(8,128)(2,1)S(1)}, u32[]{:S(2)}, u32[]{:S(2)}) %collective-permute-start.152) | collective-permute-done | bytes 262176 | tf_op jit(solution)/shard_map/ppermute | solution.py:33
  (1116 shorter events, 563.4 us)
Async XLA Ops:
  8.3 104.6 %collective-permute-start.8 = (bf16[128,256]{1,0:T(8,128)(2,1)}, bf16[128,256]{1,0:T(8,128)(2,1)}, u32[]{:S(2)}, u32[]{:S(2)}) collective-permute-start(bf16[128,256]{1,0:T(8,128)(2,1)} %get-tuple-element.274), channel_id=1, source_target_pairs={{0,24},{8,16},{16,8},{24,0},{1,25},{9,17},{17,9},{25,1},{2,26},{10... | collective-permute-start | bytes 196616 | tf_op jit(solution)/shard_map/ppermute | solution.py:33
  12.2 100.7 %collective-permute-start.7 = (bf16[128,256]{1,0:T(8,128)(2,1)}, bf16[128,256]{1,0:T(8,128)(2,1)}, u32[]{:S(2)}, u32[]{:S(2)}) collective-permute-start(bf16[128,256]{1,0:T(8,128)(2,1)} %get-tuple-element.275), channel_id=1, source_target_pairs={{0,16},{8,24},{16,0},{24,8},{1,17},{9,25},{17,1},{25,9},{2,18},{10... | collective-permute-start | bytes 196616 | tf_op jit(solution)/shard_map/ppermute | solution.py:33
  12.7 102.2 %collective-permute-start.6 = (bf16[128,256]{1,0:T(8,128)(2,1)}, bf16[128,256]{1,0:T(8,128)(2,1)}, u32[]{:S(2)}, u32[]{:S(2)}) collective-permute-start(bf16[128,256]{1,0:T(8,128)(2,1)} %get-tuple-element.276), channel_id=1, source_target_pairs={{0,8},{8,0},{16,24},{24,16},{1,9},{9,1},{17,25},{25,17},{2,10},{10... | collective-permute-start | bytes 196616 | tf_op jit(solution)/shard_map/ppermute | solution.py:33
  13.9 105.3 %collective-permute-start.25 = (bf16[128,256]{1,0:T(8,128)(2,1)}, bf16[128,256]{1,0:T(8,128)(2,1)S(1)}, u32[]{:S(2)}, u32[]{:S(2)}) collective-permute-start(bf16[128,256]{1,0:T(8,128)(2,1)} %get-tuple-element.266), channel_id=1, source_target_pairs={{0,24},{8,16},{16,8},{24,0},{1,25},{9,17},{17,9},{25,1},{2,26},{10... | collective-permute-start | bytes 196616 | tf_op jit(solution)/shard_map/ppermute | solution.py:33
  16.8 102.5 %collective-permute-start.24 = (bf16[128,256]{1,0:T(8,128)(2,1)}, bf16[128,256]{1,0:T(8,128)(2,1)}, u32[]{:S(2)}, u32[]{:S(2)}) collective-permute-start(bf16[128,256]{1,0:T(8,128)(2,1)} %get-tuple-element.267), channel_id=1, source_target_pairs={{0,16},{8,24},{16,0},{24,8},{1,17},{9,25},{17,1},{25,9},{2,18},{10... | collective-permute-start | bytes 196616 | tf_op jit(solution)/shard_map/ppermute | solution.py:33
  140.3 28.3 %collective-permute-start = (bf16[128,1024]{0,1:T(8,128)(2,1)}, bf16[128,1024]{0,1:T(8,128)(2,1)}, u32[]{:S(2)}, u32[]{:S(2)}) collective-permute-start(bf16[128,1024]{0,1:T(8,128)(2,1)} %get-tuple-element.219), channel_id=1, source_target_pairs={{0,8},{9,1},{18,26},{27,19},{4,12},{13,5},{22,30},{31,23}} | collective-permute-start | bytes 786440 | tf_op jit(solution)/shard_map/ppermute | solution.py:163
  277.1 28.3 %collective-permute-start.72 = (bf16[512,256]{0,1:T(8,128)(2,1)S(1)}, bf16[512,256]{0,1:T(8,128)(2,1)S(1)}, u32[]{:S(2)}, u32[]{:S(2)}) collective-permute-start(bf16[512,256]{0,1:T(8,128)(2,1)S(1)} %reshape_reshape.198), channel_id=1, source_target_pairs={{0,2},{1,3},{2,0},{3,1},{4,6},{5,7},{6,4},{7,5},{8,10},{9,11},{10,... | collective-permute-start | bytes 786440 | tf_op jit(solution)/shard_map/ppermute | solution.py:33
  418.8 45.1 %collective-permute-start.135 = (bf16[512,4,256]{0,2,1:T(8,128)(2,1)}, bf16[512,4,256]{0,2,1:T(8,128)(2,1)}, u32[]{:S(2)}, u32[]{:S(2)}) collective-permute-start(bf16[512,4,256]{0,2,1:T(8,128)(2,1)} %bitcast.946), channel_id=1, source_target_pairs={{0,4},{4,0},{1,5},{5,1},{2,6},{6,2},{3,7},{7,3},{8,12},{12,8},{9,1... | collective-permute-start | bytes 3145736 | tf_op jit(solution)/shard_map/ppermute | solution.py:33
  418.8 63.2 %collective-permute-start.134 = (bf16[512,4,256]{0,2,1:T(8,128)(2,1)}, bf16[512,4,256]{0,2,1:T(8,128)(2,1)}, u32[]{:S(2)}, u32[]{:S(2)}) collective-permute-start(bf16[512,4,256]{0,2,1:T(8,128)(2,1)} %bitcast.947), channel_id=1, source_target_pairs={{0,4},{4,0},{1,5},{5,1},{2,6},{6,2},{3,7},{7,3},{8,12},{12,8},{9,1... | collective-permute-start | bytes 3145736 | tf_op jit(solution)/shard_map/ppermute | solution.py:33
  476.5 29.2 %collective-permute-start.108 = (bf16[128,1024]{1,0:T(8,128)(2,1)}, bf16[128,1024]{1,0:T(8,128)(2,1)}, u32[]{:S(2)}, u32[]{:S(2)}) collective-permute-start(bf16[128,1024]{1,0:T(8,128)(2,1)} %get-tuple-element.194), channel_id=1, source_target_pairs={{0,8},{8,0},{16,24},{24,16},{1,9},{9,1},{17,25},{25,17},{2,10},{10... | collective-permute-start | bytes 786440 | tf_op jit(solution)/shard_map/ppermute | solution.py:33
  485.8 93.6 %collective-permute-start.133 = (bf16[512,4,256]{0,2,1:T(8,128)(2,1)}, bf16[512,4,256]{0,2,1:T(8,128)(2,1)}, u32[]{:S(2)}, u32[]{:S(2)}) collective-permute-start(bf16[512,4,256]{0,2,1:T(8,128)(2,1)} %fusion.32), channel_id=1, source_target_pairs={{0,4},{4,0},{1,5},{5,1},{2,6},{6,2},{3,7},{7,3},{8,12},{12,8},{9,1... | collective-permute-start | bytes 3145736 | tf_op jit(solution)/shard_map/ppermute | solution.py:33
  515.1 28.1 %collective-permute-start.113 = (bf16[128,1024]{1,0:T(8,128)(2,1)}, bf16[128,1024]{1,0:T(8,128)(2,1)}, u32[]{:S(2)}, u32[]{:S(2)}) collective-permute-start(bf16[128,1024]{1,0:T(8,128)(2,1)} %convert_element_type.563), channel_id=1, source_target_pairs={{0,24},{8,16},{16,8},{24,0},{1,25},{9,17},{17,9},{25,1},{2,26},{10... | collective-permute-start | bytes 786440 | tf_op jit(solution)/shard_map/ppermute | solution.py:33
  519.2 25.2 %collective-permute-start.112 = (bf16[128,1024]{1,0:T(8,128)(2,1)}, bf16[128,1024]{1,0:T(8,128)(2,1)}, u32[]{:S(2)}, u32[]{:S(2)}) collective-permute-start(bf16[128,1024]{1,0:T(8,128)(2,1)} %convert_element_type.563), channel_id=1, source_target_pairs={{0,16},{8,24},{16,0},{24,8},{1,17},{9,25},{17,1},{25,9},{2,18},{10... | collective-permute-start | bytes 786440 | tf_op jit(solution)/shard_map/ppermute | solution.py:33
  562.7 67.5 %collective-permute-start.132 = (bf16[512,4,256]{0,2,1:T(8,128)(2,1)}, bf16[512,4,256]{0,2,1:T(8,128)(2,1)}, u32[]{:S(2)}, u32[]{:S(2)}) collective-permute-start(bf16[512,4,256]{0,2,1:T(8,128)(2,1)} %bitcast.266), channel_id=1, source_target_pairs={{0,4},{4,0},{1,5},{5,1},{2,6},{6,2},{3,7},{7,3},{8,12},{12,8},{9,1... | collective-permute-start | bytes 3145736 | tf_op jit(solution)/shard_map/ppermute | solution.py:33
  568.5 78.7 %collective-permute-start.131 = (bf16[512,4,256]{0,2,1:T(8,128)(2,1)}, bf16[512,4,256]{0,2,1:T(8,128)(2,1)}, u32[]{:S(2)}, u32[]{:S(2)}) collective-permute-start(bf16[512,4,256]{0,2,1:T(8,128)(2,1)} %bitcast.264), channel_id=1, source_target_pairs={{0,4},{4,0},{1,5},{5,1},{2,6},{6,2},{3,7},{7,3},{8,12},{12,8},{9,1... | collective-permute-start | bytes 3145736 | tf_op jit(solution)/shard_map/ppermute | solution.py:33
  642.9 31.6 %collective-permute-start.121 = (bf16[128,1024]{1,0:T(8,128)(2,1)}, bf16[128,1024]{1,0:T(8,128)(2,1)}, u32[]{:S(2)}, u32[]{:S(2)}) collective-permute-start(bf16[128,1024]{1,0:T(8,128)(2,1)} %get-tuple-element.188), channel_id=1, source_target_pairs={{0,8},{8,0},{16,24},{24,16},{1,9},{9,1},{17,25},{25,17},{2,10},{10... | collective-permute-start | bytes 786440 | tf_op jit(solution)/shard_map/ppermute | solution.py:33
  647.1 29.4 %collective-permute-start.123 = (bf16[128,1024]{1,0:T(8,128)(2,1)}, bf16[128,1024]{1,0:T(8,128)(2,1)}, u32[]{:S(2)}, u32[]{:S(2)}) collective-permute-start(bf16[128,1024]{1,0:T(8,128)(2,1)} %get-tuple-element.189), channel_id=1, source_target_pairs={{0,24},{8,16},{16,8},{24,0},{1,25},{9,17},{17,9},{25,1},{2,26},{10... | collective-permute-start | bytes 786440 | tf_op jit(solution)/shard_map/ppermute | solution.py:33
  650.8 25.7 %collective-permute-start.122 = (bf16[128,1024]{1,0:T(8,128)(2,1)}, bf16[128,1024]{1,0:T(8,128)(2,1)}, u32[]{:S(2)}, u32[]{:S(2)}) collective-permute-start(bf16[128,1024]{1,0:T(8,128)(2,1)} %get-tuple-element.190), channel_id=1, source_target_pairs={{0,16},{8,24},{16,0},{24,8},{1,17},{9,25},{17,1},{25,9},{2,18},{10... | collective-permute-start | bytes 786440 | tf_op jit(solution)/shard_map/ppermute | solution.py:33
  651.7 117.9 %collective-permute-start.130 = (bf16[512,4,256]{0,2,1:T(8,128)(2,1)}, bf16[512,4,256]{0,2,1:T(8,128)(2,1)}, u32[]{:S(2)}, u32[]{:S(2)}) collective-permute-start(bf16[512,4,256]{0,2,1:T(8,128)(2,1)} %fusion.33), channel_id=1, source_target_pairs={{0,4},{4,0},{1,5},{5,1},{2,6},{6,2},{3,7},{7,3},{8,12},{12,8},{9,1... | collective-permute-start | bytes 3145736 | tf_op jit(solution)/shard_map/ppermute | solution.py:33
  676.5 44.9 %collective-permute-start.148 = (bf16[512,256]{0,1:T(8,128)(2,1)}, bf16[512,256]{0,1:T(8,128)(2,1)}, u32[]{:S(2)}, u32[]{:S(2)}) collective-permute-start(bf16[512,256]{0,1:T(8,128)(2,1)} %get-tuple-element.169), channel_id=1, source_target_pairs={{0,1},{1,0},{2,3},{3,2},{4,5},{5,4},{6,7},{7,6},{8,9},{9,8},{10,11... | collective-permute-start | bytes 786440 | tf_op jit(solution)/shard_map/ppermute | solution.py:33
  702.0 36.8 %collective-permute-start.149 = (bf16[512,256]{0,1:T(8,128)(2,1)}, bf16[512,256]{0,1:T(8,128)(2,1)}, u32[]{:S(2)}, u32[]{:S(2)}) collective-permute-start(bf16[512,256]{0,1:T(8,128)(2,1)} %get-tuple-element.171), channel_id=1, source_target_pairs={{0,2},{1,3},{2,0},{3,1},{4,6},{5,7},{6,4},{7,5},{8,10},{9,11},{10,... | collective-permute-start | bytes 786440 | tf_op jit(solution)/shard_map/ppermute | solution.py:33
  716.5 32.7 %collective-permute-start.126 = (bf16[128,1024]{0,1:T(8,128)(2,1)}, bf16[128,1024]{0,1:T(8,128)(2,1)}, u32[]{:S(2)}, u32[]{:S(2)}) collective-permute-start(bf16[128,1024]{0,1:T(8,128)(2,1)} %bitcast.236), channel_id=1, source_target_pairs={{0,3},{1,2},{2,1},{3,0},{4,7},{5,6},{6,5},{7,4},{8,11},{9,10},{10,... | collective-permute-start | bytes 786440 | tf_op jit(solution)/shard_map/ppermute | solution.py:33
  721.5 29.6 %collective-permute-start.125 = (bf16[128,1024]{0,1:T(8,128)(2,1)}, bf16[128,1024]{0,1:T(8,128)(2,1)}, u32[]{:S(2)}, u32[]{:S(2)}) collective-permute-start(bf16[128,1024]{0,1:T(8,128)(2,1)} %bitcast.236), channel_id=1, source_target_pairs={{0,2},{1,3},{2,0},{3,1},{4,6},{5,7},{6,4},{7,5},{8,10},{9,11},{10,... | collective-permute-start | bytes 786440 | tf_op jit(solution)/shard_map/ppermute | solution.py:33
  721.6 29.9 %collective-permute-start.124 = (bf16[128,1024]{0,1:T(8,128)(2,1)}, bf16[128,1024]{0,1:T(8,128)(2,1)}, u32[]{:S(2)}, u32[]{:S(2)}) collective-permute-start(bf16[128,1024]{0,1:T(8,128)(2,1)} %bitcast.236), channel_id=1, source_target_pairs={{0,1},{1,0},{2,3},{3,2},{4,5},{5,4},{6,7},{7,6},{8,9},{9,8},{10,11... | collective-permute-start | bytes 786440 | tf_op jit(solution)/shard_map/ppermute | solution.py:33
  (303 other events, 3244.7 us)

commit v2 on v1

--- a/solution.py
+++ b/solution.py
@@ -17,16 +17,18 @@
 f32 = jnp.float32
 
 
+def flip_list(blocks, index):
+    bit = 1
+    while bit < len(blocks):
+        turn = (index & bit) != 0
+        blocks = [jnp.where(turn, blocks[j ^ bit], blocks[j]) for j in range(len(blocks))]
+        bit *= 2
+    return blocks
+
+
 def flip(array, index, axis=0):
-    size = array.shape[axis]
-    bit = 1
-    while bit < size:
-        shape = array.shape[:axis] + (size // (2 * bit), 2, bit) + array.shape[axis + 1 :]
-        cut = array.reshape(shape)
-        turned = lax.rev(cut, (axis + 1,))
-        array = jnp.where((index & bit) != 0, turned, cut).reshape(array.shape)
-        bit *= 2
-    return array
+    blocks = [lax.index_in_dim(array, j, axis, keepdims=True) for j in range(array.shape[axis])]
+    return jnp.concatenate(flip_list(blocks, index), axis=axis)
 
 
 def swap(array, name, size, step):
@@ -42,7 +44,7 @@
 
 
 def sum_blocks(blocks, name, size):
-    total = blocks[0]
+    total = blocks[0].astype(f32)
     for step in range(1, size):
         total = total + swap(blocks[step].astype(bf16), name, size, step).astype(f32)
     return total
@@ -156,7 +158,8 @@
         return jnp.moveaxis(array, -2, -3).reshape(lead + (width,))
 
     def own_rows(array):
-        blocks = flip(array.reshape(n_t, rows, width), d)
+        cuts = array.reshape(n_t, rows, width)
+        blocks = [lax.dynamic_index_in_dim(cuts, d ^ step, 0, False) for step in range(n_t)]
         total = jnp.where(d == z, blocks[0], jnp.zeros_like(blocks[0]))
         for step in range(1, n_t):
             pairs = [(i * n_z + i, (i ^ step) * n_z + i) for i in range(n_t)]
@@ -167,14 +170,35 @@
         return jnp.concatenate(gather(array, DP, n_t), axis=0)
 
     def sum_rows(partial):
-        blocks = partial.reshape(n_t, rows, width)
+        blocks = partial.astype(bf16).reshape(n_t, rows, width)
         return sum_blocks([blocks[step] for step in range(n_t)], DP, n_t)
 
     def to_output(array):
-        blocks = flip(jnp.stack(gather(array, HEAD, n_z)), z)
-        blocks = flip(blocks, d)
-        got = deal([blocks[step] for step in range(n_t)], DP, n_t)
-        return flip(jnp.stack(got), d).reshape(1, slice_len, width)
+        planes = lax.all_gather(array, HEAD, axis=0, tiled=False)
+        blocks = [lax.dynamic_index_in_dim(planes, d ^ step, 0, False) for step in range(n_t)]
+        got = deal(blocks, DP, n_t)
+        return jnp.concatenate(flip_list(got, d), axis=0).reshape(1, slice_len, width)
+
+    def packed(layer):
+        qkv = qkv_weight[layer].reshape(cut, n_t, -1)
+        dense = dense_weight[layer].T.reshape(cut, n_t, -1)
+        up = up_weight[layer].reshape(cut, n_t, -1)
+        down = down_weight[layer].T.reshape(cut, n_t, -1)
+        return tuple(
+            [jnp.concatenate((one[:, j], two[:, j]), axis=1) for j in range(n_t)]
+            for one, two in ((qkv, dense), (up, down))
+        )
+
+    def to_planes(blocks):
+        got = deal(flip_list(blocks, d), DP, n_t)
+        return jnp.concatenate(flip_list(got, d), axis=0)
+
+    def join(planes):
+        return jnp.concatenate(gather(planes, SEQ, n_s), axis=1).transpose(1, 0, 2)
+
+    shards = [packed(layer) for layer in range(LAYERS)]
+    shards = [to_planes(shards[0][0]), shards[0][1], shards[1][0], shards[1][1]]
+    hidden = to_inner(own_rows(tokens[0])).astype(f32)
 
     wide = jnp.stack(
         (first_gain, first_shift, dense_bias, second_gain, second_shift, down_bias), axis=1
@@ -187,58 +211,34 @@
             up_bias.reshape(-1),
         ]
     )
-    small = lax.all_gather(small, (DP, SEQ, HEAD), axis=0, tiled=False)
-    small = small.reshape(n_t, n_s, n_z, -1)
+    small = lax.all_gather(small, (DP, SEQ), axis=0, tiled=False).reshape(n_t, n_s, -1)
     n_wide = LAYERS * 6 * cut
-    wide = small[:, :, 0, :n_wide].reshape(n_t, n_s, LAYERS, 6, cut)
+    wide = small[:, :, :n_wide].reshape(n_t, n_s, LAYERS, 6, cut)
     wide = flip(wide, c, 1).transpose(2, 3, 1, 0, 4).reshape(LAYERS, 6, width)
     tall = []
     begin = n_wide
-    for source in (query_bias, value_bias, up_bias):
-        size = source.shape[2]
+    tall_sizes = (HD, HD, units)
+    for size in tall_sizes:
+        size = size // (n_t * n_s)
         count = LAYERS * heads * size
-        piece = small[:, :, :, begin : begin + count].reshape(n_t, n_s, n_z, LAYERS, heads, size)
+        piece = small[:, :, begin : begin + count].reshape(n_t, n_s, LAYERS, heads, size)
         begin += count
-        piece = lax.dynamic_index_in_dim(piece, d, axis=4, keepdims=False)
-        piece = flip(piece, z, 2).transpose(3, 2, 0, 1, 4)
-        tall.append(piece.reshape(LAYERS, n_z, n_t * n_s * size))
-
-    def packed(layer):
-        qkv = qkv_weight[layer].reshape(cut, n_t, -1)
-        dense = dense_weight[layer].T.reshape(cut, n_t, -1)
-        up = up_weight[layer].reshape(cut, n_t, -1)
-        down = down_weight[layer].T.reshape(cut, n_t, -1)
-        return (jnp.concatenate((qkv, dense), axis=2), up, down)
-
-    def to_planes(array):
-        blocks = flip(array.transpose(1, 0, 2), d)
-        got = deal([blocks[step] for step in range(n_t)], DP, n_t)
-        return flip(jnp.stack(got), d).reshape(part, -1)
-
-    def along_z(array):
-        return gather(array, HEAD, n_z)
-
-    def join(blocks):
-        full = [jnp.concatenate(gather(block, SEQ, n_s), axis=0) for block in blocks]
-        return jnp.stack(full, axis=1)
-
-    hidden = to_inner(own_rows(tokens[0])).astype(f32)
-
-    weights = []
-    previous = None
-    for layer in range(LAYERS):
-        kinds = []
-        for shard in packed(layer):
-            shard = to_planes(shard)
-            if previous is not None:
-                shard = after(shard, *previous)
-            blocks = along_z(shard)
-            previous = blocks
-            kinds.append(join(blocks))
-        weights.append(kinds)
+        piece = lax.dynamic_index_in_dim(piece, d, axis=3, keepdims=False)
+        tall.append(piece.transpose(2, 0, 1, 3).reshape(LAYERS, -1))
+    tall = jnp.concatenate(tall, axis=1)
+    tall = jnp.stack(flip_list(gather(tall, HEAD, n_z), z), axis=1)
+
+    planes = lax.all_gather(shards[0], HEAD, axis=0, tiled=False)
+    messages = [planes]
+    previous = shards[0]
+    for shard in shards[1:]:
+        shard = to_planes([after(block, previous) for block in shard])
+        messages.append(lax.all_gather(shard, HEAD, axis=0, tiled=False))
+        previous = shard
+    weights = [join(planes) for planes in messages]
 
     qkv_columns = 3 * HD
-    head_ids = (z ^ jnp.arange(n_z, dtype=jnp.int32)) * heads + d
+    head_ids = jnp.arange(n_z, dtype=jnp.int32) * heads + d
     slopes = 2.0 ** (-8.0 * (head_ids + 1).astype(f32) / H)
     block_ids = (d ^ jnp.arange(n_t, dtype=jnp.int32)) * rows
     own_pos = (block_ids[:, None] + jnp.arange(rows, dtype=jnp.int32)[None]).reshape(-1)
@@ -248,15 +248,18 @@
 
     records = []
     for layer in range(LAYERS):
-        mixed, w_up, w_down = weights[layer]
+        mixed, feed = weights[2 * layer], weights[2 * layer + 1]
         w_qkv = mixed[:, :, :qkv_columns].reshape(width, -1)
         w_dense = mixed[:, :, qkv_columns:].reshape(width, -1)
-        w_up = w_up.reshape(width, -1)
-        w_down = w_down.reshape(width, -1)
+        w_up = feed[:, :, :units].reshape(width, -1)
+        w_down = feed[:, :, units:].reshape(width, -1)
         gain_one, shift_one, bias_dense, gain_two, shift_two, bias_down = (
             wide[layer, i] for i in range(6)
         )
-        bias_query, bias_value, bias_up = (piece[layer] for piece in tall)
+        bias_query, bias_value, bias_up = (
+            tall[layer, :, begin : begin + size]
+            for begin, size in ((0, HD), (HD, HD), (2 * HD, units))
+        )
         normed_one = all_rows(norm_forward(hidden, gain_one, shift_one))
         projected = product("rd,dn->rn", normed_one, w_qkv)
         projected = projected.reshape(slice_len, n_z, 3, HD)
@@ -289,18 +292,16 @@
     weight_grads = [None] * LAYERS
     wide_grads = [None] * LAYERS
     tall_grads = [None] * LAYERS
-    chain = [None]
 
     def give_back(grad):
         blocks = grad.reshape(n_s, part, n_z, -1)
-        mine = sum_blocks([blocks[step] for step in range(n_s)], SEQ, n_s)
-        if chain[0] is not None:
-            mine = after(mine, chain[0])
-        mine = sum_blocks([mine[:, step] for step in range(n_z)], HEAD, n_z).astype(bf16)
-        chain[0] = mine
-        mine = flip(mine.reshape(n_t, cut, -1), d)
-        got = deal([mine[step] for step in range(n_t)], DP, n_t)
-        return flip(jnp.stack(got, axis=1), d, 1).astype(f32)
+        mine = sum_blocks([blocks[step] for step in range(n_s)], SEQ, n_s).astype(bf16)
+        mine = mine.transpose(1, 0, 2)
+        mine = lax.psum_scatter(mine, HEAD, scatter_dimension=0, tiled=False)
+        mine = mine.reshape(n_t, cut, -1)
+        blocks = [lax.dynamic_index_in_dim(mine, d ^ step, 0, False) for step in range(n_t)]
+        got = deal(blocks, DP, n_t)
+        return jnp.stack(flip_list(got, d), axis=1).astype(f32)
 
     for layer in reversed(range(LAYERS)):
         (
@@ -313,18 +314,20 @@
         act_grad = product("rd,df->rf", grad_low, w_down)
         pre_grad = jax.vjp(gelu_tanh, pre_up)[1](act_grad)[0].astype(bf16)
         e = sum_rows(product("rf,df->rd", pre_grad, w_up))
-        down_grad = product("rd,rf->df", grad_low, activation).reshape(width, n_z, -1)
-        up_grad = product("rd,rf->df", normed_two, pre_grad).reshape(width, n_z, -1)
+        down_grad = product("rd,rf->df", grad_low, activation).astype(bf16)
+        up_grad = product("rd,rf->df", normed_two, pre_grad).astype(bf16)
+        feed_grad = jnp.concatenate(
+            (up_grad.reshape(width, n_z, -1), down_grad.reshape(width, n_z, -1)), axis=2
+        )
         up_bias_grad = jnp.sum(pre_grad, axis=0, dtype=f32).reshape(n_z, -1)
-        down_share = give_back(down_grad)
-        up_share = give_back(up_grad)
+        feed_share = give_back(feed_grad)
         part_mid, gain_two_grad, shift_two_grad = norm_backward(hidden_mid, gain_two, e)
         mid_grad = gradient + part_mid
         dense_bias_grad = jnp.sum(mid_grad, axis=0)
         mid_low = all_rows(mid_grad.astype(bf16))
         context_grad = product("rd,dc->rc", mid_low, w_dense).astype(bf16)
         context_grad = context_grad.reshape(slice_len, n_z, HD).transpose(1, 0, 2)
-        dense_grad = product("rd,rc->dc", mid_low, context).reshape(width, n_z, -1)
+        dense_grad = product("rd,rc->dc", mid_low, context).astype(bf16).reshape(width, n_z, -1)
         query_grad, key_grad, value_grad = attend_backward(
             queries, keys, values, context_grad, log_total, query_pos, key_pos, slopes
         )
@@ -336,7 +339,7 @@
         value_bias_grad = jnp.sum(both[..., HD:], axis=1, dtype=f32)
         joined = jnp.concatenate((query_grad, both), axis=2)
         joined = joined.transpose(1, 0, 2).reshape(slice_len, -1)
-        qkv_grad = product("rd,rn->dn", normed_one, joined).reshape(width, n_z, -1)
+        qkv_grad = product("rd,rn->dn", normed_one, joined).astype(bf16).reshape(width, n_z, -1)
         mixed_share = give_back(jnp.concatenate((qkv_grad, dense_grad), axis=2))
         e = sum_rows(product("rn,dn->rd", joined, w_qkv))
         part_in, gain_one_grad, shift_one_grad = norm_backward(hidden, gain_one, e)
@@ -344,8 +347,8 @@
         weight_grads[layer] = (
             mixed_share[:, :, :qkv_columns].reshape(cut, -1),
             mixed_share[:, :, qkv_columns:].reshape(cut, -1).T,
-            up_share.reshape(cut, -1),
-            down_share.reshape(cut, -1).T,
+            feed_share[:, :, :units].reshape(cut, -1),
+            feed_share[:, :, units:].reshape(cut, -1).T,
         )
         wide_grads[layer] = jnp.stack(
             (
@@ -370,14 +373,13 @@
         return total
 
     wide = jnp.stack(wide_grads).reshape(LAYERS * 6, n_s, n_t, cut)
-    sizes_tall = (HD, HD, units)
     pieces, begin = [], 0
     tall = jnp.stack(tall_grads)
-    for size in sizes_tall:
+    for size in tall_sizes:
         piece = tall[:, :, begin : begin + size]
         begin += size
         piece = piece.reshape(LAYERS, n_z, n_t, n_s, size // (n_t * n_s))
-        pieces.append(flip(piece, c, 3))
+        pieces.append(flip(flip(piece, c, 3), z, 1))
     tall = jnp.concatenate(
         [piece.transpose(3, 1, 2, 0, 4).reshape(n_s, n_z, n_t, -1) for piece in pieces], axis=3
     )
@@ -393,7 +395,7 @@
     wide = wide.reshape(LAYERS, 6, cut)
     tall = flip(jnp.stack([item[n_wide:] for item in got]), d)
     outs, begin = [], 0
-    for size in sizes_tall:
+    for size in tall_sizes:
         size = size // (n_t * n_s)
         piece = tall[:, begin : begin + LAYERS * size].reshape(n_t, LAYERS, size)
         begin += LAYERS * size

time: 819 us -> 704 us (0.86)
  starting transfers between devices: 210 us -> 131 us
  blocking collectives: 67.8 us -> 10.7 us
  waiting for transfers between devices: 227 us -> 271 us
  other arithmetic: 102 us -> 73.5 us
  local copies, waits for them, and re-layouts: 134 us -> 109 us
  matrix products: 65 us -> 81.5 us
  between operations: 5.06 us -> 18.4 us
    reduce_scatter x0 -> x4, waiting for transfers between devices: none -> 88.1 us  [give_back(): mine = lax.psum_scatter(mine, HEAD, scatter_dimension=0, tiled=False)]
    ppermute x173 -> x100, starting transfers between devices: 196 us -> 109 us  [swap(): return lax.ppermute(array, name, [(i, i ^ step) for i in range(size)])]
    ppermute x173 -> x100, waiting for transfers between devices: 227 us -> 151 us  [swap(): return lax.ppermute(array, name, [(i, i ^ step) for i in range(size)])]
    all_gather x1, blocking collectives: 67.8 us -> 10.7 us  [per_device(): lax.all_gather(small, (DP, SEQ), axis=0, tiled=False).reshape(n_t, n_s, -1)]
    another operation x91 -> x4, other arithmetic: 36.8 us -> 0.92 us  [the longest x2 0.77 us: per_device(): tall = jnp.stack(flip_list(gather(tall, HEAD, n_z), z), axis=1)]
    all_gather x0 -> x6, waiting for transfers between devices: none -> 30.8 us  [the longest x2 13.6 us: to_output(): planes = lax.all_gather(array, HEAD, axis=0, tiled=False)]
    rev x23 -> x0, local copies, waits for them, and re-layouts: 29.9 us -> none  [flip(): turned = lax.rev(cut, (axis + 1,))]
    dot_general x36, matrix products: 65 us -> 81.5 us  [product(): return jnp.einsum(spec, left, right, preferred_element_type=f32)]
  transfers between devices with their start and end apart: 179 -> 116, of which waited for: 55 -> 61; matrix products, arithmetic and copies ran while one was open for 32% -> 24% of each run, Pallas kernels for 0% -> 0%
where the time goes in v2:
time: 704 us; the launch traced here: 695 us
  waiting for transfers between devices  271 us (38%)
  starting transfers between devices  131 us (19%)
  local copies, waits for them, and re-layouts  109 us (15%)
  matrix products  81.5 us (12%)
  other arithmetic  73.5 us (10%)
  between operations  18.4 us (3%)
  blocking collectives  10.7 us (2%)
    ppermute x100, waiting for transfers between devices, swap(): return lax.ppermute(array, name, [(i, i ^ step) for i in range(size)])  151 us
    ppermute x100, starting transfers between devices, swap(): return lax.ppermute(array, name, [(i, i ^ step) for i in range(size)])  109 us
    reduce_scatter x4, waiting for transfers between devices, give_back(): mine = lax.psum_scatter(mine, HEAD, scatter_dimension=0, tiled=False)  88.1 us
    dot_general x36, matrix products, product(): return jnp.einsum(spec, left, right, preferred_element_type=f32)  81.5 us
    unnamed x422, local copies, waits for them, and re-layouts  33.3 us
    ppermute x6, starting transfers between devices, own_rows(): total = total + lax.ppermute(blocks[step], (DP, HEAD), pairs)  21 us
  transfers between devices with their start and end apart: 116, of which 61 were waited for; matrix products, arithmetic and copies ran while one was open for 24% of the time, Pallas kernels for 0%

profile of v2, /device:TPU:0, one launch (start us, length us, event | category | flops | bytes accessed | tf_op | source)
XLA Modules:
  0.0 695.3 jit_solution(15722256127668623274)
XLA Ops:
  13.8 10.7 %all-gather.5 = f32[8,1,1920]{2,1,0:T(1,128)S(1)} all-gather(f32[1,1,1920]{2,1,0:T(1,128)S(1)} %reshape.704), channel_id=2, replica_groups=mesh['dp'=4,'seq'=2,'head'=4] {'dp','seq'}, dimensions={0}, use_global_device_ids=true | all-gather | bytes 69120 | tf_op jit(solution)/shard_map/all_gather | solution.py:214
  99.5 5.1 collective-permute-done.4
  126.4 6.7 all-gather.19.cloned.1.call-done
  146.7 5.0 collective-permute-start.53
  155.8 7.1 %collective-permute-start.19 = (bf16[128,1024]{1,0:T(8,128)(2,1)}, bf16[128,1024]{1,0:T(8,128)(2,1)}, u32[]{:S(2)}, u32[]{:S(2)}) collective-permute-start(bf16[128,1024]{1,0:T(8,128)(2,1)} %add_convert_fusion.8), channel_id=1, source_target_pairs={{0,24},{8,16},{16,8},{24,0},{1,25},{9,17},{17,9},{25,1},{2,26},{10... | collective-permute-start | bytes 786440 | tf_op jit(solution)/shard_map/ppermute | solution.py:35
  202.5 6.2 collective-permute-done.29
  217.7 4.9 collective-permute-done.54
  224.1 6.6 all-gather.23.cloned.1.call-done
  254.9 6.2 collective-permute-done.37
  280.6 5.4 convert_reduce_fusion
  297.2 5.1 collective-permute-done.59
  319.1 6.6 collective-permute-done.62
  355.7 5.7 collective-permute-done.64
  361.5 5.0 collective-permute-done.66
  372.6 5.8 collective-permute-done.69
  381.1 4.7 convert_reduce_fusion.1
  390.8 5.8 collective-permute-done.70
  415.4 5.0 fusion.6
  420.4 4.9 multiply_reduce_fusion
  457.6 5.9 collective-permute-done.79
  541.0 13.6 %all-gather.13.cloned.1.call-done = bf16[4,128,1024]{2,1,0:T(8,128)(2,1)} async-done(((bf16[1,128,1024]{2,1,0:T(8,128)(2,1)}), bf16[4,128,1024]{2,1,0:T(8,128)(2,1)}) %all-gather.13.cloned.1.call-update) | async-done | bytes 1048592 | tf_op jit(solution)/shard_map/all_gather | solution.py:177
  572.1 12.2 %reduce-scatter.5.cloned.1.call-done = bf16[1,512,256]{1,2,0:T(8,128)(2,1)} async-done(((bf16[4,512,256]{1,2,0:T(8,128)(2,1)}), bf16[1,512,256]{1,2,0:T(8,128)(2,1)}) %reduce-scatter.5.cloned.1.call-update) | async-done | bytes 262160 | tf_op jit(solution)/shard_map/reduce_scatter | solution.py:300
  593.3 35.8 %reduce-scatter.11.cloned.1.call-done = bf16[1,512,512]{1,2,0:T(8,128)(2,1)} async-done(((bf16[4,512,512]{1,2,0:T(8,128)(2,1)}), bf16[1,512,512]{1,2,0:T(8,128)(2,1)}) %reduce-scatter.11.cloned.1.call-update) | async-done | bytes 524304 | tf_op jit(solution)/shard_map/reduce_scatter | solution.py:300
  634.4 40.2 %reduce-scatter.9.cloned.1.call-done = bf16[1,512,512]{1,2,0:T(8,128)(2,1)} async-done(((bf16[4,512,512]{1,2,0:T(8,128)(2,1)}), bf16[1,512,512]{1,2,0:T(8,128)(2,1)}) %reduce-scatter.9.cloned.1.call-update) | async-done | bytes 524304 | tf_op jit(solution)/shard_map/reduce_scatter | solution.py:300
  (992 shorter events, 456.7 us)
Async XLA Ops:
  7.2 78.3 %all-gather.17.cloned.1.call-start = ((), (), s32[]{:S(2)}) async-start(), calls=%async_computation.10 | async-start | bytes 1310720 | tf_op jit(solution)/shard_map/all_gather | solution.py:231
  26.0 31.2 %collective-permute-start.12 = (f32[2,384]{1,0:T(2,128)}, f32[2,384]{1,0:T(2,128)}, u32[]{:S(2)}, u32[]{:S(2)}) collective-permute-start(f32[2,384]{1,0:T(2,128)} %pad_maximum_fusion.70), channel_id=1, source_target_pairs={{0,1},{1,0},{2,3},{3,2},{4,5},{5,4},{6,7},{7,6},{8,9},{9,8},{10,11... | collective-permute-start | bytes 9224 | tf_op jit(solution)/shard_map/ppermute | solution.py:35
  27.6 29.6 %collective-permute-start.11 = (f32[2,384]{1,0:T(2,128)}, f32[2,384]{1,0:T(2,128)}, u32[]{:S(2)}, u32[]{:S(2)}) collective-permute-start(f32[2,384]{1,0:T(2,128)} %pad_maximum_fusion.70), channel_id=1, source_target_pairs={{0,2},{1,3},{2,0},{3,1},{4,6},{5,7},{6,4},{7,5},{8,10},{9,11},{10,... | collective-permute-start | bytes 9224 | tf_op jit(solution)/shard_map/ppermute | solution.py:35
  49.3 26.1 %collective-permute-start = (bf16[128,1024]{1,0:T(8,128)(2,1)}, bf16[128,1024]{1,0:T(8,128)(2,1)}, u32[]{:S(2)}, u32[]{:S(2)}) collective-permute-start(bf16[128,1024]{1,0:T(8,128)(2,1)} %get-tuple-element.236), channel_id=1, source_target_pairs={{0,8},{9,1},{18,26},{27,19},{4,12},{13,5},{22,30},{31,23}} | collective-permute-start | bytes 786440 | tf_op jit(solution)/shard_map/ppermute | solution.py:166
  57.1 76.0 %all-gather.19.cloned.1.call-start = ((), (), s32[]{:S(2)}) async-start(), calls=%async_computation.11 | async-start | bytes 2621440 | tf_op jit(solution)/shard_map/all_gather | solution.py:236
  69.2 114.1 %collective-permute-start.51 = (bf16[128,1024]{1,0:T(8,128)(2,1)}, bf16[128,1024]{1,0:T(8,128)(2,1)}, u32[]{:S(2)}, u32[]{:S(2)}) collective-permute-start(bf16[128,1024]{1,0:T(8,128)(2,1)} %get-tuple-element.218), channel_id=1, source_target_pairs={{0,8},{9,1},{18,26},{27,19},{4,12},{13,5},{22,30},{31,23}} | collective-permute-start | bytes 786440 | tf_op jit(solution)/shard_map/ppermute | solution.py:166
  74.6 114.1 %all-gather.21.cloned.1.call-start = ((), (), s32[]{:S(2)}) async-start(), calls=%async_computation.12 | async-start | bytes 1310720 | tf_op jit(solution)/shard_map/all_gather | solution.py:236
  108.8 121.9 %all-gather.23.cloned.1.call-start = ((), (), s32[]{:S(2)}) async-start(), calls=%async_computation.13 | async-start | bytes 2621440 | tf_op jit(solution)/shard_map/all_gather | solution.py:236
  111.0 26.6 %collective-permute-start.43 = (bf16[128,512]{0,1:T(8,128)(2,1)}, bf16[128,512]{0,1:T(8,128)(2,1)}, u32[]{:S(2)}, u32[]{:S(2)}) collective-permute-start(bf16[128,512]{0,1:T(8,128)(2,1)} %get-tuple-element.260), channel_id=1, source_target_pairs={{0,8},{8,0},{16,24},{24,16},{1,9},{9,1},{17,25},{25,17},{2,10},{10... | collective-permute-start | bytes 393224 | tf_op jit(solution)/shard_map/ppermute | solution.py:35
  112.5 26.6 %collective-permute-start.41 = (bf16[128,512]{0,1:T(8,128)(2,1)}, bf16[128,512]{0,1:T(8,128)(2,1)}, u32[]{:S(2)}, u32[]{:S(2)}) collective-permute-start(bf16[128,512]{0,1:T(8,128)(2,1)} %get-tuple-element.261), channel_id=1, source_target_pairs={{0,24},{8,16},{16,8},{24,0},{1,25},{9,17},{17,9},{25,1},{2,26},{10... | collective-permute-start | bytes 393224 | tf_op jit(solution)/shard_map/ppermute | solution.py:35
  113.9 26.6 %collective-permute-start.42 = (bf16[128,512]{0,1:T(8,128)(2,1)}, bf16[128,512]{0,1:T(8,128)(2,1)}, u32[]{:S(2)}, u32[]{:S(2)}) collective-permute-start(bf16[128,512]{0,1:T(8,128)(2,1)} %get-tuple-element.262), channel_id=1, source_target_pairs={{0,16},{8,24},{16,0},{24,8},{1,17},{9,25},{17,1},{25,9},{2,18},{10... | collective-permute-start | bytes 393224 | tf_op jit(solution)/shard_map/ppermute | solution.py:35
  146.7 40.0 %collective-permute-start.53 = (bf16[128,1024]{1,0:T(8,128)(2,1)}, bf16[128,1024]{1,0:T(8,128)(2,1)}, u32[]{:S(2)}, u32[]{:S(2)}) collective-permute-start(bf16[128,1024]{1,0:T(8,128)(2,1)} %get-tuple-element.219), channel_id=1, source_target_pairs={{0,24},{9,17},{18,10},{27,3},{4,28},{13,21},{22,14},{31,7}} | collective-permute-start | bytes 786440 | tf_op jit(solution)/shard_map/ppermute | solution.py:166
  186.5 343.5 %all-gather.15.cloned.1.call-start = ((), (), s32[]{:S(2)}) async-start(), calls=%async_computation.5 | async-start | bytes 1310720 | tf_op jit(solution)/shard_map/all_gather | solution.py:177
  215.2 34.1 %collective-permute-start.56 = (bf16[128,1024]{1,0:T(8,128)(2,1)S(1)}, bf16[128,1024]{1,0:T(8,128)(2,1)}, u32[]{:S(2)}, u32[]{:S(2)}) collective-permute-start(bf16[128,1024]{1,0:T(8,128)(2,1)S(1)} %reshape.661), channel_id=1, source_target_pairs={{0,24},{8,16},{16,8},{24,0},{1,25},{9,17},{17,9},{25,1},{2,26},{10... | collective-permute-start | bytes 786440 | tf_op jit(solution)/shard_map/ppermute | solution.py:35
  469.3 67.6 %reduce-scatter.7.cloned.1.call-start = ((), (), s32[]{:S(2)}) async-start(), calls=%async_computation.7 | async-start | bytes 1310720 | tf_op jit(solution)/shard_map/reduce_scatter | solution.py:300
  475.7 79.0 %all-gather.13.cloned.1.call-start = ((), (), s32[]{:S(2)}) async-start(), calls=%async_computation.4 | async-start | bytes 1310720 | tf_op jit(solution)/shard_map/all_gather | solution.py:177
  478.3 106.0 %reduce-scatter.5.cloned.1.call-start = ((), (), s32[]{:S(2)}) async-start(), calls=%async_computation.6 | async-start | bytes 1310720 | tf_op jit(solution)/shard_map/reduce_scatter | solution.py:300
  491.7 137.4 %reduce-scatter.11.cloned.1.call-start = ((), (), s32[]{:S(2)}) async-start(), calls=%async_computation.9 | async-start | bytes 2621440 | tf_op jit(solution)/shard_map/reduce_scatter | solution.py:300
  504.5 170.0 %reduce-scatter.9.cloned.1.call-start = ((), (), s32[]{:S(2)}) async-start(), calls=%async_computation.8 | async-start | bytes 2621440 | tf_op jit(solution)/shard_map/reduce_scatter | solution.py:300
  538.5 50.2 %collective-permute-start.88 = (bf16[128,256]{0,1:T(8,128)(2,1)S(1)}, bf16[128,256]{0,1:T(8,128)(2,1)S(1)}, u32[]{:S(2)}, u32[]{:S(2)}) collective-permute-start(bf16[128,256]{0,1:T(8,128)(2,1)S(1)} %copy.379), channel_id=1, source_target_pairs={{0,24},{8,16},{16,8},{24,0},{1,25},{9,17},{17,9},{25,1},{2,26},{10... | collective-permute-start | bytes 196616 | tf_op jit(solution)/shard_map/ppermute | solution.py:35
  540.2 50.3 %collective-permute-start.89 = (bf16[128,256]{0,1:T(8,128)(2,1)S(1)}, bf16[128,256]{0,1:T(8,128)(2,1)S(1)}, u32[]{:S(2)}, u32[]{:S(2)}) collective-permute-start(bf16[128,256]{0,1:T(8,128)(2,1)S(1)} %copy.380), channel_id=1, source_target_pairs={{0,16},{8,24},{16,0},{24,8},{1,17},{9,25},{17,1},{25,9},{2,18},{10... | collective-permute-start | bytes 196616 | tf_op jit(solution)/shard_map/ppermute | solution.py:35
  630.5 48.7 %collective-permute-start.96 = (bf16[128,512]{0,1:T(8,128)(2,1)S(1)}, bf16[128,512]{0,1:T(8,128)(2,1)S(1)}, u32[]{:S(2)}, u32[]{:S(2)}) collective-permute-start(bf16[128,512]{0,1:T(8,128)(2,1)S(1)} %copy.391), channel_id=1, source_target_pairs={{0,24},{8,16},{16,8},{24,0},{1,25},{9,17},{17,9},{25,1},{2,26},{10... | collective-permute-start | bytes 393224 | tf_op jit(solution)/shard_map/ppermute | solution.py:35
  633.3 48.7 %collective-permute-start.97 = (bf16[128,512]{0,1:T(8,128)(2,1)S(1)}, bf16[128,512]{0,1:T(8,128)(2,1)S(1)}, u32[]{:S(2)}, u32[]{:S(2)}) collective-permute-start(bf16[128,512]{0,1:T(8,128)(2,1)S(1)} %copy.392), channel_id=1, source_target_pairs={{0,16},{8,24},{16,0},{24,8},{1,17},{9,25},{17,1},{25,9},{2,18},{10... | collective-permute-start | bytes 393224 | tf_op jit(solution)/shard_map/ppermute | solution.py:35
  633.9 48.1 %collective-permute-start.98 = (bf16[128,512]{0,1:T(8,128)(2,1)S(1)}, bf16[128,512]{0,1:T(8,128)(2,1)S(1)}, u32[]{:S(2)}, u32[]{:S(2)}) collective-permute-start(bf16[128,512]{0,1:T(8,128)(2,1)S(1)} %copy.393), channel_id=1, source_target_pairs={{0,8},{8,0},{16,24},{24,16},{1,9},{9,1},{17,25},{25,17},{2,10},{10... | collective-permute-start | bytes 393224 | tf_op jit(solution)/shard_map/ppermute | solution.py:35
  (295 other events, 2447.2 us)
Sparse Core Ops, SparseCore 0:
  57.2 28.1 all-gather.16
  87.6 45.4 all-gather.18
  134.7 26.6 all-gather.20
  186.6 43.9 all-gather.22
  469.4 25.2 all-gather.14
  497.4 28.3 reduce-scatter.6
  528.0 26.5 all-gather.12
  557.6 26.6 reduce-scatter.4
  586.6 42.4 reduce-scatter.10
  631.4 43.1 reduce-scatter.8

commit v3 on v2

--- a/solution.py
+++ b/solution.py
@@ -41,6 +41,14 @@
 
 def deal(blocks, name, size):
     return [blocks[0]] + [swap(blocks[step], name, size, step) for step in range(1, size)]
+
+
+def meet(*groups):
+    return lax.optimization_barrier(groups)
+
+
+def add_all(blocks):
+    return functools.reduce(jnp.add, [block.astype(f32) for block in blocks])
 
 
 def sum_blocks(blocks, name, size):
@@ -166,17 +174,24 @@
             total = total + lax.ppermute(blocks[step], (DP, HEAD), pairs)
         return total
 
-    def all_rows(array):
-        return jnp.concatenate(gather(array, DP, n_t), axis=0)
-
-    def sum_rows(partial):
+    def send_rows(array):
+        return gather(array, DP, n_t)
+
+    def send_sums(partial):
         blocks = partial.astype(bf16).reshape(n_t, rows, width)
-        return sum_blocks([blocks[step] for step in range(n_t)], DP, n_t)
-
-    def to_output(array):
-        planes = lax.all_gather(array, HEAD, axis=0, tiled=False)
+        return deal([blocks[step] for step in range(n_t)], DP, n_t)
+
+    def joined_rows(blocks):
+        return jnp.concatenate(blocks, axis=0)
+
+    def to_planes_of(array):
+        return lax.all_gather(array, HEAD, axis=0, tiled=False)
+
+    def send_output(planes):
         blocks = [lax.dynamic_index_in_dim(planes, d ^ step, 0, False) for step in range(n_t)]
-        got = deal(blocks, DP, n_t)
+        return deal(blocks, DP, n_t)
+
+    def output_of(got):
         return jnp.concatenate(flip_list(got, d), axis=0).reshape(1, slice_len, width)
 
     def packed(layer):
@@ -197,45 +212,36 @@
         return jnp.concatenate(gather(planes, SEQ, n_s), axis=1).transpose(1, 0, 2)
 
     shards = [packed(layer) for layer in range(LAYERS)]
-    shards = [to_planes(shards[0][0]), shards[0][1], shards[1][0], shards[1][1]]
-    hidden = to_inner(own_rows(tokens[0])).astype(f32)
-
-    wide = jnp.stack(
-        (first_gain, first_shift, dense_bias, second_gain, second_shift, down_bias), axis=1
+    first_shard = to_planes(shards[0][0])
+    messages = [to_planes_of(first_shard)]
+    start_rows = own_rows(tokens[0])
+
+    wide = jnp.concatenate(
+        (first_gain, first_shift, dense_bias, second_gain, second_shift, down_bias), axis=0
     )
-    small = jnp.concatenate(
-        [
-            wide.reshape(-1),
-            query_bias.reshape(-1),
-            value_bias.reshape(-1),
-            up_bias.reshape(-1),
-        ]
-    )
-    small = lax.all_gather(small, (DP, SEQ), axis=0, tiled=False).reshape(n_t, n_s, -1)
-    n_wide = LAYERS * 6 * cut
-    wide = small[:, :, :n_wide].reshape(n_t, n_s, LAYERS, 6, cut)
-    wide = flip(wide, c, 1).transpose(2, 3, 1, 0, 4).reshape(LAYERS, 6, width)
+    tall = jnp.concatenate((query_bias, value_bias, up_bias), axis=2)
+    small = jnp.concatenate((wide, tall.reshape(-1, cut)), axis=0)
+    small = after(small, first_shard)
+    small = lax.all_gather(small, (DP, SEQ), axis=0, tiled=False)
+    small = small.reshape((n_t, n_s) + small.shape[1:])
+    wide = small[:, :, : 6 * LAYERS].transpose(2, 1, 0, 3)
+    wide = flip(wide, c, 1).reshape(6, LAYERS, width)
+    each = small[:, :, 6 * LAYERS :].reshape(n_t, n_s, LAYERS, heads, -1)
+    each = lax.dynamic_index_in_dim(each, d, axis=3, keepdims=False)
     tall = []
-    begin = n_wide
+    begin = 0
     tall_sizes = (HD, HD, units)
     for size in tall_sizes:
         size = size // (n_t * n_s)
-        count = LAYERS * heads * size
-        piece = small[:, :, begin : begin + count].reshape(n_t, n_s, LAYERS, heads, size)
-        begin += count
-        piece = lax.dynamic_index_in_dim(piece, d, axis=3, keepdims=False)
+        piece = each[:, :, :, begin : begin + size]
+        begin += size
         tall.append(piece.transpose(2, 0, 1, 3).reshape(LAYERS, -1))
     tall = jnp.concatenate(tall, axis=1)
     tall = jnp.stack(flip_list(gather(tall, HEAD, n_z), z), axis=1)
 
-    planes = lax.all_gather(shards[0], HEAD, axis=0, tiled=False)
-    messages = [planes]
-    previous = shards[0]
-    for shard in shards[1:]:
-        shard = to_planes([after(block, previous) for block in shard])
-        messages.append(lax.all_gather(shard, HEAD, axis=0, tiled=False))
-        previous = shard
-    weights = [join(planes) for planes in messages]
+    hidden = to_inner(start_rows).astype(f32)
+    second_shard = to_planes([after(block, small) for block in shards[0][1]])
+    messages.append(to_planes_of(second_shard))
 
     qkv_columns = 3 * HD
     head_ids = jnp.arange(n_z, dtype=jnp.int32) * heads + d
@@ -246,36 +252,52 @@
     others = (c ^ jnp.arange(n_s, dtype=jnp.int32)) * slice_len
     key_pos = (others[:, None] + own_pos[None]).reshape(-1)
 
+    cot = cotangent[0]
     records = []
     for layer in range(LAYERS):
-        mixed, feed = weights[2 * layer], weights[2 * layer + 1]
+        mixed, feed = (join(planes) for planes in messages[2 * layer : 2 * layer + 2])
         w_qkv = mixed[:, :, :qkv_columns].reshape(width, -1)
         w_dense = mixed[:, :, qkv_columns:].reshape(width, -1)
         w_up = feed[:, :, :units].reshape(width, -1)
         w_down = feed[:, :, units:].reshape(width, -1)
         gain_one, shift_one, bias_dense, gain_two, shift_two, bias_down = (
-            wide[layer, i] for i in range(6)
+            wide[i, layer] for i in range(6)
         )
         bias_query, bias_value, bias_up = (
             tall[layer, :, begin : begin + size]
             for begin, size in ((0, HD), (HD, HD), (2 * HD, units))
         )
-        normed_one = all_rows(norm_forward(hidden, gain_one, shift_one))
+        normed_one = joined_rows(send_rows(norm_forward(hidden, gain_one, shift_one)))
         projected = product("rd,dn->rn", normed_one, w_qkv)
         projected = projected.reshape(slice_len, n_z, 3, HD)
         queries = (projected[:, :, 0] + bias_query[None]).astype(bf16).transpose(1, 0, 2)
         keys = projected[:, :, 1].astype(bf16)
         values = (projected[:, :, 2] + bias_value[None]).astype(bf16)
         both = jnp.concatenate((keys, values), axis=2).transpose(1, 0, 2)
-        both = jnp.concatenate(gather(both, SEQ, n_s), axis=1)
+        both = gather(both, SEQ, n_s)
+        if layer == 0:
+            later = [to_planes([after(block, both[0]) for block in shards[1][0]])]
+            later.append(to_planes([after(block, later[0]) for block in shards[1][1]]))
+            cot_rows = own_rows(after(cot, both[0]))
+        else:
+            cot_rows = send_rows(after(cot_rows, both[0]))
+        both = jnp.concatenate(both, axis=1)
         keys, values = both[..., :HD], both[..., HD:]
         context, log_total = attend_forward(queries, keys, values, query_pos, key_pos, slopes)
         context = context.astype(bf16).transpose(1, 0, 2).reshape(slice_len, -1)
-        hidden_mid = hidden + sum_rows(product("rc,dc->rd", context, w_dense)) + bias_dense
-        normed_two = all_rows(norm_forward(hidden_mid, gain_two, shift_two))
+        got = send_sums(product("rc,dc->rd", context, w_dense))
+        if layer == 0:
+            got, later, cot_rows = meet(got, later, cot_rows)
+            messages.extend(to_planes_of(shard) for shard in later)
+            cot_rows = to_inner(cot_rows)
+        else:
+            got, cot_rows = meet(got, cot_rows)
+        hidden_mid = hidden + add_all(got) + bias_dense
+        normed_two = joined_rows(send_rows(norm_forward(hidden_mid, gain_two, shift_two)))
         pre_up = product("rd,df->rf", normed_two, w_up) + bias_up.reshape(-1)
         activation = gelu_tanh(pre_up).astype(bf16)
-        hidden_next = hidden_mid + sum_rows(product("rf,df->rd", activation, w_down)) + bias_down
+        got = send_sums(product("rf,df->rd", activation, w_down))
+        hidden_next = hidden_mid + add_all(got) + bias_down
         records.append(
             (
                 (w_qkv, w_dense, w_up, w_down, gain_one, gain_two),
@@ -285,71 +307,96 @@
         )
         hidden = hidden_next
 
-    output = to_output(to_outer(hidden.astype(bf16)))
-
-    start = to_inner(own_rows(cotangent[0]))
-    gradient = start.astype(f32)
-    weight_grads = [None] * LAYERS
+    output_low = to_outer(hidden.astype(bf16))
+
+    gradient = cot_rows[0].astype(f32)
+    grad_low = joined_rows(cot_rows)
     wide_grads = [None] * LAYERS
     tall_grads = [None] * LAYERS
 
-    def give_back(grad):
+    def core_sum(grad):
         blocks = grad.reshape(n_s, part, n_z, -1)
         mine = sum_blocks([blocks[step] for step in range(n_s)], SEQ, n_s).astype(bf16)
-        mine = mine.transpose(1, 0, 2)
-        mine = lax.psum_scatter(mine, HEAD, scatter_dimension=0, tiled=False)
+        return mine.transpose(1, 0, 2)
+
+    def head_sum(mine):
+        return lax.psum_scatter(mine, HEAD, scatter_dimension=0, tiled=False)
+
+    def send_shares(mine):
         mine = mine.reshape(n_t, cut, -1)
         blocks = [lax.dynamic_index_in_dim(mine, d ^ step, 0, False) for step in range(n_t)]
-        got = deal(blocks, DP, n_t)
+        return deal(blocks, DP, n_t)
+
+    def share_of(got):
         return jnp.stack(flip_list(got, d), axis=1).astype(f32)
 
+    feed_shares = [None] * LAYERS
+    mixed_shares = [None] * LAYERS
+    feed_sums = [None] * LAYERS
+    mixed_sums = [None] * LAYERS
     for layer in reversed(range(LAYERS)):
         (
             (w_qkv, w_dense, w_up, w_down, gain_one, gain_two),
             (hidden, hidden_mid, normed_one, normed_two),
             (queries, keys, values, log_total, context, pre_up, activation),
         ) = records[layer]
+        last = layer == LAYERS - 1
         down_bias_grad = jnp.sum(gradient, axis=0)
-        grad_low = all_rows(gradient.astype(bf16))
         act_grad = product("rd,df->rf", grad_low, w_down)
         pre_grad = jax.vjp(gelu_tanh, pre_up)[1](act_grad)[0].astype(bf16)
-        e = sum_rows(product("rf,df->rd", pre_grad, w_up))
+        got = send_sums(product("rf,df->rd", pre_grad, w_up))
         down_grad = product("rd,rf->df", grad_low, activation).astype(bf16)
         up_grad = product("rd,rf->df", normed_two, pre_grad).astype(bf16)
         feed_grad = jnp.concatenate(
             (up_grad.reshape(width, n_z, -1), down_grad.reshape(width, n_z, -1)), axis=2
         )
         up_bias_grad = jnp.sum(pre_grad, axis=0, dtype=f32).reshape(n_z, -1)
-        feed_share = give_back(feed_grad)
+        if last:
+            got, feed_grad, output_low = meet(got, feed_grad, output_low)
+            output_planes = to_planes_of(output_low)
+        else:
+            got, feed_grad, feed_got = meet(got, feed_grad, send_shares(feed_sums[layer + 1]))
+            feed_shares[layer + 1] = share_of(feed_got)
+        e = add_all(got)
         part_mid, gain_two_grad, shift_two_grad = norm_backward(hidden_mid, gain_two, e)
         mid_grad = gradient + part_mid
         dense_bias_grad = jnp.sum(mid_grad, axis=0)
-        mid_low = all_rows(mid_grad.astype(bf16))
+        got, mine = meet(send_rows(mid_grad.astype(bf16)), core_sum(feed_grad))
+        feed_sums[layer] = head_sum(mine)
+        mid_low = joined_rows(got)
         context_grad = product("rd,dc->rc", mid_low, w_dense).astype(bf16)
         context_grad = context_grad.reshape(slice_len, n_z, HD).transpose(1, 0, 2)
         dense_grad = product("rd,rc->dc", mid_low, context).astype(bf16).reshape(width, n_z, -1)
         query_grad, key_grad, value_grad = attend_backward(
             queries, keys, values, context_grad, log_total, query_pos, key_pos, slopes
         )
-        both = jnp.concatenate((key_grad, value_grad), axis=2)
+        both = jnp.concatenate((key_grad, value_grad), axis=2).astype(bf16)
         both = both.reshape(n_z, n_s, slice_len, 2 * HD)
-        both = sum_blocks([both[:, step] for step in range(n_s)], SEQ, n_s).astype(bf16)
+        got, dense_grad = meet(deal([both[:, step] for step in range(n_s)], SEQ, n_s), dense_grad)
+        both = add_all(got).astype(bf16)
         query_grad = query_grad.astype(bf16)
         query_bias_grad = jnp.sum(query_grad, axis=1, dtype=f32)
         value_bias_grad = jnp.sum(both[..., HD:], axis=1, dtype=f32)
         joined = jnp.concatenate((query_grad, both), axis=2)
         joined = joined.transpose(1, 0, 2).reshape(slice_len, -1)
+        got = send_sums(product("rn,dn->rd", joined, w_qkv))
         qkv_grad = product("rd,rn->dn", normed_one, joined).astype(bf16).reshape(width, n_z, -1)
-        mixed_share = give_back(jnp.concatenate((qkv_grad, dense_grad), axis=2))
-        e = sum_rows(product("rn,dn->rd", joined, w_qkv))
+        mixed_grad = jnp.concatenate((qkv_grad, dense_grad), axis=2)
+        if last:
+            got, mixed_grad, output_got = meet(got, mixed_grad, send_output(output_planes))
+            output = output_of(output_got)
+        else:
+            mine = core_sum(mixed_grad)
+            got, mine, mixed_got = meet(got, mine, send_shares(mixed_sums[layer + 1]))
+            mixed_shares[layer + 1] = share_of(mixed_got)
+            mixed_sums[layer] = head_sum(mine)
+        e = add_all(got)
         part_in, gain_one_grad, shift_one_grad = norm_backward(hidden, gain_one, e)
         gradient = mid_grad + part_in
-        weight_grads[layer] = (
-            mixed_share[:, :, :qkv_columns].reshape(cut, -1),
-            mixed_share[:, :, qkv_columns:].reshape(cut, -1).T,
-            feed_share[:, :, :units].reshape(cut, -1),
-            feed_share[:, :, units:].reshape(cut, -1).T,
-        )
+        if layer > 0:
+            got, mine = meet(send_rows(gradient.astype(bf16)), core_sum(mixed_grad))
+            mixed_sums[layer] = head_sum(mine)
+            grad_low = joined_rows(got)
         wide_grads[layer] = jnp.stack(
             (
                 gain_one_grad,
@@ -364,7 +411,10 @@
             (query_bias_grad, value_bias_grad, up_bias_grad), axis=1
         )
 
-    tokens_grad = to_output(to_outer(gradient.astype(bf16))).astype(f32)
+    tokens_planes = to_planes_of(to_outer(gradient.astype(bf16)))
+    feed_shares[0] = share_of(send_shares(feed_sums[0]))
+    mixed_shares[0] = share_of(send_shares(mixed_sums[0]))
+    tokens_grad = output_of(send_output(tokens_planes)).astype(f32)
 
     def fold(arrays, name, size):
         total = arrays[0]
@@ -401,9 +451,10 @@
         begin += LAYERS * size
         outs.append(piece.transpose(1, 0, 2))
     query_bias_grad, value_bias_grad, up_bias_grad = outs
-    qkv_grad, dense_grad, up_grad, down_grad = (
-        jnp.stack([weight_grads[layer][kind] for layer in range(LAYERS)]) for kind in range(4)
-    )
+    qkv_grad = jnp.stack([share[:, :, :qkv_columns].reshape(cut, -1) for share in mixed_shares])
+    dense_grad = jnp.stack([share[:, :, qkv_columns:].reshape(cut, -1).T for share in mixed_shares])
+    up_grad = jnp.stack([share[:, :, :units].reshape(cut, -1) for share in feed_shares])
+    down_grad = jnp.stack([share[:, :, units:].reshape(cut, -1).T for share in feed_shares])
     return (
         output,
         tokens_grad,

time: 704 us -> 666 us (0.946)
  waiting for transfers between devices: 271 us -> 233 us
  other arithmetic: 73.5 us -> 81.4 us
    reduce_scatter x4, waiting for transfers between devices: 88.1 us -> 47.6 us  [head_sum(): return lax.psum_scatter(mine, HEAD, scatter_dimension=0, tiled=False)]
    all_gather x6, waiting for transfers between devices: 30.8 us -> 48 us  [to_planes_of(): return lax.all_gather(array, HEAD, axis=0, tiled=False)]
    ppermute x100, waiting for transfers between devices: 151 us -> 137 us  [swap(): return lax.ppermute(array, name, [(i, i ^ step) for i in range(size)])]
    unnamed x422 -> x341, local copies, waits for them, and re-layouts: 33.3 us -> 21.9 us
    dynamic_slice x3 -> x6, local copies, waits for them, and re-layouts: 0.04 us -> 9.78 us  [the longest x5 9.76 us: send_output(): lax.dynamic_index_in_dim(planes, d ^ step, 0, False)]
    reshape x12 -> x3, local copies, waits for them, and re-layouts: 10.1 us -> 0.8 us  [the longest x1 0.67 us: per_device(): small = jnp.concatenate((wide, tall.reshape(-1, cut)), axis=0)]
  transfers between devices with their start and end apart: 116 -> 116, of which waited for: 61 -> 54; matrix products, arithmetic and copies ran while one was open for 24% -> 35% of each run, Pallas kernels for 0% -> 0%
where the time goes in v3:
time: 666 us; the launch traced here: 657 us
  waiting for transfers between devices  233 us (35%)
  starting transfers between devices  124 us (19%)
  local copies, waits for them, and re-layouts  105 us (16%)
  matrix products  87.8 us (13%)
  other arithmetic  81.4 us (12%)
  between operations  18.1 us (3%)
  blocking collectives  7.78 us (1%)
    ppermute x100, waiting for transfers between devices, swap(): return lax.ppermute(array, name, [(i, i ^ step) for i in range(size)])  137 us
    ppermute x100, starting transfers between devices, swap(): return lax.ppermute(array, name, [(i, i ^ step) for i in range(size)])  105 us
    dot_general x36, matrix products, product(): return jnp.einsum(spec, left, right, preferred_element_type=f32)  87.8 us
    all_gather x6, waiting for transfers between devices, to_planes_of(): return lax.all_gather(array, HEAD, axis=0, tiled=False)  48 us
    reduce_scatter x4, waiting for transfers between devices, head_sum(): return lax.psum_scatter(mine, HEAD, scatter_dimension=0, tiled=False)  47.6 us
    unnamed x341, local copies, waits for them, and re-layouts  21.9 us
    ppermute x6, starting transfers between devices, own_rows(): total = total + lax.ppermute(blocks[step], (DP, HEAD), pairs)  18.1 us
  transfers between devices with their start and end apart: 116, of which 54 were waited for; matrix products, arithmetic and copies ran while one was open for 35% of the time, Pallas kernels for 0%

profile of v3, /device:TPU:0, one launch (start us, length us, event | category | flops | bytes accessed | tf_op | source)
XLA Modules:
  0.0 656.6 jit_solution(5460802879742607210)
XLA Ops:
  16.1 4.7 collective-permute-start
  38.8 7.8 %all-gather.6 = f32[8,15,128]{2,1,0:T(8,128)S(1)} all-gather(f32[1,15,128]{2,1,0:T(8,128)S(1)} %bitcast.679), channel_id=2, replica_groups=mesh['dp'=4,'seq'=2,'head'=4] {'dp','seq'}, dimensions={0}, use_global_device_ids=true | all-gather | bytes 69120 | tf_op jit(solution)/shard_map/all_gather | solution.py:225
  84.9 4.8 collective-permute-done.7
  130.9 13.4 %all-gather.18.cloned.1.call-done = bf16[2048,512]{0,1:T(8,128)(2,1)} async-done(((bf16[512,512]{0,1:T(8,128)(2,1)}), bf16[2048,512]{0,1:T(8,128)(2,1)}) %all-gather.18.cloned.1.call-update) | async-done | bytes 2097168 | tf_op jit(solution)/shard_map/all_gather | solution.py:188
  159.7 5.1 collective-permute-done.15
  198.4 5.6 collective-permute-done.35
  229.5 8.9 %all-gather.22.cloned.1.call-done = bf16[2048,512]{0,1:T(8,128)(2,1)} async-done(((bf16[512,512]{0,1:T(8,128)(2,1)}), bf16[2048,512]{0,1:T(8,128)(2,1)}) %all-gather.22.cloned.1.call-update) | async-done | bytes 2097168 | tf_op jit(solution)/shard_map/all_gather | solution.py:188
  242.4 4.7 fusion.155
  257.3 6.5 collective-permute-done.43
  263.9 5.2 collective-permute-done.42
  311.2 4.6 collective-permute-done.54
  316.6 4.9 collective-permute-done.56
  336.6 21.6 %all-gather.24.cloned.1.call-done = bf16[512,1024]{0,1:T(8,128)(2,1)} async-done(((bf16[128,1024]{0,1:T(8,128)(2,1)}), bf16[512,1024]{0,1:T(8,128)(2,1)}) %all-gather.24.cloned.1.call-update) | async-done | bytes 1048592 | tf_op jit(solution)/shard_map/all_gather | solution.py:188
  380.8 5.3 fusion.31
  386.2 5.1 multiply_reduce_fusion.1
  406.1 5.3 collective-permute-done.64
  422.8 5.2 collective-permute-done.70
  428.0 5.0 collective-permute-done.69
  433.1 5.8 convert_reduce_fusion.1
  481.1 5.0 fusion.34
  486.2 5.0 multiply_reduce_fusion
  572.9 5.7 collective-permute-done.91
  579.6 11.8 %reduce-scatter.9.cloned.1.call-done = bf16[1,512,256]{1,2,0:T(8,128)(2,1)} async-done(((bf16[4,512,256]{1,2,0:T(8,128)(2,1)}), bf16[1,512,256]{1,2,0:T(8,128)(2,1)}) %reduce-scatter.9.cloned.1.call-update) | async-done | bytes 262160 | tf_op jit(solution)/shard_map/reduce_scatter | solution.py:323
  600.3 35.9 %reduce-scatter.11.cloned.1.call-done = bf16[1,512,512]{1,2,0:T(8,128)(2,1)} async-done(((bf16[4,512,512]{1,2,0:T(8,128)(2,1)}), bf16[1,512,512]{1,2,0:T(8,128)(2,1)}) %reduce-scatter.11.cloned.1.call-update) | async-done | bytes 524304 | tf_op jit(solution)/shard_map/reduce_scatter | solution.py:323
  (907 shorter events, 445.7 us)
Async XLA Ops:
  7.2 63.7 %all-gather.16.cloned.1.call-start = ((), (), s32[]{:S(2)}) async-start(), calls=%async_computation.9 | async-start | bytes 1310720 | tf_op jit(solution)/shard_map/all_gather | solution.py:188
  16.1 52.2 %collective-permute-start = (bf16[128,1024]{1,0:T(8,128)(2,1)}, bf16[128,1024]{1,0:T(8,128)(2,1)}, u32[]{:S(2)}, u32[]{:S(2)}) collective-permute-start(bf16[128,1024]{1,0:T(8,128)(2,1)} %get-tuple-element.378), channel_id=1, source_target_pairs={{0,8},{9,1},{18,26},{27,19},{4,12},{13,5},{22,30},{31,23}} | collective-permute-start | bytes 786440 | tf_op jit(solution)/shard_map/ppermute | solution.py:174
  20.8 47.5 %collective-permute-start.2 = (bf16[128,1024]{1,0:T(8,128)(2,1)S(1)}, bf16[128,1024]{1,0:T(8,128)(2,1)}, u32[]{:S(2)}, u32[]{:S(2)}) collective-permute-start(bf16[128,1024]{1,0:T(8,128)(2,1)S(1)} %get-tuple-element.379), channel_id=1, source_target_pairs={{0,24},{9,17},{18,10},{27,3},{4,28},{13,21},{22,14},{31,7}} | collective-permute-start | bytes 786440 | tf_op jit(solution)/shard_map/ppermute | solution.py:174
  38.8 105.5 %all-gather.18.cloned.1.call-start = ((), (), s32[]{:S(2)}) async-start(), calls=%async_computation.10 | async-start | bytes 2621440 | tf_op jit(solution)/shard_map/all_gather | solution.py:188
  98.2 94.3 %all-gather.20.cloned.1.call-start = ((), (), s32[]{:S(2)}) async-start(), calls=%async_computation.11 | async-start | bytes 1310720 | tf_op jit(solution)/shard_map/all_gather | solution.py:188
  109.8 42.0 %collective-permute-start.23 = (bf16[128,1024]{1,0:T(8,128)(2,1)}, bf16[128,1024]{1,0:T(8,128)(2,1)}, u32[]{:S(2)}, u32[]{:S(2)}) collective-permute-start(bf16[128,1024]{1,0:T(8,128)(2,1)} %get-tuple-element.371), channel_id=1, source_target_pairs={{0,8},{9,1},{18,26},{27,19},{4,12},{13,5},{22,30},{31,23}} | collective-permute-start | bytes 786440 | tf_op jit(solution)/shard_map/ppermute | solution.py:174
  113.3 39.1 %collective-permute-start.25 = (bf16[128,1024]{1,0:T(8,128)(2,1)}, bf16[128,1024]{1,0:T(8,128)(2,1)}, u32[]{:S(2)}, u32[]{:S(2)}) collective-permute-start(bf16[128,1024]{1,0:T(8,128)(2,1)} %get-tuple-element.372), channel_id=1, source_target_pairs={{0,24},{9,17},{18,10},{27,3},{4,28},{13,21},{22,14},{31,7}} | collective-permute-start | bytes 786440 | tf_op jit(solution)/shard_map/ppermute | solution.py:174
  115.4 38.4 %collective-permute-start.24 = (bf16[128,1024]{1,0:T(8,128)(2,1)}, bf16[128,1024]{1,0:T(8,128)(2,1)}, u32[]{:S(2)}, u32[]{:S(2)}) collective-permute-start(bf16[128,1024]{1,0:T(8,128)(2,1)} %get-tuple-element.373), channel_id=1, source_target_pairs={{0,16},{9,25},{18,2},{27,11},{4,20},{13,29},{22,6},{31,15}} | collective-permute-start | bytes 786440 | tf_op jit(solution)/shard_map/ppermute | solution.py:174
  165.0 73.5 %all-gather.22.cloned.1.call-start = ((), (), s32[]{:S(2)}) async-start(), calls=%async_computation.12 | async-start | bytes 2621440 | tf_op jit(solution)/shard_map/all_gather | solution.py:188
  170.9 187.2 %all-gather.24.cloned.1.call-start = ((), (), s32[]{:S(2)}) async-start(), calls=%async_computation.13 | async-start | bytes 1310720 | tf_op jit(solution)/shard_map/all_gather | solution.py:188
  226.0 30.3 %collective-permute-start.46 = (bf16[128,1024]{1,0:T(8,128)(2,1)S(1)}, bf16[128,1024]{1,0:T(8,128)(2,1)}, u32[]{:S(2)}, u32[]{:S(2)}) collective-permute-start(bf16[128,1024]{1,0:T(8,128)(2,1)S(1)} %reshape.640), channel_id=1, source_target_pairs={{0,24},{8,16},{16,8},{24,0},{1,25},{9,17},{17,9},{25,1},{2,26},{10... | collective-permute-start | bytes 786440 | tf_op jit(solution)/shard_map/ppermute | solution.py:35
  242.4 34.0 %collective-permute-start.47 = (bf16[4,512,512]{2,1,0:T(8,128)(2,1)}, bf16[4,512,512]{2,1,0:T(8,128)(2,1)S(1)}, u32[]{:S(2)}, u32[]{:S(2)}) collective-permute-start(bf16[4,512,512]{2,1,0:T(8,128)(2,1)} %bitcast.594), channel_id=1, source_target_pairs={{0,4},{4,0},{1,5},{5,1},{2,6},{6,2},{3,7},{7,3},{8,12},{12,8},{9,1... | collective-permute-start | bytes 6291464 | tf_op jit(solution)/shard_map/ppermute | solution.py:35
  329.8 40.3 %collective-permute-start.60 = (bf16[512,4,512]{0,2,1:T(8,128)(2,1)}, bf16[512,4,512]{0,2,1:T(8,128)(2,1)}, u32[]{:S(2)}, u32[]{:S(2)}) collective-permute-start(bf16[512,4,512]{0,2,1:T(8,128)(2,1)} %slice.741), channel_id=1, source_target_pairs={{0,4},{4,0},{1,5},{5,1},{2,6},{6,2},{3,7},{7,3},{8,12},{12,8},{9,1... | collective-permute-start | bytes 6291464 | tf_op jit(solution)/shard_map/ppermute | solution.py:35
  329.9 121.6 %reduce-scatter.5.cloned.1.call-start = ((), (), s32[]{:S(2)}) async-start(), calls=%async_computation.4 | async-start | bytes 2621440 | tf_op jit(solution)/shard_map/reduce_scatter | solution.py:323
  333.0 42.7 %collective-permute-start.59 = (bf16[128,1024]{1,0:T(8,128)(2,1)S(1)}, bf16[128,1024]{1,0:T(8,128)(2,1)}, u32[]{:S(2)}, u32[]{:S(2)}) collective-permute-start(bf16[128,1024]{1,0:T(8,128)(2,1)S(1)} %convert_element_type.429), channel_id=1, source_target_pairs={{0,24},{8,16},{16,8},{24,0},{1,25},{9,17},{17,9},{25,1},{2,26},{10... | collective-permute-start | bytes 786440 | tf_op jit(solution)/shard_map/ppermute | solution.py:35
  334.3 43.0 %collective-permute-start.58 = (bf16[128,1024]{1,0:T(8,128)(2,1)S(1)}, bf16[128,1024]{1,0:T(8,128)(2,1)}, u32[]{:S(2)}, u32[]{:S(2)}) collective-permute-start(bf16[128,1024]{1,0:T(8,128)(2,1)S(1)} %convert_element_type.429), channel_id=1, source_target_pairs={{0,16},{8,24},{16,0},{24,8},{1,17},{9,25},{17,1},{25,9},{2,18},{10... | collective-permute-start | bytes 786440 | tf_op jit(solution)/shard_map/ppermute | solution.py:35
  335.9 41.4 %collective-permute-start.57 = (bf16[128,1024]{1,0:T(8,128)(2,1)S(1)}, bf16[128,1024]{1,0:T(8,128)(2,1)}, u32[]{:S(2)}, u32[]{:S(2)}) collective-permute-start(bf16[128,1024]{1,0:T(8,128)(2,1)S(1)} %convert_element_type.429), channel_id=1, source_target_pairs={{0,8},{8,0},{16,24},{24,16},{1,9},{9,1},{17,25},{25,17},{2,10},{10... | collective-permute-start | bytes 786440 | tf_op jit(solution)/shard_map/ppermute | solution.py:35
  369.6 33.6 %collective-permute-start.65 = (bf16[128,1024]{1,0:T(8,128)(2,1)}, bf16[128,1024]{1,0:T(8,128)(2,1)S(1)}, u32[]{:S(2)}, u32[]{:S(2)}) collective-permute-start(bf16[128,1024]{1,0:T(8,128)(2,1)} %bitcast.157), channel_id=1, source_target_pairs={{0,8},{8,0},{16,24},{24,16},{1,9},{9,1},{17,25},{25,17},{2,10},{10... | collective-permute-start | bytes 786440 | tf_op jit(solution)/shard_map/ppermute | solution.py:35
  370.1 36.0 %collective-permute-start.66 = (bf16[128,1024]{1,0:T(8,128)(2,1)}, bf16[128,1024]{1,0:T(8,128)(2,1)S(1)}, u32[]{:S(2)}, u32[]{:S(2)}) collective-permute-start(bf16[128,1024]{1,0:T(8,128)(2,1)} %bitcast.158), channel_id=1, source_target_pairs={{0,16},{8,24},{16,0},{24,8},{1,17},{9,25},{17,1},{25,9},{2,18},{10... | collective-permute-start | bytes 786440 | tf_op jit(solution)/shard_map/ppermute | solution.py:35
  375.7 30.4 %collective-permute-start.67 = (bf16[128,1024]{1,0:T(8,128)(2,1)}, bf16[128,1024]{1,0:T(8,128)(2,1)}, u32[]{:S(2)}, u32[]{:S(2)}) collective-permute-start(bf16[128,1024]{1,0:T(8,128)(2,1)} %bitcast.159), channel_id=1, source_target_pairs={{0,24},{8,16},{16,8},{24,0},{1,25},{9,17},{17,9},{25,1},{2,26},{10... | collective-permute-start | bytes 786440 | tf_op jit(solution)/shard_map/ppermute | solution.py:35
  377.3 126.9 %reduce-scatter.7.cloned.1.call-start = ((), (), s32[]{:S(2)}) async-start(), calls=%async_computation.5 | async-start | bytes 1310720 | tf_op jit(solution)/shard_map/reduce_scatter | solution.py:323
  463.4 99.1 %all-gather.14.cloned.1.call-start = ((), (), s32[]{:S(2)}) async-start(), calls=%async_computation.6 | async-start | bytes 1310720 | tf_op jit(solution)/shard_map/all_gather | solution.py:188
  533.0 58.3 %reduce-scatter.9.cloned.1.call-start = ((), (), s32[]{:S(2)}) async-start(), calls=%async_computation.7 | async-start | bytes 1310720 | tf_op jit(solution)/shard_map/reduce_scatter | solution.py:323
  533.8 102.4 %reduce-scatter.11.cloned.1.call-start = ((), (), s32[]{:S(2)}) async-start(), calls=%async_computation.8 | async-start | bytes 2621440 | tf_op jit(solution)/shard_map/reduce_scatter | solution.py:323
  (252 other events, 2245.5 us)
Sparse Core Ops, SparseCore 0:
  38.9 28.2 all-gather.15
  98.4 45.9 all-gather.17
  165.1 25.8 all-gather.19
  193.0 45.3 all-gather.21
  330.0 28.0 all-gather.23
  377.4 42.1 reduce-scatter.4
  463.5 25.7 reduce-scatter.6
  533.1 29.2 all-gather.13
  565.3 25.9 reduce-scatter.8
  593.6 42.5 reduce-scatter.10

commit v4 on v3

v4 whole, which is shorter than its diff:
```python
import functools
import math

import jax
import jax.numpy as jnp
from jax import lax
from jax.experimental import pallas as pl
from jax.experimental.pallas import tpu as pltpu
from jax.sharding import PartitionSpec as P

H = 16
HD = 64
LAYERS = 2
DP, SEQ, HEAD = "dp", "seq", "head"

epsilon = 1e-05
masked_value = -1000000000.0
bf16 = jnp.bfloat16
f32 = jnp.float32


def flip_list(blocks, index):
    bit = 1
    while bit < len(blocks):
        turn = (index & bit) != 0
        blocks = [jnp.where(turn, blocks[j ^ bit], blocks[j]) for j in range(len(blocks))]
        bit *= 2
    return blocks


def flip(array, index, axis=0):
    blocks = [lax.index_in_dim(array, j, axis, keepdims=True) for j in range(array.shape[axis])]
    return jnp.concatenate(flip_list(blocks, index), axis=axis)


def swap(array, name, size, step):
    return lax.ppermute(array, name, [(i, i ^ step) for i in range(size)])


def gather(array, name, size):
    return [array] + [swap(array, name, size, step) for step in range(1, size)]


def deal(blocks, name, size):
    return [blocks[0]] + [swap(blocks[step], name, size, step) for step in range(1, size)]


def meet(*groups):
    return lax.optimization_barrier(groups)


def add_all(blocks):
    return functools.reduce(jnp.add, [block.astype(f32) for block in blocks])


def sum_blocks(blocks, name, size):
    total = blocks[0].astype(f32)
    for step in range(1, size):
        total = total + swap(blocks[step].astype(bf16), name, size, step).astype(f32)
    return total


def after(array, *others):
    return lax.optimization_barrier((array,) + others)[0]


def dot(left, right, left_dim, right_dim):
    dims = (((left_dim,), (right_dim,)), ((), ()))
    return lax.dot_general(left, right, dims, preferred_element_type=f32)


def gelu_tanh(values):
    argument = 0.7978845608028654 * (values + 0.044715 * values * values * values)
    return 0.5 * values * (1.0 + jnp.tanh(argument))


def gelu_slope(values):
    square = values * values
    bent = jnp.tanh(0.7978845608028654 * (values + 0.044715 * values * square))
    inner = 0.7978845608028654 * (1.0 + 3.0 * 0.044715 * square)
    return 0.5 * (1.0 + bent) + 0.5 * values * (1.0 - bent * bent) * inner


def norm_parts(values):
    row_mean = jnp.mean(values, axis=-1, keepdims=True)
    centred = values - row_mean
    scale = lax.rsqrt(jnp.mean(centred * centred, axis=-1, keepdims=True) + epsilon)
    return centred * scale, scale


def run(body, steps, each_in, whole_in, each_out, whole_out, scratch=(), flops=0):
    def each(array):
        zeros = (0,) * (len(array.shape) - 1)
        return pl.BlockSpec((None,) + tuple(array.shape[1:]), lambda z: (z,) + zeros)

    def whole(array):
        zeros = (0,) * len(array.shape)
        return pl.BlockSpec(tuple(array.shape), lambda z: zeros)

    counts = [len(part) for part in (each_in, whole_in, each_out, whole_out)]

    def kernel(*refs):
        parts, begin = [], 0
        for count in counts:
            parts.append(refs[begin : begin + count])
            begin += count
        body(pl.program_id(0), *parts, refs[begin:])

    arrays = list(each_in) + list(whole_in)
    shapes = list(each_out) + list(whole_out)
    moved = sum(math.prod(item.shape) * item.dtype.itemsize for item in arrays + shapes)
    return pl.pallas_call(
        kernel,
        grid=(steps,),
        in_specs=[each(item) for item in each_in] + [whole(item) for item in whole_in],
        out_specs=[each(item) for item in each_out] + [whole(item) for item in whole_out],
        out_shape=shapes,
        scratch_shapes=list(scratch),
        compiler_params=pltpu.CompilerParams(vmem_limit_bytes=48 * 1024 * 1024),
        cost_estimate=pl.CostEstimate(flops=flops, bytes_accessed=moved, transcendentals=0),
    )(*arrays)


def shape(dims, kind):
    return jax.ShapeDtypeStruct(tuple(dims), kind)


def lay(target, blocks):
    rows = blocks[0].shape[0]
    for index, block in enumerate(blocks):
        target[index * rows : (index + 1) * rows, :] = block[...]


def spread(blocks, source):
    rows = blocks[0].shape[0]
    for index, block in enumerate(blocks):
        block[...] = source[index * rows : (index + 1) * rows, :].astype(block.dtype)


def pieces(array, planes):
    part = planes[0].shape[0]
    return [array[:, s * part : (s + 1) * part] for s in range(len(planes))]


def times(array, planes, begin, end):
    total = None
    for piece, plane in zip(pieces(array, planes), planes):
        term = dot(piece, plane[:, begin:end], 1, 0)
        total = term if total is None else total + term
    return total


def add_back(acc, array, planes, begin, end):
    part = planes[0].shape[0]
    for s, plane in enumerate(planes):
        acc[:, s * part : (s + 1) * part] += dot(array, plane[:, begin:end], 1, 1)


def project(blocks, planes, bias):
    rows, width = blocks[0].shape
    length = rows * len(blocks)
    heads = planes[0].shape[0]
    n = len(planes)

    def body(z, each_in, whole_in, each_out, whole_out, scratch):
        @pl.when(z == 0)
        def _():
            lay(scratch[0], whole_in)

        got = times(scratch[0], each_in[:n], 0, 3 * HD) + each_in[n][...]
        low = got.astype(bf16)
        each_out[0][...] = low[:, :HD] * jnp.asarray(1.0 / math.sqrt(HD), bf16)
        each_out[1][...] = low[:, HD:]

    return run(
        body,
        heads,
        list(planes) + [bias],
        blocks,
        [shape((heads, length, HD), bf16), shape((heads, length, 2 * HD), bf16)],
        [],
        [pltpu.VMEM((length, width), bf16)],
        2 * heads * length * width * 3 * HD,
    )


def masked_scores(queries, both, slope, key_pos, query_pos):
    scores = dot(queries, both[:, :HD], 1, 1) + slope * key_pos
    return jnp.where(key_pos <= query_pos, scores, masked_value)


def attend(queries, both, planes, slopes, key_pos, query_pos, n_t):
    heads, length, _ = queries.shape
    n = len(planes)
    width = planes[0].shape[1] * n
    rows = length // n_t

    def body(z, each_in, whole_in, each_out, whole_out, scratch):
        kv, weights = each_in[1 : 1 + n], each_in[1 + n : 1 + 2 * n]
        slope = each_in[1 + 2 * n][:, :1]
        acc = scratch[0]

        @pl.when(z == 0)
        def _():
            acc[...] = jnp.zeros_like(acc)

        low_queries = each_in[0][...]
        scores = [
            masked_scores(low_queries, kv[s], slope, whole_in[0][s], whole_in[1][...])
            for s in range(n)
        ]
        top = functools.reduce(jnp.maximum, [jnp.max(x, axis=1, keepdims=True) for x in scores])
        shifted = [jnp.exp(x - top) for x in scores]
        total = sum(jnp.sum(x, axis=1, keepdims=True) for x in shifted)
        context = sum(dot(x.astype(bf16), kv[s][:, HD:], 1, 0) for s, x in enumerate(shifted))
        low = (context / total).astype(bf16)
        each_out[0][...] = low
        each_out[1][...] = top + jnp.log(total)
        add_back(acc, low, weights, 3 * HD, 4 * HD)

        @pl.when(z == heads - 1)
        def _():
            spread(whole_out, acc)

    out = run(
        body,
        heads,
        [queries] + list(both) + list(planes) + [slopes],
        [key_pos, query_pos],
        [shape((heads, length, HD), bf16), shape((heads, length, 1), f32)],
        [shape((rows, width), bf16)] * n_t,
        [pltpu.VMEM((length, width), f32)],
        2 * heads * length * (2 * HD * length * n + HD * width),
    )
    return out[0], out[1], out[2:]


def attend_back(blocks, queries, both, planes, context, logs, slopes, key_pos, query_pos):
    heads, length, _ = queries.shape
    n = len(planes)
    width = blocks[0].shape[1]

    def body(z, each_in, whole_in, each_out, whole_out, scratch):
        @pl.when(z == 0)
        def _():
            lay(scratch[0], whole_in[2:])

        kv, weights = each_in[1 : 1 + n], each_in[1 + n : 1 + 2 * n]
        context_ref, logs_ref, slope_ref = each_in[1 + 2 * n :]
        slope = slope_ref[:, :1]
        low_queries = each_in[0][...]
        grads = times(scratch[0], weights, 3 * HD, 4 * HD).astype(bf16)
        inner = jnp.sum(grads.astype(f32) * context_ref[...].astype(f32), axis=1, keepdims=True)
        query_grad = None
        for s in range(n):
            scores = masked_scores(low_queries, kv[s], slope, whole_in[0][s], whole_in[1][...])
            probs = jnp.exp(scores - logs_ref[...])
            prob_grad = dot(grads, kv[s][:, HD:], 1, 1)
            score_grad = (probs * (prob_grad - inner)).astype(bf16)
            term = dot(score_grad, kv[s][:, :HD], 1, 0)
            query_grad = term if query_grad is None else query_grad + term
            each_out[1 + s][:, :HD] = dot(score_grad, low_queries, 0, 0).astype(bf16)
            each_out[1 + s][:, HD:] = dot(probs.astype(bf16), grads, 0, 0).astype(bf16)
        each_out[0][...] = (query_grad * (1.0 / math.sqrt(HD))).astype(bf16)

    out = run(
        body,
        heads,
        [queries] + list(both) + list(planes) + [context, logs, slopes],
        [key_pos, query_pos] + list(blocks),
        [shape((heads, length, HD), bf16)] + [shape((heads, length, 2 * HD), bf16)] * n,
        [],
        [pltpu.VMEM((length, width), bf16)],
        2 * heads * length * (5 * HD * length * n + HD * width),
    )
    return out[0], out[1:]


def project_back(query_grad, both_grads, planes, n_t):
    heads, length, _ = query_grad.shape
    n = len(planes)
    width = planes[0].shape[1] * n
    rows = length // n_t

    def body(z, each_in, whole_in, each_out, whole_out, scratch):
        acc = scratch[0]

        @pl.when(z == 0)
        def _():
            acc[...] = jnp.zeros_like(acc)

        low = sum(item[...].astype(f32) for item in each_in[1 : 1 + n]).astype(bf16)
        joined, sums = each_out
        joined[:, :HD] = each_in[0][...]
        joined[:, HD:] = low
        sums[:, :HD] = jnp.sum(each_in[0][...].astype(f32), axis=0, keepdims=True)
        sums[:, HD:] = jnp.sum(low.astype(f32), axis=0, keepdims=True)
        add_back(acc, joined[...], each_in[1 + n :], 0, 3 * HD)

        @pl.when(z == heads - 1)
        def _():
            spread(whole_out, acc)

    out = run(
        body,
        heads,
        [query_grad] + list(both_grads) + list(planes),
        [],
        [shape((heads, length, 3 * HD), bf16), shape((heads, 1, 3 * HD), f32)],
        [shape((rows, width), bf16)] * n_t,
        [pltpu.VMEM((length, width), f32)],
        2 * heads * length * width * 3 * HD,
    )
    return out[0], out[1], out[2:]


def feed_forward(blocks, planes, bias):
    rows, width = blocks[0].shape
    length = rows * len(blocks)
    heads, _, units = bias.shape
    n = len(planes)

    def body(z, each_in, whole_in, each_out, whole_out, scratch):
        wide, acc = scratch

        @pl.when(z == 0)
        def _():
            lay(wide, whole_in)
            acc[...] = jnp.zeros_like(acc)

        pre_up = times(wide, each_in[:n], 0, units) + each_in[n][...]
        each_out[0][...] = pre_up
        low = gelu_tanh(pre_up).astype(bf16)
        each_out[1][...] = low
        add_back(acc, low, each_in[:n], units, 2 * units)

        @pl.when(z == heads - 1)
        def _():
            spread(whole_out, acc)

    out = run(
        body,
        heads,
        list(planes) + [bias],
        blocks,
        [shape((heads, length, units), f32), shape((heads, length, units), bf16)],
        [shape((rows, width), bf16)] * len(blocks),
        [pltpu.VMEM((length, width), bf16), pltpu.VMEM((length, width), f32)],
        4 * heads * length * width * units,
    )
    return out[0], out[1], out[2:]


def feed_back(blocks, planes, pre_up):
    rows, width = blocks[0].shape
    length = rows * len(blocks)
    heads, _, units = pre_up.shape
    n = len(planes)

    def body(z, each_in, whole_in, each_out, whole_out, scratch):
        wide, acc = scratch

        @pl.when(z == 0)
        def _():
            lay(wide, whole_in)
            acc[...] = jnp.zeros_like(acc)

        act_grad = times(wide, each_in[:n], units, 2 * units)
        low = (act_grad * gelu_slope(each_in[n][...])).astype(bf16)
        each_out[0][...] = low
        each_out[1][...] = jnp.sum(low.astype(f32), axis=0, keepdims=True)
        add_back(acc, low, each_in[:n], 0, units)

        @pl.when(z == heads - 1)
        def _():
            spread(whole_out, acc)

    out = run(
        body,
        heads,
        list(planes) + [pre_up],
        blocks,
        [shape((heads, length, units), bf16), shape((heads, 1, units), f32)],
        [shape((rows, width), bf16)] * len(blocks),
        [pltpu.VMEM((length, width), bf16), pltpu.VMEM((length, width), f32)],
        4 * heads * length * width * units,
    )
    return out[0], out[1], out[2:]


def weight_back(one_blocks, one, two_blocks, two, n):
    rows, width = one_blocks[0].shape
    length = rows * len(one_blocks)
    heads, _, first = one.shape
    second = two.shape[2]
    part = width // n
    half = len(one_blocks)

    def body(z, each_in, whole_in, each_out, whole_out, scratch):
        @pl.when(z == 0)
        def _():
            lay(scratch[0], whole_in[:half])
            lay(scratch[1], whole_in[half:])

        for s in range(n):
            cols = slice(s * part, (s + 1) * part)
            each_out[s][:, :first] = dot(scratch[0][:, cols], each_in[0][...], 0, 0).astype(bf16)
            each_out[s][:, first:] = dot(scratch[1][:, cols], each_in[1][...], 0, 0).astype(bf16)

    return run(
        body,
        heads,
        [one, two],
        list(one_blocks) + list(two_blocks),
        [shape((heads, part, first + second), bf16)] * n,
        [],
        [pltpu.VMEM((length, width), bf16)] * 2,
        2 * heads * length * width * (first + second),
    )


def norm_forward(values, got, bias, gain, shift):
    def body(z, each_in, whole_in, each_out, whole_out, scratch):
        start, bias_ref, gain_ref, shift_ref = whole_in[:4]
        total = start[...] + bias_ref[...]
        for item in whole_in[4:]:
            total = total + item[...].astype(f32)
        whole_out[0][...] = total
        xhat, _ = norm_parts(total)
        whole_out[1][...] = (xhat * gain_ref[...] + shift_ref[...]).astype(bf16)

    return run(
        body,
        1,
        [],
        [values, bias[None], gain[None], shift[None]] + list(got),
        [],
        [shape(values.shape, f32), shape(values.shape, bf16)],
    )


def norm_back(values, gradient, got, gain):
    width = values.shape[1]

    def body(z, each_in, whole_in, each_out, whole_out, scratch):
        e = sum(item[...].astype(f32) for item in whole_in[3:])
        xhat, scale = norm_parts(whole_in[0][...])
        eg = e * whole_in[2][...]
        back = scale * (
            eg
            - jnp.mean(eg, axis=-1, keepdims=True)
            - xhat * jnp.mean(eg * xhat, axis=-1, keepdims=True)
        )
        fresh = whole_in[1][...] + back
        whole_out[0][...] = fresh
        whole_out[1][...] = fresh.astype(bf16)
        whole_out[2][0:1, :] = jnp.sum(e * xhat, axis=0, keepdims=True)
        whole_out[2][1:2, :] = jnp.sum(e, axis=0, keepdims=True)
        whole_out[2][2:3, :] = jnp.sum(fresh, axis=0, keepdims=True)

    return run(
        body,
        1,
        [],
        [values, gradient, gain[None]] + list(got),
        [],
        [shape(values.shape, f32), shape(values.shape, bf16), shape((3, width), f32)],
    )


def per_device(
    sizes,
    tokens,
    qkv_weight,
    dense_weight,
    up_weight,
    down_weight,
    first_gain,
    first_shift,
    query_bias,
    value_bias,
    dense_bias,
    second_gain,
    second_shift,
    up_bias,
    down_bias,
    cotangent,
):
    n_t, n_s, n_z = sizes
    seq_count, slice_len, width = tokens.shape
    assert seq_count == 1 and n_t == n_z
    d, c, z = (lax.axis_index(name) for name in (DP, SEQ, HEAD))
    rows = slice_len // n_t
    cut = qkv_weight.shape[1]
    part = cut * n_t
    heads = query_bias.shape[1]
    assert heads == n_t
    units = up_bias.shape[2] * n_t * n_s

    def to_inner(array):
        lead = array.shape[:-1]
        array = array.reshape(lead + (n_t, n_s, cut))
        array = jnp.moveaxis(array, -2, -3)
        return flip(array, c, len(lead)).reshape(lead + (width,))

    def to_outer(array):
        lead = array.shape[:-1]
        array = flip(array.reshape(lead + (n_s, n_t, cut)), c, len(lead))
        return jnp.moveaxis(array, -2, -3).reshape(lead + (width,))

    def own_rows(array):
        cuts = array.reshape(n_t, rows, width)
        blocks = [lax.dynamic_index_in_dim(cuts, d ^ step, 0, False) for step in range(n_t)]
        total = jnp.where(d == z, blocks[0], jnp.zeros_like(blocks[0]))
        for step in range(1, n_t):
            pairs = [(i * n_z + i, (i ^ step) * n_z + i) for i in range(n_t)]
            total = total + lax.ppermute(blocks[step], (DP, HEAD), pairs)
        return total

    def send_rows(array):
        return gather(array, DP, n_t)

    def send_sums(blocks):
        return deal(blocks, DP, n_t)

    def to_planes_of(array):
        return lax.all_gather(array, HEAD, axis=0, tiled=False)

    def send_output(planes):
        blocks = [lax.dynamic_index_in_dim(planes, d ^ step, 0, False) for step in range(n_t)]
        return deal(blocks, DP, n_t)

    def output_of(got):
        return jnp.concatenate(flip_list(got, d), axis=0).reshape(1, slice_len, width)

    def packed(layer):
        qkv = qkv_weight[layer].reshape(cut, n_t, -1)
        dense = dense_weight[layer].T.reshape(cut, n_t, -1)
        up = up_weight[layer].reshape(cut, n_t, -1)
        down = down_weight[layer].T.reshape(cut, n_t, -1)
        return tuple(
            [jnp.concatenate((one[:, j], two[:, j]), axis=1) for j in range(n_t)]
            for one, two in ((qkv, dense), (up, down))
        )

    def to_planes(blocks):
        got = deal(flip_list(blocks, d), DP, n_t)
        return jnp.concatenate(flip_list(got, d), axis=0)

    def join(planes):
        return gather(planes, SEQ, n_s)

    shards = [packed(layer) for layer in range(LAYERS)]
    first_shard = to_planes(shards[0][0])
    messages = [to_planes_of(first_shard)]
    start_rows = own_rows(tokens[0])

    wide = jnp.concatenate(
        (first_gain, first_shift, dense_bias, second_gain, second_shift, down_bias), axis=0
    )
    tall = jnp.concatenate((query_bias, value_bias, up_bias), axis=2)
    small = jnp.concatenate((wide, tall.reshape(-1, cut)), axis=0)
    small = after(small, first_shard)
    small = lax.all_gather(small, (DP, SEQ), axis=0, tiled=False)
    small = small.reshape((n_t, n_s) + small.shape[1:])
    wide = small[:, :, : 6 * LAYERS].transpose(2, 1, 0, 3)
    wide = flip(wide, c, 1).reshape(6, LAYERS, width)
    each = small[:, :, 6 * LAYERS :].reshape(n_t, n_s, LAYERS, heads, -1)
    each = lax.dynamic_index_in_dim(each, d, axis=3, keepdims=False)
    tall = []
    begin = 0
    tall_sizes = (HD, HD, units)
    for size in tall_sizes:
        size = size // (n_t * n_s)
        piece = each[:, :, :, begin : begin + size]
        begin += size
        tall.append(piece.transpose(2, 0, 1, 3).reshape(LAYERS, -1))
    tall = jnp.concatenate(tall, axis=1)
    tall = jnp.stack(flip_list(gather(tall, HEAD, n_z), z), axis=1)

    hidden = to_inner(start_rows).astype(f32)
    second_shard = to_planes([after(block, small) for block in shards[0][1]])
    messages.append(to_planes_of(second_shard))

    qkv_columns = 3 * HD
    head_ids = jnp.arange(n_z, dtype=jnp.int32) * heads + d
    slopes = 2.0 ** (-8.0 * (head_ids + 1).astype(f32) / H)
    slopes = jnp.broadcast_to(slopes[:, None, None], (n_z, 1, 128))
    block_ids = (d ^ jnp.arange(n_t, dtype=jnp.int32)) * rows
    own_pos = (block_ids[:, None] + jnp.arange(rows, dtype=jnp.int32)[None]).reshape(-1)
    query_pos = (c * slice_len + own_pos).astype(f32)[:, None]
    others = (c ^ jnp.arange(n_s, dtype=jnp.int32)) * slice_len
    key_pos = (others[:, None] + own_pos[None]).astype(f32)[:, None, :]
    none = jnp.zeros((width,), f32)

    cot = cotangent[0]
    records = []
    _, low = norm_forward(hidden, [], none, wide[0, 0], wide[1, 0])
    for layer in range(LAYERS):
        mixed, feed = (join(planes) for planes in messages[2 * layer : 2 * layer + 2])
        gain_one, _, bias_dense, gain_two, shift_two, bias_down = (wide[i, layer] for i in range(6))
        zeros = jnp.zeros((n_z, HD), f32)
        bias_qkv = jnp.concatenate((tall[layer, :, :HD], zeros, tall[layer, :, HD : 2 * HD]), 1)
        bias_up = tall[layer, :, 2 * HD :][:, None]
        normed_one = send_rows(low)
        queries, both = project(normed_one, mixed, bias_qkv[:, None])
        both = gather(both, SEQ, n_s)
        if layer == 0:
            later = [to_planes([after(block, both[0]) for block in shards[1][0]])]
            later.append(to_planes([after(block, later[0]) for block in shards[1][1]]))
            cot_rows = own_rows(after(cot, both[0]))
        else:
            cot_rows = send_rows(after(cot_rows, both[0]))
        context, logs, out = attend(queries, both, mixed, slopes, key_pos, query_pos, n_t)
        got = send_sums(out)
        if layer == 0:
            got, later, cot_rows = meet(got, later, cot_rows)
            messages.extend(to_planes_of(shard) for shard in later)
            cot_rows = to_inner(cot_rows)
        else:
            got, cot_rows = meet(got, cot_rows)
        hidden_mid, low = norm_forward(hidden, got, bias_dense, gain_two, shift_two)
        normed_two = send_rows(low)
        pre_up, activation, out = feed_forward(normed_two, feed, bias_up)
        got = send_sums(out)
        records.append(
            (
                (mixed, feed, gain_one, gain_two),
                (hidden, hidden_mid, normed_one, normed_two),
                (queries, both, logs, context, pre_up, activation),
            )
        )
        if layer + 1 < LAYERS:
            hidden, low = norm_forward(
                hidden_mid, got, bias_down, wide[0, layer + 1], wide[1, layer + 1]
            )
        else:
            hidden = hidden_mid + add_all(got) + bias_down

    output_low = to_outer(hidden.astype(bf16))

    gradient = cot_rows[0].astype(f32)
    grad_low = cot_rows
    down_bias_grad = jnp.sum(gradient, axis=0, keepdims=True)
    wide_grads = [None] * LAYERS
    tall_grads = [None] * LAYERS

    def core_sum(blocks):
        return sum_blocks(blocks, SEQ, n_s).astype(bf16)

    def head_sum(mine):
        return lax.psum_scatter(mine, HEAD, scatter_dimension=0, tiled=False)

    def send_shares(mine):
        mine = mine.reshape(n_t, cut, -1)
        blocks = [lax.dynamic_index_in_dim(mine, d ^ step, 0, False) for step in range(n_t)]
        return deal(blocks, DP, n_t)

    def share_of(got):
        return jnp.stack(flip_list(got, d), axis=1).astype(f32)

    feed_shares = [None] * LAYERS
    mixed_shares = [None] * LAYERS
    feed_sums = [None] * LAYERS
    mixed_sums = [None] * LAYERS
    for layer in reversed(range(LAYERS)):
        (
            (mixed, feed, gain_one, gain_two),
            (hidden, hidden_mid, normed_one, normed_two),
            (queries, both, logs, context, pre_up, activation),
        ) = records[layer]
        last = layer == LAYERS - 1
        pre_grad, up_bias_grad, out = feed_back(grad_low, feed, pre_up)
        got = send_sums(out)
        feed_grad = weight_back(normed_two, pre_grad, grad_low, activation, n_s)
        if last:
            got, feed_grad, output_low = meet(got, feed_grad, output_low)
            output_planes = to_planes_of(output_low)
        else:
            got, feed_grad, feed_got = meet(got, feed_grad, send_shares(feed_sums[layer + 1]))
            feed_shares[layer + 1] = share_of(feed_got)
        mid_grad, low, sums_two = norm_back(hidden_mid, gradient, got, gain_two)
        mid_low = send_rows(low)
        mine = core_sum(feed_grad)
        if last:
            mid_low, mine = meet(mid_low, mine)
        else:
            mid_low, mine, mixed_got = meet(mid_low, mine, send_shares(mixed_sums[layer + 1]))
            mixed_shares[layer + 1] = share_of(mixed_got)
        feed_sums[layer] = head_sum(mine)
        query_grad, both_grads = attend_back(
            mid_low, queries, both, mixed, context, logs, slopes, key_pos, query_pos
        )
        got = deal(both_grads, SEQ, n_s)
        joined, qkv_sums, out = project_back(query_grad, got, mixed, n_t)
        got = send_sums(out)
        mixed_grad = weight_back(normed_one, joined, mid_low, context, n_s)
        if last:
            planes = after(output_planes, joined)
            got, mixed_grad, output_got = meet(got, mixed_grad, send_output(planes))
            output = output_of(output_got)
        else:
            mine = core_sum(mixed_grad)
            got, mine, feed_got = meet(got, mine, send_shares(after(feed_sums[layer], joined)))
            feed_shares[layer] = share_of(feed_got)
            mixed_sums[layer] = head_sum(mine)
        gradient, low, sums_one = norm_back(hidden, mid_grad, got, gain_one)
        if layer > 0:
            grad_low, mine = meet(send_rows(low), core_sum(mixed_grad))
            mixed_sums[layer] = head_sum(mine)
        wide_grads[layer] = jnp.stack(
            (
                sums_one[0],
                sums_one[1],
                sums_two[2],
                sums_two[0],
                sums_two[1],
                down_bias_grad[0],
            )
        )
        down_bias_grad = sums_one[2:3]
        tall_grads[layer] = jnp.concatenate(
            (qkv_sums[:, 0, :HD], qkv_sums[:, 0, 2 * HD :], up_bias_grad[:, 0]), axis=1
        )

    tokens_planes = to_planes_of(to_outer(low))
    mixed_shares[0] = share_of(send_shares(mixed_sums[0]))
    tokens_grad = output_of(send_output(tokens_planes)).astype(f32)

    def fold(arrays, name, size):
        total = arrays[0]
        for step in range(1, size):
            total = total + swap(arrays[step], name, size, step)
        return total

    wide = jnp.stack(wide_grads).reshape(LAYERS * 6, n_s, n_t, cut)
    pieces, begin = [], 0
    tall = jnp.stack(tall_grads)
    for size in tall_sizes:
        piece = tall[:, :, begin : begin + size]
        begin += size
        piece = piece.reshape(LAYERS, n_z, n_t, n_s, size // (n_t * n_s))
        pieces.append(flip(flip(piece, c, 3), z, 1))
    tall = jnp.concatenate(
        [piece.transpose(3, 1, 2, 0, 4).reshape(n_s, n_z, n_t, -1) for piece in pieces], axis=3
    )
    wide = wide.transpose(1, 2, 0, 3).reshape(n_s, n_t, -1)
    n_wide = wide.shape[2]
    wide = jnp.broadcast_to(wide[:, None], (n_s, n_z) + wide.shape[1:])
    joint = jnp.concatenate((wide, tall), axis=3)
    joint = fold([joint[step] for step in range(n_s)], SEQ, n_s)
    joint = fold([joint[step] for step in range(n_z)], HEAD, n_z)
    joint = flip(joint, d)
    got = deal([joint[step] for step in range(n_t)], DP, n_t)
    wide = functools.reduce(jnp.add, [item[:n_wide] for item in got])
    wide = wide.reshape(LAYERS, 6, cut)
    tall = flip(jnp.stack([item[n_wide:] for item in got]), d)
    outs, begin = [], 0
    for size in tall_sizes:
        size = size // (n_t * n_s)
        piece = tall[:, begin : begin + LAYERS * size].reshape(n_t, LAYERS, size)
        begin += LAYERS * size
        outs.append(piece.transpose(1, 0, 2))
    query_bias_grad, value_bias_grad, up_bias_grad = outs
    qkv_grad = jnp.stack([share[:, :, :qkv_columns].reshape(cut, -1) for share in mixed_shares])
    dense_grad = jnp.stack([share[:, :, qkv_columns:].reshape(cut, -1).T for share in mixed_shares])
    up_grad = jnp.stack([share[:, :, :units].reshape(cut, -1) for share in feed_shares])
    down_grad = jnp.stack([share[:, :, units:].reshape(cut, -1).T for share in feed_shares])
    return (
        output,
        tokens_grad,
        qkv_grad,
        dense_grad,
        up_grad,
        down_grad,
        wide[:, 0],
        wide[:, 1],
        query_bias_grad,
        value_bias_grad,
        wide[:, 2],
        wide[:, 3],
        wide[:, 4],
        up_bias_grad,
        wide[:, 5],
    )


def solution(mesh):
    sizes = tuple(mesh.shape[name] for name in (DP, SEQ, HEAD))
    rows = P(DP, SEQ, None)
    tall = P(None, (DP, SEQ), HEAD)
    flat = P(None, HEAD, (DP, SEQ))
    vector = P(None, (DP, SEQ))
    params = (
        tall,
        flat,
        tall,
        flat,
        vector,
        vector,
        flat,
        flat,
        vector,
        vector,
        vector,
        flat,
        vector,
    )
    return jax.shard_map(
        functools.partial(per_device, sizes),
        mesh=mesh,
        in_specs=(rows,) + params + (rows,),
        out_specs=(rows, rows) + params,
        check_vma=False,
    )
```

time: 666 us -> 666 us (level)
  Pallas kernels: 0 us -> 120 us
  matrix products: 87.8 us -> 0 us
  other arithmetic: 81.4 us -> 43.3 us
    pallas_call x0 -> x24, Pallas kernels: none -> 120 us  [run(): pl.pallas_call(kernel, grid=(steps,), in_specs=[each(item) for item in ea...]
    dot_general x36 -> x0, matrix products: 87.8 us -> none  [product(): return jnp.einsum(spec, left, right, preferred_element_type=f32)]
    all_gather x6, waiting for transfers between devices: 48 us -> 92.9 us  [to_planes_of(): return lax.all_gather(array, HEAD, axis=0, tiled=False)]
    reduce_scatter x4, waiting for transfers between devices: 47.6 us -> 16.9 us  [head_sum(): return lax.psum_scatter(mine, HEAD, scatter_dimension=0, tiled=False)]
    unnamed x341 -> x287, local copies, waits for them, and re-layouts: 21.9 us -> 44.6 us
    slice x25 -> x15, local copies, waits for them, and re-layouts: 29.3 us -> 7.08 us  [the longest x2 2.62 us: per_device(): share[:, :, :units].reshape(cut, -1)]
    transpose x10 -> x0, other arithmetic: 18 us -> none  [the longest x4 12 us: core_sum(): return mine.transpose(1, 0, 2)]
    reduce_sum x19 -> x1, other arithmetic: 14.7 us -> 0.05 us  [per_device(): down_bias_grad = jnp.sum(gradient, axis=0, keepdims=True)]
  transfers between devices with their start and end apart: 116 -> 116, of which waited for: 54 -> 45; matrix products, arithmetic and copies ran while one was open for 35% -> 16% of each run, Pallas kernels for 0% -> 17%
where the time goes in v4:
time: 666 us; the launch traced here: 656 us
  waiting for transfers between devices  239 us (36%)
  starting transfers between devices  125 us (19%)
  Pallas kernels  120 us (18%)
  local copies, waits for them, and re-layouts  104 us (16%)
  other arithmetic  43.3 us (7%)
  between operations  16.9 us (3%)
  blocking collectives  7.76 us (1%)
    ppermute x100, waiting for transfers between devices, swap(): return lax.ppermute(array, name, [(i, i ^ step) for i in range(size)])  128 us
    pallas_call x24, Pallas kernels, run(): pl.pallas_call(kernel, grid=(steps,), in_specs=[each(item) for item in ea...  120 us
    ppermute x100, starting transfers between devices, swap(): return lax.ppermute(array, name, [(i, i ^ step) for i in range(size)])  107 us
    all_gather x6, waiting for transfers between devices, to_planes_of(): return lax.all_gather(array, HEAD, axis=0, tiled=False)  92.9 us
    unnamed x287, local copies, waits for them, and re-layouts  44.6 us
    ppermute x6, starting transfers between devices, own_rows(): total = total + lax.ppermute(blocks[step], (DP, HEAD), pairs)  17.8 us
    reduce_scatter x4, waiting for transfers between devices, head_sum(): return lax.psum_scatter(mine, HEAD, scatter_dimension=0, tiled=False)  16.9 us
  transfers between devices with their start and end apart: 116, of which 45 were waited for; matrix products, arithmetic and copies ran while one was open for 16% of the time, Pallas kernels for 17%

profile of v4, /device:TPU:0, one launch (start us, length us, event | category | flops | bytes accessed | tf_op | source)
XLA Modules:
  0.0 655.5 jit_solution(12374028737911094716)
XLA Ops:
  36.3 7.8 %all-gather.6 = f32[8,15,128]{2,1,0:T(8,128)S(1)} all-gather(f32[1,15,128]{2,1,0:T(8,128)S(1)} %bitcast.478), channel_id=3, replica_groups=mesh['dp'=4,'seq'=2,'head'=4] {'dp','seq'}, dimensions={0}, use_global_device_ids=true | all-gather | bytes 69120 | tf_op jit(solution)/shard_map/all_gather | solution.py:564
  61.4 16.7 %all-gather.16.cloned.1.call-done = bf16[2048,256]{0,1:T(8,128)(2,1)} async-done(((bf16[512,256]{0,1:T(8,128)(2,1)}), bf16[2048,256]{0,1:T(8,128)(2,1)}) %all-gather.16.cloned.1.call-update) | async-done | bytes 1048592 | tf_op jit(solution)/shard_map/all_gather | solution.py:527
  87.7 5.5 collective-permute-done.10.refs_4_.refs_3_
  93.2 6.4 collective-permute-done.11.refs_5_.refs_4_
  125.3 9.6 %shard_map.264 = (bf16[4,512,64]{2,1,0:T(8,128)(2,1)S(1)}, f32[4,512,1]{2,1,0:T(8,128)S(1)}, bf16[128,1024]{1,0:T(8,128)(2,1)S(1)}, bf16[128,1024]{1,0:T(8,128)(...) custom-call(bf16[4,512,64]{2,1,0:T(8,128)(2,1)S(1)} %get-tuple-element.188.refs_0_, ...), custom_call_target="tpu_custom_call" | custom-call | flops 805306368 | bytes 4734976 | tf_op jit(solution)/shard_map/pallas_call | solution.py:112
  152.7 23.8 %all-gather.18.cloned.1.call-done = bf16[2048,256]{0,1:T(8,128)(2,1)} async-done(((bf16[512,256]{0,1:T(8,128)(2,1)}), bf16[2048,256]{0,1:T(8,128)(2,1)}) %all-gather.18.cloned.1.call-update) | async-done | bytes 1048592 | tf_op jit(solution)/shard_map/all_gather | solution.py:527
  181.3 42.5 %all-gather.22.cloned.1.call-done = bf16[2048,512]{1,0:T(8,128)(2,1)} async-done(((bf16[512,512]{1,0:T(8,128)(2,1)}), bf16[2048,512]{1,0:T(8,128)(2,1)}) %all-gather.22.cloned.1.call-update) | async-done | bytes 2097168 | tf_op jit(solution)/shard_map/all_gather | solution.py:527
  223.9 7.1 %shard_map.266 = (f32[4,512,256]{2,1,0:T(8,128)S(1)}, bf16[4,512,256]{2,1,0:T(8,128)(2,1)S(1)}, bf16[128,1024]{1,0:T(8,128)(2,1)S(1)}, bf16[128,1024]{1,0:T(8,12...) custom-call(bf16[4,512,512]{2,1,0:T(8,128)(2,1)} %bitcast.422, ...), custom_call_target="tpu_custom_call" | custom-call | flops 2147483648 | bytes 9441280 | tf_op jit(solution)/shard_map/pallas_call | solution.py:112
  235.9 5.6 collective-permute-done.34.refs_5_
  241.5 6.4 collective-permute-done.35.refs_6_
  278.2 9.0 %shard_map.269 = (bf16[4,512,64]{2,1,0:T(8,128)(2,1)S(1)}, f32[4,512,1]{2,1,0:T(8,128)S(1)}, bf16[128,1024]{1,0:T(8,128)(2,1)S(1)}, bf16[128,1024]{1,0:T(8,128)(...) custom-call(bf16[4,512,64]{2,1,0:T(8,128)(2,1)S(1)} %copy-done.19, ...), custom_call_target="tpu_custom_call" | custom-call | flops 805306368 | bytes 4734976 | tf_op jit(solution)/shard_map/pallas_call | solution.py:112
  290.7 5.7 collective-permute-done.41.refs_5_
  305.0 5.8 collective-permute-done.48.refs_4_.refs_3_
  315.0 6.9 %shard_map.271 = (f32[4,512,256]{2,1,0:T(8,128)S(1)}, bf16[4,512,256]{2,1,0:T(8,128)(2,1)S(1)}, bf16[128,1024]{1,0:T(8,128)(2,1)S(1)}, bf16[128,1024]{1,0:T(8,12...) custom-call(bf16[4,512,512]{2,1,0:T(8,128)(2,1)} %bitcast.425, ...), custom_call_target="tpu_custom_call" | custom-call | flops 2147483648 | bytes 9441280 | tf_op jit(solution)/shard_map/pallas_call | solution.py:112
  326.7 8.1 %shard_map.272 = (bf16[4,512,256]{2,1,0:T(8,128)(2,1)S(1)}, f32[4,1,256]{2,1,0:T(1,128)S(1)}, bf16[128,1024]{1,0:T(8,128)(2,1)S(1)}, bf16[128,1024]{1,0:T(8,128)...) custom-call(bf16[4,512,512]{2,1,0:T(8,128)(2,1)S(1)} %bitcast.426, ...), custom_call_target="tpu_custom_call" | custom-call | flops 2147483648 | bytes 9441280 | tf_op jit(solution)/shard_map/pallas_call | solution.py:112
  365.4 5.5 collective-permute-done.58.refs_12_.refs_8_
  371.0 12.1 %shard_map.275 = (bf16[4,512,64]{2,1,0:T(8,128)(2,1)S(1)}, bf16[4,512,128]{2,1,0:T(8,128)(2,1)S(1)}, bf16[4,512,128]{2,1,0:T(8,128)(2,1)}) custom-call(bf16[4,512,64]{2,1,0:T(8,128)(2,1)S(1)} %copy-done.20, bf16[4,512,128]{2,1,0:T(8,128)(2,1)} %get-tuple-element.220.refs_1_, bf16[4,512,128]{2,1,0:T(8,128)(2,1)} %collective-permute-done.40.refs_2_, ...), custom_call_target="tpu_custom_call" | custom-call | flops 1610612736 | bytes 6045696 | tf_op jit(solution)/shard_map/pallas_call | solution.py:112
  420.0 6.6 %collective-permute-done.63.refs_5_ = bf16[128,1024]{1,0:T(8,128)(2,1)} collective-permute-done((bf16[128,1024]{1,0:T(8,128)(2,1)}, bf16[128,1024]{1,0:T(8,128)(2,1)}, u32[]{:S(2)}, u32[]{:S(2)}) %collective-permute-start.63) | collective-permute-done | bytes 262176 | tf_op jit(solution)/shard_map/ppermute | solution.py:37
  446.5 8.1 %shard_map.279 = (bf16[4,512,256]{2,1,0:T(8,128)(2,1)S(1)}, f32[4,1,256]{2,1,0:T(1,128)S(1)}, bf16[128,1024]{1,0:T(8,128)(2,1)S(1)}, bf16[128,1024]{1,0:T(8,128)...) custom-call(bf16[4,512,512]{2,1,0:T(8,128)(2,1)S(1)} %bitcast.423, ...), custom_call_target="tpu_custom_call" | custom-call | flops 2147483648 | bytes 9441280 | tf_op jit(solution)/shard_map/pallas_call | solution.py:112
  471.7 5.5 shard_map.280
  512.5 11.9 %shard_map.282 = (bf16[4,512,64]{2,1,0:T(8,128)(2,1)S(1)}, bf16[4,512,128]{2,1,0:T(8,128)(2,1)S(1)}, bf16[4,512,128]{2,1,0:T(8,128)(2,1)}) custom-call(bf16[4,512,64]{2,1,0:T(8,128)(2,1)S(1)} %copy-done.17, bf16[4,512,128]{2,1,0:T(8,128)(2,1)} %get-tuple-element.189.refs_1_, bf16[4,512,128]{2,1,0:T(8,128)(2,1)} %collective-permute-done.13.refs_2_, ...), custom_call_target="tpu_custom_call" | custom-call | flops 1610612736 | bytes 6045696 | tf_op jit(solution)/shard_map/pallas_call | solution.py:112
  568.1 7.2 %collective-permute-done.87.refs_5_ = bf16[128,1024]{1,0:T(8,128)(2,1)S(1)} collective-permute-done((bf16[128,1024]{1,0:T(8,128)(2,1)}, bf16[128,1024]{1,0:T(8,128)(2,1)S(1)}, u32[]{:S(2)}, u32[]{:S(2)}) %collective-permute-start.87) | collective-permute-done | bytes 262176 | tf_op jit(solution)/shard_map/ppermute | solution.py:37
  599.0 10.0 %all-gather.14.cloned.1.call-done = bf16[4,128,1024]{2,1,0:T(8,128)(2,1)} async-done(((bf16[1,128,1024]{2,1,0:T(8,128)(2,1)}), bf16[4,128,1024]{2,1,0:T(8,128)(2,1)}) %all-gather.14.cloned.1.call-update) | async-done | bytes 1048592 | tf_op jit(solution)/shard_map/all_gather | solution.py:527
  626.0 11.5 %reduce-scatter.11.cloned.1.call-done = bf16[1,512,256]{2,1,0:T(8,128)(2,1)} async-done(((bf16[4,512,256]{2,1,0:T(8,128)(2,1)}), bf16[1,512,256]{2,1,0:T(8,128)(2,1)}) %reduce-scatter.11.cloned.1.call-update) | async-done | bytes 262160 | tf_op jit(solution)/shard_map/reduce_scatter | solution.py:652
  (752 shorter events, 393.5 us)
Async XLA Ops:
  7.2 70.9 %all-gather.16.cloned.1.call-start = ((), (), s32[]{:S(2)}) async-start(), calls=%async_computation.9 | async-start | bytes 1310720 | tf_op jit(solution)/shard_map/all_gather | solution.py:527
  10.3 24.3 %collective-permute-start.1 = (bf16[128,256]{0,1:T(8,128)(2,1)}, bf16[128,256]{0,1:T(8,128)(2,1)}, u32[]{:S(2)}, u32[]{:S(2)}) collective-permute-start(bf16[128,256]{0,1:T(8,128)(2,1)} %get-tuple-element.438), channel_id=1, source_target_pairs={{0,16},{8,24},{16,0},{24,8},{1,17},{9,25},{17,1},{25,9},{2,18},{10... | collective-permute-start | bytes 196616 | tf_op jit(solution)/shard_map/ppermute | solution.py:37
  13.3 21.3 %collective-permute-start.2 = (bf16[128,256]{0,1:T(8,128)(2,1)}, bf16[128,256]{0,1:T(8,128)(2,1)}, u32[]{:S(2)}, u32[]{:S(2)}) collective-permute-start(bf16[128,256]{0,1:T(8,128)(2,1)} %get-tuple-element.555), channel_id=1, source_target_pairs={{0,8},{8,0},{16,24},{24,16},{1,9},{9,1},{17,25},{25,17},{2,10},{10... | collective-permute-start | bytes 196616 | tf_op jit(solution)/shard_map/ppermute | solution.py:37
  16.3 63.3 %collective-permute-start.7 = (bf16[128,1024]{1,0:T(8,128)(2,1)}, bf16[128,1024]{1,0:T(8,128)(2,1)}, u32[]{:S(2)}, u32[]{:S(2)}) collective-permute-start(bf16[128,1024]{1,0:T(8,128)(2,1)} %get-tuple-element.463), channel_id=1, source_target_pairs={{0,8},{9,1},{18,26},{27,19},{4,12},{13,5},{22,30},{31,23}} | collective-permute-start | bytes 786440 | tf_op jit(solution)/shard_map/ppermute | solution.py:517
  21.0 58.6 %collective-permute-start.8 = (bf16[128,1024]{1,0:T(8,128)(2,1)}, bf16[128,1024]{1,0:T(8,128)(2,1)}, u32[]{:S(2)}, u32[]{:S(2)}) collective-permute-start(bf16[128,1024]{1,0:T(8,128)(2,1)} %get-tuple-element.465), channel_id=1, source_target_pairs={{0,16},{9,25},{18,2},{27,11},{4,20},{13,29},{22,6},{31,15}} | collective-permute-start | bytes 786440 | tf_op jit(solution)/shard_map/ppermute | solution.py:517
  49.4 99.7 %all-gather.20.cloned.1.call-start = ((), (), s32[]{:S(2)}) async-start(), calls=%async_computation.11 | async-start | bytes 2621440 | tf_op jit(solution)/shard_map/all_gather | solution.py:527
  56.3 23.3 %collective-permute-start.9 = (bf16[128,1024]{1,0:T(8,128)(2,1)}, bf16[128,1024]{1,0:T(8,128)(2,1)}, u32[]{:S(2)}, u32[]{:S(2)}) collective-permute-start(bf16[128,1024]{1,0:T(8,128)(2,1)} %get-tuple-element.464), channel_id=1, source_target_pairs={{0,24},{9,17},{18,10},{27,3},{4,28},{13,21},{22,14},{31,7}} | collective-permute-start | bytes 786440 | tf_op jit(solution)/shard_map/ppermute | solution.py:517
  61.4 115.1 %all-gather.18.cloned.1.call-start = ((), (), s32[]{:S(2)}) async-start(), calls=%async_computation.10 | async-start | bytes 1310720 | tf_op jit(solution)/shard_map/all_gather | solution.py:527
  119.9 21.2 %collective-permute-start.24 = (bf16[128,1024]{1,0:T(8,128)(2,1)}, bf16[128,1024]{1,0:T(8,128)(2,1)}, u32[]{:S(2)}, u32[]{:S(2)}) collective-permute-start(bf16[128,1024]{1,0:T(8,128)(2,1)} %get-tuple-element.462), channel_id=1, source_target_pairs={{0,16},{9,25},{18,2},{27,11},{4,20},{13,29},{22,6},{31,15}} | collective-permute-start | bytes 786440 | tf_op jit(solution)/shard_map/ppermute | solution.py:517
  148.5 75.4 %all-gather.22.cloned.1.call-start = ((), (), s32[]{:S(2)}) async-start(), calls=%async_computation.12 | async-start | bytes 2621440 | tf_op jit(solution)/shard_map/all_gather | solution.py:527
  149.1 235.6 %all-gather.24.cloned.1.call-start = ((), (), s32[]{:S(2)}) async-start(), calls=%async_computation.13 | async-start | bytes 1310720 | tf_op jit(solution)/shard_map/all_gather | solution.py:527
  149.2 74.8 %collective-permute-start.30 = (bf16[4,512,512]{2,1,0:T(8,128)(2,1)}, bf16[4,512,512]{2,1,0:T(8,128)(2,1)}, u32[]{:S(2)}, u32[]{:S(2)}) collective-permute-start(bf16[4,512,512]{2,1,0:T(8,128)(2,1)} %bitcast.421), channel_id=1, source_target_pairs={{0,4},{4,0},{1,5},{5,1},{2,6},{6,2},{3,7},{7,3},{8,12},{12,8},{9,1... | collective-permute-start | bytes 6291464 | tf_op jit(solution)/shard_map/ppermute | solution.py:37
  151.1 30.2 %collective-permute-start.31 = (bf16[128,1024]{1,0:T(8,128)(2,1)}, bf16[128,1024]{1,0:T(8,128)(2,1)}, u32[]{:S(2)}, u32[]{:S(2)}) collective-permute-start(bf16[128,1024]{1,0:T(8,128)(2,1)} %get-tuple-element.213.refs_3_.refs_2_), channel_id=1, source_target_pairs={{0,8},{8,0},{16,24},{24,16},{1,9},{9,1},{17,25},{25,17},{2,10},{10... | collective-permute-start | bytes 786440 | tf_op jit(solution)/shard_map/ppermute | solution.py:37
  178.3 86.3 %collective-permute-start.26 = (bf16[4,512,256]{2,1,0:T(8,128)(2,1)S(1)}, bf16[4,512,256]{2,1,0:T(8,128)(2,1)S(1)}, u32[]{:S(2)}, u32[]{:S(2)}) collective-permute-start(bf16[4,512,256]{2,1,0:T(8,128)(2,1)S(1)} %bitcast.416), channel_id=1, source_target_pairs={{0,4},{4,0},{1,5},{5,1},{2,6},{6,2},{3,7},{7,3},{8,12},{12,8},{9,1... | collective-permute-start | bytes 3145736 | tf_op jit(solution)/shard_map/ppermute | solution.py:37
  178.3 45.6 %collective-permute-start.32 = (bf16[128,1024]{1,0:T(8,128)(2,1)}, bf16[128,1024]{1,0:T(8,128)(2,1)}, u32[]{:S(2)}, u32[]{:S(2)}) collective-permute-start(bf16[128,1024]{1,0:T(8,128)(2,1)} %get-tuple-element.213.refs_3_.refs_2_), channel_id=1, source_target_pairs={{0,16},{8,24},{16,0},{24,8},{1,17},{9,25},{17,1},{25,9},{2,18},{10... | collective-permute-start | bytes 786440 | tf_op jit(solution)/shard_map/ppermute | solution.py:37
  179.9 44.0 %collective-permute-start.33 = (bf16[128,1024]{1,0:T(8,128)(2,1)}, bf16[128,1024]{1,0:T(8,128)(2,1)}, u32[]{:S(2)}, u32[]{:S(2)}) collective-permute-start(bf16[128,1024]{1,0:T(8,128)(2,1)} %get-tuple-element.213.refs_3_.refs_2_), channel_id=1, source_target_pairs={{0,24},{8,16},{16,8},{24,0},{1,25},{9,17},{17,9},{25,1},{2,26},{10... | collective-permute-start | bytes 786440 | tf_op jit(solution)/shard_map/ppermute | solution.py:37
  223.9 91.1 %collective-permute-start.47 = (bf16[4,512,512]{2,1,0:T(8,128)(2,1)}, bf16[4,512,512]{2,1,0:T(8,128)(2,1)}, u32[]{:S(2)}, u32[]{:S(2)}) collective-permute-start(bf16[4,512,512]{2,1,0:T(8,128)(2,1)} %bitcast.424), channel_id=1, source_target_pairs={{0,4},{4,0},{1,5},{5,1},{2,6},{6,2},{3,7},{7,3},{8,12},{12,8},{9,1... | collective-permute-start | bytes 6291464 | tf_op jit(solution)/shard_map/ppermute | solution.py:37
  352.3 107.1 %reduce-scatter.5.cloned.1.call-start = ((), (), s32[]{:S(2)}) async-start(), calls=%async_computation.4 | async-start | bytes 2621440 | tf_op jit(solution)/shard_map/reduce_scatter | solution.py:652
  370.9 113.2 %reduce-scatter.7.cloned.1.call-start = ((), (), s32[]{:S(2)}) async-start(), calls=%async_computation.5 | async-start | bytes 1310720 | tf_op jit(solution)/shard_map/reduce_scatter | solution.py:652
  405.5 21.1 %collective-permute-start.63 = (bf16[128,1024]{1,0:T(8,128)(2,1)}, bf16[128,1024]{1,0:T(8,128)(2,1)}, u32[]{:S(2)}, u32[]{:S(2)}) collective-permute-start(bf16[128,1024]{1,0:T(8,128)(2,1)} %get-tuple-element.270), channel_id=1, source_target_pairs={{0,16},{8,24},{16,0},{24,8},{1,17},{9,25},{17,1},{25,9},{2,18},{10... | collective-permute-start | bytes 786440 | tf_op jit(solution)/shard_map/ppermute | solution.py:37
  459.1 100.9 %reduce-scatter.9.cloned.1.call-start = ((), (), s32[]{:S(2)}) async-start(), calls=%async_computation.6 | async-start | bytes 2621440 | tf_op jit(solution)/shard_map/reduce_scatter | solution.py:652
  477.3 20.9 %collective-permute-start.81 = (bf16[4,512,512]{2,1,0:T(8,128)(2,1)}, bf16[4,512,512]{2,1,0:T(8,128)(2,1)}, u32[]{:S(2)}, u32[]{:S(2)}) collective-permute-start(bf16[4,512,512]{2,1,0:T(8,128)(2,1)} %get-tuple-element.313), channel_id=1, source_target_pairs={{0,4},{4,0},{1,5},{5,1},{2,6},{6,2},{3,7},{7,3},{8,12},{12,8},{9,1... | collective-permute-start | bytes 6291464 | tf_op jit(solution)/shard_map/ppermute | solution.py:37
  509.1 99.8 %all-gather.14.cloned.1.call-start = ((), (), s32[]{:S(2)}) async-start(), calls=%async_computation.7 | async-start | bytes 1310720 | tf_op jit(solution)/shard_map/all_gather | solution.py:527
  580.8 56.6 %reduce-scatter.11.cloned.1.call-start = ((), (), s32[]{:S(2)}) async-start(), calls=%async_computation.8 | async-start | bytes 1310720 | tf_op jit(solution)/shard_map/reduce_scatter | solution.py:652
  (223 other events, 2139.8 us)
Sparse Core Ops, SparseCore 0:
  49.5 28.4 all-gather.15
  80.2 45.4 all-gather.19
  148.6 27.7 all-gather.17
  178.4 45.3 all-gather.21
  352.4 28.0 all-gather.23
  383.3 42.1 reduce-scatter.4
  459.2 24.8 reduce-scatter.6
  509.2 41.7 reduce-scatter.8
  581.0 27.9 all-gather.13
  611.7 25.6 reduce-scatter.10

commit v5 on v4

--- a/solution.py
+++ b/solution.py
@@ -15,6 +15,7 @@
 
 epsilon = 1e-05
 masked_value = -1000000000.0
+VMEM_LIMIT = 48 * 1024 * 1024
 bf16 = jnp.bfloat16
 f32 = jnp.float32
 
@@ -23,7 +24,10 @@
     bit = 1
     while bit < len(blocks):
         turn = (index & bit) != 0
-        blocks = [jnp.where(turn, blocks[j ^ bit], blocks[j]) for j in range(len(blocks))]
+        blocks = [
+            jax.tree.map(lambda x, y: jnp.where(turn, x, y), blocks[j ^ bit], blocks[j])
+            for j in range(len(blocks))
+        ]
         bit *= 2
     return blocks
 
@@ -43,6 +47,10 @@
 
 def deal(blocks, name, size):
     return [blocks[0]] + [swap(blocks[step], name, size, step) for step in range(1, size)]
+
+
+def exchange(array, name):
+    return lax.all_to_all(array, name, 0, 0, tiled=True)
 
 
 def meet(*groups):
@@ -116,7 +124,7 @@
         out_specs=[each(item) for item in each_out] + [whole(item) for item in whole_out],
         out_shape=shapes,
         scratch_shapes=list(scratch),
-        compiler_params=pltpu.CompilerParams(vmem_limit_bytes=48 * 1024 * 1024),
+        compiler_params=pltpu.CompilerParams(vmem_limit_bytes=VMEM_LIMIT),
         cost_estimate=pl.CostEstimate(flops=flops, bytes_accessed=moved, transcendentals=0),
     )(*arrays)
 
@@ -137,51 +145,56 @@
         block[...] = source[index * rows : (index + 1) * rows, :].astype(block.dtype)
 
 
-def pieces(array, planes):
-    part = planes[0].shape[0]
-    return [array[:, s * part : (s + 1) * part] for s in range(len(planes))]
-
-
 def times(array, planes, begin, end):
+    part = array.shape[1] // len(planes)
     total = None
-    for piece, plane in zip(pieces(array, planes), planes):
-        term = dot(piece, plane[:, begin:end], 1, 0)
+    for s, plane in enumerate(planes):
+        term = dot(array[:, s * part : (s + 1) * part], plane[:part, begin:end], 1, 0)
         total = term if total is None else total + term
     return total
 
 
 def add_back(acc, array, planes, begin, end):
-    part = planes[0].shape[0]
+    part = acc.shape[1] // len(planes)
     for s, plane in enumerate(planes):
-        acc[:, s * part : (s + 1) * part] += dot(array, plane[:, begin:end], 1, 1)
-
-
-def project(blocks, planes, bias):
+        acc[:, s * part : (s + 1) * part] += dot(array, plane[:part, begin:end], 1, 1)
+
+
+def project(blocks, planes, bias, gain=None, shift=None):
     rows, width = blocks[0].shape
     length = rows * len(blocks)
     heads = planes[0].shape[0]
-    n = len(planes)
+    n, n_blocks = len(planes), len(blocks)
+    vectors = [] if gain is None else [gain[None], shift[None]]
 
     def body(z, each_in, whole_in, each_out, whole_out, scratch):
+        wide = scratch[0]
+
         @pl.when(z == 0)
         def _():
-            lay(scratch[0], whole_in)
-
-        got = times(scratch[0], each_in[:n], 0, 3 * HD) + each_in[n][...]
+            lay(wide, whole_in[:n_blocks])
+            if vectors:
+                gain_ref, shift_ref = whole_in[n_blocks:]
+                normed = wide[...].astype(f32) * gain_ref[...] + shift_ref[...]
+                wide[...] = normed.astype(bf16)
+                spread(whole_out, wide)
+
+        got = times(wide, each_in[:n], 0, 3 * HD) + each_in[n][...]
         low = got.astype(bf16)
         each_out[0][...] = low[:, :HD] * jnp.asarray(1.0 / math.sqrt(HD), bf16)
         each_out[1][...] = low[:, HD:]
 
-    return run(
+    out = run(
         body,
         heads,
         list(planes) + [bias],
-        blocks,
+        list(blocks) + vectors,
         [shape((heads, length, HD), bf16), shape((heads, length, 2 * HD), bf16)],
-        [],
+        [shape((rows, width), bf16)] * n_blocks if vectors else [],
         [pltpu.VMEM((length, width), bf16)],
         2 * heads * length * width * 3 * HD,
     )
+    return out[0], out[1], out[2:] or blocks
 
 
 def masked_scores(queries, both, slope, key_pos, query_pos):
@@ -189,10 +202,9 @@
     return jnp.where(key_pos <= query_pos, scores, masked_value)
 
 
-def attend(queries, both, planes, slopes, key_pos, query_pos, n_t):
+def attend(queries, both, planes, slopes, key_pos, query_pos, n_t, width):
     heads, length, _ = queries.shape
     n = len(planes)
-    width = planes[0].shape[1] * n
     rows = length // n_t
 
     def body(z, each_in, whole_in, each_out, whole_out, scratch):
@@ -276,10 +288,9 @@
     return out[0], out[1:]
 
 
-def project_back(query_grad, both_grads, planes, n_t):
+def project_back(query_grad, both_grads, planes, n_t, width):
     heads, length, _ = query_grad.shape
     n = len(planes)
-    width = planes[0].shape[1] * n
     rows = length // n_t
 
     def body(z, each_in, whole_in, each_out, whole_out, scratch):
@@ -497,16 +508,18 @@
     assert heads == n_t
     units = up_bias.shape[2] * n_t * n_s
 
+    def chunks(array):
+        return [array[..., j * cut : (j + 1) * cut] for j in range(n_t * n_s)]
+
     def to_inner(array):
-        lead = array.shape[:-1]
-        array = array.reshape(lead + (n_t, n_s, cut))
-        array = jnp.moveaxis(array, -2, -3)
-        return flip(array, c, len(lead)).reshape(lead + (width,))
+        parts = chunks(array)
+        by_seq = flip_list([parts[s::n_s] for s in range(n_s)], c)
+        return jnp.concatenate([part for group in by_seq for part in group], axis=-1)
 
     def to_outer(array):
-        lead = array.shape[:-1]
-        array = flip(array.reshape(lead + (n_s, n_t, cut)), c, len(lead))
-        return jnp.moveaxis(array, -2, -3).reshape(lead + (width,))
+        parts = chunks(array)
+        by_seq = flip_list([parts[k * n_t : (k + 1) * n_t] for k in range(n_s)], c)
+        return jnp.concatenate([by_seq[s][t] for t in range(n_t) for s in range(n_s)], axis=-1)
 
     def own_rows(array):
         cuts = array.reshape(n_t, rows, width)
@@ -527,60 +540,62 @@
         return lax.all_gather(array, HEAD, axis=0, tiled=False)
 
     def send_output(planes):
-        blocks = [lax.dynamic_index_in_dim(planes, d ^ step, 0, False) for step in range(n_t)]
-        return deal(blocks, DP, n_t)
-
-    def output_of(got):
-        return jnp.concatenate(flip_list(got, d), axis=0).reshape(1, slice_len, width)
-
-    def packed(layer):
-        qkv = qkv_weight[layer].reshape(cut, n_t, -1)
-        dense = dense_weight[layer].T.reshape(cut, n_t, -1)
-        up = up_weight[layer].reshape(cut, n_t, -1)
-        down = down_weight[layer].T.reshape(cut, n_t, -1)
-        return tuple(
-            [jnp.concatenate((one[:, j], two[:, j]), axis=1) for j in range(n_t)]
-            for one, two in ((qkv, dense), (up, down))
-        )
+        return exchange(planes, DP).reshape(1, slice_len, width)
+
+    def packed_mixed(layer):
+        qkv = qkv_weight[layer].reshape(cut, n_t, -1).transpose(1, 0, 2)
+        dense = dense_weight[layer].reshape(n_t, -1, cut).transpose(0, 2, 1)
+        return jnp.concatenate((qkv, dense), axis=2)
+
+    def packed_feed(layer):
+        up = up_weight[layer].reshape(cut, n_t, -1).transpose(1, 0, 2)
+        down = down_weight[layer].reshape(n_t, -1, cut).transpose(0, 2, 1)
+        return jnp.concatenate((up, down), axis=2)
 
     def to_planes(blocks):
-        got = deal(flip_list(blocks, d), DP, n_t)
-        return jnp.concatenate(flip_list(got, d), axis=0)
+        return exchange(blocks, DP).reshape(part, -1)
 
     def join(planes):
         return gather(planes, SEQ, n_s)
 
-    shards = [packed(layer) for layer in range(LAYERS)]
-    first_shard = to_planes(shards[0][0])
-    messages = [to_planes_of(first_shard)]
-    start_rows = own_rows(tokens[0])
-
     wide = jnp.concatenate(
         (first_gain, first_shift, dense_bias, second_gain, second_shift, down_bias), axis=0
     )
-    tall = jnp.concatenate((query_bias, value_bias, up_bias), axis=2)
-    small = jnp.concatenate((wide, tall.reshape(-1, cut)), axis=0)
-    small = after(small, first_shard)
-    small = lax.all_gather(small, (DP, SEQ), axis=0, tiled=False)
-    small = small.reshape((n_t, n_s) + small.shape[1:])
-    wide = small[:, :, : 6 * LAYERS].transpose(2, 1, 0, 3)
-    wide = flip(wide, c, 1).reshape(6, LAYERS, width)
-    each = small[:, :, 6 * LAYERS :].reshape(n_t, n_s, LAYERS, heads, -1)
-    each = lax.dynamic_index_in_dim(each, d, axis=3, keepdims=False)
+    tall = jnp.concatenate((query_bias, value_bias, up_bias), axis=2).transpose(1, 0, 2)
+    n_wide, n_tall = 6 * LAYERS * cut, LAYERS * tall.shape[2]
+    columns = 4 * HD
+    extra = -(-(n_wide + n_tall) // (16 * columns)) * 16
+    small = jnp.concatenate(
+        (
+            jnp.broadcast_to(wide.reshape(1, -1), (n_t, n_wide)),
+            tall.reshape(n_t, -1),
+            jnp.zeros((n_t, extra * columns - n_wide - n_tall), f32),
+        ),
+        axis=1,
+    )
+    small = small.astype(bf16).reshape(n_t, extra, columns)
+    first = exchange(jnp.concatenate((packed_mixed(0), small), axis=1), DP)
+    first_shard = jnp.concatenate(
+        (first[:, :cut].reshape(part, columns), first[:, cut:].reshape(-1, columns)), axis=0
+    )
+    messages = [to_planes_of(first_shard)]
+    hidden = to_inner(own_rows(tokens[0])).astype(f32)
+    second_shard = to_planes(after(packed_feed(0), first_shard))
+    messages.append(to_planes_of(second_shard))
+    mixed = join(messages[0])
+    small = jnp.stack([plane[:, part:].reshape(n_z, n_t, -1) for plane in mixed]).astype(f32)
+    wide = small[:, 0, :, :n_wide].reshape(n_s, n_t, 6 * LAYERS, cut)
+    wide = wide.transpose(2, 0, 1, 3).reshape(6, LAYERS, width)
+    each = small[:, :, :, n_wide : n_wide + n_tall].reshape(n_s, n_z, n_t, LAYERS, -1)
+    each = jnp.stack(flip_list([each[k] for k in range(n_s)], c)).transpose(3, 1, 2, 0, 4)
     tall = []
     begin = 0
     tall_sizes = (HD, HD, units)
     for size in tall_sizes:
         size = size // (n_t * n_s)
-        piece = each[:, :, :, begin : begin + size]
+        tall.append(each[..., begin : begin + size].reshape(LAYERS, n_z, -1))
         begin += size
-        tall.append(piece.transpose(2, 0, 1, 3).reshape(LAYERS, -1))
-    tall = jnp.concatenate(tall, axis=1)
-    tall = jnp.stack(flip_list(gather(tall, HEAD, n_z), z), axis=1)
-
-    hidden = to_inner(start_rows).astype(f32)
-    second_shard = to_planes([after(block, small) for block in shards[0][1]])
-    messages.append(to_planes_of(second_shard))
+    tall = jnp.concatenate(tall, axis=2)
 
     qkv_columns = 3 * HD
     head_ids = jnp.arange(n_z, dtype=jnp.int32) * heads + d
@@ -591,28 +606,29 @@
     query_pos = (c * slice_len + own_pos).astype(f32)[:, None]
     others = (c ^ jnp.arange(n_s, dtype=jnp.int32)) * slice_len
     key_pos = (others[:, None] + own_pos[None]).astype(f32)[:, None, :]
-    none = jnp.zeros((width,), f32)
-
     cot = cotangent[0]
     records = []
-    _, low = norm_forward(hidden, [], none, wide[0, 0], wide[1, 0])
+    low = norm_parts(hidden)[0].astype(bf16)
     for layer in range(LAYERS):
-        mixed, feed = (join(planes) for planes in messages[2 * layer : 2 * layer + 2])
-        gain_one, _, bias_dense, gain_two, shift_two, bias_down = (wide[i, layer] for i in range(6))
+        gain_one, shift_one, bias_dense, gain_two, shift_two, bias_down = (wide[i, layer] for i in range(6))
         zeros = jnp.zeros((n_z, HD), f32)
         bias_qkv = jnp.concatenate((tall[layer, :, :HD], zeros, tall[layer, :, HD : 2 * HD]), 1)
         bias_up = tall[layer, :, 2 * HD :][:, None]
         normed_one = send_rows(low)
-        queries, both = project(normed_one, mixed, bias_qkv[:, None])
+        if layer > 0:
+            mixed = join(after(messages[2 * layer], out[0]))
+        affine = (gain_one, shift_one) if layer == 0 else ()
+        queries, both, normed_one = project(normed_one, mixed, bias_qkv[:, None], *affine)
         both = gather(both, SEQ, n_s)
         if layer == 0:
-            later = [to_planes([after(block, both[0]) for block in shards[1][0]])]
-            later.append(to_planes([after(block, later[0]) for block in shards[1][1]]))
+            later = [to_planes(after(packed_mixed(1), both[0]))]
+            later.append(to_planes(after(packed_feed(1), later[0])))
             cot_rows = own_rows(after(cot, both[0]))
         else:
             cot_rows = send_rows(after(cot_rows, both[0]))
-        context, logs, out = attend(queries, both, mixed, slopes, key_pos, query_pos, n_t)
+        context, logs, out = attend(queries, both, mixed, slopes, key_pos, query_pos, n_t, width)
         got = send_sums(out)
+        feed = join(after(messages[2 * layer + 1], out[0]))
         if layer == 0:
             got, later, cot_rows = meet(got, later, cot_rows)
             messages.extend(to_planes_of(shard) for shard in later)
@@ -652,12 +668,7 @@
         return lax.psum_scatter(mine, HEAD, scatter_dimension=0, tiled=False)
 
     def send_shares(mine):
-        mine = mine.reshape(n_t, cut, -1)
-        blocks = [lax.dynamic_index_in_dim(mine, d ^ step, 0, False) for step in range(n_t)]
-        return deal(blocks, DP, n_t)
-
-    def share_of(got):
-        return jnp.stack(flip_list(got, d), axis=1).astype(f32)
+        return exchange(mine.reshape(n_t, cut, -1), DP)
 
     feed_shares = [None] * LAYERS
     mixed_shares = [None] * LAYERS
@@ -677,33 +688,28 @@
             got, feed_grad, output_low = meet(got, feed_grad, output_low)
             output_planes = to_planes_of(output_low)
         else:
-            got, feed_grad, feed_got = meet(got, feed_grad, send_shares(feed_sums[layer + 1]))
-            feed_shares[layer + 1] = share_of(feed_got)
+            got, feed_grad = meet(got, feed_grad)
         mid_grad, low, sums_two = norm_back(hidden_mid, gradient, got, gain_two)
         mid_low = send_rows(low)
         mine = core_sum(feed_grad)
         if last:
             mid_low, mine = meet(mid_low, mine)
         else:
-            mid_low, mine, mixed_got = meet(mid_low, mine, send_shares(mixed_sums[layer + 1]))
-            mixed_shares[layer + 1] = share_of(mixed_got)
+            feed_share = send_shares(after(feed_sums[layer + 1], low))
+            mid_low, mine, feed_shares[layer + 1] = meet(mid_low, mine, feed_share)
         feed_sums[layer] = head_sum(mine)
         query_grad, both_grads = attend_back(
             mid_low, queries, both, mixed, context, logs, slopes, key_pos, query_pos
         )
         got = deal(both_grads, SEQ, n_s)
-        joined, qkv_sums, out = project_back(query_grad, got, mixed, n_t)
+        joined, qkv_sums, out = project_back(query_grad, got, mixed, n_t, width)
         got = send_sums(out)
         mixed_grad = weight_back(normed_one, joined, mid_low, context, n_s)
         if last:
             planes = after(output_planes, joined)
-            got, mixed_grad, output_got = meet(got, mixed_grad, send_output(planes))
-            output = output_of(output_got)
+            got, mixed_grad, output = meet(got, mixed_grad, send_output(planes))
         else:
-            mine = core_sum(mixed_grad)
-            got, mine, feed_got = meet(got, mine, send_shares(after(feed_sums[layer], joined)))
-            feed_shares[layer] = share_of(feed_got)
-            mixed_sums[layer] = head_sum(mine)
+            mixed_sums[layer] = head_sum(after(core_sum(mixed_grad), feed_sums[layer]))
         gradient, low, sums_one = norm_back(hidden, mid_grad, got, gain_one)
         if layer > 0:
             grad_low, mine = meet(send_rows(low), core_sum(mixed_grad))
@@ -724,8 +730,11 @@
         )
 
     tokens_planes = to_planes_of(to_outer(low))
-    mixed_shares[0] = share_of(send_shares(mixed_sums[0]))
-    tokens_grad = output_of(send_output(tokens_planes)).astype(f32)
+    mixed_shares[1] = send_shares(after(mixed_sums[1], low))
+    feed_shares[0] = send_shares(after(feed_sums[0], low))
+    mixed_shares[0] = send_shares(mixed_sums[0])
+    tokens_grad = send_output(tokens_planes).astype(f32)
+    feed_shares = [after(share, low) for share in feed_shares]
 
     def fold(arrays, name, size):
         total = arrays[0]
@@ -762,10 +771,18 @@
         begin += LAYERS * size
         outs.append(piece.transpose(1, 0, 2))
     query_bias_grad, value_bias_grad, up_bias_grad = outs
-    qkv_grad = jnp.stack([share[:, :, :qkv_columns].reshape(cut, -1) for share in mixed_shares])
-    dense_grad = jnp.stack([share[:, :, qkv_columns:].reshape(cut, -1).T for share in mixed_shares])
-    up_grad = jnp.stack([share[:, :, :units].reshape(cut, -1) for share in feed_shares])
-    down_grad = jnp.stack([share[:, :, units:].reshape(cut, -1).T for share in feed_shares])
+    def rows_first(shares, begin, end):
+        parts = [share[:, :, begin:end].transpose(1, 0, 2).reshape(cut, -1) for share in shares]
+        return jnp.stack(parts).astype(f32)
+
+    def columns_first(shares, begin, end):
+        parts = [share[:, :, begin:end].transpose(0, 2, 1).reshape(-1, cut) for share in shares]
+        return jnp.stack(parts).astype(f32)
+
+    qkv_grad = rows_first(mixed_shares, 0, qkv_columns)
+    dense_grad = columns_first(mixed_shares, qkv_columns, columns)
+    up_grad = rows_first(feed_shares, 0, units)
+    down_grad = columns_first(feed_shares, units, 2 * units)
     return (
         output,
         tokens_grad,

time: 666 us -> 623 us (0.935)
  waiting for transfers between devices: 239 us -> 192 us
  local copies, waits for them, and re-layouts: 104 us -> 129 us
  Pallas kernels: 120 us -> 111 us
  blocking collectives: 7.76 us -> 0 us
    all_gather x6, waiting for transfers between devices: 92.9 us -> 42.1 us  [to_planes_of(): return lax.all_gather(array, HEAD, axis=0, tiled=False)]
    unnamed x287 -> x335, local copies, waits for them, and re-layouts: 44.6 us -> 91.4 us
    ppermute x100 -> x67, starting transfers between devices: 107 us -> 64.1 us  [swap(): return lax.ppermute(array, name, [(i, i ^ step) for i in range(size)])]
    all_to_all x0 -> x10, starting transfers between devices: none -> 37.3 us  [exchange(): return lax.all_to_all(array, name, 0, 0, tiled=True)]
    all_to_all x0 -> x10, waiting for transfers between devices: none -> 23.1 us  [exchange(): return lax.all_to_all(array, name, 0, 0, tiled=True)]
    reduce_scatter x4, waiting for transfers between devices: 16.9 us -> 1.01 us  [head_sum(): return lax.psum_scatter(mine, HEAD, scatter_dimension=0, tiled=False)]
    dynamic_slice x16 -> x0, local copies, waits for them, and re-layouts: 12.5 us -> none  [the longest x5 7.88 us: send_output(): lax.dynamic_index_in_dim(planes, d ^ step, 0, False)]
    pallas_call x24 -> x23, Pallas kernels: 120 us -> 111 us  [run(): pl.pallas_call(kernel, grid=(steps,), in_specs=[each(item) for item in ea...]
  transfers between devices with their start and end apart: 116 -> 93, of which waited for: 45 -> 39; matrix products, arithmetic and copies ran while one was open for 16% -> 13% of each run, Pallas kernels for 17% -> 17%
where the time goes in v5:
time: 623 us; the launch traced here: 612 us
  waiting for transfers between devices  192 us (31%)
  local copies, waits for them, and re-layouts  129 us (21%)
  starting transfers between devices  121 us (19%)
  Pallas kernels  111 us (18%)
  other arithmetic  43.4 us (7%)
  between operations  16.4 us (3%)
    ppermute x67, waiting for transfers between devices, swap(): return lax.ppermute(array, name, [(i, i ^ step) for i in range(size)])  126 us
    pallas_call x23, Pallas kernels, run(): pl.pallas_call(kernel, grid=(steps,), in_specs=[each(item) for item in ea...  111 us
    unnamed x335, local copies, waits for them, and re-layouts  91.4 us
    ppermute x67, starting transfers between devices, swap(): return lax.ppermute(array, name, [(i, i ^ step) for i in range(size)])  64.1 us
    all_gather x6, waiting for transfers between devices, to_planes_of(): return lax.all_gather(array, HEAD, axis=0, tiled=False)  42.1 us
    all_to_all x10, starting transfers between devices, exchange(): return lax.all_to_all(array, name, 0, 0, tiled=True)  37.3 us
    all_to_all x10, waiting for transfers between devices, exchange(): return lax.all_to_all(array, name, 0, 0, tiled=True)  23.1 us
    ppermute x6, starting transfers between devices, own_rows(): total = total + lax.ppermute(blocks[step], (DP, HEAD), pairs)  18.2 us
  transfers between devices with their start and end apart: 93, of which 39 were waited for; matrix products, arithmetic and copies ran while one was open for 13% of the time, Pallas kernels for 17%

profile of v5, /device:TPU:0, one launch (start us, length us, event | category | flops | bytes accessed | tf_op | source)
XLA Modules:
  0.0 612.1 jit_solution(16063000259244656212)
XLA Ops:
  8.6 5.6 collective-permute-start.1
  39.7 22.5 %all-gather.14.cloned.1.call-done = bf16[2304,256]{1,0:T(8,128)(2,1)} async-done(((bf16[576,256]{1,0:T(8,128)(2,1)}), bf16[2304,256]{1,0:T(8,128)(2,1)}) %all-gather.14.cloned.1.call-update) | async-done | bytes 1179664 | tf_op jit(solution)/shard_map/all_gather | solution.py:540
  123.8 9.8 %shard_map.263 = (bf16[4,512,64]{2,1,0:T(8,128)(2,1)S(1)}, f32[4,512,1]{2,1,0:T(8,128)S(1)}, bf16[128,1024]{1,0:T(8,128)(2,1)S(1)}, bf16[128,1024]{1,0:T(8,128)(...) custom-call(bf16[4,512,64]{2,1,0:T(8,128)(2,1)S(1)} %get-tuple-element.168.refs_0_, ...), custom_call_target="tpu_custom_call" | custom-call | flops 805306368 | bytes 4997120 | tf_op jit(solution)/shard_map/pallas_call | solution.py:120
  155.0 5.5 collective-permute-done.15.refs_4_.refs_3_
  160.4 6.0 collective-permute-done.16.refs_5_.refs_4_
  166.4 6.9 %shard_map.265 = (f32[4,512,256]{2,1,0:T(8,128)S(1)}, bf16[4,512,256]{2,1,0:T(8,128)(2,1)S(1)}, bf16[128,1024]{1,0:T(8,128)(2,1)S(1)}, bf16[128,1024]{1,0:T(8,12...) custom-call(bf16[4,512,512]{2,1,0:T(8,128)(2,1)} %all-gather.12.cloned.1.call-done.refs_0_, ...), custom_call_target="tpu_custom_call" | custom-call | flops 2147483648 | bytes 9441280 | tf_op jit(solution)/shard_map/pallas_call | solution.py:120
  182.0 5.8 collective-permute-done.19.refs_5_
  188.5 5.4 collective-permute-done.21.refs_7_
  199.5 5.7 collective-permute-done.22.refs_4_.refs_3_
  215.6 8.8 %shard_map.268 = (bf16[4,512,64]{2,1,0:T(8,128)(2,1)S(1)}, f32[4,512,1]{2,1,0:T(8,128)S(1)}, bf16[128,1024]{1,0:T(8,128)(2,1)S(1)}, bf16[128,1024]{1,0:T(8,128)(...) custom-call(bf16[4,512,64]{2,1,0:T(8,128)(2,1)S(1)} %get-tuple-element.192.refs_0_, ...), custom_call_target="tpu_custom_call" | custom-call | flops 805306368 | bytes 4734976 | tf_op jit(solution)/shard_map/pallas_call | solution.py:120
  260.6 6.2 %collective-permute-done.27.refs_6_ = bf16[128,1024]{1,0:T(8,128)(2,1)S(1)} collective-permute-done((bf16[128,1024]{1,0:T(8,128)(2,1)}, bf16[128,1024]{1,0:T(8,128)(2,1)S(1)}, u32[]{:S(2)}, u32[]{:S(2)}) %collective-permute-start.27) | collective-permute-done | bytes 262176 | tf_op jit(solution)/shard_map/ppermute | solution.py:41
  284.5 6.9 %shard_map.270 = (f32[4,512,256]{2,1,0:T(8,128)S(1)}, bf16[4,512,256]{2,1,0:T(8,128)(2,1)S(1)}, bf16[128,1024]{1,0:T(8,128)(2,1)S(1)}, bf16[128,1024]{1,0:T(8,12...) custom-call(bf16[4,512,512]{2,1,0:T(8,128)(2,1)} %bitcast.247, ...), custom_call_target="tpu_custom_call" | custom-call | flops 2147483648 | bytes 9441280 | tf_op jit(solution)/shard_map/pallas_call | solution.py:120
  296.2 8.2 %shard_map.271 = (bf16[4,512,256]{2,1,0:T(8,128)(2,1)S(1)}, f32[4,1,256]{2,1,0:T(1,128)S(1)}, bf16[128,1024]{1,0:T(8,128)(2,1)S(1)}, bf16[128,1024]{1,0:T(8,128)...) custom-call(bf16[4,512,512]{2,1,0:T(8,128)(2,1)S(1)} %bitcast.248, ...), custom_call_target="tpu_custom_call" | custom-call | flops 2147483648 | bytes 9441280 | tf_op jit(solution)/shard_map/pallas_call | solution.py:120
  306.4 5.4 shard_map.272
  313.8 5.6 collective-permute-done.38.refs_6_
  341.3 11.9 %shard_map.274 = (bf16[4,512,64]{2,1,0:T(8,128)(2,1)S(1)}, bf16[4,512,128]{2,1,0:T(8,128)(2,1)S(1)}, bf16[4,512,128]{2,1,0:T(8,128)(2,1)}) custom-call(bf16[4,512,64]{2,1,0:T(8,128)(2,1)S(1)} %copy-done.18, bf16[4,512,128]{2,1,0:T(8,128)(2,1)S(1)} %copy-done.20, bf16[4,512,128]{2,1,0:T(8,128)(2,1)S(1)} %copy-done.22, bf16[4,512,256]{2,1,0:T(8,128)(2,1)S(1)} %bitcast.244, ...), custom_call_target="tpu_custom_call" | custom-call | flops 1610612736 | bytes 6045696 | tf_op jit(solution)/shard_map/pallas_call | solution.py:120
  383.9 6.2 %collective-permute-done.47.refs_4_ = bf16[128,1024]{1,0:T(8,128)(2,1)S(1)} collective-permute-done((bf16[128,1024]{1,0:T(8,128)(2,1)}, bf16[128,1024]{1,0:T(8,128)(2,1)S(1)}, u32[]{:S(2)}, u32[]{:S(2)}) %collective-permute-start.47) | collective-permute-done | bytes 262176 | tf_op jit(solution)/shard_map/ppermute | solution.py:41
  411.8 5.5 collective-permute-done.51.refs_5_.refs_8_
  420.6 7.4 %shard_map.278 = (bf16[4,512,256]{2,1,0:T(8,128)(2,1)S(1)}, f32[4,1,256]{2,1,0:T(1,128)S(1)}, bf16[128,1024]{1,0:T(8,128)(2,1)S(1)}, bf16[128,1024]{1,0:T(8,128)...) custom-call(bf16[4,512,512]{2,1,0:T(8,128)(2,1)S(1)} %copy-done.86, ...), custom_call_target="tpu_custom_call" | custom-call | flops 2147483648 | bytes 9441280 | tf_op jit(solution)/shard_map/pallas_call | solution.py:120
  433.5 5.2 shard_map.279
  456.0 6.9 %collective-permute-done.57.refs_11_.refs_7_ = bf16[128,1024]{1,0:T(8,128)(2,1)S(1)} collective-permute-done((bf16[128,1024]{1,0:T(8,128)(2,1)S(1)}, bf16[128,1024]{1,0:T(8,128)(2,1)S(1)}, u32[]{:S(2)}, u32[]{:S(2)}) %collective-permute-start.57) | collective-permute-done | bytes 262176 | tf_op jit(solution)/shard_map/ppermute | solution.py:41
  475.8 11.6 %shard_map.281 = (bf16[4,512,64]{2,1,0:T(8,128)(2,1)S(1)}, bf16[4,512,128]{2,1,0:T(8,128)(2,1)S(1)}, bf16[4,512,128]{2,1,0:T(8,128)(2,1)}) custom-call(bf16[4,512,64]{2,1,0:T(8,128)(2,1)S(1)} %copy-done.12, bf16[4,512,128]{2,1,0:T(8,128)(2,1)S(1)} %copy-done.14, bf16[4,512,128]{2,1,0:T(8,128)(2,1)S(1)} %copy-done.16, bf16[4,576,256]{2,1,0:T(8,128)(2,1)} %bitcast.237, ...), custom_call_target="tpu_custom_call" | custom-call | flops 1610612736 | bytes 6307840 | tf_op jit(solution)/shard_map/pallas_call | solution.py:120
  540.7 19.5 %all-gather.22.cloned.1.call-done = bf16[512,1024]{1,0:T(8,128)(2,1)} async-done(((bf16[128,1024]{1,0:T(8,128)(2,1)}), bf16[512,1024]{1,0:T(8,128)(2,1)}) %all-gather.22.cloned.1.call-update) | async-done | bytes 1048592 | tf_op jit(solution)/shard_map/all_gather | solution.py:540
  564.5 13.0 %all-to-all-done.6 = bf16[4,128,1024]{2,1,0:T(8,128)(2,1)S(1)} async-done(((bf16[4,128,1024]{2,1,0:T(8,128)(2,1)}), bf16[4,128,1024]{2,1,0:T(8,128)(2,1)S(1)}, u32[]{:S(2)}, u32[]{:S(2)}) %all-to-all-start.6) | async-done | bytes 1048608 | tf_op jit(solution)/shard_map/all_to_all | solution.py:53
  (725 shorter events, 394.1 us)
Async XLA Ops:
  8.6 29.6 %collective-permute-start.1 = (bf16[128,1024]{1,0:T(8,128)(2,1)S(1)}, bf16[128,1024]{1,0:T(8,128)(2,1)}, u32[]{:S(2)}, u32[]{:S(2)}) collective-permute-start(bf16[128,1024]{1,0:T(8,128)(2,1)S(1)} %get-tuple-element.396), channel_id=1, source_target_pairs={{0,8},{9,1},{18,26},{27,19},{4,12},{13,5},{22,30},{31,23}} | collective-permute-start | bytes 786440 | tf_op jit(solution)/shard_map/ppermute | solution.py:530
  14.1 24.1 %collective-permute-start.2 = (bf16[128,1024]{1,0:T(8,128)(2,1)S(1)}, bf16[128,1024]{1,0:T(8,128)(2,1)}, u32[]{:S(2)}, u32[]{:S(2)}) collective-permute-start(bf16[128,1024]{1,0:T(8,128)(2,1)S(1)} %get-tuple-element.398), channel_id=1, source_target_pairs={{0,16},{9,25},{18,2},{27,11},{4,20},{13,29},{22,6},{31,15}} | collective-permute-start | bytes 786440 | tf_op jit(solution)/shard_map/ppermute | solution.py:530
  25.9 36.3 %all-gather.14.cloned.1.call-start = ((), (), s32[]{:S(2)}) async-start(), calls=%async_computation.19 | async-start | bytes 1474560 | tf_op jit(solution)/shard_map/all_gather | solution.py:540
  34.6 27.7 %all-to-all-start.3 = ((bf16[4,128,512]{2,1,0:T(8,128)(2,1)}), bf16[4,128,512]{2,1,0:T(8,128)(2,1)S(1)}, u32[]{:S(2)}, u32[]{:S(2)}) async-start(bf16[4,128,512]{2,1,0:T(8,128)(2,1)} %pad_maximum_fusion.2), calls=%async_computation.3 | async-start | bytes 1048576 | tf_op jit(solution)/shard_map/all_to_all | solution.py:53
  38.1 111.9 %all-gather.12.cloned.1.call-start = ((), (), s32[]{:S(2)}) async-start(), calls=%async_computation.14 | async-start | bytes 2621440 | tf_op jit(solution)/shard_map/all_gather | solution.py:540
  63.7 24.0 %collective-permute-start.4 = (bf16[128,1024]{1,0:T(8,128)(2,1)S(1)}, bf16[128,1024]{1,0:T(8,128)(2,1)S(1)}, u32[]{:S(2)}, u32[]{:S(2)}) collective-permute-start(bf16[128,1024]{1,0:T(8,128)(2,1)S(1)} %multiply_convert_fusion.refs_3_), channel_id=1, source_target_pairs={{0,8},{8,0},{16,24},{24,16},{1,9},{9,1},{17,25},{25,17},{2,10},{10... | collective-permute-start | bytes 786440 | tf_op jit(solution)/shard_map/ppermute | solution.py:41
  65.2 23.2 %collective-permute-start.5 = (bf16[128,1024]{1,0:T(8,128)(2,1)S(1)}, bf16[128,1024]{1,0:T(8,128)(2,1)S(1)}, u32[]{:S(2)}, u32[]{:S(2)}) collective-permute-start(bf16[128,1024]{1,0:T(8,128)(2,1)S(1)} %multiply_convert_fusion.refs_3_), channel_id=1, source_target_pairs={{0,16},{8,24},{16,0},{24,8},{1,17},{9,25},{17,1},{25,9},{2,18},{10... | collective-permute-start | bytes 786440 | tf_op jit(solution)/shard_map/ppermute | solution.py:41
  99.2 24.5 %collective-permute-start.7 = (bf16[4,512,128]{2,1,0:T(8,128)(2,1)S(1)}, bf16[4,512,128]{2,1,0:T(8,128)(2,1)S(1)}, u32[]{:S(2)}, u32[]{:S(2)}) collective-permute-start(bf16[4,512,128]{2,1,0:T(8,128)(2,1)S(1)} %get-tuple-element.169.refs_1_), channel_id=1, source_target_pairs={{0,4},{4,0},{1,5},{5,1},{2,6},{6,2},{3,7},{7,3},{8,12},{12,8},{9,1... | collective-permute-start | bytes 1572872 | tf_op jit(solution)/shard_map/ppermute | solution.py:41
  108.1 30.6 %collective-permute-start.11 = (bf16[128,1024]{1,0:T(8,128)(2,1)}, bf16[128,1024]{1,0:T(8,128)(2,1)}, u32[]{:S(2)}, u32[]{:S(2)}) collective-permute-start(bf16[128,1024]{1,0:T(8,128)(2,1)} %get-tuple-element.393), channel_id=1, source_target_pairs={{0,8},{9,1},{18,26},{27,19},{4,12},{13,5},{22,30},{31,23}} | collective-permute-start | bytes 786440 | tf_op jit(solution)/shard_map/ppermute | solution.py:530
  112.7 26.1 %collective-permute-start.12 = (bf16[128,1024]{1,0:T(8,128)(2,1)}, bf16[128,1024]{1,0:T(8,128)(2,1)}, u32[]{:S(2)}, u32[]{:S(2)}) collective-permute-start(bf16[128,1024]{1,0:T(8,128)(2,1)} %get-tuple-element.395), channel_id=1, source_target_pairs={{0,16},{9,25},{18,2},{27,11},{4,20},{13,29},{22,6},{31,15}} | collective-permute-start | bytes 786440 | tf_op jit(solution)/shard_map/ppermute | solution.py:530
  114.7 24.1 %collective-permute-start.13 = (bf16[128,1024]{1,0:T(8,128)(2,1)}, bf16[128,1024]{1,0:T(8,128)(2,1)}, u32[]{:S(2)}, u32[]{:S(2)}) collective-permute-start(bf16[128,1024]{1,0:T(8,128)(2,1)} %get-tuple-element.394), channel_id=1, source_target_pairs={{0,24},{9,17},{18,10},{27,3},{4,28},{13,21},{22,14},{31,7}} | collective-permute-start | bytes 786440 | tf_op jit(solution)/shard_map/ppermute | solution.py:530
  123.4 55.1 %all-gather.16.cloned.1.call-start = ((), (), s32[]{:S(2)}) async-start(), calls=%async_computation.20 | async-start | bytes 1310720 | tf_op jit(solution)/shard_map/all_gather | solution.py:540
  150.0 81.5 %all-gather.18.cloned.1.call-start = ((), (), s32[]{:S(2)}) async-start(), calls=%async_computation.21 | async-start | bytes 2621440 | tf_op jit(solution)/shard_map/all_gather | solution.py:540
  150.6 214.7 %all-gather.20.cloned.1.call-start = ((), (), s32[]{:S(2)}) async-start(), calls=%async_computation.22 | async-start | bytes 1310720 | tf_op jit(solution)/shard_map/all_gather | solution.py:540
  178.5 31.5 %collective-permute-start.18 = (bf16[4,512,256]{2,1,0:T(8,128)(2,1)}, bf16[4,512,256]{2,1,0:T(8,128)(2,1)S(1)}, u32[]{:S(2)}, u32[]{:S(2)}) collective-permute-start(bf16[4,512,256]{2,1,0:T(8,128)(2,1)} %bitcast.241), channel_id=1, source_target_pairs={{0,4},{4,0},{1,5},{5,1},{2,6},{6,2},{3,7},{7,3},{8,12},{12,8},{9,1... | collective-permute-start | bytes 3145736 | tf_op jit(solution)/shard_map/ppermute | solution.py:41
  231.5 52.0 %collective-permute-start.32 = (bf16[4,512,512]{2,1,0:T(8,128)(2,1)}, bf16[4,512,512]{2,1,0:T(8,128)(2,1)}, u32[]{:S(2)}, u32[]{:S(2)}) collective-permute-start(bf16[4,512,512]{2,1,0:T(8,128)(2,1)} %bitcast.246), channel_id=1, source_target_pairs={{0,4},{4,0},{1,5},{5,1},{2,6},{6,2},{3,7},{7,3},{8,12},{12,8},{9,1... | collective-permute-start | bytes 6291464 | tf_op jit(solution)/shard_map/ppermute | solution.py:41
  319.5 124.3 %reduce-scatter.5.cloned.1.call-start = ((), (), s32[]{:S(2)}) async-start(), calls=%async_computation.15 | async-start | bytes 2621440 | tf_op jit(solution)/shard_map/reduce_scatter | solution.py:668
  365.3 31.3 %all-to-all-start.4 = ((bf16[4,128,1024]{2,1,0:T(8,128)(2,1)}), bf16[4,128,1024]{2,1,0:T(8,128)(2,1)}, u32[]{:S(2)}, u32[]{:S(2)}) async-start(bf16[4,128,1024]{2,1,0:T(8,128)(2,1)} %bitcast.261), calls=%async_computation.4 | async-start | bytes 2097152 | tf_op jit(solution)/shard_map/all_to_all | solution.py:53
  369.6 153.1 %reduce-scatter.11.cloned.1.call-start = ((), (), s32[]{:S(2)}) async-start(), calls=%async_computation.18 | async-start | bytes 1310720 | tf_op jit(solution)/shard_map/reduce_scatter | solution.py:668
  443.8 25.9 %all-to-all-start.5 = ((bf16[4,128,512]{2,1,0:T(8,128)(2,1)}), bf16[4,128,512]{2,1,0:T(8,128)(2,1)}, u32[]{:S(2)}, u32[]{:S(2)}) async-start(bf16[4,128,512]{2,1,0:T(8,128)(2,1)} %bitcast.276), calls=%async_computation.6 | async-start | bytes 1048576 | tf_op jit(solution)/shard_map/all_to_all | solution.py:53
  448.0 87.0 %reduce-scatter.7.cloned.1.call-start = ((), (), s32[]{:S(2)}) async-start(), calls=%async_computation.16 | async-start | bytes 2621440 | tf_op jit(solution)/shard_map/reduce_scatter | solution.py:668
  489.5 70.7 %all-gather.22.cloned.1.call-start = ((), (), s32[]{:S(2)}) async-start(), calls=%async_computation.23 | async-start | bytes 1310720 | tf_op jit(solution)/shard_map/all_gather | solution.py:540
  527.9 61.8 %reduce-scatter.9.cloned.1.call-start = ((), (), s32[]{:S(2)}) async-start(), calls=%async_computation.17 | async-start | bytes 1310720 | tf_op jit(solution)/shard_map/reduce_scatter | solution.py:668
  538.5 25.4 %collective-permute-start.72 = (f32[1632]{0:T(1024)S(1)}, f32[1632]{0:T(1024)S(1)}, u32[]{:S(2)}, u32[]{:S(2)}) collective-permute-start(f32[1632]{0:T(1024)S(1)} %get-tuple-element.383), channel_id=1, source_target_pairs={{0,24},{8,16},{16,8},{24,0},{1,25},{9,17},{17,9},{25,1},{2,26},{10... | collective-permute-start | bytes 19592 | tf_op jit(solution)/shard_map/ppermute | solution.py:41
  (234 other events, 1929.6 us)
Sparse Core Ops, SparseCore 0:
  32.4 29.7 all-gather.13
  64.3 45.0 all-gather.11
  150.1 26.0 all-gather.15
  178.2 45.3 all-gather.17
  319.6 25.6 all-gather.19
  354.9 41.5 reduce-scatter.4
  442.5 24.8 reduce-scatter.10
  489.6 41.0 reduce-scatter.6
  533.0 27.2 all-gather.21
  563.1 26.6 reduce-scatter.8

commit v6 on v5

--- a/solution.py
+++ b/solution.py
@@ -15,7 +15,7 @@
 
 epsilon = 1e-05
 masked_value = -1000000000.0
-VMEM_LIMIT = 48 * 1024 * 1024
+VMEM_LIMIT = 60 * 1024 * 1024
 bf16 = jnp.bfloat16
 f32 = jnp.float32
 
@@ -160,12 +160,12 @@
         acc[:, s * part : (s + 1) * part] += dot(array, plane[:part, begin:end], 1, 1)
 
 
-def project(blocks, planes, bias, gain=None, shift=None):
+def project(blocks, planes, bias, vectors=None, gain=None, shift=None):
     rows, width = blocks[0].shape
     length = rows * len(blocks)
     heads = planes[0].shape[0]
     n, n_blocks = len(planes), len(blocks)
-    vectors = [] if gain is None else [gain[None], shift[None]]
+    vectors = [] if gain is None else [vectors]
 
     def body(z, each_in, whole_in, each_out, whole_out, scratch):
         wide = scratch[0]
@@ -174,8 +174,9 @@
         def _():
             lay(wide, whole_in[:n_blocks])
             if vectors:
-                gain_ref, shift_ref = whole_in[n_blocks:]
-                normed = wide[...].astype(f32) * gain_ref[...] + shift_ref[...]
+                lines = whole_in[n_blocks]
+                normed = wide[...].astype(f32) * lines[gain : gain + 1, :]
+                normed = normed + lines[shift : shift + 1, :]
                 wide[...] = normed.astype(bf16)
                 spread(whole_out, wide)
 
@@ -430,53 +431,136 @@
     )
 
 
-def norm_forward(values, got, bias, gain, shift):
-    def body(z, each_in, whole_in, each_out, whole_out, scratch):
-        start, bias_ref, gain_ref, shift_ref = whole_in[:4]
-        total = start[...] + bias_ref[...]
-        for item in whole_in[4:]:
+def norm_forward(values, got, vectors, bias, gain, shift):
+    def body(z, each_in, whole_in, each_out, whole_out, scratch):
+        start, rows = whole_in[:2]
+        total = start[...] + rows[bias : bias + 1, :]
+        for item in whole_in[2:]:
             total = total + item[...].astype(f32)
         whole_out[0][...] = total
         xhat, _ = norm_parts(total)
-        whole_out[1][...] = (xhat * gain_ref[...] + shift_ref[...]).astype(bf16)
-
-    return run(
-        body,
-        1,
-        [],
-        [values, bias[None], gain[None], shift[None]] + list(got),
-        [],
-        [shape(values.shape, f32), shape(values.shape, bf16)],
-    )
-
-
-def norm_back(values, gradient, got, gain):
+        normed = xhat * rows[gain : gain + 1, :] + rows[shift : shift + 1, :]
+        whole_out[1][...] = normed.astype(bf16)
+
+    shapes = [shape(values.shape, f32), shape(values.shape, bf16)]
+    return run(body, 1, [], [values, vectors] + list(got), [], shapes)
+
+
+def norm_back(values, gradient, got, vectors, gain):
     width = values.shape[1]
 
     def body(z, each_in, whole_in, each_out, whole_out, scratch):
         e = sum(item[...].astype(f32) for item in whole_in[3:])
         xhat, scale = norm_parts(whole_in[0][...])
-        eg = e * whole_in[2][...]
+        eg = e * whole_in[2][gain : gain + 1, :]
         back = scale * (
             eg
             - jnp.mean(eg, axis=-1, keepdims=True)
             - xhat * jnp.mean(eg * xhat, axis=-1, keepdims=True)
         )
-        fresh = whole_in[1][...] + back
+        fresh = whole_in[1][...].astype(f32) + back
         whole_out[0][...] = fresh
         whole_out[1][...] = fresh.astype(bf16)
         whole_out[2][0:1, :] = jnp.sum(e * xhat, axis=0, keepdims=True)
         whole_out[2][1:2, :] = jnp.sum(e, axis=0, keepdims=True)
         whole_out[2][2:3, :] = jnp.sum(fresh, axis=0, keepdims=True)
 
-    return run(
-        body,
-        1,
-        [],
-        [values, gradient, gain[None]] + list(got),
-        [],
-        [shape(values.shape, f32), shape(values.shape, bf16), shape((3, width), f32)],
-    )
+    shapes = [shape(values.shape, f32), shape(values.shape, bf16), shape((3, width), f32)]
+    return run(body, 1, [], [values, gradient, vectors] + list(got), [], shapes)
+
+
+def turn_columns(array, turn, counts, inward):
+    n_t, n_s = counts
+    cut = array.shape[1] // (n_t * n_s)
+    parts = [array[:, j * cut : (j + 1) * cut] for j in range(n_t * n_s)]
+    index = turn[:, :cut]
+    if inward:
+        groups = flip_list([parts[s::n_s] for s in range(n_s)], index)
+        return [part for group in groups for part in group]
+    groups = flip_list([parts[k * n_t : (k + 1) * n_t] for k in range(n_s)], index)
+    return [groups[s][t] for t in range(n_t) for s in range(n_s)]
+
+
+def store_columns(target, parts):
+    cut = parts[0].shape[1]
+    for j, part in enumerate(parts):
+        target[:, j * cut : (j + 1) * cut] = part.astype(target.dtype)
+
+
+def first_norm(items, turn, counts):
+    dims = items[0].shape
+
+    def body(z, each_in, whole_in, each_out, whole_out, scratch):
+        total = sum(item[...].astype(f32) for item in whole_in[1:])
+        store_columns(whole_out[0], turn_columns(total, whole_in[0][...], counts, True))
+        whole_out[1][...] = norm_parts(whole_out[0][...])[0].astype(bf16)
+
+    return run(body, 1, [], [turn] + list(items), [], [shape(dims, f32), shape(dims, bf16)])
+
+
+def turned_sum(items, turn, counts, inward, bias=None):
+    dims = items[0].shape
+
+    def body(z, each_in, whole_in, each_out, whole_out, scratch):
+        count = len(whole_in) - (0 if bias is None else 1)
+        total = sum(item[...].astype(f32) for item in whole_in[1:count])
+        if bias is not None:
+            total = total + whole_in[count][bias : bias + 1, :]
+        store_columns(whole_out[0], turn_columns(total, whole_in[0][...], counts, inward))
+
+    return run(body, 1, [], [turn] + list(items), [], [shape(dims, bf16)])[0]
+
+
+def unpack(planes, turn, counts, width, layers, spare):
+    n_t, n_s = counts
+    heads, _, columns = planes[0].shape
+    part, cut = width // n_s, width // (n_s * n_t)
+    small = HD // (n_t * n_s)
+    units = columns
+    unit = units // (n_t * n_s)
+    half = columns // 2
+
+    def kernel(*refs):
+        ex, index, outs = refs[:n_s], refs[n_s], refs[n_s + 1 :]
+        vectors, qkv, up = outs[0], outs[1 : 1 + layers], outs[1 + layers :]
+        for layer in range(layers):
+            qkv[layer][...] = jnp.zeros_like(qkv[layer])
+        for t in range(n_t):
+            rows = slice(t * spare, (t + 1) * spare)
+            for k in range(n_s):
+                place = (k * n_t + t) * cut
+                vectors[:, place : place + cut] = ex[k][0, rows, :cut].astype(f32)
+            for head in range(heads):
+                blocks = [ex[k][head, rows, half:].astype(f32) for k in range(n_s)]
+                blocks = flip_list(blocks, index[:, :half])
+                for s in range(n_s):
+                    place = t * n_s + s
+                    for layer in range(layers):
+                        row = blocks[s][layer : layer + 1, :]
+                        at = place * small
+                        qkv[layer][head, :, at : at + small] = row[:, :small]
+                        at += 2 * HD
+                        qkv[layer][head, :, at : at + small] = row[:, small : 2 * small]
+                        at = place * unit
+                        up[layer][head, :, at : at + unit] = row[:, 2 * small : 2 * small + unit]
+
+    block = pl.BlockSpec((heads, n_t * spare, columns), lambda i: (0, part // (n_t * spare), 0))
+    shapes = [shape((spare, width), f32)]
+    shapes += [shape((heads, 1, 3 * HD), f32)] * layers
+    shapes += [shape((heads, 1, units), f32)] * layers
+
+    def whole(dims):
+        return pl.BlockSpec(dims, lambda i: (0,) * len(dims))
+
+    out = pl.pallas_call(
+        kernel,
+        grid=(1,),
+        in_specs=[block] * n_s + [whole(turn.shape)],
+        out_specs=[whole(item.shape) for item in shapes],
+        out_shape=shapes,
+        compiler_params=pltpu.CompilerParams(vmem_limit_bytes=VMEM_LIMIT),
+    )(*planes, turn)
+    return out[0], out[1 : 1 + layers], out[1 + layers :]
 
 
 def per_device(
@@ -508,27 +592,11 @@
     assert heads == n_t
     units = up_bias.shape[2] * n_t * n_s
 
-    def chunks(array):
-        return [array[..., j * cut : (j + 1) * cut] for j in range(n_t * n_s)]
-
-    def to_inner(array):
-        parts = chunks(array)
-        by_seq = flip_list([parts[s::n_s] for s in range(n_s)], c)
-        return jnp.concatenate([part for group in by_seq for part in group], axis=-1)
-
-    def to_outer(array):
-        parts = chunks(array)
-        by_seq = flip_list([parts[k * n_t : (k + 1) * n_t] for k in range(n_s)], c)
-        return jnp.concatenate([by_seq[s][t] for t in range(n_t) for s in range(n_s)], axis=-1)
-
-    def own_rows(array):
-        cuts = array.reshape(n_t, rows, width)
-        blocks = [lax.dynamic_index_in_dim(cuts, d ^ step, 0, False) for step in range(n_t)]
-        total = jnp.where(d == z, blocks[0], jnp.zeros_like(blocks[0]))
-        for step in range(1, n_t):
-            pairs = [(i * n_z + i, (i ^ step) * n_z + i) for i in range(n_t)]
-            total = total + lax.ppermute(blocks[step], (DP, HEAD), pairs)
-        return total
+    def spread_rows(array):
+        return exchange(array.reshape(n_t, rows, width), DP)
+
+    def own_rows(blocks):
+        return lax.dynamic_index_in_dim(blocks, z, 0, False)
 
     def send_rows(array):
         return gather(array, DP, n_t)
@@ -558,44 +626,35 @@
     def join(planes):
         return gather(planes, SEQ, n_s)
 
+    counts = (n_t, n_s)
+    turn = jnp.full((1, 128), c, jnp.int32)
     wide = jnp.concatenate(
         (first_gain, first_shift, dense_bias, second_gain, second_shift, down_bias), axis=0
     )
     tall = jnp.concatenate((query_bias, value_bias, up_bias), axis=2).transpose(1, 0, 2)
-    n_wide, n_tall = 6 * LAYERS * cut, LAYERS * tall.shape[2]
-    columns = 4 * HD
-    extra = -(-(n_wide + n_tall) // (16 * columns)) * 16
-    small = jnp.concatenate(
-        (
-            jnp.broadcast_to(wide.reshape(1, -1), (n_t, n_wide)),
-            tall.reshape(n_t, -1),
-            jnp.zeros((n_t, extra * columns - n_wide - n_tall), f32),
-        ),
-        axis=1,
-    )
-    small = small.astype(bf16).reshape(n_t, extra, columns)
-    first = exchange(jnp.concatenate((packed_mixed(0), small), axis=1), DP)
+    columns, spare = 4 * HD, 16
+    half = columns // 2
+    wide = jnp.pad(wide, ((0, spare - 6 * LAYERS), (0, half - cut)))
+    tall = jnp.pad(tall, ((0, 0), (0, spare - LAYERS), (0, half - tall.shape[2])))
+    small = jnp.concatenate((jnp.broadcast_to(wide[None], (n_t, spare, half)), tall), axis=2)
+    first = jnp.concatenate((packed_mixed(0), small.astype(bf16)), axis=1)
+    first = exchange(first, DP)
     first_shard = jnp.concatenate(
         (first[:, :cut].reshape(part, columns), first[:, cut:].reshape(-1, columns)), axis=0
     )
     messages = [to_planes_of(first_shard)]
-    hidden = to_inner(own_rows(tokens[0])).astype(f32)
-    second_shard = to_planes(after(packed_feed(0), first_shard))
-    messages.append(to_planes_of(second_shard))
-    mixed = join(messages[0])
-    small = jnp.stack([plane[:, part:].reshape(n_z, n_t, -1) for plane in mixed]).astype(f32)
-    wide = small[:, 0, :, :n_wide].reshape(n_s, n_t, 6 * LAYERS, cut)
-    wide = wide.transpose(2, 0, 1, 3).reshape(6, LAYERS, width)
-    each = small[:, :, :, n_wide : n_wide + n_tall].reshape(n_s, n_z, n_t, LAYERS, -1)
-    each = jnp.stack(flip_list([each[k] for k in range(n_s)], c)).transpose(3, 1, 2, 0, 4)
-    tall = []
-    begin = 0
+    hidden, low = first_norm([own_rows(spread_rows(tokens[0]))], turn, counts)
+    normed_one = send_rows(low)
+    rest = jnp.concatenate((packed_feed(0), packed_mixed(1), packed_feed(1)), axis=2)
+    rest = to_planes(after(rest, low))
+    messages.append(to_planes_of(rest[:, : 2 * units]))
+    later = [rest[:, 2 * units : 2 * units + columns], rest[:, 2 * units + columns :]]
+    mixed = join(after(messages[0], normed_one[-1]))
+    vectors, biases_qkv, biases_up = unpack(mixed, turn, counts, width, LAYERS, spare)
     tall_sizes = (HD, HD, units)
-    for size in tall_sizes:
-        size = size // (n_t * n_s)
-        tall.append(each[..., begin : begin + size].reshape(LAYERS, n_z, -1))
-        begin += size
-    tall = jnp.concatenate(tall, axis=2)
+
+    def vector(kind, layer):
+        return kind * LAYERS + layer
 
     qkv_columns = 3 * HD
     head_ids = jnp.arange(n_z, dtype=jnp.int32) * heads + d
@@ -608,56 +667,57 @@
     key_pos = (others[:, None] + own_pos[None]).astype(f32)[:, None, :]
     cot = cotangent[0]
     records = []
-    low = norm_parts(hidden)[0].astype(bf16)
     for layer in range(LAYERS):
-        gain_one, shift_one, bias_dense, gain_two, shift_two, bias_down = (wide[i, layer] for i in range(6))
-        zeros = jnp.zeros((n_z, HD), f32)
-        bias_qkv = jnp.concatenate((tall[layer, :, :HD], zeros, tall[layer, :, HD : 2 * HD]), 1)
-        bias_up = tall[layer, :, 2 * HD :][:, None]
-        normed_one = send_rows(low)
         if layer > 0:
+            normed_one = send_rows(low)
             mixed = join(after(messages[2 * layer], out[0]))
-        affine = (gain_one, shift_one) if layer == 0 else ()
-        queries, both, normed_one = project(normed_one, mixed, bias_qkv[:, None], *affine)
+        affine = (vectors, vector(0, 0), vector(1, 0)) if layer == 0 else ()
+        queries, both, normed_one = project(normed_one, mixed, biases_qkv[layer], *affine)
         both = gather(both, SEQ, n_s)
         if layer == 0:
-            later = [to_planes(after(packed_mixed(1), both[0]))]
-            later.append(to_planes(after(packed_feed(1), later[0])))
-            cot_rows = own_rows(after(cot, both[0]))
+            cot_rows = spread_rows(after(cot, both[0]))
         else:
             cot_rows = send_rows(after(cot_rows, both[0]))
         context, logs, out = attend(queries, both, mixed, slopes, key_pos, query_pos, n_t, width)
+        if layer == 0:
+            out, cot_rows = meet(out, cot_rows)
         got = send_sums(out)
         feed = join(after(messages[2 * layer + 1], out[0]))
         if layer == 0:
-            got, later, cot_rows = meet(got, later, cot_rows)
+            got, later = meet(got, later)
             messages.extend(to_planes_of(shard) for shard in later)
-            cot_rows = to_inner(cot_rows)
+            cot_rows = turned_sum([own_rows(cot_rows)], turn, counts, True)
         else:
             got, cot_rows = meet(got, cot_rows)
-        hidden_mid, low = norm_forward(hidden, got, bias_dense, gain_two, shift_two)
+        hidden_mid, low = norm_forward(
+            hidden, got, vectors, vector(2, layer), vector(3, layer), vector(4, layer)
+        )
         normed_two = send_rows(low)
-        pre_up, activation, out = feed_forward(normed_two, feed, bias_up)
+        pre_up, activation, out = feed_forward(normed_two, feed, biases_up[layer])
         got = send_sums(out)
         records.append(
             (
-                (mixed, feed, gain_one, gain_two),
+                (mixed, feed),
                 (hidden, hidden_mid, normed_one, normed_two),
                 (queries, both, logs, context, pre_up, activation),
             )
         )
         if layer + 1 < LAYERS:
             hidden, low = norm_forward(
-                hidden_mid, got, bias_down, wide[0, layer + 1], wide[1, layer + 1]
+                hidden_mid,
+                got,
+                vectors,
+                vector(5, layer),
+                vector(0, layer + 1),
+                vector(1, layer + 1),
             )
-        else:
-            hidden = hidden_mid + add_all(got) + bias_down
-
-    output_low = to_outer(hidden.astype(bf16))
-
-    gradient = cot_rows[0].astype(f32)
+
+    last_bias = vector(5, LAYERS - 1)
+    output_low = turned_sum([hidden_mid] + list(got) + [vectors], turn, counts, False, last_bias)
+
+    gradient = cot_rows[0]
     grad_low = cot_rows
-    down_bias_grad = jnp.sum(gradient, axis=0, keepdims=True)
+    down_bias_grad = jnp.sum(gradient, axis=0, keepdims=True, dtype=f32)
     wide_grads = [None] * LAYERS
     tall_grads = [None] * LAYERS
 
@@ -676,7 +736,7 @@
     mixed_sums = [None] * LAYERS
     for layer in reversed(range(LAYERS)):
         (
-            (mixed, feed, gain_one, gain_two),
+            (mixed, feed),
             (hidden, hidden_mid, normed_one, normed_two),
             (queries, both, logs, context, pre_up, activation),
         ) = records[layer]
@@ -689,18 +749,22 @@
             output_planes = to_planes_of(output_low)
         else:
             got, feed_grad = meet(got, feed_grad)
-        mid_grad, low, sums_two = norm_back(hidden_mid, gradient, got, gain_two)
+        mid_grad, low, sums_two = norm_back(
+            hidden_mid, gradient, got, vectors, vector(3, layer)
+        )
         mid_low = send_rows(low)
         mine = core_sum(feed_grad)
         if last:
             mid_low, mine = meet(mid_low, mine)
         else:
-            feed_share = send_shares(after(feed_sums[layer + 1], low))
-            mid_low, mine, feed_shares[layer + 1] = meet(mid_low, mine, feed_share)
+            mid_low, mine = meet(mid_low, mine)
         feed_sums[layer] = head_sum(mine)
         query_grad, both_grads = attend_back(
             mid_low, queries, both, mixed, context, logs, slopes, key_pos, query_pos
         )
+        if not last:
+            feed_share = send_shares(after(feed_sums[layer + 1], mid_low[-1]))
+            both_grads, feed_shares[layer + 1] = meet(both_grads, feed_share)
         got = deal(both_grads, SEQ, n_s)
         joined, qkv_sums, out = project_back(query_grad, got, mixed, n_t, width)
         got = send_sums(out)
@@ -710,7 +774,9 @@
             got, mixed_grad, output = meet(got, mixed_grad, send_output(planes))
         else:
             mixed_sums[layer] = head_sum(after(core_sum(mixed_grad), feed_sums[layer]))
-        gradient, low, sums_one = norm_back(hidden, mid_grad, got, gain_one)
+        gradient, low, sums_one = norm_back(
+            hidden, mid_grad, got, vectors, vector(0, layer)
+        )
         if layer > 0:
             grad_low, mine = meet(send_rows(low), core_sum(mixed_grad))
             mixed_sums[layer] = head_sum(mine)
@@ -729,7 +795,8 @@
             (qkv_sums[:, 0, :HD], qkv_sums[:, 0, 2 * HD :], up_bias_grad[:, 0]), axis=1
         )
 
-    tokens_planes = to_planes_of(to_outer(low))
+    low_outer = turned_sum([low], turn, counts, False)
+    tokens_planes = to_planes_of(after(low_outer, mixed_sums[0]))
     mixed_shares[1] = send_shares(after(mixed_sums[1], low))
     feed_shares[0] = send_shares(after(feed_sums[0], low))
     mixed_shares[0] = send_shares(mixed_sums[0])

time: 623 us -> 559 us (0.90)
  local copies, waits for them, and re-layouts: 129 us -> 42.6 us
  Pallas kernels: 111 us -> 156 us
  other arithmetic: 43.4 us -> 20.5 us
  starting transfers between devices: 121 us -> 98.4 us
  blocking collectives: 0 us -> 18.8 us
    unnamed x335 -> x159, local copies, waits for them, and re-layouts: 91.4 us -> 19.1 us
    pallas_call x23 -> x27, Pallas kernels: 111 us -> 155 us  [run(): pl.pallas_call(kernel, grid=(steps,), in_specs=[each(item) for item in ea...]
    all_gather x6, waiting for transfers between devices: 42.1 us -> 12.8 us  [to_planes_of(): return lax.all_gather(array, HEAD, axis=0, tiled=False)]
    ppermute x67, waiting for transfers between devices: 126 us -> 150 us  [swap(): return lax.ppermute(array, name, [(i, i ^ step) for i in range(size)])]
    all_to_all x0 -> x1, blocking collectives: none -> 18.8 us  [exchange(): return lax.all_to_all(array, name, 0, 0, tiled=True)]
    ppermute x6 -> x0, starting transfers between devices: 18.2 us -> none  [own_rows(): total = total + lax.ppermute(blocks[step], (DP, HEAD), pairs)]
    all_to_all x10 -> x9, waiting for transfers between devices: 23.1 us -> 33.3 us  [exchange(): return lax.all_to_all(array, name, 0, 0, tiled=True)]
    unnamed x28 -> x0, other arithmetic: 8.73 us -> none
  transfers between devices with their start and end apart: 93 -> 86, of which waited for: 39 -> 45; matrix products, arithmetic and copies ran while one was open for 13% -> 7% of each run, Pallas kernels for 17% -> 27%
where the time goes in v6:
time: 559 us; the launch traced here: 551 us
  waiting for transfers between devices  198 us (35%)
  Pallas kernels  156 us (28%)
  starting transfers between devices  98.4 us (18%)
  local copies, waits for them, and re-layouts  42.6 us (8%)
  other arithmetic  20.5 us (4%)
  blocking collectives  18.8 us (3%)
  between operations  15.9 us (3%)
    pallas_call x27, Pallas kernels, run(): pl.pallas_call(kernel, grid=(steps,), in_specs=[each(item) for item in ea...  155 us
    ppermute x67, waiting for transfers between devices, swap(): return lax.ppermute(array, name, [(i, i ^ step) for i in range(size)])  150 us
    ppermute x67, starting transfers between devices, swap(): return lax.ppermute(array, name, [(i, i ^ step) for i in range(size)])  62.9 us
    all_to_all x9, starting transfers between devices, exchange(): return lax.all_to_all(array, name, 0, 0, tiled=True)  34.4 us
    all_to_all x9, waiting for transfers between devices, exchange(): return lax.all_to_all(array, name, 0, 0, tiled=True)  33.3 us
    unnamed x159, local copies, waits for them, and re-layouts  19.1 us
    all_to_all x1, blocking collectives, exchange(): return lax.all_to_all(array, name, 0, 0, tiled=True)  18.8 us
    all_gather x6, waiting for transfers between devices, to_planes_of(): return lax.all_gather(array, HEAD, axis=0, tiled=False)  12.8 us
  transfers between devices with their start and end apart: 86, of which 45 were waited for; matrix products, arithmetic and copies ran while one was open for 7% of the time, Pallas kernels for 27%

profile of v6, /device:TPU:0, one launch (start us, length us, event | category | flops | bytes accessed | tf_op | source)
XLA Modules:
  0.0 550.7 jit_solution(5938249397711306304)
XLA Ops:
  31.8 9.4 %all-to-all-done.1 = bf16[4,128,1024]{2,1,0:T(8,128)(2,1)S(1)} async-done(((bf16[4,128,1024]{2,1,0:T(8,128)(2,1)}), bf16[4,128,1024]{2,1,0:T(8,128)(2,1)S(1)}, u32[]{:S(2)}, u32[]{:S(2)}) %all-to-all-start.1) | async-done | bytes 1048608 | tf_op jit(solution)/shard_map/all_to_all | solution.py:53
  44.3 18.8 %all_to_all.50 = bf16[4,128,1280]{1,2,0:T(8,128)(2,1)S(1)} all-to-all(bf16[4,128,1280]{1,2,0:T(8,128)(2,1)S(1)} %constant_dynamic-update-slice_fusion), channel_id=1, replica_groups=mesh['dp'=4,'seq'=2,'head'=4] {'dp'}, dimensions={0} | all-to-all | bytes 2621440 | tf_op jit(solution)/shard_map/all_to_all | solution.py:53
  65.8 6.4 %collective-permute-done.refs_6_ = bf16[128,1024]{1,0:T(8,128)(2,1)S(1)} collective-permute-done((bf16[128,1024]{1,0:T(8,128)(2,1)S(1)}, bf16[128,1024]{1,0:T(8,128)(2,1)S(1)}, u32[]{:S(2)}, u32[]{:S(2)}) %collective-permute-start) | collective-permute-done | bytes 262176 | tf_op jit(solution)/shard_map/ppermute | solution.py:41
  94.5 10.5 %shard_map.265 = (bf16[4,512,64]{2,1,0:T(8,128)(2,1)}, f32[4,512,1]{2,1,0:T(8,128)}, bf16[128,1024]{1,0:T(8,128)(2,1)}, bf16[128,1024]{1,0:T(8,128)(2,1)}, bf16[...) custom-call(bf16[4,512,64]{2,1,0:T(8,128)(2,1)} %get-tuple-element.184.refs_0_, ...), custom_call_target="tpu_custom_call" | custom-call | flops 805306368 | bytes 4997120 | tf_op jit(solution)/shard_map/pallas_call | solution.py:120
  114.9 6.1 %collective-permute-done.6.refs_4_ = bf16[128,1024]{1,0:T(8,128)(2,1)S(1)} collective-permute-done((bf16[128,1024]{1,0:T(8,128)(2,1)}, bf16[128,1024]{1,0:T(8,128)(2,1)S(1)}, u32[]{:S(2)}, u32[]{:S(2)}) %collective-permute-start.6) | collective-permute-done | bytes 262176 | tf_op jit(solution)/shard_map/ppermute | solution.py:41
  127.8 10.6 %collective-permute-done.10.refs_5_.refs_4_ = bf16[128,1024]{1,0:T(8,128)(2,1)S(1)} collective-permute-done((bf16[128,1024]{1,0:T(8,128)(2,1)}, bf16[128,1024]{1,0:T(8,128)(2,1)S(1)}, u32[]{:S(2)}, u32[]{:S(2)}) %collective-permute-start.10) | collective-permute-done | bytes 262176 | tf_op jit(solution)/shard_map/ppermute | solution.py:41
  140.4 8.7 %shard_map.267 = (f32[4,512,256]{2,1,0:T(8,128)}, bf16[4,512,256]{2,1,0:T(8,128)(2,1)}, bf16[128,1024]{1,0:T(8,128)(2,1)}, bf16[128,1024]{1,0:T(8,128)(2,1)}, bf...) custom-call(bf16[4,512,512]{2,1,0:T(8,128)(2,1)} %bitcast.228, bf16[4,512,512]{2,1,0:T(8,128)(2,1)} %collective-permute-done.8.refs_1_, ...), custom_call_target="tpu_custom_call" | custom-call | flops 2147483648 | bytes 9441280 | tf_op jit(solution)/shard_map/pallas_call | solution.py:120
  158.7 6.4 %collective-permute-done.14.refs_4_ = bf16[128,1024]{1,0:T(8,128)(2,1)S(1)} collective-permute-done((bf16[128,1024]{1,0:T(8,128)(2,1)}, bf16[128,1024]{1,0:T(8,128)(2,1)S(1)}, u32[]{:S(2)}, u32[]{:S(2)}) %collective-permute-start.14) | collective-permute-done | bytes 262176 | tf_op jit(solution)/shard_map/ppermute | solution.py:41
  171.9 6.0 %collective-permute-done.16.refs_4_.refs_3_ = bf16[128,1024]{1,0:T(8,128)(2,1)S(1)} collective-permute-done((bf16[128,1024]{1,0:T(8,128)(2,1)}, bf16[128,1024]{1,0:T(8,128)(2,1)S(1)}, u32[]{:S(2)}, u32[]{:S(2)}) %collective-permute-start.16) | collective-permute-done | bytes 262176 | tf_op jit(solution)/shard_map/ppermute | solution.py:41
  192.1 10.5 %shard_map.270 = (bf16[4,512,64]{2,1,0:T(8,128)(2,1)}, f32[4,512,1]{2,1,0:T(8,128)}, bf16[128,1024]{1,0:T(8,128)(2,1)}, bf16[128,1024]{1,0:T(8,128)(2,1)}, bf16[...) custom-call(bf16[4,512,64]{2,1,0:T(8,128)(2,1)} %get-tuple-element.213.refs_0_, ...), custom_call_target="tpu_custom_call" | custom-call | flops 805306368 | bytes 4734976 | tf_op jit(solution)/shard_map/pallas_call | solution.py:120
  239.0 5.9 %collective-permute-done.27.refs_4_.refs_3_ = bf16[128,1024]{1,0:T(8,128)(2,1)S(1)} collective-permute-done((bf16[128,1024]{1,0:T(8,128)(2,1)}, bf16[128,1024]{1,0:T(8,128)(2,1)S(1)}, u32[]{:S(2)}, u32[]{:S(2)}) %collective-permute-start.27) | collective-permute-done | bytes 262176 | tf_op jit(solution)/shard_map/ppermute | solution.py:41
  244.9 5.8 %collective-permute-done.28.refs_5_.refs_4_ = bf16[128,1024]{1,0:T(8,128)(2,1)S(1)} collective-permute-done((bf16[128,1024]{1,0:T(8,128)(2,1)}, bf16[128,1024]{1,0:T(8,128)(2,1)S(1)}, u32[]{:S(2)}, u32[]{:S(2)}) %collective-permute-start.28) | collective-permute-done | bytes 262176 | tf_op jit(solution)/shard_map/ppermute | solution.py:41
  252.2 8.7 %shard_map.273 = (f32[4,512,256]{2,1,0:T(8,128)}, bf16[4,512,256]{2,1,0:T(8,128)(2,1)}, bf16[128,1024]{1,0:T(8,128)(2,1)}, bf16[128,1024]{1,0:T(8,128)(2,1)}, bf...) custom-call(bf16[4,512,512]{2,1,0:T(8,128)(2,1)} %bitcast.231, bf16[4,512,512]{2,1,0:T(8,128)(2,1)} %copy-done.59, ...), custom_call_target="tpu_custom_call" | custom-call | flops 2147483648 | bytes 9441280 | tf_op jit(solution)/shard_map/pallas_call | solution.py:120
  264.4 9.0 %shard_map.274 = (bf16[4,512,256]{2,1,0:T(8,128)(2,1)}, f32[4,1,256]{2,1,0:T(1,128)}, bf16[128,1024]{1,0:T(8,128)(2,1)}, bf16[128,1024]{1,0:T(8,128)(2,1)}, bf16...) custom-call(bf16[4,512,512]{2,1,0:T(8,128)(2,1)} %bitcast.232, bf16[4,512,512]{2,1,0:T(8,128)(2,1)} %copy-done.59, ...), custom_call_target="tpu_custom_call" | custom-call | flops 2147483648 | bytes 9441280 | tf_op jit(solution)/shard_map/pallas_call | solution.py:120
  277.0 6.3 %shard_map.275 = (bf16[4,512,512]{2,1,0:T(8,128)(2,1)}, bf16[4,512,512]{2,1,0:T(8,128)(2,1)}) custom-call(bf16[4,512,256]{2,1,0:T(8,128)(2,1)} %get-tuple-element.242.refs_0_, bf16[4,512,256]{2,1,0:T(8,128)(2,1)} %get-tuple-element.243.refs_1_, bf16[128,1024]{1,0:T(8,128)(2,1)} %get-tuple-element.233.refs_3_.refs_2_, bf16[128,1024]{1,0:T(8,128)(2,1)} %copy-done.66, ...), custom_call_target="tpu_custom_call" | custom-call | flops 2147483648 | bytes 8388608 | tf_op jit(solution)/shard_map/pallas_call | solution.py:120
  305.7 12.5 %shard_map.278 = (bf16[4,512,64]{2,1,0:T(8,128)(2,1)}, bf16[4,512,128]{2,1,0:T(8,128)(2,1)}, bf16[4,512,128]{2,1,0:T(8,128)(2,1)}) custom-call(bf16[4,512,64]{2,1,0:T(8,128)(2,1)} %get-tuple-element.213.refs_0_, bf16[4,512,128]{2,1,0:T(8,128)(2,1)} %get-tuple-element.214.refs_1_, bf16[4,512,128]{2,1,0:T(8,128)(2,1)} %copy-done.6, ...), custom_call_target="tpu_custom_call" | custom-call | flops 1610612736 | bytes 6045696 | tf_op jit(solution)/shard_map/pallas_call | solution.py:120
  334.0 6.1 %shard_map.280 = (bf16[4,512,256]{2,1,0:T(8,128)(2,1)}, bf16[4,512,256]{2,1,0:T(8,128)(2,1)}) custom-call(bf16[4,512,192]{2,1,0:T(8,128)(2,1)} %get-tuple-element.268.refs_0_, bf16[4,512,64]{2,1,0:T(8,128)(2,1)} %get-tuple-element.215.refs_5_.refs_1_, bf16[128,1024]{1,0:T(8,128)(2,1)} %get-tuple-element.212.refs_3_.refs_2_, bf16[128,1024]{1,0:T(8,128)(2,1)} %copy-done.18, ...), custom_call_target="tpu_custom_call" | custom-call | flops 1073741824 | bytes 5242880 | tf_op jit(solution)/shard_map/pallas_call | solution.py:120
  340.2 10.9 %collective-permute-done.41.refs_4_ = bf16[128,1024]{1,0:T(8,128)(2,1)S(1)} collective-permute-done((bf16[128,1024]{1,0:T(8,128)(2,1)S(1)}, bf16[128,1024]{1,0:T(8,128)(2,1)S(1)}, u32[]{:S(2)}, u32[]{:S(2)}) %collective-permute-start.41) | collective-permute-done | bytes 262176 | tf_op jit(solution)/shard_map/ppermute | solution.py:41
  374.8 9.0 %shard_map.282 = (bf16[4,512,256]{2,1,0:T(8,128)(2,1)}, f32[4,1,256]{2,1,0:T(1,128)}, bf16[128,1024]{1,0:T(8,128)(2,1)}, bf16[128,1024]{1,0:T(8,128)(2,1)}, bf16...) custom-call(bf16[4,512,512]{2,1,0:T(8,128)(2,1)} %bitcast.229, bf16[4,512,512]{2,1,0:T(8,128)(2,1)} %collective-permute-done.8.refs_1_, ...), custom_call_target="tpu_custom_call" | custom-call | flops 2147483648 | bytes 9441280 | tf_op jit(solution)/shard_map/pallas_call | solution.py:120
  387.3 6.3 %shard_map.283 = (bf16[4,512,512]{2,1,0:T(8,128)(2,1)}, bf16[4,512,512]{2,1,0:T(8,128)(2,1)}) custom-call(bf16[4,512,256]{2,1,0:T(8,128)(2,1)} %get-tuple-element.292.refs_0_, bf16[4,512,256]{2,1,0:T(8,128)(2,1)} %get-tuple-element.293.refs_1_, bf16[128,1024]{1,0:T(8,128)(2,1)} %get-tuple-element.204.refs_3_.refs_2_, bf16[128,1024]{1,0:T(8,128)(2,1)} %copy-done.62, ...), custom_call_target="tpu_custom_call" | custom-call | flops 2147483648 | bytes 8388608 | tf_op jit(solution)/shard_map/pallas_call | solution.py:120
  420.5 12.6 %shard_map.285 = (bf16[4,512,64]{2,1,0:T(8,128)(2,1)}, bf16[4,512,128]{2,1,0:T(8,128)(2,1)}, bf16[4,512,128]{2,1,0:T(8,128)(2,1)}) custom-call(bf16[4,512,64]{2,1,0:T(8,128)(2,1)} %get-tuple-element.184.refs_0_, bf16[4,512,128]{2,1,0:T(8,128)(2,1)} %get-tuple-element.185.refs_1_, bf16[4,512,128]{2,1,0:T(8,128)(2,1)} %copy-done.5, ...), custom_call_target="tpu_custom_call" | custom-call | flops 1610612736 | bytes 6307840 | tf_op jit(solution)/shard_map/pallas_call | solution.py:120
  447.1 6.2 %shard_map.289 = (bf16[4,512,256]{2,1,0:T(8,128)(2,1)}, bf16[4,512,256]{2,1,0:T(8,128)(2,1)}) custom-call(bf16[4,512,192]{2,1,0:T(8,128)(2,1)} %get-tuple-element.322.refs_0_, bf16[4,512,64]{2,1,0:T(8,128)(2,1)} %get-tuple-element.301.refs_5_.refs_1_, bf16[128,1024]{1,0:T(8,128)(2,1)} %get-tuple-element.323.refs_2_, ...), custom_call_target="tpu_custom_call" | custom-call | flops 1073741824 | bytes 5242880 | tf_op jit(solution)/shard_map/pallas_call | solution.py:120
  487.8 12.4 %all-gather.23.cloned.1.call-done = bf16[512,1024]{1,0:T(8,128)(2,1)} async-done(((bf16[128,1024]{1,0:T(8,128)(2,1)}), bf16[512,1024]{1,0:T(8,128)(2,1)}) %all-gather.23.cloned.1.call-update) | async-done | bytes 1048592 | tf_op jit(solution)/shard_map/all_gather | solution.py:608
  504.5 13.0 %all-to-all-done.6 = bf16[4,128,1024]{2,1,0:T(8,128)(2,1)S(1)} async-done(((bf16[4,128,1024]{2,1,0:T(8,128)(2,1)}), bf16[4,128,1024]{2,1,0:T(8,128)(2,1)S(1)}, u32[]{:S(2)}, u32[]{:S(2)}) %all-to-all-start.6) | async-done | bytes 1048608 | tf_op jit(solution)/shard_map/all_to_all | solution.py:53
  (466 shorter events, 316.8 us)
Async XLA Ops:
  28.6 43.6 %all-gather.13.cloned.1.call-start = ((), (), s32[]{:S(2)}) async-start(), calls=%async_computation.18 | async-start | bytes 1474560 | tf_op jit(solution)/shard_map/all_gather | solution.py:608
  30.5 90.6 %all-gather.17.cloned.1.call-start = ((), (), s32[]{:S(2)}) async-start(), calls=%async_computation.20 | async-start | bytes 2621440 | tf_op jit(solution)/shard_map/all_gather | solution.py:608
  87.2 18.2 %all-to-all-start.2 = ((bf16[4,128,1024]{2,1,0:T(8,128)(2,1)}), bf16[4,128,1024]{2,1,0:T(8,128)(2,1)}, u32[]{:S(2)}, u32[]{:S(2)}) async-start(bf16[4,128,1024]{2,1,0:T(8,128)(2,1)} %bitcast.186), calls=%async_computation.2 | async-start | bytes 2097152 | tf_op jit(solution)/shard_map/all_to_all | solution.py:53
  91.6 57.7 %all-gather.15.cloned.1.call-start = ((), (), s32[]{:S(2)}) async-start(), calls=%async_computation.19 | async-start | bytes 1310720 | tf_op jit(solution)/shard_map/all_gather | solution.py:608
  121.0 81.6 %all-gather.19.cloned.1.call-start = ((), (), s32[]{:S(2)}) async-start(), calls=%async_computation.21 | async-start | bytes 2621440 | tf_op jit(solution)/shard_map/all_gather | solution.py:608
  121.1 18.6 %collective-permute-start.8 = (bf16[4,512,512]{2,1,0:T(8,128)(2,1)}, bf16[4,512,512]{2,1,0:T(8,128)(2,1)}, u32[]{:S(2)}, u32[]{:S(2)}) collective-permute-start(bf16[4,512,512]{2,1,0:T(8,128)(2,1)} %bitcast.227), channel_id=1, source_target_pairs={{0,4},{4,0},{1,5},{5,1},{2,6},{6,2},{3,7},{7,3},{8,12},{12,8},{9,1... | collective-permute-start | bytes 6291464 | tf_op jit(solution)/shard_map/ppermute | solution.py:41
  121.6 205.1 %all-gather.21.cloned.1.call-start = ((), (), s32[]{:S(2)}) async-start(), calls=%async_computation.22 | async-start | bytes 1310720 | tf_op jit(solution)/shard_map/all_gather | solution.py:608
  149.4 33.7 %collective-permute-start.12 = (bf16[4,512,256]{2,1,0:T(8,128)(2,1)}, bf16[4,512,256]{2,1,0:T(8,128)(2,1)S(1)}, u32[]{:S(2)}, u32[]{:S(2)}) collective-permute-start(bf16[4,512,256]{2,1,0:T(8,128)(2,1)} %bitcast.177), channel_id=1, source_target_pairs={{0,4},{4,0},{1,5},{5,1},{2,6},{6,2},{3,7},{7,3},{8,12},{12,8},{9,1... | collective-permute-start | bytes 3145736 | tf_op jit(solution)/shard_map/ppermute | solution.py:41
  202.7 48.1 %collective-permute-start.26 = (bf16[4,512,512]{2,1,0:T(8,128)(2,1)}, bf16[4,512,512]{2,1,0:T(8,128)(2,1)S(1)}, u32[]{:S(2)}, u32[]{:S(2)}) collective-permute-start(bf16[4,512,512]{2,1,0:T(8,128)(2,1)} %bitcast.230), channel_id=1, source_target_pairs={{0,4},{4,0},{1,5},{5,1},{2,6},{6,2},{3,7},{7,3},{8,12},{12,8},{9,1... | collective-permute-start | bytes 6291464 | tf_op jit(solution)/shard_map/ppermute | solution.py:41
  261.5 21.8 %collective-permute-start.34 = (bf16[128,1024]{1,0:T(8,128)(2,1)}, bf16[128,1024]{1,0:T(8,128)(2,1)S(1)}, u32[]{:S(2)}, u32[]{:S(2)}) collective-permute-start(bf16[128,1024]{1,0:T(8,128)(2,1)} %get-tuple-element.248), channel_id=1, source_target_pairs={{0,16},{8,24},{16,0},{24,8},{1,17},{9,25},{17,1},{25,9},{2,18},{10... | collective-permute-start | bytes 786440 | tf_op jit(solution)/shard_map/ppermute | solution.py:41
  263.0 20.3 %collective-permute-start.35 = (bf16[128,1024]{1,0:T(8,128)(2,1)}, bf16[128,1024]{1,0:T(8,128)(2,1)S(1)}, u32[]{:S(2)}, u32[]{:S(2)}) collective-permute-start(bf16[128,1024]{1,0:T(8,128)(2,1)} %get-tuple-element.249), channel_id=1, source_target_pairs={{0,24},{8,16},{16,8},{24,0},{1,25},{9,17},{17,9},{25,1},{2,26},{10... | collective-permute-start | bytes 786440 | tf_op jit(solution)/shard_map/ppermute | solution.py:41
  286.5 130.0 %reduce-scatter.5.cloned.1.call-start = ((), (), s32[]{:S(2)}) async-start(), calls=%async_computation.14 | async-start | bytes 2621440 | tf_op jit(solution)/shard_map/reduce_scatter | solution.py:728
  326.7 30.2 %all-to-all-start.4 = ((bf16[4,128,1024]{2,1,0:T(8,128)(2,1)}), bf16[4,128,1024]{2,1,0:T(8,128)(2,1)S(1)}, u32[]{:S(2)}, u32[]{:S(2)}) async-start(bf16[4,128,1024]{2,1,0:T(8,128)(2,1)} %bitcast.188), calls=%async_computation.4 | async-start | bytes 2097152 | tf_op jit(solution)/shard_map/all_to_all | solution.py:53
  330.4 137.5 %reduce-scatter.11.cloned.1.call-start = ((), (), s32[]{:S(2)}) async-start(), calls=%async_computation.17 | async-start | bytes 1310720 | tf_op jit(solution)/shard_map/reduce_scatter | solution.py:728
  330.5 20.6 %collective-permute-start.41 = (bf16[128,1024]{1,0:T(8,128)(2,1)S(1)}, bf16[128,1024]{1,0:T(8,128)(2,1)S(1)}, u32[]{:S(2)}, u32[]{:S(2)}) collective-permute-start(bf16[128,1024]{1,0:T(8,128)(2,1)S(1)} %copy-done.72), channel_id=1, source_target_pairs={{0,8},{8,0},{16,24},{24,16},{1,9},{9,1},{17,25},{25,17},{2,10},{10... | collective-permute-start | bytes 786440 | tf_op jit(solution)/shard_map/ppermute | solution.py:41
  332.4 18.6 %collective-permute-start.42 = (bf16[128,1024]{1,0:T(8,128)(2,1)S(1)}, bf16[128,1024]{1,0:T(8,128)(2,1)S(1)}, u32[]{:S(2)}, u32[]{:S(2)}) collective-permute-start(bf16[128,1024]{1,0:T(8,128)(2,1)S(1)} %copy-done.71), channel_id=1, source_target_pairs={{0,16},{8,24},{16,0},{24,8},{1,17},{9,25},{17,1},{25,9},{2,18},{10... | collective-permute-start | bytes 786440 | tf_op jit(solution)/shard_map/ppermute | solution.py:41
  333.9 23.0 %collective-permute-start.43 = (bf16[128,1024]{1,0:T(8,128)(2,1)S(1)}, bf16[128,1024]{1,0:T(8,128)(2,1)}, u32[]{:S(2)}, u32[]{:S(2)}) collective-permute-start(bf16[128,1024]{1,0:T(8,128)(2,1)S(1)} %copy-done.70), channel_id=1, source_target_pairs={{0,24},{8,16},{16,8},{24,0},{1,25},{9,17},{17,9},{25,1},{2,26},{10... | collective-permute-start | bytes 786440 | tf_op jit(solution)/shard_map/ppermute | solution.py:41
  398.3 81.9 %reduce-scatter.7.cloned.1.call-start = ((), (), s32[]{:S(2)}) async-start(), calls=%async_computation.15 | async-start | bytes 2621440 | tf_op jit(solution)/shard_map/reduce_scatter | solution.py:728
  420.1 80.1 %all-gather.23.cloned.1.call-start = ((), (), s32[]{:S(2)}) async-start(), calls=%async_computation.23 | async-start | bytes 1310720 | tf_op jit(solution)/shard_map/all_gather | solution.py:608
  453.3 24.4 %collective-permute-start.59 = (bf16[4,512,256]{2,1,0:T(8,128)(2,1)}, bf16[4,512,256]{2,1,0:T(8,128)(2,1)}, u32[]{:S(2)}, u32[]{:S(2)}) collective-permute-start(bf16[4,512,256]{2,1,0:T(8,128)(2,1)} %get-tuple-element.328), channel_id=1, source_target_pairs={{0,4},{4,0},{1,5},{5,1},{2,6},{6,2},{3,7},{7,3},{8,12},{12,8},{9,1... | collective-permute-start | bytes 3145736 | tf_op jit(solution)/shard_map/ppermute | solution.py:41
  469.7 18.1 %all-to-all-start.8 = ((bf16[4,128,256]{1,2,0:T(8,128)(2,1)}), bf16[4,128,256]{1,2,0:T(8,128)(2,1)S(1)}, u32[]{:S(2)}, u32[]{:S(2)}) async-start(bf16[4,128,256]{1,2,0:T(8,128)(2,1)} %copy.155), calls=%async_computation.12 | async-start | bytes 524288 | tf_op jit(solution)/shard_map/all_to_all | solution.py:53
  473.1 56.6 %reduce-scatter.9.cloned.1.call-start = ((), (), s32[]{:S(2)}) async-start(), calls=%async_computation.16 | async-start | bytes 1310720 | tf_op jit(solution)/shard_map/reduce_scatter | solution.py:728
  485.6 18.3 %collective-permute-start.66 = (f32[1632]{0:T(1024)S(1)}, f32[1632]{0:T(1024)S(1)}, u32[]{:S(2)}, u32[]{:S(2)}) collective-permute-start(f32[1632]{0:T(1024)S(1)} %get-tuple-element.422), channel_id=1, source_target_pairs={{0,24},{8,16},{16,8},{24,0},{1,25},{9,17},{17,9},{25,1},{2,26},{10... | collective-permute-start | bytes 19592 | tf_op jit(solution)/shard_map/ppermute | solution.py:41
  500.2 17.3 %all-to-all-start.6 = ((bf16[4,128,1024]{2,1,0:T(8,128)(2,1)}), bf16[4,128,1024]{2,1,0:T(8,128)(2,1)S(1)}, u32[]{:S(2)}, u32[]{:S(2)}) async-start(bf16[4,128,1024]{2,1,0:T(8,128)(2,1)} %bitcast.187), calls=%async_computation.7 | async-start | bytes 2097152 | tf_op jit(solution)/shard_map/all_to_all | solution.py:53
  (137 other events, 1154.4 us)
Sparse Core Ops, SparseCore 0:
  31.6 32.1 all-gather.12
  65.9 45.0 all-gather.16
  121.1 28.1 all-gather.14
  150.8 45.3 all-gather.18
  286.7 27.1 all-gather.20
  316.0 43.3 reduce-scatter.4
  398.4 26.8 reduce-scatter.10
  428.2 42.4 reduce-scatter.6
  472.9 27.2 all-gather.22
  503.0 26.6 reduce-scatter.8

commit v7 on v6

--- a/solution.py
+++ b/solution.py
@@ -403,11 +403,20 @@
 def weight_back(one_blocks, one, two_blocks, two, n):
     rows, width = one_blocks[0].shape
     length = rows * len(one_blocks)
-    heads, _, first = one.shape
-    second = two.shape[2]
+    heads, _, first = one[0].shape
+    second = two[0].shape[2]
     part = width // n
     half = len(one_blocks)
 
+    def summed(wide, cols, items):
+        total, begin = None, 0
+        for item in items:
+            end = begin + item.shape[0]
+            term = dot(wide[begin:end, cols], item[...], 0, 0)
+            total = term if total is None else total + term
+            begin = end
+        return total.astype(bf16)
+
     def body(z, each_in, whole_in, each_out, whole_out, scratch):
         @pl.when(z == 0)
         def _():
@@ -416,13 +425,13 @@
 
         for s in range(n):
             cols = slice(s * part, (s + 1) * part)
-            each_out[s][:, :first] = dot(scratch[0][:, cols], each_in[0][...], 0, 0).astype(bf16)
-            each_out[s][:, first:] = dot(scratch[1][:, cols], each_in[1][...], 0, 0).astype(bf16)
+            each_out[s][:, :first] = summed(scratch[0], cols, each_in[: len(one)])
+            each_out[s][:, first:] = summed(scratch[1], cols, each_in[len(one) :])
 
     return run(
         body,
         heads,
-        [one, two],
+        list(one) + list(two),
         list(one_blocks) + list(two_blocks),
         [shape((heads, part, first + second), bf16)] * n,
         [],
@@ -601,6 +610,9 @@
     def send_rows(array):
         return gather(array, DP, n_t)
 
+    def in_halves(blocks):
+        return [blocks]
+
     def send_sums(blocks):
         return deal(blocks, DP, n_t)
 
@@ -645,11 +657,10 @@
     messages = [to_planes_of(first_shard)]
     hidden, low = first_norm([own_rows(spread_rows(tokens[0]))], turn, counts)
     normed_one = send_rows(low)
-    rest = jnp.concatenate((packed_feed(0), packed_mixed(1), packed_feed(1)), axis=2)
-    rest = to_planes(after(rest, low))
-    messages.append(to_planes_of(rest[:, : 2 * units]))
-    later = [rest[:, 2 * units : 2 * units + columns], rest[:, 2 * units + columns :]]
-    mixed = join(after(messages[0], normed_one[-1]))
+    normed_one, pack = meet(normed_one, packed_feed(0))
+    messages.append(to_planes_of(to_planes(pack)))
+    messages[0], normed_one = meet(messages[0], normed_one)
+    mixed = join(messages[0])
     vectors, biases_qkv, biases_up = unpack(mixed, turn, counts, width, LAYERS, spare)
     tall_sizes = (HD, HD, units)
 
@@ -670,31 +681,43 @@
     for layer in range(LAYERS):
         if layer > 0:
             normed_one = send_rows(low)
-            mixed = join(after(messages[2 * layer], out[0]))
+            normed_one, messages[2 * layer] = meet(normed_one, messages[2 * layer])
+            mixed = join(messages[2 * layer])
         affine = (vectors, vector(0, 0), vector(1, 0)) if layer == 0 else ()
         queries, both, normed_one = project(normed_one, mixed, biases_qkv[layer], *affine)
         both = gather(both, SEQ, n_s)
         if layer == 0:
-            cot_rows = spread_rows(after(cot, both[0]))
+            later = jnp.concatenate((packed_mixed(1), packed_feed(1)), axis=2)
+            both, later = meet(both, later)
+            later = to_planes(later)
         else:
-            cot_rows = send_rows(after(cot_rows, both[0]))
+            both, cot_rows = meet(both, cot_rows)
+            cot_rows = send_rows(cot_rows)
         context, logs, out = attend(queries, both, mixed, slopes, key_pos, query_pos, n_t, width)
         if layer == 0:
+            out, later = meet(out, later)
+        else:
             out, cot_rows = meet(out, cot_rows)
         got = send_sums(out)
-        feed = join(after(messages[2 * layer + 1], out[0]))
+        got, messages[2 * layer + 1] = meet(got, messages[2 * layer + 1])
+        feed = join(messages[2 * layer + 1])
         if layer == 0:
             got, later = meet(got, later)
-            messages.extend(to_planes_of(shard) for shard in later)
-            cot_rows = turned_sum([own_rows(cot_rows)], turn, counts, True)
-        else:
-            got, cot_rows = meet(got, cot_rows)
+            messages.append(to_planes_of(later[:, :columns]))
+            messages.append(to_planes_of(later[:, columns:]))
         hidden_mid, low = norm_forward(
             hidden, got, vectors, vector(2, layer), vector(3, layer), vector(4, layer)
         )
         normed_two = send_rows(low)
-        pre_up, activation, out = feed_forward(normed_two, feed, biases_up[layer])
+        if layer == 0:
+            normed_two, cot_rows = meet(normed_two, cot)
+            cot_rows = spread_rows(cot_rows)
+        halves = [feed_forward(part, feed, biases_up[layer]) for part in in_halves(normed_two)]
+        pre_up, activation, out = (list(item) for item in zip(*halves))
+        out = [block for part in out for block in part]
         got = send_sums(out)
+        if layer == 0:
+            got, cot_rows = meet(got, turned_sum([own_rows(cot_rows)], turn, counts, True))
         records.append(
             (
                 (mixed, feed),
@@ -741,44 +764,48 @@
             (queries, both, logs, context, pre_up, activation),
         ) = records[layer]
         last = layer == LAYERS - 1
-        pre_grad, up_bias_grad, out = feed_back(grad_low, feed, pre_up)
-        got = send_sums(out)
+        halves = [
+            feed_back(part, feed, kept) for part, kept in zip(in_halves(grad_low), pre_up)
+        ]
+        pre_grad, up_bias_grad, out = (list(item) for item in zip(*halves))
+        got = send_sums([block for part in out for block in part])
+        up_bias_grad = functools.reduce(jnp.add, up_bias_grad)
         feed_grad = weight_back(normed_two, pre_grad, grad_low, activation, n_s)
         if last:
             got, feed_grad, output_low = meet(got, feed_grad, output_low)
             output_planes = to_planes_of(output_low)
         else:
-            got, feed_grad = meet(got, feed_grad)
+            got, feed_grad, mixed_sums[1] = meet(got, feed_grad, mixed_sums[1])
         mid_grad, low, sums_two = norm_back(
             hidden_mid, gradient, got, vectors, vector(3, layer)
         )
         mid_low = send_rows(low)
-        mine = core_sum(feed_grad)
         if last:
-            mid_low, mine = meet(mid_low, mine)
+            mid_low, mine = meet(mid_low, core_sum(feed_grad))
         else:
-            mid_low, mine = meet(mid_low, mine)
+            mid_low, mine, output_planes = meet(mid_low, core_sum(feed_grad), output_planes)
         feed_sums[layer] = head_sum(mine)
         query_grad, both_grads = attend_back(
             mid_low, queries, both, mixed, context, logs, slopes, key_pos, query_pos
         )
         if not last:
-            feed_share = send_shares(after(feed_sums[layer + 1], mid_low[-1]))
-            both_grads, feed_shares[layer + 1] = meet(both_grads, feed_share)
+            both_grads, output = meet(both_grads, send_output(output_planes))
         got = deal(both_grads, SEQ, n_s)
         joined, qkv_sums, out = project_back(query_grad, got, mixed, n_t, width)
         got = send_sums(out)
-        mixed_grad = weight_back(normed_one, joined, mid_low, context, n_s)
+        mixed_grad = weight_back(normed_one, [joined], mid_low, [context], n_s)
         if last:
-            planes = after(output_planes, joined)
-            got, mixed_grad, output = meet(got, mixed_grad, send_output(planes))
+            got, mixed_grad, output_planes = meet(got, mixed_grad, output_planes)
         else:
-            mixed_sums[layer] = head_sum(after(core_sum(mixed_grad), feed_sums[layer]))
+            got, feed_sums[0] = meet(got, feed_sums[0])
+            mixed_sums[layer] = head_sum(core_sum(mixed_grad))
         gradient, low, sums_one = norm_back(
             hidden, mid_grad, got, vectors, vector(0, layer)
         )
         if layer > 0:
-            grad_low, mine = meet(send_rows(low), core_sum(mixed_grad))
+            grad_low, mine, feed_sums[layer] = meet(
+                send_rows(low), core_sum(mixed_grad), feed_sums[layer]
+            )
             mixed_sums[layer] = head_sum(mine)
         wide_grads[layer] = jnp.stack(
             (
@@ -796,12 +823,16 @@
         )
 
     low_outer = turned_sum([low], turn, counts, False)
-    tokens_planes = to_planes_of(after(low_outer, mixed_sums[0]))
-    mixed_shares[1] = send_shares(after(mixed_sums[1], low))
-    feed_shares[0] = send_shares(after(feed_sums[0], low))
+    low_outer, mixed_sums[0] = meet(low_outer, mixed_sums[0])
+    tokens_planes = to_planes_of(low_outer)
+    low_outer, mixed_sums[1], feed_sums[0], feed_sums[1] = meet(
+        low_outer, mixed_sums[1], feed_sums[0], feed_sums[1]
+    )
+    feed_shares[1] = send_shares(feed_sums[1])
+    mixed_shares[1] = send_shares(mixed_sums[1])
+    feed_shares[0] = send_shares(feed_sums[0])
     mixed_shares[0] = send_shares(mixed_sums[0])
     tokens_grad = send_output(tokens_planes).astype(f32)
-    feed_shares = [after(share, low) for share in feed_shares]
 
     def fold(arrays, name, size):
         total = arrays[0]

time: 559 us -> 539 us (0.964)
  waiting for transfers between devices: 198 us -> 184 us
  local copies, waits for them, and re-layouts: 42.6 us -> 34.4 us
    ppermute x67, waiting for transfers between devices: 150 us -> 134 us  [swap(): return lax.ppermute(array, name, [(i, i ^ step) for i in range(size)])]
    reduce_scatter x4, waiting for transfers between devices: 1 us -> 16.2 us  [head_sum(): return lax.psum_scatter(mine, HEAD, scatter_dimension=0, tiled=False)]
    all_gather x6, waiting for transfers between devices: 12.8 us -> 0.07 us  [to_planes_of(): return lax.all_gather(array, HEAD, axis=0, tiled=False)]
    unnamed x159 -> x156, local copies, waits for them, and re-layouts: 19.1 us -> 15.8 us
    all_to_all x1 -> x2, blocking collectives: 18.8 us -> 21.6 us  [exchange(): return lax.all_to_all(array, name, 0, 0, tiled=True)]
  transfers between devices with their start and end apart: 86 -> 86, of which waited for: 45 -> 46; matrix products, arithmetic and copies ran while one was open for 7% -> 6% of each run, Pallas kernels for 27% -> 28%
where the time goes in v7:
time: 539 us; the launch traced here: 531 us
  waiting for transfers between devices  184 us (34%)
  Pallas kernels  157 us (29%)
  starting transfers between devices  98 us (18%)
  local copies, waits for them, and re-layouts  34.4 us (6%)
  blocking collectives  21.6 us (4%)
  other arithmetic  20.8 us (4%)
  between operations  15.9 us (3%)
    pallas_call x27, Pallas kernels, run(): pl.pallas_call(kernel, grid=(steps,), in_specs=[each(item) for item in ea...  155 us
    ppermute x67, waiting for transfers between devices, swap(): return lax.ppermute(array, name, [(i, i ^ step) for i in range(size)])  134 us
    ppermute x67, starting transfers between devices, swap(): return lax.ppermute(array, name, [(i, i ^ step) for i in range(size)])  65.2 us
    all_to_all x9, waiting for transfers between devices, exchange(): return lax.all_to_all(array, name, 0, 0, tiled=True)  32.9 us
    all_to_all x9, starting transfers between devices, exchange(): return lax.all_to_all(array, name, 0, 0, tiled=True)  31.7 us
    all_to_all x2, blocking collectives, exchange(): return lax.all_to_all(array, name, 0, 0, tiled=True)  21.6 us
    reduce_scatter x4, waiting for transfers between devices, head_sum(): return lax.psum_scatter(mine, HEAD, scatter_dimension=0, tiled=False)  16.2 us
    unnamed x156, local copies, waits for them, and re-layouts  15.8 us
  transfers between devices with their start and end apart: 86, of which 46 were waited for; matrix products, arithmetic and copies ran while one was open for 6% of the time, Pallas kernels for 28%

profile of v7, /device:TPU:0, one launch (start us, length us, event | category | flops | bytes accessed | tf_op | source)
XLA Modules:
  0.0 531.0 jit_solution(9699082549593346075)
XLA Ops:
  13.6 11.4 %all_to_all.55 = bf16[4,144,256]{2,1,0:T(8,128)(2,1)S(1)} all-to-all(bf16[4,144,256]{2,1,0:T(8,128)(2,1)S(1)} %copy.149), channel_id=1, replica_groups=mesh['dp'=4,'seq'=2,'head'=4] {'dp'}, dimensions={0} | all-to-all | bytes 589824 | tf_op jit(solution)/shard_map/all_to_all | solution.py:53
  29.8 12.3 %all-to-all-done.1 = bf16[4,128,1024]{2,1,0:T(8,128)(2,1)S(1)} async-done(((bf16[4,128,1024]{2,1,0:T(8,128)(2,1)}), bf16[4,128,1024]{2,1,0:T(8,128)(2,1)S(1)}, u32[]{:S(2)}, u32[]{:S(2)}) %all-to-all-start.1) | async-done | bytes 1048608 | tf_op jit(solution)/shard_map/all_to_all | solution.py:53
  58.4 10.2 %all_to_all.56 = bf16[4,128,512]{2,1,0:T(8,128)(2,1)} all-to-all(bf16[4,128,512]{2,1,0:T(8,128)(2,1)S(1)} %pad_maximum_fusion.1), channel_id=1, replica_groups=mesh['dp'=4,'seq'=2,'head'=4] {'dp'}, dimensions={0} | all-to-all | bytes 1048576 | tf_op jit(solution)/shard_map/all_to_all | solution.py:53
  88.2 10.5 %shard_map.265 = (bf16[4,512,64]{2,1,0:T(8,128)(2,1)}, f32[4,512,1]{2,1,0:T(8,128)}, bf16[128,1024]{1,0:T(8,128)(2,1)}, bf16[128,1024]{1,0:T(8,128)(2,1)}, bf16[...) custom-call(bf16[4,512,64]{2,1,0:T(8,128)(2,1)} %get-tuple-element.231.refs_0_, ...), custom_call_target="tpu_custom_call" | custom-call | flops 805306368 | bytes 4997120 | tf_op jit(solution)/shard_map/pallas_call | solution.py:120
  102.6 5.9 %collective-permute-done.5.refs_3_ = bf16[128,1024]{1,0:T(8,128)(2,1)S(1)} collective-permute-done((bf16[128,1024]{1,0:T(8,128)(2,1)}, bf16[128,1024]{1,0:T(8,128)(2,1)S(1)}, u32[]{:S(2)}, u32[]{:S(2)}) %collective-permute-start.5) | collective-permute-done | bytes 262176 | tf_op jit(solution)/shard_map/ppermute | solution.py:41
  108.4 6.2 %collective-permute-done.6.refs_4_ = bf16[128,1024]{1,0:T(8,128)(2,1)S(1)} collective-permute-done((bf16[128,1024]{1,0:T(8,128)(2,1)}, bf16[128,1024]{1,0:T(8,128)(2,1)S(1)}, u32[]{:S(2)}, u32[]{:S(2)}) %collective-permute-start.6) | collective-permute-done | bytes 262176 | tf_op jit(solution)/shard_map/ppermute | solution.py:41
  121.5 11.0 %collective-permute-done.10.refs_5_.refs_4_ = bf16[128,1024]{1,0:T(8,128)(2,1)S(1)} collective-permute-done((bf16[128,1024]{1,0:T(8,128)(2,1)}, bf16[128,1024]{1,0:T(8,128)(2,1)S(1)}, u32[]{:S(2)}, u32[]{:S(2)}) %collective-permute-start.10) | collective-permute-done | bytes 262176 | tf_op jit(solution)/shard_map/ppermute | solution.py:41
  138.4 8.7 %shard_map.267 = (f32[4,512,256]{2,1,0:T(8,128)}, bf16[4,512,256]{2,1,0:T(8,128)(2,1)}, bf16[128,1024]{1,0:T(8,128)(2,1)}, bf16[128,1024]{1,0:T(8,128)(2,1)}, bf...) custom-call(bf16[4,512,512]{2,1,0:T(8,128)(2,1)} %all-gather.12.cloned.1.call-done.refs_0_, ...), custom_call_target="tpu_custom_call" | custom-call | flops 2147483648 | bytes 9441280 | tf_op jit(solution)/shard_map/pallas_call | solution.py:120
  169.6 6.0 %collective-permute-done.15.refs_4_.refs_3_ = bf16[128,1024]{1,0:T(8,128)(2,1)S(1)} collective-permute-done((bf16[128,1024]{1,0:T(8,128)(2,1)}, bf16[128,1024]{1,0:T(8,128)(2,1)S(1)}, u32[]{:S(2)}, u32[]{:S(2)}) %collective-permute-start.15) | collective-permute-done | bytes 262176 | tf_op jit(solution)/shard_map/ppermute | solution.py:41
  193.7 10.5 %shard_map.271 = (bf16[4,512,64]{2,1,0:T(8,128)(2,1)}, f32[4,512,1]{2,1,0:T(8,128)}, bf16[128,1024]{1,0:T(8,128)(2,1)}, bf16[128,1024]{1,0:T(8,128)(2,1)}, bf16[...) custom-call(bf16[4,512,64]{2,1,0:T(8,128)(2,1)} %get-tuple-element.283.refs_0_, ...), custom_call_target="tpu_custom_call" | custom-call | flops 805306368 | bytes 4734976 | tf_op jit(solution)/shard_map/pallas_call | solution.py:120
  209.9 6.0 %collective-permute-done.23.refs_3_ = bf16[128,1024]{1,0:T(8,128)(2,1)S(1)} collective-permute-done((bf16[128,1024]{1,0:T(8,128)(2,1)}, bf16[128,1024]{1,0:T(8,128)(2,1)S(1)}, u32[]{:S(2)}, u32[]{:S(2)}) %collective-permute-start.23) | collective-permute-done | bytes 262176 | tf_op jit(solution)/shard_map/ppermute | solution.py:41
  226.7 5.9 %collective-permute-done.27.refs_4_.refs_3_ = bf16[128,1024]{1,0:T(8,128)(2,1)S(1)} collective-permute-done((bf16[128,1024]{1,0:T(8,128)(2,1)}, bf16[128,1024]{1,0:T(8,128)(2,1)S(1)}, u32[]{:S(2)}, u32[]{:S(2)}) %collective-permute-start.27) | collective-permute-done | bytes 262176 | tf_op jit(solution)/shard_map/ppermute | solution.py:41
  239.1 8.7 %shard_map.273 = (f32[4,512,256]{2,1,0:T(8,128)}, bf16[4,512,256]{2,1,0:T(8,128)(2,1)}, bf16[128,1024]{1,0:T(8,128)(2,1)}, bf16[128,1024]{1,0:T(8,128)(2,1)}, bf...) custom-call(bf16[4,512,512]{2,1,0:T(8,128)(2,1)} %bitcast.227, bf16[4,512,512]{2,1,0:T(8,128)(2,1)} %copy-done.59, ...), custom_call_target="tpu_custom_call" | custom-call | flops 2147483648 | bytes 9441280 | tf_op jit(solution)/shard_map/pallas_call | solution.py:120
  251.3 9.0 %shard_map.274 = (bf16[4,512,256]{2,1,0:T(8,128)(2,1)}, f32[4,1,256]{2,1,0:T(1,128)}, bf16[128,1024]{1,0:T(8,128)(2,1)}, bf16[128,1024]{1,0:T(8,128)(2,1)}, bf16...) custom-call(bf16[4,512,512]{2,1,0:T(8,128)(2,1)} %bitcast.228, bf16[4,512,512]{2,1,0:T(8,128)(2,1)} %copy-done.59, ...), custom_call_target="tpu_custom_call" | custom-call | flops 2147483648 | bytes 9441280 | tf_op jit(solution)/shard_map/pallas_call | solution.py:120
  263.9 6.3 %shard_map.275 = (bf16[4,512,512]{2,1,0:T(8,128)(2,1)}, bf16[4,512,512]{2,1,0:T(8,128)(2,1)}) custom-call(bf16[4,512,256]{2,1,0:T(8,128)(2,1)} %get-tuple-element.314.refs_0_, bf16[4,512,256]{2,1,0:T(8,128)(2,1)} %get-tuple-element.315.refs_1_, bf16[128,1024]{1,0:T(8,128)(2,1)} %get-tuple-element.305.refs_3_.refs_2_, bf16[128,1024]{1,0:T(8,128)(2,1)} %copy-done.68, ...), custom_call_target="tpu_custom_call" | custom-call | flops 2147483648 | bytes 8388608 | tf_op jit(solution)/shard_map/pallas_call | solution.py:120
  292.8 12.5 %shard_map.278 = (bf16[4,512,64]{2,1,0:T(8,128)(2,1)}, bf16[4,512,128]{2,1,0:T(8,128)(2,1)}, bf16[4,512,128]{2,1,0:T(8,128)(2,1)}) custom-call(bf16[4,512,64]{2,1,0:T(8,128)(2,1)} %get-tuple-element.283.refs_0_, bf16[4,512,128]{2,1,0:T(8,128)(2,1)} %get-tuple-element.286.refs_1_, bf16[4,512,128]{2,1,0:T(8,128)(2,1)} %copy-done.8, ...), custom_call_target="tpu_custom_call" | custom-call | flops 1610612736 | bytes 6045696 | tf_op jit(solution)/shard_map/pallas_call | solution.py:120
  317.3 6.1 %shard_map.280 = (bf16[4,512,256]{2,1,0:T(8,128)(2,1)}, bf16[4,512,256]{2,1,0:T(8,128)(2,1)}) custom-call(bf16[4,512,192]{2,1,0:T(8,128)(2,1)} %get-tuple-element.343.refs_0_, bf16[4,512,64]{2,1,0:T(8,128)(2,1)} %get-tuple-element.327.refs_5_.refs_1_, bf16[128,1024]{1,0:T(8,128)(2,1)} %get-tuple-element.279.refs_3_.refs_2_, bf16[128,1024]{1,0:T(8,128)(2,1)} %copy-done.16, ...), custom_call_target="tpu_custom_call" | custom-call | flops 1073741824 | bytes 5242880 | tf_op jit(solution)/shard_map/pallas_call | solution.py:120
  347.9 9.0 %shard_map.282 = (bf16[4,512,256]{2,1,0:T(8,128)(2,1)}, f32[4,1,256]{2,1,0:T(1,128)}, bf16[128,1024]{1,0:T(8,128)(2,1)}, bf16[128,1024]{1,0:T(8,128)(2,1)}, bf16...) custom-call(bf16[4,512,512]{2,1,0:T(8,128)(2,1)} %all-gather.12.cloned.1.call-done.refs_0_, ...), custom_call_target="tpu_custom_call" | custom-call | flops 2147483648 | bytes 9441280 | tf_op jit(solution)/shard_map/pallas_call | solution.py:120
  360.5 6.3 %shard_map.283 = (bf16[4,512,512]{2,1,0:T(8,128)(2,1)}, bf16[4,512,512]{2,1,0:T(8,128)(2,1)}) custom-call(bf16[4,512,256]{2,1,0:T(8,128)(2,1)} %get-tuple-element.365.refs_0_, bf16[4,512,256]{2,1,0:T(8,128)(2,1)} %get-tuple-element.366.refs_1_, bf16[128,1024]{1,0:T(8,128)(2,1)} %get-tuple-element.261.refs_3_.refs_2_, bf16[128,1024]{1,0:T(8,128)(2,1)} %copy-done.62, ...), custom_call_target="tpu_custom_call" | custom-call | flops 2147483648 | bytes 8388608 | tf_op jit(solution)/shard_map/pallas_call | solution.py:120
  389.0 6.4 %collective-permute-done.52.refs_12_.refs_8_ = bf16[128,1024]{1,0:T(8,128)(2,1)S(1)} collective-permute-done((bf16[128,1024]{1,0:T(8,128)(2,1)}, bf16[128,1024]{1,0:T(8,128)(2,1)S(1)}, u32[]{:S(2)}, u32[]{:S(2)}) %collective-permute-start.52) | collective-permute-done | bytes 262176 | tf_op jit(solution)/shard_map/ppermute | solution.py:41
  400.1 12.6 %shard_map.285 = (bf16[4,512,64]{2,1,0:T(8,128)(2,1)}, bf16[4,512,128]{2,1,0:T(8,128)(2,1)}, bf16[4,512,128]{2,1,0:T(8,128)(2,1)}) custom-call(bf16[4,512,64]{2,1,0:T(8,128)(2,1)} %get-tuple-element.231.refs_0_, bf16[4,512,128]{2,1,0:T(8,128)(2,1)} %get-tuple-element.233.refs_1_, bf16[4,512,128]{2,1,0:T(8,128)(2,1)} %copy-done.7, ...), custom_call_target="tpu_custom_call" | custom-call | flops 1610612736 | bytes 6307840 | tf_op jit(solution)/shard_map/pallas_call | solution.py:120
  423.0 6.2 %shard_map.289 = (bf16[4,512,256]{2,1,0:T(8,128)(2,1)}, bf16[4,512,256]{2,1,0:T(8,128)(2,1)}) custom-call(bf16[4,512,192]{2,1,0:T(8,128)(2,1)} %get-tuple-element.400.refs_0_, bf16[4,512,64]{2,1,0:T(8,128)(2,1)} %get-tuple-element.235.refs_5_.refs_1_, bf16[128,1024]{1,0:T(8,128)(2,1)} %get-tuple-element.401.refs_2_, ...), custom_call_target="tpu_custom_call" | custom-call | flops 1073741824 | bytes 5242880 | tf_op jit(solution)/shard_map/pallas_call | solution.py:120
  457.8 10.6 %reduce-scatter.11.cloned.1.call-done = bf16[1,512,256]{2,1,0:T(8,128)(2,1)} async-done(((bf16[4,512,256]{2,1,0:T(8,128)(2,1)}), bf16[1,512,256]{2,1,0:T(8,128)(2,1)}) %reduce-scatter.11.cloned.1.call-update) | async-done | bytes 262160 | tf_op jit(solution)/shard_map/reduce_scatter | solution.py:751
  490.7 6.4 %all-to-all-done.9 = bf16[4,128,512]{2,1,0:T(8,128)(2,1)S(1)} async-done(((bf16[4,128,512]{2,1,0:T(8,128)(2,1)}), bf16[4,128,512]{2,1,0:T(8,128)(2,1)S(1)}, u32[]{:S(2)}, u32[]{:S(2)}) %all-to-all-start.9) | async-done | bytes 524320 | tf_op jit(solution)/shard_map/all_to_all | solution.py:53
  (467 shorter events, 310.4 us)
Async XLA Ops:
  7.2 61.4 %all-gather.14.cloned.1.call-start = ((), (), s32[]{:S(2)}) async-start(), calls=%async_computation.20 | async-start | bytes 1474560 | tf_op jit(solution)/shard_map/all_gather | solution.py:620
  25.8 16.3 %all-to-all-start.1 = ((bf16[4,128,1024]{2,1,0:T(8,128)(2,1)}), bf16[4,128,1024]{2,1,0:T(8,128)(2,1)S(1)}, u32[]{:S(2)}, u32[]{:S(2)}) async-start(bf16[4,128,1024]{2,1,0:T(8,128)(2,1)} %bitcast.8), calls=%async_computation.1 | async-start | bytes 2097152 | tf_op jit(solution)/shard_map/all_to_all | solution.py:53
  29.5 85.2 %all-gather.12.cloned.1.call-start = ((), (), s32[]{:S(2)}) async-start(), calls=%async_computation.15 | async-start | bytes 2621440 | tf_op jit(solution)/shard_map/all_gather | solution.py:620
  82.4 16.3 %all-to-all-start.2 = ((bf16[4,128,768]{1,2,0:T(8,128)(2,1)}), bf16[4,128,768]{1,2,0:T(8,128)(2,1)S(1)}, u32[]{:S(2)}, u32[]{:S(2)}) async-start(bf16[4,128,768]{1,2,0:T(8,128)(2,1)} %pad_maximum_fusion), calls=%async_computation.2 | async-start | bytes 1572864 | tf_op jit(solution)/shard_map/all_to_all | solution.py:53
  85.9 83.7 %all-gather.16.cloned.1.call-start = ((), (), s32[]{:S(2)}) async-start(), calls=%async_computation.21 | async-start | bytes 1310720 | tf_op jit(solution)/shard_map/all_gather | solution.py:620
  114.7 23.7 %collective-permute-start.8 = (bf16[4,512,512]{2,1,0:T(8,128)(2,1)}, bf16[4,512,512]{2,1,0:T(8,128)(2,1)}, u32[]{:S(2)}, u32[]{:S(2)}) collective-permute-start(bf16[4,512,512]{2,1,0:T(8,128)(2,1)} %all-gather.12.cloned.1.call-done.refs_0_), channel_id=1, source_target_pairs={{0,4},{4,0},{1,5},{5,1},{2,6},{6,2},{3,7},{7,3},{8,12},{12,8},{9,1... | collective-permute-start | bytes 6291464 | tf_op jit(solution)/shard_map/ppermute | solution.py:41
  118.0 14.5 %collective-permute-start.10 = (bf16[128,1024]{1,0:T(8,128)(2,1)}, bf16[128,1024]{1,0:T(8,128)(2,1)S(1)}, u32[]{:S(2)}, u32[]{:S(2)}) collective-permute-start(bf16[128,1024]{1,0:T(8,128)(2,1)} %get-tuple-element.261.refs_3_.refs_2_), channel_id=1, source_target_pairs={{0,16},{8,24},{16,0},{24,8},{1,17},{9,25},{17,1},{25,9},{2,18},{10... | collective-permute-start | bytes 786440 | tf_op jit(solution)/shard_map/ppermute | solution.py:41
  133.7 18.3 %all-to-all-start.4 = ((bf16[4,128,1024]{2,1,0:T(8,128)(2,1)}), bf16[4,128,1024]{2,1,0:T(8,128)(2,1)S(1)}, u32[]{:S(2)}, u32[]{:S(2)}) async-start(bf16[4,128,1024]{2,1,0:T(8,128)(2,1)} %bitcast.26), calls=%async_computation.4 | async-start | bytes 2097152 | tf_op jit(solution)/shard_map/all_to_all | solution.py:53
  137.2 72.7 %all-gather.18.cloned.1.call-start = ((), (), s32[]{:S(2)}) async-start(), calls=%async_computation.22 | async-start | bytes 2621440 | tf_op jit(solution)/shard_map/all_gather | solution.py:620
  138.1 185.3 %all-gather.20.cloned.1.call-start = ((), (), s32[]{:S(2)}) async-start(), calls=%async_computation.23 | async-start | bytes 1310720 | tf_op jit(solution)/shard_map/all_gather | solution.py:620
  219.9 17.8 %collective-permute-start.26 = (bf16[4,512,512]{2,1,0:T(8,128)(2,1)}, bf16[4,512,512]{2,1,0:T(8,128)(2,1)S(1)}, u32[]{:S(2)}, u32[]{:S(2)}) collective-permute-start(bf16[4,512,512]{2,1,0:T(8,128)(2,1)} %bitcast.226), channel_id=1, source_target_pairs={{0,4},{4,0},{1,5},{5,1},{2,6},{6,2},{3,7},{7,3},{8,12},{12,8},{9,1... | collective-permute-start | bytes 6291464 | tf_op jit(solution)/shard_map/ppermute | solution.py:41
  247.8 15.0 %collective-permute-start.33 = (bf16[128,1024]{1,0:T(8,128)(2,1)}, bf16[128,1024]{1,0:T(8,128)(2,1)S(1)}, u32[]{:S(2)}, u32[]{:S(2)}) collective-permute-start(bf16[128,1024]{1,0:T(8,128)(2,1)} %get-tuple-element.319), channel_id=1, source_target_pairs={{0,8},{8,0},{16,24},{24,16},{1,9},{9,1},{17,25},{25,17},{2,10},{10... | collective-permute-start | bytes 786440 | tf_op jit(solution)/shard_map/ppermute | solution.py:41
  249.0 21.2 %collective-permute-start.34 = (bf16[128,1024]{1,0:T(8,128)(2,1)}, bf16[128,1024]{1,0:T(8,128)(2,1)S(1)}, u32[]{:S(2)}, u32[]{:S(2)}) collective-permute-start(bf16[128,1024]{1,0:T(8,128)(2,1)} %get-tuple-element.320), channel_id=1, source_target_pairs={{0,16},{8,24},{16,0},{24,8},{1,17},{9,25},{17,1},{25,9},{2,18},{10... | collective-permute-start | bytes 786440 | tf_op jit(solution)/shard_map/ppermute | solution.py:41
  250.2 20.0 %collective-permute-start.35 = (bf16[128,1024]{1,0:T(8,128)(2,1)}, bf16[128,1024]{1,0:T(8,128)(2,1)S(1)}, u32[]{:S(2)}, u32[]{:S(2)}) collective-permute-start(bf16[128,1024]{1,0:T(8,128)(2,1)} %get-tuple-element.321), channel_id=1, source_target_pairs={{0,24},{8,16},{16,8},{24,0},{1,25},{9,17},{17,9},{25,1},{2,26},{10... | collective-permute-start | bytes 786440 | tf_op jit(solution)/shard_map/ppermute | solution.py:41
  273.4 74.4 %reduce-scatter.5.cloned.1.call-start = ((), (), s32[]{:S(2)}) async-start(), calls=%async_computation.16 | async-start | bytes 2621440 | tf_op jit(solution)/shard_map/reduce_scatter | solution.py:751
  292.0 84.7 %reduce-scatter.7.cloned.1.call-start = ((), (), s32[]{:S(2)}) async-start(), calls=%async_computation.17 | async-start | bytes 1310720 | tf_op jit(solution)/shard_map/reduce_scatter | solution.py:751
  347.8 97.6 %reduce-scatter.9.cloned.1.call-start = ((), (), s32[]{:S(2)}) async-start(), calls=%async_computation.18 | async-start | bytes 2621440 | tf_op jit(solution)/shard_map/reduce_scatter | solution.py:751
  381.2 14.3 %collective-permute-start.52 = (bf16[128,1024]{1,0:T(8,128)(2,1)}, bf16[128,1024]{1,0:T(8,128)(2,1)S(1)}, u32[]{:S(2)}, u32[]{:S(2)}) collective-permute-start(bf16[128,1024]{1,0:T(8,128)(2,1)} %get-tuple-element.378.refs_10_.refs_6_), channel_id=1, source_target_pairs={{0,16},{8,24},{16,0},{24,8},{1,17},{9,25},{17,1},{25,9},{2,18},{10... | collective-permute-start | bytes 786440 | tf_op jit(solution)/shard_map/ppermute | solution.py:41
  396.2 16.9 %all-to-all-start.5 = ((bf16[4,128,1024]{2,1,0:T(8,128)(2,1)}), bf16[4,128,1024]{2,1,0:T(8,128)(2,1)S(1)}, u32[]{:S(2)}, u32[]{:S(2)}) async-start(bf16[4,128,1024]{2,1,0:T(8,128)(2,1)} %bitcast.30), calls=%async_computation.7 | async-start | bytes 2097152 | tf_op jit(solution)/shard_map/all_to_all | solution.py:53
  399.7 68.7 %reduce-scatter.11.cloned.1.call-start = ((), (), s32[]{:S(2)}) async-start(), calls=%async_computation.19 | async-start | bytes 1310720 | tf_op jit(solution)/shard_map/reduce_scatter | solution.py:751
  436.0 71.2 %all-gather.22.cloned.1.call-start = ((), (), s32[]{:S(2)}) async-start(), calls=%async_computation.24 | async-start | bytes 1310720 | tf_op jit(solution)/shard_map/all_gather | solution.py:620
  451.6 21.4 %collective-permute-start.61 = (f32[4,1632]{1,0:T(4,128)S(1)}, f32[4,1632]{1,0:T(4,128)S(1)}, u32[]{:S(2)}, u32[]{:S(2)}) collective-permute-start(f32[4,1632]{1,0:T(4,128)S(1)} %get-tuple-element.519), channel_id=1, source_target_pairs={{0,1},{1,0},{2,3},{3,2},{4,5},{5,4},{6,7},{7,6},{8,9},{9,8},{10,11... | collective-permute-start | bytes 78344 | tf_op jit(solution)/shard_map/ppermute | solution.py:41
  451.7 21.3 %collective-permute-start.62 = (f32[4,1632]{1,0:T(4,128)S(1)}, f32[4,1632]{1,0:T(4,128)S(1)}, u32[]{:S(2)}, u32[]{:S(2)}) collective-permute-start(f32[4,1632]{1,0:T(4,128)S(1)} %get-tuple-element.521), channel_id=1, source_target_pairs={{0,2},{1,3},{2,0},{3,1},{4,6},{5,7},{6,4},{7,5},{8,10},{9,11},{10,... | collective-permute-start | bytes 78344 | tf_op jit(solution)/shard_map/ppermute | solution.py:41
  453.9 19.1 %collective-permute-start.63 = (f32[4,1632]{1,0:T(4,128)S(1)}, f32[4,1632]{1,0:T(4,128)S(1)}, u32[]{:S(2)}, u32[]{:S(2)}) collective-permute-start(f32[4,1632]{1,0:T(4,128)S(1)} %get-tuple-element.520), channel_id=1, source_target_pairs={{0,3},{1,2},{2,1},{3,0},{4,7},{5,6},{6,5},{7,4},{8,11},{9,10},{10,... | collective-permute-start | bytes 78344 | tf_op jit(solution)/shard_map/ppermute | solution.py:41
  (138 other events, 1195.9 us)
Sparse Core Ops, SparseCore 0:
  25.9 29.8 all-gather.13
  68.7 45.7 all-gather.11
  116.1 27.8 all-gather.15
  145.4 45.3 all-gather.17
  273.6 28.6 all-gather.19
  304.4 43.3 reduce-scatter.4
  350.2 26.4 reduce-scatter.6
  395.6 41.6 reduce-scatter.8
  440.2 28.1 reduce-scatter.10
  470.4 26.5 all-gather.21

commit v8 on v7

--- a/solution.py
+++ b/solution.py
@@ -650,15 +650,18 @@
     tall = jnp.pad(tall, ((0, 0), (0, spare - LAYERS), (0, half - tall.shape[2])))
     small = jnp.concatenate((jnp.broadcast_to(wide[None], (n_t, spare, half)), tall), axis=2)
     first = jnp.concatenate((packed_mixed(0), small.astype(bf16)), axis=1)
-    first = exchange(first, DP)
+    feed_rows = jnp.pad(packed_feed(0), ((0, 0), (0, spare), (0, 0)))
+    first = exchange(jnp.concatenate((first, feed_rows), axis=2), DP)
+    second_shard = first[:, :cut, columns:].reshape(part, -1)
+    first = first[:, :, :columns]
     first_shard = jnp.concatenate(
         (first[:, :cut].reshape(part, columns), first[:, cut:].reshape(-1, columns)), axis=0
     )
     messages = [to_planes_of(first_shard)]
     hidden, low = first_norm([own_rows(spread_rows(tokens[0]))], turn, counts)
     normed_one = send_rows(low)
-    normed_one, pack = meet(normed_one, packed_feed(0))
-    messages.append(to_planes_of(to_planes(pack)))
+    normed_one, second_shard = meet(normed_one, second_shard)
+    messages.append(to_planes_of(second_shard))
     messages[0], normed_one = meet(messages[0], normed_one)
     mixed = join(messages[0])
     vectors, biases_qkv, biases_up = unpack(mixed, turn, counts, width, LAYERS, spare)
@@ -823,15 +826,19 @@
         )
 
     low_outer = turned_sum([low], turn, counts, False)
-    low_outer, mixed_sums[0] = meet(low_outer, mixed_sums[0])
-    tokens_planes = to_planes_of(low_outer)
-    low_outer, mixed_sums[1], feed_sums[0], feed_sums[1] = meet(
-        low_outer, mixed_sums[1], feed_sums[0], feed_sums[1]
-    )
+    low_outer, mixed_sums[1], feed_sums[1] = meet(low_outer, mixed_sums[1], feed_sums[1])
     feed_shares[1] = send_shares(feed_sums[1])
     mixed_shares[1] = send_shares(mixed_sums[1])
+    low_outer, mixed_sums[0], feed_shares[1], mixed_shares[1] = meet(
+        low_outer, mixed_sums[0], feed_shares[1], mixed_shares[1]
+    )
+    tokens_planes = to_planes_of(low_outer)
+    mixed_sums[0], feed_sums[0] = meet(mixed_sums[0], feed_sums[0])
     feed_shares[0] = send_shares(feed_sums[0])
     mixed_shares[0] = send_shares(mixed_sums[0])
+    tokens_planes, feed_shares[0], mixed_shares[0] = meet(
+        tokens_planes, feed_shares[0], mixed_shares[0]
+    )
     tokens_grad = send_output(tokens_planes).astype(f32)
 
     def fold(arrays, name, size):

time: 539 us -> 530 us (0.983)
  waiting for transfers between devices: 184 us -> 175 us
    all_gather x6, waiting for transfers between devices: 0.07 us -> 12.7 us  [to_planes_of(): return lax.all_gather(array, HEAD, axis=0, tiled=False)]
    reduce_scatter x4, waiting for transfers between devices: 16.2 us -> 5.25 us  [head_sum(): return lax.psum_scatter(mine, HEAD, scatter_dimension=0, tiled=False)]
    ppermute x67, waiting for transfers between devices: 134 us -> 124 us  [swap(): return lax.ppermute(array, name, [(i, i ^ step) for i in range(size)])]
    all_to_all x2 -> x1, blocking collectives: 21.6 us -> 17.4 us  [exchange(): return lax.all_to_all(array, name, 0, 0, tiled=True)]
    unnamed x156 -> x179, local copies, waits for them, and re-layouts: 15.8 us -> 15.5 us
  transfers between devices with their start and end apart: 86 -> 86, of which waited for: 46 -> 47; matrix products, arithmetic and copies ran while one was open for 6% -> 8% of each run, Pallas kernels for 28% -> 28%
where the time goes in v8:
time: 530 us; the launch traced here: 522 us
  waiting for transfers between devices  175 us (33%)
  Pallas kernels  157 us (30%)
  starting transfers between devices  97.5 us (18%)
  local copies, waits for them, and re-layouts  39.3 us (7%)
  other arithmetic  20.1 us (4%)
  blocking collectives  17.4 us (3%)
  between operations  16 us (3%)
    pallas_call x27, Pallas kernels, run(): pl.pallas_call(kernel, grid=(steps,), in_specs=[each(item) for item in ea...  155 us
    ppermute x67, waiting for transfers between devices, swap(): return lax.ppermute(array, name, [(i, i ^ step) for i in range(size)])  124 us
    ppermute x67, starting transfers between devices, swap(): return lax.ppermute(array, name, [(i, i ^ step) for i in range(size)])  65.1 us
    all_to_all x9, waiting for transfers between devices, exchange(): return lax.all_to_all(array, name, 0, 0, tiled=True)  32.9 us
    all_to_all x9, starting transfers between devices, exchange(): return lax.all_to_all(array, name, 0, 0, tiled=True)  31.4 us
    all_to_all x1, blocking collectives, exchange(): return lax.all_to_all(array, name, 0, 0, tiled=True)  17.4 us
    unnamed x179, local copies, waits for them, and re-layouts  15.5 us
    all_gather x6, waiting for transfers between devices, to_planes_of(): return lax.all_gather(array, HEAD, axis=0, tiled=False)  12.7 us
  transfers between devices with their start and end apart: 86, of which 47 were waited for; matrix products, arithmetic and copies ran while one was open for 8% of the time, Pallas kernels for 28%

profile of v8, /device:TPU:0, one launch (start us, length us, event | category | flops | bytes accessed | tf_op | source)
XLA Modules:
  0.0 522.0 jit_solution(1347172210136476661)
XLA Ops:
  12.4 17.4 %all_to_all.50 = bf16[4,144,768]{2,1,0:T(8,128)(2,1)S(1)} all-to-all(bf16[4,144,768]{2,1,0:T(8,128)(2,1)S(1)} %copy.147), channel_id=1, replica_groups=mesh['dp'=4,'seq'=2,'head'=4] {'dp'}, dimensions={0} | all-to-all | bytes 1769472 | tf_op jit(solution)/shard_map/all_to_all | solution.py:53
  34.2 12.4 %all-to-all-done.1 = bf16[4,128,1024]{2,1,0:T(8,128)(2,1)S(1)} async-done(((bf16[4,128,1024]{2,1,0:T(8,128)(2,1)}), bf16[4,128,1024]{2,1,0:T(8,128)(2,1)S(1)}, u32[]{:S(2)}, u32[]{:S(2)}) %all-to-all-start.1) | async-done | bytes 1048608 | tf_op jit(solution)/shard_map/all_to_all | solution.py:53
  68.9 5.7 %shard_map.264 = (bf16[4,512,64]{2,1,0:T(8,128)(2,1)}, bf16[4,512,128]{2,1,0:T(8,128)(2,1)}, bf16[128,1024]{1,0:T(8,128)(2,1)}, bf16[128,1024]{1,0:T(8,128)(2,1)...) custom-call(bf16[4,576,256]{2,1,0:T(8,128)(2,1)} %bitcast.175, bf16[4,576,256]{2,1,0:T(8,128)(2,1)} %copy-done, ...), custom_call_target="tpu_custom_call" | custom-call | flops 805306368 | bytes 5311488 | tf_op jit(solution)/shard_map/pallas_call | solution.py:120
  82.6 10.5 %shard_map.265 = (bf16[4,512,64]{2,1,0:T(8,128)(2,1)}, f32[4,512,1]{2,1,0:T(8,128)}, bf16[128,1024]{1,0:T(8,128)(2,1)}, bf16[128,1024]{1,0:T(8,128)(2,1)}, bf16[...) custom-call(bf16[4,512,64]{2,1,0:T(8,128)(2,1)} %get-tuple-element.238.refs_0_, ...), custom_call_target="tpu_custom_call" | custom-call | flops 805306368 | bytes 4997120 | tf_op jit(solution)/shard_map/pallas_call | solution.py:120
  97.0 12.6 %all-gather.15.cloned.1.call-done = bf16[2048,512]{1,0:T(8,128)(2,1)} async-done(((bf16[512,512]{1,0:T(8,128)(2,1)}), bf16[2048,512]{1,0:T(8,128)(2,1)}) %all-gather.15.cloned.1.call-update) | async-done | bytes 2097168 | tf_op jit(solution)/shard_map/all_gather | solution.py:620
  116.5 10.9 %collective-permute-done.10.refs_5_.refs_4_ = bf16[128,1024]{1,0:T(8,128)(2,1)S(1)} collective-permute-done((bf16[128,1024]{1,0:T(8,128)(2,1)}, bf16[128,1024]{1,0:T(8,128)(2,1)S(1)}, u32[]{:S(2)}, u32[]{:S(2)}) %collective-permute-start.10) | collective-permute-done | bytes 262176 | tf_op jit(solution)/shard_map/ppermute | solution.py:41
  133.4 8.7 %shard_map.267 = (f32[4,512,256]{2,1,0:T(8,128)}, bf16[4,512,256]{2,1,0:T(8,128)(2,1)}, bf16[128,1024]{1,0:T(8,128)(2,1)}, bf16[128,1024]{1,0:T(8,128)(2,1)}, bf...) custom-call(bf16[4,512,512]{2,1,0:T(8,128)(2,1)} %bitcast.228, bf16[4,512,512]{2,1,0:T(8,128)(2,1)} %collective-permute-done.8.refs_1_, ...), custom_call_target="tpu_custom_call" | custom-call | flops 2147483648 | bytes 9441280 | tf_op jit(solution)/shard_map/pallas_call | solution.py:120
  164.4 6.0 %collective-permute-done.15.refs_4_.refs_3_ = bf16[128,1024]{1,0:T(8,128)(2,1)S(1)} collective-permute-done((bf16[128,1024]{1,0:T(8,128)(2,1)}, bf16[128,1024]{1,0:T(8,128)(2,1)S(1)}, u32[]{:S(2)}, u32[]{:S(2)}) %collective-permute-start.15) | collective-permute-done | bytes 262176 | tf_op jit(solution)/shard_map/ppermute | solution.py:41
  188.5 10.6 %shard_map.271 = (bf16[4,512,64]{2,1,0:T(8,128)(2,1)}, f32[4,512,1]{2,1,0:T(8,128)}, bf16[128,1024]{1,0:T(8,128)(2,1)}, bf16[128,1024]{1,0:T(8,128)(2,1)}, bf16[...) custom-call(bf16[4,512,64]{2,1,0:T(8,128)(2,1)} %get-tuple-element.290.refs_0_, ...), custom_call_target="tpu_custom_call" | custom-call | flops 805306368 | bytes 4734976 | tf_op jit(solution)/shard_map/pallas_call | solution.py:120
  204.0 6.0 %collective-permute-done.23.refs_3_ = bf16[128,1024]{1,0:T(8,128)(2,1)S(1)} collective-permute-done((bf16[128,1024]{1,0:T(8,128)(2,1)}, bf16[128,1024]{1,0:T(8,128)(2,1)S(1)}, u32[]{:S(2)}, u32[]{:S(2)}) %collective-permute-start.23) | collective-permute-done | bytes 262176 | tf_op jit(solution)/shard_map/ppermute | solution.py:41
  220.7 5.9 %collective-permute-done.27.refs_4_.refs_3_ = bf16[128,1024]{1,0:T(8,128)(2,1)S(1)} collective-permute-done((bf16[128,1024]{1,0:T(8,128)(2,1)}, bf16[128,1024]{1,0:T(8,128)(2,1)S(1)}, u32[]{:S(2)}, u32[]{:S(2)}) %collective-permute-start.27) | collective-permute-done | bytes 262176 | tf_op jit(solution)/shard_map/ppermute | solution.py:41
  233.2 8.6 %shard_map.273 = (f32[4,512,256]{2,1,0:T(8,128)}, bf16[4,512,256]{2,1,0:T(8,128)(2,1)}, bf16[128,1024]{1,0:T(8,128)(2,1)}, bf16[128,1024]{1,0:T(8,128)(2,1)}, bf...) custom-call(bf16[4,512,512]{2,1,0:T(8,128)(2,1)} %bitcast.231, bf16[4,512,512]{2,1,0:T(8,128)(2,1)} %copy-done.70, ...), custom_call_target="tpu_custom_call" | custom-call | flops 2147483648 | bytes 9441280 | tf_op jit(solution)/shard_map/pallas_call | solution.py:120
  245.4 9.0 %shard_map.274 = (bf16[4,512,256]{2,1,0:T(8,128)(2,1)}, f32[4,1,256]{2,1,0:T(1,128)}, bf16[128,1024]{1,0:T(8,128)(2,1)}, bf16[128,1024]{1,0:T(8,128)(2,1)}, bf16...) custom-call(bf16[4,512,512]{2,1,0:T(8,128)(2,1)} %bitcast.232, bf16[4,512,512]{2,1,0:T(8,128)(2,1)} %copy-done.70, ...), custom_call_target="tpu_custom_call" | custom-call | flops 2147483648 | bytes 9441280 | tf_op jit(solution)/shard_map/pallas_call | solution.py:120
  257.9 6.3 %shard_map.275 = (bf16[4,512,512]{2,1,0:T(8,128)(2,1)}, bf16[4,512,512]{2,1,0:T(8,128)(2,1)}) custom-call(bf16[4,512,256]{2,1,0:T(8,128)(2,1)} %get-tuple-element.321.refs_0_, bf16[4,512,256]{2,1,0:T(8,128)(2,1)} %get-tuple-element.322.refs_1_, bf16[128,1024]{1,0:T(8,128)(2,1)} %get-tuple-element.312.refs_3_.refs_2_, bf16[128,1024]{1,0:T(8,128)(2,1)} %copy-done.79, ...), custom_call_target="tpu_custom_call" | custom-call | flops 2147483648 | bytes 8388608 | tf_op jit(solution)/shard_map/pallas_call | solution.py:120
  286.7 12.5 %shard_map.278 = (bf16[4,512,64]{2,1,0:T(8,128)(2,1)}, bf16[4,512,128]{2,1,0:T(8,128)(2,1)}, bf16[4,512,128]{2,1,0:T(8,128)(2,1)}) custom-call(bf16[4,512,64]{2,1,0:T(8,128)(2,1)} %get-tuple-element.290.refs_0_, bf16[4,512,128]{2,1,0:T(8,128)(2,1)} %get-tuple-element.293.refs_1_, bf16[4,512,128]{2,1,0:T(8,128)(2,1)} %copy-done.7, ...), custom_call_target="tpu_custom_call" | custom-call | flops 1610612736 | bytes 6045696 | tf_op jit(solution)/shard_map/pallas_call | solution.py:120
  311.1 6.1 %shard_map.280 = (bf16[4,512,256]{2,1,0:T(8,128)(2,1)}, bf16[4,512,256]{2,1,0:T(8,128)(2,1)}) custom-call(bf16[4,512,192]{2,1,0:T(8,128)(2,1)} %get-tuple-element.350.refs_0_, bf16[4,512,64]{2,1,0:T(8,128)(2,1)} %get-tuple-element.334.refs_5_.refs_1_, bf16[128,1024]{1,0:T(8,128)(2,1)} %get-tuple-element.286.refs_3_.refs_2_, bf16[128,1024]{1,0:T(8,128)(2,1)} %copy-done.17, ...), custom_call_target="tpu_custom_call" | custom-call | flops 1073741824 | bytes 5242880 | tf_op jit(solution)/shard_map/pallas_call | solution.py:120
  341.8 9.0 %shard_map.282 = (bf16[4,512,256]{2,1,0:T(8,128)(2,1)}, f32[4,1,256]{2,1,0:T(1,128)}, bf16[128,1024]{1,0:T(8,128)(2,1)}, bf16[128,1024]{1,0:T(8,128)(2,1)}, bf16...) custom-call(bf16[4,512,512]{2,1,0:T(8,128)(2,1)} %bitcast.229, bf16[4,512,512]{2,1,0:T(8,128)(2,1)} %collective-permute-done.8.refs_1_, ...), custom_call_target="tpu_custom_call" | custom-call | flops 2147483648 | bytes 9441280 | tf_op jit(solution)/shard_map/pallas_call | solution.py:120
  354.3 6.3 %shard_map.283 = (bf16[4,512,512]{2,1,0:T(8,128)(2,1)}, bf16[4,512,512]{2,1,0:T(8,128)(2,1)}) custom-call(bf16[4,512,256]{2,1,0:T(8,128)(2,1)} %get-tuple-element.372.refs_0_, bf16[4,512,256]{2,1,0:T(8,128)(2,1)} %get-tuple-element.373.refs_1_, bf16[128,1024]{1,0:T(8,128)(2,1)} %get-tuple-element.268.refs_3_.refs_2_, bf16[128,1024]{1,0:T(8,128)(2,1)} %copy-done.73, ...), custom_call_target="tpu_custom_call" | custom-call | flops 2147483648 | bytes 8388608 | tf_op jit(solution)/shard_map/pallas_call | solution.py:120
  382.7 6.4 %collective-permute-done.52.refs_12_.refs_8_ = bf16[128,1024]{1,0:T(8,128)(2,1)S(1)} collective-permute-done((bf16[128,1024]{1,0:T(8,128)(2,1)}, bf16[128,1024]{1,0:T(8,128)(2,1)S(1)}, u32[]{:S(2)}, u32[]{:S(2)}) %collective-permute-start.52) | collective-permute-done | bytes 262176 | tf_op jit(solution)/shard_map/ppermute | solution.py:41
  393.8 12.6 %shard_map.285 = (bf16[4,512,64]{2,1,0:T(8,128)(2,1)}, bf16[4,512,128]{2,1,0:T(8,128)(2,1)}, bf16[4,512,128]{2,1,0:T(8,128)(2,1)}) custom-call(bf16[4,512,64]{2,1,0:T(8,128)(2,1)} %get-tuple-element.238.refs_0_, bf16[4,512,128]{2,1,0:T(8,128)(2,1)} %get-tuple-element.240.refs_1_, bf16[4,512,128]{2,1,0:T(8,128)(2,1)} %copy-done.6, ...), custom_call_target="tpu_custom_call" | custom-call | flops 1610612736 | bytes 6307840 | tf_op jit(solution)/shard_map/pallas_call | solution.py:120
  409.8 5.5 %shard_map.286 = (bf16[4,512,192]{2,1,0:T(8,128)(2,1)}, f32[4,1,192]{2,1,0:T(1,128)}, bf16[128,1024]{1,0:T(8,128)(2,1)}, bf16[128,1024]{1,0:T(8,128)(2,1)}, bf16...) custom-call(bf16[4,512,64]{2,1,0:T(8,128)(2,1)} %get-tuple-element.394.refs_0_, ...), custom_call_target="tpu_custom_call" | custom-call | flops 805306368 | bytes 5508096 | tf_op jit(solution)/shard_map/pallas_call | solution.py:120
  416.7 6.2 %shard_map.289 = (bf16[4,512,256]{2,1,0:T(8,128)(2,1)}, bf16[4,512,256]{2,1,0:T(8,128)(2,1)}) custom-call(bf16[4,512,192]{2,1,0:T(8,128)(2,1)} %get-tuple-element.410.refs_0_, bf16[4,512,64]{2,1,0:T(8,128)(2,1)} %get-tuple-element.242.refs_5_.refs_1_, bf16[128,1024]{1,0:T(8,128)(2,1)} %get-tuple-element.411.refs_2_, ...), custom_call_target="tpu_custom_call" | custom-call | flops 1073741824 | bytes 5242880 | tf_op jit(solution)/shard_map/pallas_call | solution.py:120
  449.9 6.1 %all-to-all-done.6 = bf16[4,128,256]{1,2,0:T(8,128)(2,1)S(1)} async-done(((bf16[4,128,256]{1,2,0:T(8,128)(2,1)}), bf16[4,128,256]{1,2,0:T(8,128)(2,1)S(1)}, u32[]{:S(2)}, u32[]{:S(2)}) %all-to-all-start.6) | async-done | bytes 262176 | tf_op jit(solution)/shard_map/all_to_all | solution.py:53
  490.9 5.9 %all-to-all-done.7 = bf16[4,128,512]{2,1,0:T(8,128)(2,1)S(1)} async-done(((bf16[4,128,512]{2,1,0:T(8,128)(2,1)}), bf16[4,128,512]{2,1,0:T(8,128)(2,1)S(1)}, u32[]{:S(2)}, u32[]{:S(2)}) %all-to-all-start.7) | async-done | bytes 524320 | tf_op jit(solution)/shard_map/all_to_all | solution.py:53
  (489 shorter events, 298.8 us)
Async XLA Ops:
  7.3 55.6 %all-gather.13.cloned.1.call-start = ((), (), s32[]{:S(2)}) async-start(), calls=%async_computation.18 | async-start | bytes 1474560 | tf_op jit(solution)/shard_map/all_gather | solution.py:620
  30.6 16.0 %all-to-all-start.1 = ((bf16[4,128,1024]{2,1,0:T(8,128)(2,1)}), bf16[4,128,1024]{2,1,0:T(8,128)(2,1)S(1)}, u32[]{:S(2)}, u32[]{:S(2)}) async-start(bf16[4,128,1024]{2,1,0:T(8,128)(2,1)} %bitcast.12), calls=%async_computation.1 | async-start | bytes 2097152 | tf_op jit(solution)/shard_map/all_to_all | solution.py:53
  34.2 75.4 %all-gather.15.cloned.1.call-start = ((), (), s32[]{:S(2)}) async-start(), calls=%async_computation.19 | async-start | bytes 2621440 | tf_op jit(solution)/shard_map/all_gather | solution.py:620
  76.8 16.3 %all-to-all-start.2 = ((bf16[4,128,768]{1,2,0:T(8,128)(2,1)}), bf16[4,128,768]{1,2,0:T(8,128)(2,1)S(1)}, u32[]{:S(2)}, u32[]{:S(2)}) async-start(bf16[4,128,768]{1,2,0:T(8,128)(2,1)} %pad_maximum_fusion), calls=%async_computation.2 | async-start | bytes 1572864 | tf_op jit(solution)/shard_map/all_to_all | solution.py:53
  80.3 84.1 %all-gather.17.cloned.1.call-start = ((), (), s32[]{:S(2)}) async-start(), calls=%async_computation.20 | async-start | bytes 1310720 | tf_op jit(solution)/shard_map/all_gather | solution.py:620
  93.4 16.2 %collective-permute-start.5 = (bf16[128,1024]{1,0:T(8,128)(2,1)}, bf16[128,1024]{1,0:T(8,128)(2,1)S(1)}, u32[]{:S(2)}, u32[]{:S(2)}) collective-permute-start(bf16[128,1024]{1,0:T(8,128)(2,1)} %get-tuple-element.251), channel_id=1, source_target_pairs={{0,8},{8,0},{16,24},{24,16},{1,9},{9,1},{17,25},{25,17},{2,10},{10... | collective-permute-start | bytes 786440 | tf_op jit(solution)/shard_map/ppermute | solution.py:41
  95.4 14.2 %collective-permute-start.6 = (bf16[128,1024]{1,0:T(8,128)(2,1)}, bf16[128,1024]{1,0:T(8,128)(2,1)S(1)}, u32[]{:S(2)}, u32[]{:S(2)}) collective-permute-start(bf16[128,1024]{1,0:T(8,128)(2,1)} %get-tuple-element.252), channel_id=1, source_target_pairs={{0,16},{8,24},{16,0},{24,8},{1,17},{9,25},{17,1},{25,9},{2,18},{10... | collective-permute-start | bytes 786440 | tf_op jit(solution)/shard_map/ppermute | solution.py:41
  109.6 23.8 %collective-permute-start.8 = (bf16[4,512,512]{2,1,0:T(8,128)(2,1)}, bf16[4,512,512]{2,1,0:T(8,128)(2,1)}, u32[]{:S(2)}, u32[]{:S(2)}) collective-permute-start(bf16[4,512,512]{2,1,0:T(8,128)(2,1)} %bitcast.227), channel_id=1, source_target_pairs={{0,4},{4,0},{1,5},{5,1},{2,6},{6,2},{3,7},{7,3},{8,12},{12,8},{9,1... | collective-permute-start | bytes 6291464 | tf_op jit(solution)/shard_map/ppermute | solution.py:41
  113.0 14.4 %collective-permute-start.10 = (bf16[128,1024]{1,0:T(8,128)(2,1)}, bf16[128,1024]{1,0:T(8,128)(2,1)S(1)}, u32[]{:S(2)}, u32[]{:S(2)}) collective-permute-start(bf16[128,1024]{1,0:T(8,128)(2,1)} %get-tuple-element.268.refs_3_.refs_2_), channel_id=1, source_target_pairs={{0,16},{8,24},{16,0},{24,8},{1,17},{9,25},{17,1},{25,9},{2,18},{10... | collective-permute-start | bytes 786440 | tf_op jit(solution)/shard_map/ppermute | solution.py:41
  128.7 18.2 %all-to-all-start.3 = ((bf16[4,128,1024]{2,1,0:T(8,128)(2,1)}), bf16[4,128,1024]{2,1,0:T(8,128)(2,1)S(1)}, u32[]{:S(2)}, u32[]{:S(2)}) async-start(bf16[4,128,1024]{2,1,0:T(8,128)(2,1)} %bitcast.28), calls=%async_computation.3 | async-start | bytes 2097152 | tf_op jit(solution)/shard_map/all_to_all | solution.py:53
  132.3 71.7 %all-gather.19.cloned.1.call-start = ((), (), s32[]{:S(2)}) async-start(), calls=%async_computation.21 | async-start | bytes 2621440 | tf_op jit(solution)/shard_map/all_gather | solution.py:620
  133.2 184.1 %all-gather.21.cloned.1.call-start = ((), (), s32[]{:S(2)}) async-start(), calls=%async_computation.22 | async-start | bytes 1310720 | tf_op jit(solution)/shard_map/all_gather | solution.py:620
  214.0 17.8 %collective-permute-start.26 = (bf16[4,512,512]{2,1,0:T(8,128)(2,1)}, bf16[4,512,512]{2,1,0:T(8,128)(2,1)S(1)}, u32[]{:S(2)}, u32[]{:S(2)}) collective-permute-start(bf16[4,512,512]{2,1,0:T(8,128)(2,1)} %bitcast.230), channel_id=1, source_target_pairs={{0,4},{4,0},{1,5},{5,1},{2,6},{6,2},{3,7},{7,3},{8,12},{12,8},{9,1... | collective-permute-start | bytes 6291464 | tf_op jit(solution)/shard_map/ppermute | solution.py:41
  241.8 15.0 %collective-permute-start.33 = (bf16[128,1024]{1,0:T(8,128)(2,1)}, bf16[128,1024]{1,0:T(8,128)(2,1)S(1)}, u32[]{:S(2)}, u32[]{:S(2)}) collective-permute-start(bf16[128,1024]{1,0:T(8,128)(2,1)} %get-tuple-element.326), channel_id=1, source_target_pairs={{0,8},{8,0},{16,24},{24,16},{1,9},{9,1},{17,25},{25,17},{2,10},{10... | collective-permute-start | bytes 786440 | tf_op jit(solution)/shard_map/ppermute | solution.py:41
  242.9 21.3 %collective-permute-start.34 = (bf16[128,1024]{1,0:T(8,128)(2,1)}, bf16[128,1024]{1,0:T(8,128)(2,1)S(1)}, u32[]{:S(2)}, u32[]{:S(2)}) collective-permute-start(bf16[128,1024]{1,0:T(8,128)(2,1)} %get-tuple-element.327), channel_id=1, source_target_pairs={{0,16},{8,24},{16,0},{24,8},{1,17},{9,25},{17,1},{25,9},{2,18},{10... | collective-permute-start | bytes 786440 | tf_op jit(solution)/shard_map/ppermute | solution.py:41
  244.2 20.0 %collective-permute-start.35 = (bf16[128,1024]{1,0:T(8,128)(2,1)}, bf16[128,1024]{1,0:T(8,128)(2,1)S(1)}, u32[]{:S(2)}, u32[]{:S(2)}) collective-permute-start(bf16[128,1024]{1,0:T(8,128)(2,1)} %get-tuple-element.328), channel_id=1, source_target_pairs={{0,24},{8,16},{16,8},{24,0},{1,25},{9,17},{17,9},{25,1},{2,26},{10... | collective-permute-start | bytes 786440 | tf_op jit(solution)/shard_map/ppermute | solution.py:41
  267.4 74.1 %reduce-scatter.5.cloned.1.call-start = ((), (), s32[]{:S(2)}) async-start(), calls=%async_computation.14 | async-start | bytes 2621440 | tf_op jit(solution)/shard_map/reduce_scatter | solution.py:754
  286.0 84.4 %reduce-scatter.7.cloned.1.call-start = ((), (), s32[]{:S(2)}) async-start(), calls=%async_computation.15 | async-start | bytes 1310720 | tf_op jit(solution)/shard_map/reduce_scatter | solution.py:754
  341.5 97.6 %reduce-scatter.9.cloned.1.call-start = ((), (), s32[]{:S(2)}) async-start(), calls=%async_computation.16 | async-start | bytes 2621440 | tf_op jit(solution)/shard_map/reduce_scatter | solution.py:754
  374.8 14.3 %collective-permute-start.52 = (bf16[128,1024]{1,0:T(8,128)(2,1)}, bf16[128,1024]{1,0:T(8,128)(2,1)S(1)}, u32[]{:S(2)}, u32[]{:S(2)}) collective-permute-start(bf16[128,1024]{1,0:T(8,128)(2,1)} %get-tuple-element.385.refs_10_.refs_6_), channel_id=1, source_target_pairs={{0,16},{8,24},{16,0},{24,8},{1,17},{9,25},{17,1},{25,9},{2,18},{10... | collective-permute-start | bytes 786440 | tf_op jit(solution)/shard_map/ppermute | solution.py:41
  389.9 17.0 %all-to-all-start.4 = ((bf16[4,128,1024]{2,1,0:T(8,128)(2,1)}), bf16[4,128,1024]{2,1,0:T(8,128)(2,1)S(1)}, u32[]{:S(2)}, u32[]{:S(2)}) async-start(bf16[4,128,1024]{2,1,0:T(8,128)(2,1)} %bitcast.32), calls=%async_computation.6 | async-start | bytes 2097152 | tf_op jit(solution)/shard_map/all_to_all | solution.py:53
  393.4 70.6 %reduce-scatter.11.cloned.1.call-start = ((), (), s32[]{:S(2)}) async-start(), calls=%async_computation.17 | async-start | bytes 1310720 | tf_op jit(solution)/shard_map/reduce_scatter | solution.py:754
  459.5 37.3 %all-gather.23.cloned.1.call-start = ((), (), s32[]{:S(2)}) async-start(), calls=%async_computation.23 | async-start | bytes 1310720 | tf_op jit(solution)/shard_map/all_gather | solution.py:620
  496.8 15.3 %all-to-all-start.9 = ((bf16[4,128,1024]{2,1,0:T(8,128)(2,1)}), bf16[4,128,1024]{2,1,0:T(8,128)(2,1)S(1)}, u32[]{:S(2)}, u32[]{:S(2)}) async-start(bf16[4,128,1024]{2,1,0:T(8,128)(2,1)} %bitcast.193), calls=%async_computation.13 | async-start | bytes 2097152 | tf_op jit(solution)/shard_map/all_to_all | solution.py:53
  (151 other events, 1155.4 us)
Sparse Core Ops, SparseCore 0:
  30.7 30.0 all-gather.12
  63.0 46.4 all-gather.14
  111.1 27.1 all-gather.16
  139.8 45.3 all-gather.18
  267.6 28.3 all-gather.20
  298.1 43.3 reduce-scatter.4
  343.9 26.4 reduce-scatter.6
  389.3 41.6 reduce-scatter.8
  433.9 26.4 reduce-scatter.10
  467.9 26.1 all-gather.22

commit v9 on v8

--- a/solution.py
+++ b/solution.py
@@ -16,6 +16,7 @@
 epsilon = 1e-05
 masked_value = -1000000000.0
 VMEM_LIMIT = 60 * 1024 * 1024
+SMALL_LIMIT = 16 * 1024 * 1024
 bf16 = jnp.bfloat16
 f32 = jnp.float32
 
@@ -124,7 +125,7 @@
         out_specs=[each(item) for item in each_out] + [whole(item) for item in whole_out],
         out_shape=shapes,
         scratch_shapes=list(scratch),
-        compiler_params=pltpu.CompilerParams(vmem_limit_bytes=VMEM_LIMIT),
+        compiler_params=pltpu.CompilerParams(vmem_limit_bytes=VMEM_LIMIT if steps > 1 else SMALL_LIMIT),
         cost_estimate=pl.CostEstimate(flops=flops, bytes_accessed=moved, transcendentals=0),
     )(*arrays)
 

time: 530 us -> 520 us (0.981)
  Pallas kernels: 157 us -> 139 us
  waiting for transfers between devices: 175 us -> 184 us
    pallas_call x27, Pallas kernels: 155 us -> 137 us  [run(): pl.pallas_call(kernel, grid=(steps,), in_specs=[each(item) for item in ea...]
    all_to_all x9, waiting for transfers between devices: 32.9 us -> 38.5 us  [exchange(): return lax.all_to_all(array, name, 0, 0, tiled=True)]
    unnamed x179 -> x167, local copies, waits for them, and re-layouts: 15.5 us -> 19.7 us
  transfers between devices with their start and end apart: 86 -> 86, of which waited for: 47 -> 45; matrix products, arithmetic and copies ran while one was open for 8% -> 6% of each run, Pallas kernels for 28% -> 25%
where the time goes in v9:
time: 520 us; the launch traced here: 512 us
  waiting for transfers between devices  184 us (35%)
  Pallas kernels  139 us (27%)
  starting transfers between devices  98.5 us (19%)
  local copies, waits for them, and re-layouts  38.3 us (7%)
  other arithmetic  18.3 us (4%)
  blocking collectives  17.4 us (3%)
  between operations  16.1 us (3%)
    pallas_call x27, Pallas kernels, run(): pl.pallas_call(kernel, grid=(steps,), in_specs=[each(item) for item in ea...  137 us
    ppermute x67, waiting for transfers between devices, swap(): return lax.ppermute(array, name, [(i, i ^ step) for i in range(size)])  129 us
    ppermute x67, starting transfers between devices, swap(): return lax.ppermute(array, name, [(i, i ^ step) for i in range(size)])  65.3 us
    all_to_all x9, waiting for transfers between devices, exchange(): return lax.all_to_all(array, name, 0, 0, tiled=True)  38.5 us
    all_to_all x9, starting transfers between devices, exchange(): return lax.all_to_all(array, name, 0, 0, tiled=True)  32.2 us
    unnamed x167, local copies, waits for them, and re-layouts  19.7 us
    all_to_all x1, blocking collectives, exchange(): return lax.all_to_all(array, name, 0, 0, tiled=True)  17.4 us
    all_gather x6, waiting for transfers between devices, to_planes_of(): return lax.all_gather(array, HEAD, axis=0, tiled=False)  13.8 us
  transfers between devices with their start and end apart: 86, of which 45 were waited for; matrix products, arithmetic and copies ran while one was open for 6% of the time, Pallas kernels for 25%

profile of v9, /device:TPU:0, one launch (start us, length us, event | category | flops | bytes accessed | tf_op | source)
XLA Modules:
  0.0 511.6 jit_solution(14061221436571080545)
XLA Ops:
  13.8 17.4 %all_to_all.50 = bf16[4,144,768]{2,1,0:T(8,128)(2,1)S(1)} all-to-all(bf16[4,144,768]{2,1,0:T(8,128)(2,1)S(1)} %copy.147), channel_id=1, replica_groups=mesh['dp'=4,'seq'=2,'head'=4] {'dp'}, dimensions={0} | all-to-all | bytes 1769472 | tf_op jit(solution)/shard_map/all_to_all | solution.py:54
  35.6 12.4 %all-to-all-done.1 = bf16[4,128,1024]{2,1,0:T(8,128)(2,1)S(1)} async-done(((bf16[4,128,1024]{2,1,0:T(8,128)(2,1)}), bf16[4,128,1024]{2,1,0:T(8,128)(2,1)S(1)}, u32[]{:S(2)}, u32[]{:S(2)}) %all-to-all-start.1) | async-done | bytes 1048608 | tf_op jit(solution)/shard_map/all_to_all | solution.py:54
  82.0 10.5 %shard_map.265 = (bf16[4,512,64]{2,1,0:T(8,128)(2,1)}, f32[4,512,1]{2,1,0:T(8,128)}, bf16[128,1024]{1,0:T(8,128)(2,1)}, bf16[128,1024]{1,0:T(8,128)(2,1)}, bf16[...) custom-call(bf16[4,512,64]{2,1,0:T(8,128)(2,1)} %get-tuple-element.238.refs_0_, ...), custom_call_target="tpu_custom_call" | custom-call | flops 805306368 | bytes 4997120 | tf_op jit(solution)/shard_map/pallas_call | solution.py:121
  96.5 13.0 %all-gather.15.cloned.1.call-done = bf16[2048,512]{1,0:T(8,128)(2,1)} async-done(((bf16[512,512]{1,0:T(8,128)(2,1)}), bf16[2048,512]{1,0:T(8,128)(2,1)}) %all-gather.15.cloned.1.call-update) | async-done | bytes 2097168 | tf_op jit(solution)/shard_map/all_gather | solution.py:621
  114.2 10.8 %collective-permute-done.10.refs_5_.refs_4_ = bf16[128,1024]{1,0:T(8,128)(2,1)S(1)} collective-permute-done((bf16[128,1024]{1,0:T(8,128)(2,1)S(1)}, bf16[128,1024]{1,0:T(8,128)(2,1)S(1)}, u32[]{:S(2)}, u32[]{:S(2)}) %collective-permute-start.10) | collective-permute-done | bytes 262176 | tf_op jit(solution)/shard_map/ppermute | solution.py:42
  131.8 8.7 %shard_map.267 = (f32[4,512,256]{2,1,0:T(8,128)}, bf16[4,512,256]{2,1,0:T(8,128)(2,1)}, bf16[128,1024]{1,0:T(8,128)(2,1)}, bf16[128,1024]{1,0:T(8,128)(2,1)}, bf...) custom-call(bf16[4,512,512]{2,1,0:T(8,128)(2,1)} %bitcast.231, bf16[4,512,512]{2,1,0:T(8,128)(2,1)} %collective-permute-done.8.refs_1_, ...), custom_call_target="tpu_custom_call" | custom-call | flops 2147483648 | bytes 9441280 | tf_op jit(solution)/shard_map/pallas_call | solution.py:121
  186.5 10.5 %shard_map.271 = (bf16[4,512,64]{2,1,0:T(8,128)(2,1)}, f32[4,512,1]{2,1,0:T(8,128)}, bf16[128,1024]{1,0:T(8,128)(2,1)}, bf16[128,1024]{1,0:T(8,128)(2,1)}, bf16[...) custom-call(bf16[4,512,64]{2,1,0:T(8,128)(2,1)} %get-tuple-element.290.refs_0_, ...), custom_call_target="tpu_custom_call" | custom-call | flops 805306368 | bytes 4734976 | tf_op jit(solution)/shard_map/pallas_call | solution.py:121
  202.6 6.0 %collective-permute-done.23.refs_3_ = bf16[128,1024]{1,0:T(8,128)(2,1)S(1)} collective-permute-done((bf16[128,1024]{1,0:T(8,128)(2,1)}, bf16[128,1024]{1,0:T(8,128)(2,1)S(1)}, u32[]{:S(2)}, u32[]{:S(2)}) %collective-permute-start.23) | collective-permute-done | bytes 262176 | tf_op jit(solution)/shard_map/ppermute | solution.py:42
  223.1 6.2 %collective-permute-done.28.refs_5_.refs_4_ = bf16[128,1024]{1,0:T(8,128)(2,1)S(1)} collective-permute-done((bf16[128,1024]{1,0:T(8,128)(2,1)S(1)}, bf16[128,1024]{1,0:T(8,128)(2,1)S(1)}, u32[]{:S(2)}, u32[]{:S(2)}) %collective-permute-start.28) | collective-permute-done | bytes 262176 | tf_op jit(solution)/shard_map/ppermute | solution.py:42
  230.2 8.7 %shard_map.273 = (f32[4,512,256]{2,1,0:T(8,128)}, bf16[4,512,256]{2,1,0:T(8,128)(2,1)}, bf16[128,1024]{1,0:T(8,128)(2,1)}, bf16[128,1024]{1,0:T(8,128)(2,1)}, bf...) custom-call(bf16[4,512,512]{2,1,0:T(8,128)(2,1)} %bitcast.234, bf16[4,512,512]{2,1,0:T(8,128)(2,1)} %collective-permute-done.26.refs_1_, ...), custom_call_target="tpu_custom_call" | custom-call | flops 2147483648 | bytes 9441280 | tf_op jit(solution)/shard_map/pallas_call | solution.py:121
  242.4 9.0 %shard_map.274 = (bf16[4,512,256]{2,1,0:T(8,128)(2,1)}, f32[4,1,256]{2,1,0:T(1,128)}, bf16[128,1024]{1,0:T(8,128)(2,1)}, bf16[128,1024]{1,0:T(8,128)(2,1)}, bf16...) custom-call(bf16[4,512,512]{2,1,0:T(8,128)(2,1)} %bitcast.235, bf16[4,512,512]{2,1,0:T(8,128)(2,1)} %collective-permute-done.26.refs_1_, ...), custom_call_target="tpu_custom_call" | custom-call | flops 2147483648 | bytes 9441280 | tf_op jit(solution)/shard_map/pallas_call | solution.py:121
  255.0 6.3 %shard_map.275 = (bf16[4,512,512]{2,1,0:T(8,128)(2,1)}, bf16[4,512,512]{2,1,0:T(8,128)(2,1)}) custom-call(bf16[4,512,256]{2,1,0:T(8,128)(2,1)} %get-tuple-element.321.refs_0_, bf16[4,512,256]{2,1,0:T(8,128)(2,1)} %get-tuple-element.322.refs_1_, bf16[128,1024]{1,0:T(8,128)(2,1)} %copy-done.23, bf16[128,1024]{1,0:T(8,128)(2,1)} %copy-done.73, ...), custom_call_target="tpu_custom_call" | custom-call | flops 2147483648 | bytes 8388608 | tf_op jit(solution)/shard_map/pallas_call | solution.py:121
  276.5 6.3 %collective-permute-done.37.refs_12_.refs_8_ = bf16[128,1024]{1,0:T(8,128)(2,1)S(1)} collective-permute-done((bf16[128,1024]{1,0:T(8,128)(2,1)}, bf16[128,1024]{1,0:T(8,128)(2,1)S(1)}, u32[]{:S(2)}, u32[]{:S(2)}) %collective-permute-start.37) | collective-permute-done | bytes 262176 | tf_op jit(solution)/shard_map/ppermute | solution.py:42
  283.6 12.5 %shard_map.278 = (bf16[4,512,64]{2,1,0:T(8,128)(2,1)}, bf16[4,512,128]{2,1,0:T(8,128)(2,1)}, bf16[4,512,128]{2,1,0:T(8,128)(2,1)}) custom-call(bf16[4,512,64]{2,1,0:T(8,128)(2,1)} %get-tuple-element.290.refs_0_, bf16[4,512,128]{2,1,0:T(8,128)(2,1)} %get-tuple-element.293.refs_1_, bf16[4,512,128]{2,1,0:T(8,128)(2,1)} %copy-done.30, ...), custom_call_target="tpu_custom_call" | custom-call | flops 1610612736 | bytes 6045696 | tf_op jit(solution)/shard_map/pallas_call | solution.py:121
  308.2 6.2 %shard_map.280 = (bf16[4,512,256]{2,1,0:T(8,128)(2,1)}, bf16[4,512,256]{2,1,0:T(8,128)(2,1)}) custom-call(bf16[4,512,192]{2,1,0:T(8,128)(2,1)} %get-tuple-element.350.refs_0_, bf16[4,512,64]{2,1,0:T(8,128)(2,1)} %get-tuple-element.334.refs_5_.refs_1_, bf16[128,1024]{1,0:T(8,128)(2,1)} %copy-done.3, bf16[128,1024]{1,0:T(8,128)(2,1)} %copy-done.41, ...), custom_call_target="tpu_custom_call" | custom-call | flops 1073741824 | bytes 5242880 | tf_op jit(solution)/shard_map/pallas_call | solution.py:121
  333.1 6.5 %collective-permute-done.45.refs_5_.refs_8_ = bf16[128,1024]{1,0:T(8,128)(2,1)S(1)} collective-permute-done((bf16[128,1024]{1,0:T(8,128)(2,1)}, bf16[128,1024]{1,0:T(8,128)(2,1)S(1)}, u32[]{:S(2)}, u32[]{:S(2)}) %collective-permute-start.45) | collective-permute-done | bytes 262176 | tf_op jit(solution)/shard_map/ppermute | solution.py:42
  340.4 9.0 %shard_map.282 = (bf16[4,512,256]{2,1,0:T(8,128)(2,1)}, f32[4,1,256]{2,1,0:T(1,128)}, bf16[128,1024]{1,0:T(8,128)(2,1)}, bf16[128,1024]{1,0:T(8,128)(2,1)}, bf16...) custom-call(bf16[4,512,512]{2,1,0:T(8,128)(2,1)} %bitcast.232, bf16[4,512,512]{2,1,0:T(8,128)(2,1)} %collective-permute-done.8.refs_1_, ...), custom_call_target="tpu_custom_call" | custom-call | flops 2147483648 | bytes 9441280 | tf_op jit(solution)/shard_map/pallas_call | solution.py:121
  353.0 6.4 %shard_map.283 = (bf16[4,512,512]{2,1,0:T(8,128)(2,1)}, bf16[4,512,512]{2,1,0:T(8,128)(2,1)}) custom-call(bf16[4,512,256]{2,1,0:T(8,128)(2,1)} %get-tuple-element.372.refs_0_, bf16[4,512,256]{2,1,0:T(8,128)(2,1)} %get-tuple-element.373.refs_1_, bf16[128,1024]{1,0:T(8,128)(2,1)} %copy-done.22, bf16[128,1024]{1,0:T(8,128)(2,1)} %copy-done.69, ...), custom_call_target="tpu_custom_call" | custom-call | flops 2147483648 | bytes 8388608 | tf_op jit(solution)/shard_map/pallas_call | solution.py:121
  377.0 6.4 %collective-permute-done.52.refs_12_.refs_8_ = bf16[128,1024]{1,0:T(8,128)(2,1)S(1)} collective-permute-done((bf16[128,1024]{1,0:T(8,128)(2,1)S(1)}, bf16[128,1024]{1,0:T(8,128)(2,1)S(1)}, u32[]{:S(2)}, u32[]{:S(2)}) %collective-permute-start.52) | collective-permute-done | bytes 262176 | tf_op jit(solution)/shard_map/ppermute | solution.py:42
  388.1 12.5 %shard_map.285 = (bf16[4,512,64]{2,1,0:T(8,128)(2,1)}, bf16[4,512,128]{2,1,0:T(8,128)(2,1)}, bf16[4,512,128]{2,1,0:T(8,128)(2,1)}) custom-call(bf16[4,512,64]{2,1,0:T(8,128)(2,1)} %get-tuple-element.238.refs_0_, bf16[4,512,128]{2,1,0:T(8,128)(2,1)} %get-tuple-element.240.refs_1_, bf16[4,512,128]{2,1,0:T(8,128)(2,1)} %copy-done.29, ...), custom_call_target="tpu_custom_call" | custom-call | flops 1610612736 | bytes 6307840 | tf_op jit(solution)/shard_map/pallas_call | solution.py:121
  411.1 6.1 %shard_map.289 = (bf16[4,512,256]{2,1,0:T(8,128)(2,1)}, bf16[4,512,256]{2,1,0:T(8,128)(2,1)}) custom-call(bf16[4,512,192]{2,1,0:T(8,128)(2,1)} %get-tuple-element.410.refs_0_, bf16[4,512,64]{2,1,0:T(8,128)(2,1)} %get-tuple-element.242.refs_5_.refs_1_, bf16[128,1024]{1,0:T(8,128)(2,1)} %get-tuple-element.411.refs_2_, ...), custom_call_target="tpu_custom_call" | custom-call | flops 1073741824 | bytes 5242880 | tf_op jit(solution)/shard_map/pallas_call | solution.py:121
  427.4 6.2 %collective-permute-done.57.refs_5_ = bf16[128,1024]{1,0:T(8,128)(2,1)S(1)} collective-permute-done((bf16[128,1024]{1,0:T(8,128)(2,1)}, bf16[128,1024]{1,0:T(8,128)(2,1)S(1)}, u32[]{:S(2)}, u32[]{:S(2)}) %collective-permute-start.57) | collective-permute-done | bytes 262176 | tf_op jit(solution)/shard_map/ppermute | solution.py:42
  440.4 6.1 %all-to-all-done.6 = bf16[4,128,256]{1,2,0:T(8,128)(2,1)S(1)} async-done(((bf16[4,128,256]{1,2,0:T(8,128)(2,1)}), bf16[4,128,256]{1,2,0:T(8,128)(2,1)S(1)}, u32[]{:S(2)}, u32[]{:S(2)}) %all-to-all-start.6) | async-done | bytes 262176 | tf_op jit(solution)/shard_map/all_to_all | solution.py:54
  480.6 5.9 %all-to-all-done.7 = bf16[4,128,512]{2,1,0:T(8,128)(2,1)S(1)} async-done(((bf16[4,128,512]{2,1,0:T(8,128)(2,1)}), bf16[4,128,512]{2,1,0:T(8,128)(2,1)S(1)}, u32[]{:S(2)}, u32[]{:S(2)}) %all-to-all-start.7) | async-done | bytes 524320 | tf_op jit(solution)/shard_map/all_to_all | solution.py:54
  (477 shorter events, 285.8 us)
Async XLA Ops:
  7.3 55.0 %all-gather.13.cloned.1.call-start = ((), (), s32[]{:S(2)}) async-start(), calls=%async_computation.18 | async-start | bytes 1474560 | tf_op jit(solution)/shard_map/all_gather | solution.py:621
  32.0 16.0 %all-to-all-start.1 = ((bf16[4,128,1024]{2,1,0:T(8,128)(2,1)}), bf16[4,128,1024]{2,1,0:T(8,128)(2,1)S(1)}, u32[]{:S(2)}, u32[]{:S(2)}) async-start(bf16[4,128,1024]{2,1,0:T(8,128)(2,1)} %bitcast.193), calls=%async_computation.1 | async-start | bytes 2097152 | tf_op jit(solution)/shard_map/all_to_all | solution.py:54
  35.6 73.9 %all-gather.15.cloned.1.call-start = ((), (), s32[]{:S(2)}) async-start(), calls=%async_computation.19 | async-start | bytes 2621440 | tf_op jit(solution)/shard_map/all_gather | solution.py:621
  76.1 16.5 %all-to-all-start.2 = ((bf16[4,128,768]{1,2,0:T(8,128)(2,1)}), bf16[4,128,768]{1,2,0:T(8,128)(2,1)S(1)}, u32[]{:S(2)}, u32[]{:S(2)}) async-start(bf16[4,128,768]{1,2,0:T(8,128)(2,1)} %pad_maximum_fusion), calls=%async_computation.2 | async-start | bytes 1572864 | tf_op jit(solution)/shard_map/all_to_all | solution.py:54
  79.7 81.4 %all-gather.17.cloned.1.call-start = ((), (), s32[]{:S(2)}) async-start(), calls=%async_computation.20 | async-start | bytes 1310720 | tf_op jit(solution)/shard_map/all_gather | solution.py:621
  92.8 16.6 %collective-permute-start.5 = (bf16[128,1024]{1,0:T(8,128)(2,1)}, bf16[128,1024]{1,0:T(8,128)(2,1)S(1)}, u32[]{:S(2)}, u32[]{:S(2)}) collective-permute-start(bf16[128,1024]{1,0:T(8,128)(2,1)} %get-tuple-element.251), channel_id=1, source_target_pairs={{0,8},{8,0},{16,24},{24,16},{1,9},{9,1},{17,25},{25,17},{2,10},{10... | collective-permute-start | bytes 786440 | tf_op jit(solution)/shard_map/ppermute | solution.py:42
  94.9 14.5 %collective-permute-start.6 = (bf16[128,1024]{1,0:T(8,128)(2,1)}, bf16[128,1024]{1,0:T(8,128)(2,1)S(1)}, u32[]{:S(2)}, u32[]{:S(2)}) collective-permute-start(bf16[128,1024]{1,0:T(8,128)(2,1)} %get-tuple-element.252), channel_id=1, source_target_pairs={{0,16},{8,24},{16,0},{24,8},{1,17},{9,25},{17,1},{25,9},{2,18},{10... | collective-permute-start | bytes 786440 | tf_op jit(solution)/shard_map/ppermute | solution.py:42
  109.5 22.2 %collective-permute-start.8 = (bf16[4,512,512]{2,1,0:T(8,128)(2,1)}, bf16[4,512,512]{2,1,0:T(8,128)(2,1)}, u32[]{:S(2)}, u32[]{:S(2)}) collective-permute-start(bf16[4,512,512]{2,1,0:T(8,128)(2,1)} %bitcast.230), channel_id=1, source_target_pairs={{0,4},{4,0},{1,5},{5,1},{2,6},{6,2},{3,7},{7,3},{8,12},{12,8},{9,1... | collective-permute-start | bytes 6291464 | tf_op jit(solution)/shard_map/ppermute | solution.py:42
  110.7 14.4 %collective-permute-start.10 = (bf16[128,1024]{1,0:T(8,128)(2,1)S(1)}, bf16[128,1024]{1,0:T(8,128)(2,1)S(1)}, u32[]{:S(2)}, u32[]{:S(2)}) collective-permute-start(bf16[128,1024]{1,0:T(8,128)(2,1)S(1)} %get-tuple-element.268.refs_3_.refs_2_), channel_id=1, source_target_pairs={{0,16},{8,24},{16,0},{24,8},{1,17},{9,25},{17,1},{25,9},{2,18},{10... | collective-permute-start | bytes 786440 | tf_op jit(solution)/shard_map/ppermute | solution.py:42
  126.3 19.1 %all-to-all-start.3 = ((bf16[4,128,1024]{2,1,0:T(8,128)(2,1)}), bf16[4,128,1024]{2,1,0:T(8,128)(2,1)}, u32[]{:S(2)}, u32[]{:S(2)}) async-start(bf16[4,128,1024]{2,1,0:T(8,128)(2,1)} %bitcast.194), calls=%async_computation.3 | async-start | bytes 2097152 | tf_op jit(solution)/shard_map/all_to_all | solution.py:54
  130.6 72.0 %all-gather.19.cloned.1.call-start = ((), (), s32[]{:S(2)}) async-start(), calls=%async_computation.21 | async-start | bytes 2621440 | tf_op jit(solution)/shard_map/all_gather | solution.py:621
  131.5 182.9 %all-gather.21.cloned.1.call-start = ((), (), s32[]{:S(2)}) async-start(), calls=%async_computation.22 | async-start | bytes 1310720 | tf_op jit(solution)/shard_map/all_gather | solution.py:621
  212.6 16.7 %collective-permute-start.26 = (bf16[4,512,512]{2,1,0:T(8,128)(2,1)}, bf16[4,512,512]{2,1,0:T(8,128)(2,1)}, u32[]{:S(2)}, u32[]{:S(2)}) collective-permute-start(bf16[4,512,512]{2,1,0:T(8,128)(2,1)} %bitcast.233), channel_id=1, source_target_pairs={{0,4},{4,0},{1,5},{5,1},{2,6},{6,2},{3,7},{7,3},{8,12},{12,8},{9,1... | collective-permute-start | bytes 6291464 | tf_op jit(solution)/shard_map/ppermute | solution.py:42
  238.9 14.6 %collective-permute-start.33 = (bf16[128,1024]{1,0:T(8,128)(2,1)}, bf16[128,1024]{1,0:T(8,128)(2,1)S(1)}, u32[]{:S(2)}, u32[]{:S(2)}) collective-permute-start(bf16[128,1024]{1,0:T(8,128)(2,1)} %get-tuple-element.326), channel_id=1, source_target_pairs={{0,8},{8,0},{16,24},{24,16},{1,9},{9,1},{17,25},{25,17},{2,10},{10... | collective-permute-start | bytes 786440 | tf_op jit(solution)/shard_map/ppermute | solution.py:42
  239.7 21.6 %collective-permute-start.34 = (bf16[128,1024]{1,0:T(8,128)(2,1)}, bf16[128,1024]{1,0:T(8,128)(2,1)S(1)}, u32[]{:S(2)}, u32[]{:S(2)}) collective-permute-start(bf16[128,1024]{1,0:T(8,128)(2,1)} %get-tuple-element.327), channel_id=1, source_target_pairs={{0,16},{8,24},{16,0},{24,8},{1,17},{9,25},{17,1},{25,9},{2,18},{10... | collective-permute-start | bytes 786440 | tf_op jit(solution)/shard_map/ppermute | solution.py:42
  240.9 20.4 %collective-permute-start.35 = (bf16[128,1024]{1,0:T(8,128)(2,1)}, bf16[128,1024]{1,0:T(8,128)(2,1)S(1)}, u32[]{:S(2)}, u32[]{:S(2)}) collective-permute-start(bf16[128,1024]{1,0:T(8,128)(2,1)} %get-tuple-element.328), channel_id=1, source_target_pairs={{0,24},{8,16},{16,8},{24,0},{1,25},{9,17},{17,9},{25,1},{2,26},{10... | collective-permute-start | bytes 786440 | tf_op jit(solution)/shard_map/ppermute | solution.py:42
  264.6 75.0 %reduce-scatter.5.cloned.1.call-start = ((), (), s32[]{:S(2)}) async-start(), calls=%async_computation.14 | async-start | bytes 2621440 | tf_op jit(solution)/shard_map/reduce_scatter | solution.py:755
  282.8 83.5 %reduce-scatter.7.cloned.1.call-start = ((), (), s32[]{:S(2)}) async-start(), calls=%async_computation.15 | async-start | bytes 1310720 | tf_op jit(solution)/shard_map/reduce_scatter | solution.py:755
  325.3 14.3 %collective-permute-start.45 = (bf16[128,1024]{1,0:T(8,128)(2,1)}, bf16[128,1024]{1,0:T(8,128)(2,1)S(1)}, u32[]{:S(2)}, u32[]{:S(2)}) collective-permute-start(bf16[128,1024]{1,0:T(8,128)(2,1)} %get-tuple-element.364.refs_3_.refs_6_), channel_id=1, source_target_pairs={{0,16},{8,24},{16,0},{24,8},{1,17},{9,25},{17,1},{25,9},{2,18},{10... | collective-permute-start | bytes 786440 | tf_op jit(solution)/shard_map/ppermute | solution.py:42
  339.6 93.9 %reduce-scatter.9.cloned.1.call-start = ((), (), s32[]{:S(2)}) async-start(), calls=%async_computation.16 | async-start | bytes 2621440 | tf_op jit(solution)/shard_map/reduce_scatter | solution.py:755
  384.2 17.0 %all-to-all-start.4 = ((bf16[4,128,1024]{2,1,0:T(8,128)(2,1)}), bf16[4,128,1024]{2,1,0:T(8,128)(2,1)S(1)}, u32[]{:S(2)}, u32[]{:S(2)}) async-start(bf16[4,128,1024]{2,1,0:T(8,128)(2,1)} %bitcast.195), calls=%async_computation.6 | async-start | bytes 2097152 | tf_op jit(solution)/shard_map/all_to_all | solution.py:54
  387.8 67.2 %reduce-scatter.11.cloned.1.call-start = ((), (), s32[]{:S(2)}) async-start(), calls=%async_computation.17 | async-start | bytes 1310720 | tf_op jit(solution)/shard_map/reduce_scatter | solution.py:755
  450.0 36.6 %all-gather.23.cloned.1.call-start = ((), (), s32[]{:S(2)}) async-start(), calls=%async_computation.23 | async-start | bytes 1310720 | tf_op jit(solution)/shard_map/all_gather | solution.py:621
  486.6 15.2 %all-to-all-start.9 = ((bf16[4,128,1024]{2,1,0:T(8,128)(2,1)}), bf16[4,128,1024]{2,1,0:T(8,128)(2,1)S(1)}, u32[]{:S(2)}, u32[]{:S(2)}) async-start(bf16[4,128,1024]{2,1,0:T(8,128)(2,1)} %bitcast.196), calls=%async_computation.13 | async-start | bytes 2097152 | tf_op jit(solution)/shard_map/all_to_all | solution.py:54
  (145 other events, 1183.4 us)
Sparse Core Ops, SparseCore 0:
  32.1 30.0 all-gather.12
  64.4 45.0 all-gather.14
  111.0 26.6 all-gather.16
  139.2 45.3 all-gather.18
  264.7 27.1 all-gather.20
  294.0 43.3 reduce-scatter.4
  339.8 26.4 reduce-scatter.6
  383.6 41.6 reduce-scatter.8
  428.2 26.6 reduce-scatter.10
  458.4 26.0 all-gather.22

commit v10 on v9

--- a/solution.py
+++ b/solution.py
@@ -568,7 +568,7 @@
         in_specs=[block] * n_s + [whole(turn.shape)],
         out_specs=[whole(item.shape) for item in shapes],
         out_shape=shapes,
-        compiler_params=pltpu.CompilerParams(vmem_limit_bytes=VMEM_LIMIT),
+        compiler_params=pltpu.CompilerParams(vmem_limit_bytes=SMALL_LIMIT),
     )(*planes, turn)
     return out[0], out[1 : 1 + layers], out[1 + layers :]
 

time: 520 us -> 528 us (1.015)
  local copies, waits for them, and re-layouts: 38.3 us -> 52.7 us
  waiting for transfers between devices: 184 us -> 176 us
    unnamed x167 -> x175, local copies, waits for them, and re-layouts: 19.7 us -> 24.7 us
  transfers between devices with their start and end apart: 86 -> 86, of which waited for: 45 -> 43; matrix products, arithmetic and copies ran while one was open for 6% -> 9% of each run, Pallas kernels for 25% -> 25%
where the time goes in v10:
time: 528 us; the launch traced here: 520 us
  waiting for transfers between devices  176 us (33%)
  Pallas kernels  137 us (26%)
  starting transfers between devices  98.8 us (19%)
  local copies, waits for them, and re-layouts  52.7 us (10%)
  other arithmetic  22.3 us (4%)
  blocking collectives  17.4 us (3%)
  between operations  15.9 us (3%)
    pallas_call x27, Pallas kernels, run(): pl.pallas_call(kernel, grid=(steps,), in_specs=[each(item) for item in ea...  137 us
    ppermute x67, waiting for transfers between devices, swap(): return lax.ppermute(array, name, [(i, i ^ step) for i in range(size)])  128 us
    ppermute x67, starting transfers between devices, swap(): return lax.ppermute(array, name, [(i, i ^ step) for i in range(size)])  65.7 us
    all_to_all x9, waiting for transfers between devices, exchange(): return lax.all_to_all(array, name, 0, 0, tiled=True)  33.3 us
    all_to_all x9, starting transfers between devices, exchange(): return lax.all_to_all(array, name, 0, 0, tiled=True)  32.1 us
    unnamed x175, local copies, waits for them, and re-layouts  24.7 us
    all_to_all x1, blocking collectives, exchange(): return lax.all_to_all(array, name, 0, 0, tiled=True)  17.4 us
    all_gather x6, waiting for transfers between devices, to_planes_of(): return lax.all_gather(array, HEAD, axis=0, tiled=False)  11.2 us
  transfers between devices with their start and end apart: 86, of which 43 were waited for; matrix products, arithmetic and copies ran while one was open for 9% of the time, Pallas kernels for 25%

profile of v10, /device:TPU:0, one launch (start us, length us, event | category | flops | bytes accessed | tf_op | source)
XLA Modules:
  0.0 519.6 jit_solution(607197079974855733)
XLA Ops:
  13.8 17.4 %all_to_all.50 = bf16[4,144,768]{2,1,0:T(8,128)(2,1)S(1)} all-to-all(bf16[4,144,768]{2,1,0:T(8,128)(2,1)S(1)} %copy.147), channel_id=1, replica_groups=mesh['dp'=4,'seq'=2,'head'=4] {'dp'}, dimensions={0} | all-to-all | bytes 1769472 | tf_op jit(solution)/shard_map/all_to_all | solution.py:54
  35.6 12.4 %all-to-all-done.1 = bf16[4,128,1024]{2,1,0:T(8,128)(2,1)S(1)} async-done(((bf16[4,128,1024]{2,1,0:T(8,128)(2,1)}), bf16[4,128,1024]{2,1,0:T(8,128)(2,1)S(1)}, u32[]{:S(2)}, u32[]{:S(2)}) %all-to-all-start.1) | async-done | bytes 1048608 | tf_op jit(solution)/shard_map/all_to_all | solution.py:54
  70.1 5.8 %shard_map.264 = (bf16[4,512,64]{2,1,0:T(8,128)(2,1)}, bf16[4,512,128]{2,1,0:T(8,128)(2,1)}, bf16[128,1024]{1,0:T(8,128)(2,1)}, bf16[128,1024]{1,0:T(8,128)(2,1)...) custom-call(bf16[4,576,256]{2,1,0:T(8,128)(2,1)} %bitcast.174, bf16[4,576,256]{2,1,0:T(8,128)(2,1)} %copy-done.1, ...), custom_call_target="tpu_custom_call" | custom-call | flops 805306368 | bytes 5311488 | tf_op jit(solution)/shard_map/pallas_call | solution.py:121
  83.9 10.5 %shard_map.265 = (bf16[4,512,64]{2,1,0:T(8,128)(2,1)}, f32[4,512,1]{2,1,0:T(8,128)}, bf16[128,1024]{1,0:T(8,128)(2,1)}, bf16[128,1024]{1,0:T(8,128)(2,1)}, bf16[...) custom-call(bf16[4,512,64]{2,1,0:T(8,128)(2,1)} %get-tuple-element.238.refs_0_, ...), custom_call_target="tpu_custom_call" | custom-call | flops 805306368 | bytes 4997120 | tf_op jit(solution)/shard_map/pallas_call | solution.py:121
  98.3 11.2 %all-gather.15.cloned.1.call-done = bf16[2048,512]{1,0:T(8,128)(2,1)} async-done(((bf16[512,512]{1,0:T(8,128)(2,1)}), bf16[2048,512]{1,0:T(8,128)(2,1)}) %all-gather.15.cloned.1.call-update) | async-done | bytes 2097168 | tf_op jit(solution)/shard_map/all_gather | solution.py:621
  115.1 10.8 %collective-permute-done.10.refs_5_.refs_4_ = bf16[128,1024]{1,0:T(8,128)(2,1)S(1)} collective-permute-done((bf16[128,1024]{1,0:T(8,128)(2,1)S(1)}, bf16[128,1024]{1,0:T(8,128)(2,1)S(1)}, u32[]{:S(2)}, u32[]{:S(2)}) %collective-permute-start.10) | collective-permute-done | bytes 262176 | tf_op jit(solution)/shard_map/ppermute | solution.py:42
  132.6 8.7 %shard_map.267 = (f32[4,512,256]{2,1,0:T(8,128)}, bf16[4,512,256]{2,1,0:T(8,128)(2,1)}, bf16[128,1024]{1,0:T(8,128)(2,1)}, bf16[128,1024]{1,0:T(8,128)(2,1)}, bf...) custom-call(bf16[4,512,512]{2,1,0:T(8,128)(2,1)} %bitcast.231, bf16[4,512,512]{2,1,0:T(8,128)(2,1)} %collective-permute-done.8.refs_1_, ...), custom_call_target="tpu_custom_call" | custom-call | flops 2147483648 | bytes 9441280 | tf_op jit(solution)/shard_map/pallas_call | solution.py:121
  162.0 5.8 %collective-permute-done.15.refs_4_.refs_3_ = bf16[128,1024]{1,0:T(8,128)(2,1)S(1)} collective-permute-done((bf16[128,1024]{1,0:T(8,128)(2,1)S(1)}, bf16[128,1024]{1,0:T(8,128)(2,1)S(1)}, u32[]{:S(2)}, u32[]{:S(2)}) %collective-permute-start.15) | collective-permute-done | bytes 262176 | tf_op jit(solution)/shard_map/ppermute | solution.py:42
  187.3 10.5 %shard_map.271 = (bf16[4,512,64]{2,1,0:T(8,128)(2,1)}, f32[4,512,1]{2,1,0:T(8,128)}, bf16[128,1024]{1,0:T(8,128)(2,1)}, bf16[128,1024]{1,0:T(8,128)(2,1)}, bf16[...) custom-call(bf16[4,512,64]{2,1,0:T(8,128)(2,1)} %get-tuple-element.290.refs_0_, ...), custom_call_target="tpu_custom_call" | custom-call | flops 805306368 | bytes 4734976 | tf_op jit(solution)/shard_map/pallas_call | solution.py:121
  202.8 6.0 %collective-permute-done.23.refs_3_ = bf16[128,1024]{1,0:T(8,128)(2,1)S(1)} collective-permute-done((bf16[128,1024]{1,0:T(8,128)(2,1)}, bf16[128,1024]{1,0:T(8,128)(2,1)S(1)}, u32[]{:S(2)}, u32[]{:S(2)}) %collective-permute-start.23) | collective-permute-done | bytes 262176 | tf_op jit(solution)/shard_map/ppermute | solution.py:42
  230.3 8.7 %shard_map.273 = (f32[4,512,256]{2,1,0:T(8,128)}, bf16[4,512,256]{2,1,0:T(8,128)(2,1)}, bf16[128,1024]{1,0:T(8,128)(2,1)}, bf16[128,1024]{1,0:T(8,128)(2,1)}, bf...) custom-call(bf16[4,512,512]{2,1,0:T(8,128)(2,1)} %bitcast.234, bf16[4,512,512]{2,1,0:T(8,128)(2,1)} %collective-permute-done.26.refs_1_, ...), custom_call_target="tpu_custom_call" | custom-call | flops 2147483648 | bytes 9441280 | tf_op jit(solution)/shard_map/pallas_call | solution.py:121
  242.6 9.0 %shard_map.274 = (bf16[4,512,256]{2,1,0:T(8,128)(2,1)}, f32[4,1,256]{2,1,0:T(1,128)}, bf16[128,1024]{1,0:T(8,128)(2,1)}, bf16[128,1024]{1,0:T(8,128)(2,1)}, bf16...) custom-call(bf16[4,512,512]{2,1,0:T(8,128)(2,1)} %bitcast.235, bf16[4,512,512]{2,1,0:T(8,128)(2,1)} %collective-permute-done.26.refs_1_, ...), custom_call_target="tpu_custom_call" | custom-call | flops 2147483648 | bytes 9441280 | tf_op jit(solution)/shard_map/pallas_call | solution.py:121
  255.1 6.3 %shard_map.275 = (bf16[4,512,512]{2,1,0:T(8,128)(2,1)}, bf16[4,512,512]{2,1,0:T(8,128)(2,1)}) custom-call(bf16[4,512,256]{2,1,0:T(8,128)(2,1)} %get-tuple-element.321.refs_0_, bf16[4,512,256]{2,1,0:T(8,128)(2,1)} %get-tuple-element.322.refs_1_, bf16[128,1024]{1,0:T(8,128)(2,1)} %copy-done.28, bf16[128,1024]{1,0:T(8,128)(2,1)} %copy-done.77, ...), custom_call_target="tpu_custom_call" | custom-call | flops 2147483648 | bytes 8388608 | tf_op jit(solution)/shard_map/pallas_call | solution.py:121
  278.1 5.8 %collective-permute-done.37.refs_12_.refs_8_ = bf16[128,1024]{1,0:T(8,128)(2,1)S(1)} collective-permute-done((bf16[128,1024]{1,0:T(8,128)(2,1)}, bf16[128,1024]{1,0:T(8,128)(2,1)S(1)}, u32[]{:S(2)}, u32[]{:S(2)}) %collective-permute-start.37) | collective-permute-done | bytes 262176 | tf_op jit(solution)/shard_map/ppermute | solution.py:42
  284.7 12.5 %shard_map.278 = (bf16[4,512,64]{2,1,0:T(8,128)(2,1)}, bf16[4,512,128]{2,1,0:T(8,128)(2,1)}, bf16[4,512,128]{2,1,0:T(8,128)(2,1)}) custom-call(bf16[4,512,64]{2,1,0:T(8,128)(2,1)} %get-tuple-element.290.refs_0_, bf16[4,512,128]{2,1,0:T(8,128)(2,1)} %get-tuple-element.293.refs_1_, bf16[4,512,128]{2,1,0:T(8,128)(2,1)} %copy-done.34, ...), custom_call_target="tpu_custom_call" | custom-call | flops 1610612736 | bytes 6045696 | tf_op jit(solution)/shard_map/pallas_call | solution.py:121
  309.2 6.1 %shard_map.280 = (bf16[4,512,256]{2,1,0:T(8,128)(2,1)}, bf16[4,512,256]{2,1,0:T(8,128)(2,1)}) custom-call(bf16[4,512,192]{2,1,0:T(8,128)(2,1)} %get-tuple-element.350.refs_0_, bf16[4,512,64]{2,1,0:T(8,128)(2,1)} %get-tuple-element.334.refs_5_.refs_1_, bf16[128,1024]{1,0:T(8,128)(2,1)} %copy-done.6, bf16[128,1024]{1,0:T(8,128)(2,1)} %copy-done.46, ...), custom_call_target="tpu_custom_call" | custom-call | flops 1073741824 | bytes 5242880 | tf_op jit(solution)/shard_map/pallas_call | solution.py:121
  341.1 9.1 %shard_map.282 = (bf16[4,512,256]{2,1,0:T(8,128)(2,1)}, f32[4,1,256]{2,1,0:T(1,128)}, bf16[128,1024]{1,0:T(8,128)(2,1)}, bf16[128,1024]{1,0:T(8,128)(2,1)}, bf16...) custom-call(bf16[4,512,512]{2,1,0:T(8,128)(2,1)} %bitcast.232, bf16[4,512,512]{2,1,0:T(8,128)(2,1)} %collective-permute-done.8.refs_1_, ...), custom_call_target="tpu_custom_call" | custom-call | flops 2147483648 | bytes 9441280 | tf_op jit(solution)/shard_map/pallas_call | solution.py:121
  353.7 6.4 %shard_map.283 = (bf16[4,512,512]{2,1,0:T(8,128)(2,1)}, bf16[4,512,512]{2,1,0:T(8,128)(2,1)}) custom-call(bf16[4,512,256]{2,1,0:T(8,128)(2,1)} %get-tuple-element.372.refs_0_, bf16[4,512,256]{2,1,0:T(8,128)(2,1)} %get-tuple-element.373.refs_1_, bf16[128,1024]{1,0:T(8,128)(2,1)} %copy-done.27, bf16[128,1024]{1,0:T(8,128)(2,1)} %copy-done.73, ...), custom_call_target="tpu_custom_call" | custom-call | flops 2147483648 | bytes 8388608 | tf_op jit(solution)/shard_map/pallas_call | solution.py:121
  378.9 6.4 %collective-permute-done.52.refs_12_.refs_8_ = bf16[128,1024]{1,0:T(8,128)(2,1)S(1)} collective-permute-done((bf16[128,1024]{1,0:T(8,128)(2,1)S(1)}, bf16[128,1024]{1,0:T(8,128)(2,1)S(1)}, u32[]{:S(2)}, u32[]{:S(2)}) %collective-permute-start.52) | collective-permute-done | bytes 262176 | tf_op jit(solution)/shard_map/ppermute | solution.py:42
  390.0 12.5 %shard_map.285 = (bf16[4,512,64]{2,1,0:T(8,128)(2,1)}, bf16[4,512,128]{2,1,0:T(8,128)(2,1)}, bf16[4,512,128]{2,1,0:T(8,128)(2,1)}) custom-call(bf16[4,512,64]{2,1,0:T(8,128)(2,1)} %get-tuple-element.238.refs_0_, bf16[4,512,128]{2,1,0:T(8,128)(2,1)} %get-tuple-element.240.refs_1_, bf16[4,512,128]{2,1,0:T(8,128)(2,1)} %copy-done.33, ...), custom_call_target="tpu_custom_call" | custom-call | flops 1610612736 | bytes 6307840 | tf_op jit(solution)/shard_map/pallas_call | solution.py:121
  414.1 6.2 %shard_map.289 = (bf16[4,512,256]{2,1,0:T(8,128)(2,1)}, bf16[4,512,256]{2,1,0:T(8,128)(2,1)}) custom-call(bf16[4,512,192]{2,1,0:T(8,128)(2,1)} %get-tuple-element.410.refs_0_, bf16[4,512,64]{2,1,0:T(8,128)(2,1)} %get-tuple-element.242.refs_5_.refs_1_, bf16[128,1024]{1,0:T(8,128)(2,1)} %get-tuple-element.411.refs_2_, ...), custom_call_target="tpu_custom_call" | custom-call | flops 1073741824 | bytes 5242880 | tf_op jit(solution)/shard_map/pallas_call | solution.py:121
  430.7 5.9 %collective-permute-done.57.refs_5_ = bf16[128,1024]{1,0:T(8,128)(2,1)S(1)} collective-permute-done((bf16[128,1024]{1,0:T(8,128)(2,1)}, bf16[128,1024]{1,0:T(8,128)(2,1)S(1)}, u32[]{:S(2)}, u32[]{:S(2)}) %collective-permute-start.57) | collective-permute-done | bytes 262176 | tf_op jit(solution)/shard_map/ppermute | solution.py:42
  445.1 6.1 %all-to-all-done.6 = bf16[4,128,256]{1,2,0:T(8,128)(2,1)S(1)} async-done(((bf16[4,128,256]{1,2,0:T(8,128)(2,1)}), bf16[4,128,256]{1,2,0:T(8,128)(2,1)S(1)}, u32[]{:S(2)}, u32[]{:S(2)}) %all-to-all-start.6) | async-done | bytes 262176 | tf_op jit(solution)/shard_map/all_to_all | solution.py:54
  486.0 5.9 %all-to-all-done.7 = bf16[4,128,512]{2,1,0:T(8,128)(2,1)S(1)} async-done(((bf16[4,128,512]{2,1,0:T(8,128)(2,1)}), bf16[4,128,512]{2,1,0:T(8,128)(2,1)S(1)}, u32[]{:S(2)}, u32[]{:S(2)}) %all-to-all-start.7) | async-done | bytes 524320 | tf_op jit(solution)/shard_map/all_to_all | solution.py:54
  (484 shorter events, 297.8 us)
Async XLA Ops:
  7.3 55.6 %all-gather.13.cloned.1.call-start = ((), (), s32[]{:S(2)}) async-start(), calls=%async_computation.18 | async-start | bytes 1474560 | tf_op jit(solution)/shard_map/all_gather | solution.py:621
  32.0 16.0 %all-to-all-start.1 = ((bf16[4,128,1024]{2,1,0:T(8,128)(2,1)}), bf16[4,128,1024]{2,1,0:T(8,128)(2,1)S(1)}, u32[]{:S(2)}, u32[]{:S(2)}) async-start(bf16[4,128,1024]{2,1,0:T(8,128)(2,1)} %bitcast.192), calls=%async_computation.1 | async-start | bytes 2097152 | tf_op jit(solution)/shard_map/all_to_all | solution.py:54
  35.6 73.9 %all-gather.15.cloned.1.call-start = ((), (), s32[]{:S(2)}) async-start(), calls=%async_computation.19 | async-start | bytes 2621440 | tf_op jit(solution)/shard_map/all_gather | solution.py:621
  78.1 16.3 %all-to-all-start.2 = ((bf16[4,128,768]{1,2,0:T(8,128)(2,1)}), bf16[4,128,768]{1,2,0:T(8,128)(2,1)S(1)}, u32[]{:S(2)}, u32[]{:S(2)}) async-start(bf16[4,128,768]{1,2,0:T(8,128)(2,1)} %pad_maximum_fusion), calls=%async_computation.2 | async-start | bytes 1572864 | tf_op jit(solution)/shard_map/all_to_all | solution.py:54
  81.6 80.4 %all-gather.17.cloned.1.call-start = ((), (), s32[]{:S(2)}) async-start(), calls=%async_computation.20 | async-start | bytes 1310720 | tf_op jit(solution)/shard_map/all_gather | solution.py:621
  94.7 14.8 %collective-permute-start.5 = (bf16[128,1024]{1,0:T(8,128)(2,1)}, bf16[128,1024]{1,0:T(8,128)(2,1)S(1)}, u32[]{:S(2)}, u32[]{:S(2)}) collective-permute-start(bf16[128,1024]{1,0:T(8,128)(2,1)} %get-tuple-element.251), channel_id=1, source_target_pairs={{0,8},{8,0},{16,24},{24,16},{1,9},{9,1},{17,25},{25,17},{2,10},{10... | collective-permute-start | bytes 786440 | tf_op jit(solution)/shard_map/ppermute | solution.py:42
  110.4 22.2 %collective-permute-start.8 = (bf16[4,512,512]{2,1,0:T(8,128)(2,1)}, bf16[4,512,512]{2,1,0:T(8,128)(2,1)}, u32[]{:S(2)}, u32[]{:S(2)}) collective-permute-start(bf16[4,512,512]{2,1,0:T(8,128)(2,1)} %bitcast.230), channel_id=1, source_target_pairs={{0,4},{4,0},{1,5},{5,1},{2,6},{6,2},{3,7},{7,3},{8,12},{12,8},{9,1... | collective-permute-start | bytes 6291464 | tf_op jit(solution)/shard_map/ppermute | solution.py:42
  111.5 14.4 %collective-permute-start.10 = (bf16[128,1024]{1,0:T(8,128)(2,1)S(1)}, bf16[128,1024]{1,0:T(8,128)(2,1)S(1)}, u32[]{:S(2)}, u32[]{:S(2)}) collective-permute-start(bf16[128,1024]{1,0:T(8,128)(2,1)S(1)} %get-tuple-element.268.refs_3_.refs_2_), channel_id=1, source_target_pairs={{0,16},{8,24},{16,0},{24,8},{1,17},{9,25},{17,1},{25,9},{2,18},{10... | collective-permute-start | bytes 786440 | tf_op jit(solution)/shard_map/ppermute | solution.py:42
  127.1 19.1 %all-to-all-start.3 = ((bf16[4,128,1024]{2,1,0:T(8,128)(2,1)}), bf16[4,128,1024]{2,1,0:T(8,128)(2,1)}, u32[]{:S(2)}, u32[]{:S(2)}) async-start(bf16[4,128,1024]{2,1,0:T(8,128)(2,1)} %bitcast.193), calls=%async_computation.3 | async-start | bytes 2097152 | tf_op jit(solution)/shard_map/all_to_all | solution.py:54
  131.4 71.4 %all-gather.19.cloned.1.call-start = ((), (), s32[]{:S(2)}) async-start(), calls=%async_computation.21 | async-start | bytes 2621440 | tf_op jit(solution)/shard_map/all_gather | solution.py:621
  132.3 183.0 %all-gather.21.cloned.1.call-start = ((), (), s32[]{:S(2)}) async-start(), calls=%async_computation.22 | async-start | bytes 1310720 | tf_op jit(solution)/shard_map/all_gather | solution.py:621
  213.3 16.2 %collective-permute-start.26 = (bf16[4,512,512]{2,1,0:T(8,128)(2,1)}, bf16[4,512,512]{2,1,0:T(8,128)(2,1)}, u32[]{:S(2)}, u32[]{:S(2)}) collective-permute-start(bf16[4,512,512]{2,1,0:T(8,128)(2,1)} %bitcast.233), channel_id=1, source_target_pairs={{0,4},{4,0},{1,5},{5,1},{2,6},{6,2},{3,7},{7,3},{8,12},{12,8},{9,1... | collective-permute-start | bytes 6291464 | tf_op jit(solution)/shard_map/ppermute | solution.py:42
  239.0 14.6 %collective-permute-start.33 = (bf16[128,1024]{1,0:T(8,128)(2,1)}, bf16[128,1024]{1,0:T(8,128)(2,1)S(1)}, u32[]{:S(2)}, u32[]{:S(2)}) collective-permute-start(bf16[128,1024]{1,0:T(8,128)(2,1)} %get-tuple-element.326), channel_id=1, source_target_pairs={{0,8},{8,0},{16,24},{24,16},{1,9},{9,1},{17,25},{25,17},{2,10},{10... | collective-permute-start | bytes 786440 | tf_op jit(solution)/shard_map/ppermute | solution.py:42
  240.4 21.1 %collective-permute-start.34 = (bf16[128,1024]{1,0:T(8,128)(2,1)}, bf16[128,1024]{1,0:T(8,128)(2,1)S(1)}, u32[]{:S(2)}, u32[]{:S(2)}) collective-permute-start(bf16[128,1024]{1,0:T(8,128)(2,1)} %get-tuple-element.327), channel_id=1, source_target_pairs={{0,16},{8,24},{16,0},{24,8},{1,17},{9,25},{17,1},{25,9},{2,18},{10... | collective-permute-start | bytes 786440 | tf_op jit(solution)/shard_map/ppermute | solution.py:42
  241.1 20.4 %collective-permute-start.35 = (bf16[128,1024]{1,0:T(8,128)(2,1)}, bf16[128,1024]{1,0:T(8,128)(2,1)S(1)}, u32[]{:S(2)}, u32[]{:S(2)}) collective-permute-start(bf16[128,1024]{1,0:T(8,128)(2,1)} %get-tuple-element.328), channel_id=1, source_target_pairs={{0,24},{8,16},{16,8},{24,0},{1,25},{9,17},{17,9},{25,1},{2,26},{10... | collective-permute-start | bytes 786440 | tf_op jit(solution)/shard_map/ppermute | solution.py:42
  265.3 75.1 %reduce-scatter.5.cloned.1.call-start = ((), (), s32[]{:S(2)}) async-start(), calls=%async_computation.14 | async-start | bytes 2621440 | tf_op jit(solution)/shard_map/reduce_scatter | solution.py:755
  269.6 14.3 %collective-permute-start.37 = (bf16[128,1024]{1,0:T(8,128)(2,1)}, bf16[128,1024]{1,0:T(8,128)(2,1)S(1)}, u32[]{:S(2)}, u32[]{:S(2)}) collective-permute-start(bf16[128,1024]{1,0:T(8,128)(2,1)} %get-tuple-element.339.refs_10_.refs_6_), channel_id=1, source_target_pairs={{0,16},{8,24},{16,0},{24,8},{1,17},{9,25},{17,1},{25,9},{2,18},{10... | collective-permute-start | bytes 786440 | tf_op jit(solution)/shard_map/ppermute | solution.py:42
  283.9 84.3 %reduce-scatter.7.cloned.1.call-start = ((), (), s32[]{:S(2)}) async-start(), calls=%async_computation.15 | async-start | bytes 1310720 | tf_op jit(solution)/shard_map/reduce_scatter | solution.py:755
  340.4 96.1 %reduce-scatter.9.cloned.1.call-start = ((), (), s32[]{:S(2)}) async-start(), calls=%async_computation.16 | async-start | bytes 2621440 | tf_op jit(solution)/shard_map/reduce_scatter | solution.py:755
  371.3 14.1 %collective-permute-start.52 = (bf16[128,1024]{1,0:T(8,128)(2,1)S(1)}, bf16[128,1024]{1,0:T(8,128)(2,1)S(1)}, u32[]{:S(2)}, u32[]{:S(2)}) collective-permute-start(bf16[128,1024]{1,0:T(8,128)(2,1)S(1)} %get-tuple-element.385.refs_10_.refs_6_), channel_id=1, source_target_pairs={{0,16},{8,24},{16,0},{24,8},{1,17},{9,25},{17,1},{25,9},{2,18},{10... | collective-permute-start | bytes 786440 | tf_op jit(solution)/shard_map/ppermute | solution.py:42
  386.2 17.0 %all-to-all-start.4 = ((bf16[4,128,1024]{2,1,0:T(8,128)(2,1)}), bf16[4,128,1024]{2,1,0:T(8,128)(2,1)S(1)}, u32[]{:S(2)}, u32[]{:S(2)}) async-start(bf16[4,128,1024]{2,1,0:T(8,128)(2,1)} %bitcast.194), calls=%async_computation.6 | async-start | bytes 2097152 | tf_op jit(solution)/shard_map/all_to_all | solution.py:54
  389.7 69.5 %reduce-scatter.11.cloned.1.call-start = ((), (), s32[]{:S(2)}) async-start(), calls=%async_computation.17 | async-start | bytes 1310720 | tf_op jit(solution)/shard_map/reduce_scatter | solution.py:755
  454.7 37.2 %all-gather.23.cloned.1.call-start = ((), (), s32[]{:S(2)}) async-start(), calls=%async_computation.23 | async-start | bytes 1310720 | tf_op jit(solution)/shard_map/all_gather | solution.py:621
  491.9 17.9 %all-to-all-start.9 = ((bf16[4,128,1024]{2,1,0:T(8,128)(2,1)}), bf16[4,128,1024]{2,1,0:T(8,128)(2,1)S(1)}, u32[]{:S(2)}, u32[]{:S(2)}) async-start(bf16[4,128,1024]{2,1,0:T(8,128)(2,1)} %bitcast.195), calls=%async_computation.13 | async-start | bytes 2097152 | tf_op jit(solution)/shard_map/all_to_all | solution.py:54
  (148 other events, 1133.7 us)
Sparse Core Ops, SparseCore 0:
  32.1 30.0 all-gather.12
  64.4 45.0 all-gather.14
  111.2 28.3 all-gather.16
  141.0 45.3 all-gather.18
  265.4 28.3 all-gather.20
  295.9 43.3 reduce-scatter.4
  341.7 26.4 reduce-scatter.6
  385.5 41.6 reduce-scatter.8
  430.1 26.4 reduce-scatter.10
  463.0 26.0 all-gather.22
